TPU v7x, 32 devices: a whole 2x2x4 slice. The times are simulated.
32 devices in a mesh: head: 4 (over y, core), blk: 8 (over z, x).
Axes of the slice: x: 2, y: 2, z: 4, core: 2. Of those that a mesh axis runs over, the one named last changes fastest.
Arguments:
- tokens: bfloat16 [48, 512, 1024], P('blk', 'head'), may hold values from -6 to 6
- wq: bfloat16 [1024, 1024], P(('head', 'blk')), may hold values from -0.1875 to 0.1875
- wk: bfloat16 [1024, 1024], P(('head', 'blk')), may hold values from -0.1875 to 0.1875
- wv: bfloat16 [1024, 1024], P(('head', 'blk')), may hold values from -0.1875 to 0.1875
- wo: bfloat16 [1024, 1024], P(('head', 'blk')), may hold values from -0.75 to 0.75
- w_up: bfloat16 [1024, 4096], P(None, ('head', 'blk')), may hold values from -0.1875 to 0.1875
- w_down: bfloat16 [4096, 1024], P(('head', 'blk')), may hold values from -0.125 to 0.125
- gain_one: bfloat16 [1024], P(('head', 'blk')), may hold values from 0.5 to 1.5
- gain_two: bfloat16 [1024], P(('head', 'blk')), may hold values from 0.5 to 1.5
- w_comp: bfloat16 [3, 1024, 1024], P(None, ('head', 'blk')), may hold values from -0.109375 to 0.109375
- lengths: int32 [8], replicated, may hold values from 2 to 11, as said below
- grad_out: bfloat16 [48, 512, 1024], P('blk', 'head'), may hold values from -8 to 8
Outputs:
- out: bfloat16 [48, 512, 1024], P('blk', 'head')
- compressed: bfloat16 [48, 170, 1024], P('blk', None, 'head')
- grad_tokens: bfloat16 [48, 512, 1024], P('blk', 'head')
- grad_wq: float32 [1024, 1024], P(('head', 'blk'))
- grad_wk: float32 [1024, 1024], P(('head', 'blk'))
- grad_wv: float32 [1024, 1024], P(('head', 'blk'))
- grad_wo: float32 [1024, 1024], P(('head', 'blk'))
- grad_up: float32 [1024, 4096], P(None, ('head', 'blk'))
- grad_down: float32 [4096, 1024], P(('head', 'blk'))
- grad_gain_one: float32 [1024], P(('head', 'blk'))
- grad_gain_two: float32 [1024], P(('head', 'blk'))
- grad_comp: float32 [3, 1024, 1024], P(None, ('head', 'blk'))
Inputs may be any that keep to these rules, and one draw needn't show every extreme that they name: lengths of the 8 sequences in segments of 512 tokens, taken in order; they sum to 48; the first is the longest with exactly 11; no sequence but the first begins at a segment index that is a multiple of 6.
All inputs are finite; a program needn't handle non-finite values.
Results may differ from a plain program's by a relative error of at most 0.018.
Values may be sent and summed in bfloat16 or wider, within the bound.
No kernel may reach another device: no remote copies, remote signals or barrier semaphores. Data moves between devices by JAX's collectives and lax.ppermute only.
A program may use at most 320 MiB of HBM per device.

v0:
```python
import jax
import jax.numpy as jnp
from jax import lax
from jax.sharding import PartitionSpec as P

HD = 128
RATE = 3
CSEGS = 3


EPS = 1e-05
NEG = -1e30
ROWS_IN = (((0,), (0,)), ((), ()))
COLS_IN = (((1,), (1,)), ((), ()))


def passed_along(value, axis, steps):
    count = lax.axis_size(axis)
    leading, last = (max(0, -steps), min(count, count - steps))
    return lax.ppermute(value, axis, [(source, source + steps) for source in range(leading, last)])


def layer_norm(values, gain):
    average = jnp.mean(values, axis=-1, keepdims=True)
    center = values - average
    variance = jnp.mean(center * center, axis=-1, keepdims=True)
    return center * lax.rsqrt(variance + EPS) * gain


def silu_slope(values):
    sig = jax.nn.sigmoid(values)
    return sig * (1.0 + values * (1.0 - sig))


def key_layout(seg_len, comp_rows, comp_segs, rate):
    groups = []
    places = []
    for lag in range(comp_segs + 1, 1, -1):
        groups.append(jnp.full((comp_rows,), lag, jnp.int32))
        places.append(rate * jnp.arange(comp_rows, dtype=jnp.int32) + rate // 2 - lag * seg_len)
    groups.append(jnp.full((seg_len,), 1, jnp.int32))
    places.append(jnp.arange(seg_len, dtype=jnp.int32) - seg_len)
    groups.append(jnp.zeros((seg_len,), jnp.int32))
    places.append(jnp.arange(seg_len, dtype=jnp.int32))
    return (jnp.concatenate(groups), jnp.concatenate(places))


def make_scores(query_heads, key_heads, group, place, seg_place, slopes):
    seg_len = query_heads.shape[0]
    positions = jnp.arange(seg_len, dtype=jnp.int32)
    allowed = (group[None, :] <= seg_place) & (place[None, :] <= positions[:, None])
    distance = (positions[:, None] - place[None, :]).astype(jnp.float32)
    raw = jnp.einsum("qhd,khd->hqk", query_heads, key_heads, preferred_element_type=jnp.float32)
    scores = raw * HD ** (-0.5) - slopes[:, None, None] * distance[None]
    return jnp.where(allowed[None], scores, NEG)


def per_device(tokens, wq, wk, wv, wo, w_up, w_down, gain_one, gain_two, w_comp, lengths, grad_out):
    seg_count, quarter, width = tokens.shape
    head_groups = lax.axis_size("head")
    seg_len = quarter * head_groups
    head_cols = width // head_groups
    local_heads = head_cols // HD
    comp_rows = seg_len // RATE
    window = CSEGS + 1
    head_index = lax.axis_index("head")
    blk_index = lax.axis_index("blk")
    col_start = head_index * head_cols
    token_count = seg_count * quarter
    gathered = (
        lax.all_gather(wq, ("head", "blk"), axis=0, tiled=True),
        lax.all_gather(wk, ("head", "blk"), axis=0, tiled=True),
        lax.all_gather(wv, ("head", "blk"), axis=0, tiled=True),
        lax.all_gather(wo, ("head", "blk"), axis=0, tiled=True),
        lax.all_gather(gain_one, ("head", "blk"), axis=0, tiled=True),
        lax.all_gather(gain_two, ("head", "blk"), axis=0, tiled=True),
    )
    wq_all, wk_all, wv_all, wo_all, gain_first, gain_second = gathered
    up_cols, down_rows, comp_part = (
        lax.all_gather(w_up, "blk", axis=1, tiled=True),
        lax.all_gather(w_down, "blk", axis=0, tiled=True),
        lax.all_gather(w_comp, "blk", axis=1, tiled=True),
    )
    comp_matrix = comp_part.reshape(RATE * head_cols, width)
    gain_first = gain_first.astype(jnp.float32)
    gain_second = gain_second.astype(jnp.float32)
    up_all, down_all = (
        lax.all_gather(up_cols, "head", axis=1, tiled=True),
        lax.all_gather(down_rows, "head", axis=0, tiled=True),
    )
    token_rows = tokens.reshape(token_count, width).astype(jnp.float32)
    normed = layer_norm(token_rows, gain_first).astype(jnp.bfloat16)
    query = jnp.dot(normed, wq_all, preferred_element_type=jnp.float32).astype(jnp.bfloat16)
    key = jnp.dot(normed, wk_all, preferred_element_type=jnp.float32).astype(jnp.bfloat16)
    value = jnp.dot(normed, wv_all, preferred_element_type=jnp.float32).astype(jnp.bfloat16)
    split_shape = (seg_count, quarter, head_groups, head_cols)
    heads_q, heads_k, heads_v, heads_x = (
        lax.all_to_all(query.reshape(split_shape), "head", split_axis=2, concat_axis=1, tiled=True),
        lax.all_to_all(key.reshape(split_shape), "head", split_axis=2, concat_axis=1, tiled=True),
        lax.all_to_all(value.reshape(split_shape), "head", split_axis=2, concat_axis=1, tiled=True),
        lax.all_to_all(
            normed.reshape(split_shape), "head", split_axis=2, concat_axis=1, tiled=True
        ),
    )
    local_shape = (seg_count, seg_len, head_cols)
    heads_q = heads_q.reshape(local_shape)
    heads_k = heads_k.reshape(local_shape)
    heads_v = heads_v.reshape(local_shape)
    heads_x = heads_x.reshape(local_shape)
    grouped = heads_x[:, : RATE * comp_rows].reshape(seg_count * comp_rows, RATE * head_cols)
    packed_part = jnp.dot(grouped, comp_matrix, preferred_element_type=jnp.float32)
    packed = lax.psum(packed_part.astype(jnp.bfloat16), "head")
    wk_mine = lax.dynamic_slice_in_dim(wk_all, col_start, head_cols, 1)
    wv_mine = lax.dynamic_slice_in_dim(wv_all, col_start, head_cols, 1)
    comp_key = jnp.dot(packed, wk_mine, preferred_element_type=jnp.float32).astype(jnp.bfloat16)
    comp_value = jnp.dot(packed, wv_mine, preferred_element_type=jnp.float32).astype(jnp.bfloat16)
    comp_pair = jnp.concatenate([comp_key, comp_value], 1).reshape(
        seg_count, comp_rows, 2 * head_cols
    )
    own_pair = jnp.concatenate([heads_k, heads_v], 2)
    recv_mem = jnp.zeros((1, seg_len, 2 * head_cols), jnp.bfloat16)
    recv_comp = jnp.zeros((window, comp_rows, 2 * head_cols), jnp.bfloat16)
    tail_mem = jnp.concatenate([recv_mem, own_pair], 0)[seg_count:]
    tail_comp = jnp.concatenate([recv_comp, comp_pair], 0)[seg_count:]
    recv_mem, recv_comp = passed_along((tail_mem, tail_comp), "blk", 1)
    comp_ext = jnp.concatenate([recv_comp, comp_pair], 0)
    mem_ext = jnp.concatenate([recv_mem, own_pair], 0)
    pieces = [comp_ext[window - lag : window - lag + seg_count] for lag in range(CSEGS + 1, 1, -1)]
    pairs = jnp.concatenate(pieces + [mem_ext[:seg_count], own_pair], 1)
    starts = jnp.cumsum(lengths) - lengths
    seg_ids = blk_index * seg_count + jnp.arange(seg_count, dtype=jnp.int32)
    seg_place = seg_ids - jnp.max(
        jnp.where(starts[None, :] <= seg_ids[:, None], starts[None, :], 0), axis=1
    )
    head_ids = head_index * local_heads + jnp.arange(local_heads, dtype=jnp.int32)
    slopes = jnp.exp2(-head_ids.astype(jnp.float32)) / 64.0
    group, place = key_layout(seg_len, comp_rows, CSEGS, RATE)

    def attend_fwd(args):
        query_seg, pair_seg, place_seg = args
        query_heads = query_seg.reshape(seg_len, local_heads, HD)
        key_heads = pair_seg[:, :head_cols].reshape(-1, local_heads, HD)
        value_heads = pair_seg[:, head_cols:].reshape(-1, local_heads, HD)
        scores = make_scores(query_heads, key_heads, group, place, place_seg, slopes)
        row_top = jnp.max(scores, axis=-1, keepdims=True)
        weights = jnp.exp(scores - row_top)
        total = jnp.sum(weights, axis=-1, keepdims=True)
        probs = (weights / total).astype(jnp.bfloat16)
        result = jnp.einsum("hqk,khd->qhd", probs, value_heads, preferred_element_type=jnp.float32)
        return (result.reshape(seg_len, head_cols).astype(jnp.bfloat16), row_top + jnp.log(total))

    attn_out, log_total = lax.map(attend_fwd, (heads_q, pairs, seg_place))
    mixed = lax.all_to_all(
        attn_out.reshape(seg_count, seg_len, 1, head_cols),
        "head",
        split_axis=1,
        concat_axis=2,
        tiled=True,
    ).reshape(token_count, width)
    branch = jnp.dot(mixed, wo_all, preferred_element_type=jnp.float32)
    hidden = token_rows + branch
    normed_two = layer_norm(hidden, gain_second).astype(jnp.bfloat16)
    lifted = jnp.dot(normed_two, up_all, preferred_element_type=jnp.float32)
    active = jax.nn.silu(lifted).astype(jnp.bfloat16)
    ffn_term = jnp.dot(active, down_all, preferred_element_type=jnp.float32)
    result_rows = hidden + ffn_term
    out_tokens = result_rows.astype(jnp.bfloat16).reshape(tokens.shape)
    compressed = lax.dynamic_slice_in_dim(packed, col_start, head_cols, 1).reshape(
        seg_count, comp_rows, head_cols
    )
    upstream = grad_out.reshape(token_count, width)
    grad_down_full = lax.dot_general(active, upstream, ROWS_IN, preferred_element_type=jnp.float32)
    grad_active = lax.dot_general(upstream, down_all, COLS_IN, preferred_element_type=jnp.float32)
    grad_lifted = (grad_active * silu_slope(lifted)).astype(jnp.bfloat16)
    grad_up_full = lax.dot_general(
        normed_two, grad_lifted, ROWS_IN, preferred_element_type=jnp.float32
    )
    grad_normed_two = lax.dot_general(
        grad_lifted, up_all, COLS_IN, preferred_element_type=jnp.float32
    )
    up_part, down_part = (
        lax.psum_scatter(
            grad_up_full.astype(jnp.bfloat16), "head", scatter_dimension=1, tiled=True
        ).astype(jnp.float32),
        lax.psum_scatter(
            grad_down_full.astype(jnp.bfloat16), "head", scatter_dimension=0, tiled=True
        ).astype(jnp.float32),
    )
    second_value, second_pull = jax.vjp(layer_norm, hidden, gain_second)
    grad_hidden_norm, grad_gain_two = second_pull(grad_normed_two)
    grad_hidden = upstream.astype(jnp.float32) + grad_hidden_norm
    grad_branch = grad_hidden.astype(jnp.bfloat16)
    grad_wo = lax.dot_general(mixed, grad_branch, ROWS_IN, preferred_element_type=jnp.float32)
    grad_mixed = lax.dot_general(
        grad_branch, wo_all, COLS_IN, preferred_element_type=jnp.float32
    ).astype(jnp.bfloat16)
    grad_heads = lax.all_to_all(
        grad_mixed.reshape(split_shape), "head", split_axis=2, concat_axis=1, tiled=True
    ).reshape(local_shape)

    def attend_back(args):
        query_seg, pair_seg, place_seg, lse_seg, grad_seg = args
        query_heads = query_seg.reshape(seg_len, local_heads, HD)
        key_heads = pair_seg[:, :head_cols].reshape(-1, local_heads, HD)
        value_heads = pair_seg[:, head_cols:].reshape(-1, local_heads, HD)
        scores = make_scores(query_heads, key_heads, group, place, place_seg, slopes)
        probs = jnp.exp(scores - lse_seg)
        grad_seg_heads = grad_seg.reshape(seg_len, local_heads, HD)
        grad_probs = jnp.einsum(
            "qhd,khd->hqk", grad_seg_heads, value_heads, preferred_element_type=jnp.float32
        )
        grad_scores = (
            probs * (grad_probs - jnp.sum(probs * grad_probs, axis=-1, keepdims=True))
        ).astype(jnp.bfloat16)
        grad_query_seg = jnp.einsum(
            "hqk,khd->qhd", grad_scores, key_heads, preferred_element_type=jnp.float32
        ) * HD ** (-0.5)
        grad_key_seg = jnp.einsum(
            "hqk,qhd->khd", grad_scores, query_heads, preferred_element_type=jnp.float32
        ) * HD ** (-0.5)
        grad_value_seg = jnp.einsum(
            "hqk,qhd->khd",
            probs.astype(jnp.bfloat16),
            grad_seg_heads,
            preferred_element_type=jnp.float32,
        )
        key_count = pair_seg.shape[0]
        grad_pair_seg = jnp.concatenate(
            [
                grad_key_seg.reshape(key_count, head_cols),
                grad_value_seg.reshape(key_count, head_cols),
            ],
            1,
        )
        return (grad_query_seg.reshape(seg_len, head_cols).astype(jnp.bfloat16), grad_pair_seg)

    grad_query, grad_pairs = lax.map(
        attend_back, (heads_q, pairs, seg_place, log_total, grad_heads)
    )
    grad_comp_ext = jnp.zeros((window + seg_count, comp_rows, 2 * head_cols), jnp.float32)
    for piece_index in range(CSEGS):
        lag = CSEGS + 1 - piece_index
        piece = grad_pairs[:, piece_index * comp_rows : (piece_index + 1) * comp_rows]
        grad_comp_ext = grad_comp_ext + jnp.pad(piece, ((window - lag, lag), (0, 0), (0, 0)))
    mem_start = CSEGS * comp_rows
    grad_mem = grad_pairs[:, mem_start : mem_start + seg_len]
    grad_own = grad_pairs[:, mem_start + seg_len :]
    grad_mem_ext = jnp.pad(grad_mem, ((0, 1), (0, 0), (0, 0))) + jnp.pad(
        grad_own, ((1, 0), (0, 0), (0, 0))
    )
    back_mem = grad_mem_ext[:1]
    own_pair_grad = grad_mem_ext[1:]
    back_comp = grad_comp_ext[:window]
    comp_pair_grad = grad_comp_ext[window:]
    got_mem = passed_along(back_mem.astype(jnp.bfloat16), "blk", -1).astype(back_mem.dtype)
    got_comp = passed_along(back_comp.astype(jnp.bfloat16), "blk", -1).astype(back_comp.dtype)
    joined_mem = jnp.pad(got_mem, ((seg_count, 0), (0, 0), (0, 0)))
    own_pair_grad = own_pair_grad + joined_mem[1:]
    joined_comp = jnp.pad(got_comp, ((seg_count, 0), (0, 0), (0, 0)))
    comp_pair_grad = comp_pair_grad + joined_comp[window:]
    grad_key_heads = own_pair_grad[..., :head_cols].astype(jnp.bfloat16)
    grad_value_heads = own_pair_grad[..., head_cols:].astype(jnp.bfloat16)
    comp_grad_rows = comp_pair_grad.reshape(seg_count * comp_rows, 2 * head_cols).astype(
        jnp.bfloat16
    )
    grad_comp_key = comp_grad_rows[:, :head_cols]
    grad_comp_value = comp_grad_rows[:, head_cols:]
    grad_packed_part = lax.dot_general(
        grad_comp_key, wk_mine, COLS_IN, preferred_element_type=jnp.float32
    ) + lax.dot_general(grad_comp_value, wv_mine, COLS_IN, preferred_element_type=jnp.float32)
    grad_packed = lax.psum(grad_packed_part.astype(jnp.bfloat16), "head")
    comp_key_term = lax.dot_general(
        packed, grad_comp_key, ROWS_IN, preferred_element_type=jnp.float32
    )
    comp_value_term = lax.dot_general(
        packed, grad_comp_value, ROWS_IN, preferred_element_type=jnp.float32
    )
    grad_grouped = lax.dot_general(
        grad_packed, comp_matrix, COLS_IN, preferred_element_type=jnp.float32
    ).astype(jnp.bfloat16)
    grad_comp_term = lax.dot_general(
        grouped, grad_packed, ROWS_IN, preferred_element_type=jnp.float32
    ).reshape(RATE, head_cols, width)
    grad_sent = jnp.pad(
        grad_grouped.reshape(seg_count, RATE * comp_rows, head_cols),
        ((0, 0), (0, seg_len - RATE * comp_rows), (0, 0)),
    )
    back_shape = (seg_count, seg_len, 1, head_cols)
    token_q, token_k, token_v, token_x = (
        lax.all_to_all(
            grad_query.reshape(back_shape), "head", split_axis=1, concat_axis=2, tiled=True
        ),
        lax.all_to_all(
            grad_key_heads.reshape(back_shape), "head", split_axis=1, concat_axis=2, tiled=True
        ),
        lax.all_to_all(
            grad_value_heads.reshape(back_shape), "head", split_axis=1, concat_axis=2, tiled=True
        ),
        lax.all_to_all(
            grad_sent.reshape(back_shape), "head", split_axis=1, concat_axis=2, tiled=True
        ),
    )
    token_q = token_q.reshape(token_count, width)
    token_k = token_k.reshape(token_count, width)
    token_v = token_v.reshape(token_count, width)
    token_x = token_x.reshape(token_count, width)
    grad_normed = lax.dot_general(token_q, wq_all, COLS_IN, preferred_element_type=jnp.float32)
    grad_normed = grad_normed + lax.dot_general(
        token_k, wk_all, COLS_IN, preferred_element_type=jnp.float32
    )
    grad_normed = grad_normed + lax.dot_general(
        token_v, wv_all, COLS_IN, preferred_element_type=jnp.float32
    )
    grad_normed = grad_normed + token_x.astype(jnp.float32)
    first_value, first_pull = jax.vjp(layer_norm, token_rows, gain_first)
    grad_rows_norm, grad_gain_one = first_pull(grad_normed)
    grad_tokens = (grad_hidden + grad_rows_norm).astype(jnp.bfloat16).reshape(tokens.shape)
    grad_wq = lax.dot_general(normed, token_q, ROWS_IN, preferred_element_type=jnp.float32)
    grad_wk = lax.dot_general(normed, token_k, ROWS_IN, preferred_element_type=jnp.float32)
    grad_wv = lax.dot_general(normed, token_v, ROWS_IN, preferred_element_type=jnp.float32)
    grad_wk = grad_wk + lax.dynamic_update_slice_in_dim(
        jnp.zeros_like(grad_wk), comp_key_term, col_start, 1
    )
    grad_wv = grad_wv + lax.dynamic_update_slice_in_dim(
        jnp.zeros_like(grad_wv), comp_value_term, col_start, 1
    )
    blk_summed = (
        lax.psum_scatter(
            up_part.astype(jnp.bfloat16), "blk", scatter_dimension=1, tiled=True
        ).astype(jnp.float32),
        lax.psum_scatter(
            down_part.astype(jnp.bfloat16), "blk", scatter_dimension=0, tiled=True
        ).astype(jnp.float32),
        lax.psum_scatter(
            grad_comp_term.astype(jnp.bfloat16), "blk", scatter_dimension=1, tiled=True
        ).astype(jnp.float32),
    )
    summed = (
        lax.psum_scatter(grad_wq, ("head", "blk"), scatter_dimension=0, tiled=True),
        lax.psum_scatter(grad_wk, ("head", "blk"), scatter_dimension=0, tiled=True),
        lax.psum_scatter(grad_wv, ("head", "blk"), scatter_dimension=0, tiled=True),
        lax.psum_scatter(grad_wo, ("head", "blk"), scatter_dimension=0, tiled=True),
        lax.psum_scatter(grad_gain_one, ("head", "blk"), scatter_dimension=0, tiled=True),
        lax.psum_scatter(grad_gain_two, ("head", "blk"), scatter_dimension=0, tiled=True),
    )
    return (
        out_tokens,
        compressed,
        grad_tokens,
        summed[0],
        summed[1],
        summed[2],
        summed[3],
        blk_summed[0],
        blk_summed[1],
        summed[4],
        summed[5],
        blk_summed[2],
    )


def solution(mesh):
    return jax.shard_map(
        per_device,
        mesh=mesh,
        in_specs=(
            P("blk", "head", None),
            P(("head", "blk"), None),
            P(("head", "blk"), None),
            P(("head", "blk"), None),
            P(("head", "blk"), None),
            P(None, ("head", "blk")),
            P(("head", "blk"), None),
            P(("head", "blk")),
            P(("head", "blk")),
            P(None, ("head", "blk"), None),
            P(),
            P("blk", "head", None),
        ),
        out_specs=(
            P("blk", "head", None),
            P("blk", None, "head"),
            P("blk", "head", None),
            P(("head", "blk"), None),
            P(("head", "blk"), None),
            P(("head", "blk"), None),
            P(("head", "blk"), None),
            P(None, ("head", "blk")),
            P(("head", "blk"), None),
            P(("head", "blk")),
            P(("head", "blk")),
            P(None, ("head", "blk"), None),
        ),
        check_vma=False,
    )
```

profile of v0, /device:TPU:24, one launch (start us, length us, event | category | flops | bytes accessed | tf_op | source)
XLA Modules:
  0.0 1825.2 jit_solution(15373347080117919265)
XLA Ops:
  11.7 39.6 %all-reduce.13 = (bf16[1024]{0:T(1024)(128)(2,1)S(1)}, bf16[1024]{0:T(1024)(128)(2,1)S(1)}) all-reduce(bf16[1024]{0:T(1024)(128)(2,1)S(1)} %dynamic-update-slice.2, bf16[1024]{0:T(1024)(128)(2,1)S(1)} %dynamic-update-slice.3), channel_id=1, replica_groups=mesh['head'=4,'blk'=8] {'head','blk'}, use_global_device_ids=true, to_apply=%add.8 | all-reduce | flops 2048 | bytes 8192
  54.9 23.4 %all_to_all.144 = bf16[6,128,4,256]{1,3,0,2:T(8,128)(2,1)S(1)} all-to-all(bf16[6,128,4,256]{1,3,0,2:T(8,128)(2,1)S(1)} %copy.245), channel_id=1, replica_groups=mesh['head'=4,'blk'=8] {'head'}, dimensions={2} | all-to-all | bytes 3145728 | tf_op jit(solution)/shard_map/all_to_all | solution.py:101
  110.1 54.0 %all-gather.14.cloned.1.call-done = bf16[1024,1024]{1,0:T(8,128)(2,1)} async-done(((bf16[32,1024]{1,0:T(8,128)(2,1)}), bf16[1024,1024]{1,0:T(8,128)(2,1)}) %all-gather.14.cloned.1.call-update) | async-done | bytes 2097168 | tf_op jit(solution)/shard_map/all_gather | solution.py:73
  174.3 48.2 %all-gather.12.cloned.1.call-done = bf16[1024,1024]{1,0:T(8,128)(2,1)} async-done(((bf16[32,1024]{1,0:T(8,128)(2,1)}), bf16[1024,1024]{1,0:T(8,128)(2,1)}) %all-gather.12.cloned.1.call-update) | async-done | bytes 2097168 | tf_op jit(solution)/shard_map/all_gather | solution.py:72
  235.1 52.1 %all-reduce.17.cloned.1.call-done = bf16[1020,1024]{1,0:T(8,128)(2,1)} async-done(((bf16[1020,1024]{1,0:T(8,128)(2,1)}), bf16[1020,1024]{1,0:T(8,128)(2,1)}) %all-reduce.17.cloned.1.call-update) | async-done | bytes 2088976 | tf_op jit(solution)/shard_map/psum | solution.py:112
  304.9 44.1 %all-gather.16.cloned.1.call-done = bf16[1024,1024]{1,0:T(8,128)(2,1)} async-done(((bf16[32,1024]{1,0:T(8,128)(2,1)}), bf16[1024,1024]{1,0:T(8,128)(2,1)}) %all-gather.16.cloned.1.call-update) | async-done | bytes 2097168 | tf_op jit(solution)/shard_map/all_gather | solution.py:71
  365.2 33.9 %all-gather.24.cloned.1.call-done = bf16[1024,1024]{1,0:T(8,128)(2,1)} async-done(((bf16[128,1024]{1,0:T(8,128)(2,1)}), bf16[1024,1024]{1,0:T(8,128)(2,1)}) %all-gather.24.cloned.1.call-update) | async-done | bytes 2097168 | tf_op jit(solution)/shard_map/all_gather | solution.py:81
  430.3 56.9 %concatenate.25 = bf16[6,1534,512]{2,1,0:T(8,128)(2,1)} concatenate(bf16[6,170,512]{2,1,0:T(8,128)(2,1)} %get-tuple-element.283, bf16[6,170,512]{2,1,0:T(8,128)(2,1)} %get-tuple-element.282, bf16[6,170,512]{2,1,0:T(8,128)(2,1)} %get-tuple-element.281, bf16[6,512,512]{2,1,0:T(8,128)(2,1)} %get-tuple-element.280, bf16[6,512,512]{2,1,0:T(8,128)(2,1)} %get-tuple-element.279), dimensions={1} | concatenate | bytes 18849792 | tf_op jit(solution)/shard_map/concatenate | solution.py:129
  500.1 59.5 %while.26 = (s32[]{:T(128)}, bf16[6,512,256]{1,2,0:T(8,128)(2,1)S(1)}, f32[6,2,512,1]{2,1,3,0:T(2,128)S(1)}, bf16[6,1534,512]{1,2,0:T(8,128)(2,1)}, s32[6]{0:T(1...) while((s32[]{:T(128)}, ...), condition=%wide.region_8.9_spmd.clone, body=%wide.region_5.8_spmd.clone.sunk | while | flops 823239168 | bytes 36185220 | solution.py:152
  566.5 32.3 %all-to-all-done.4 = bf16[6,512,1,256]{3,0,2,1:T(8,128)(2,1)S(1)} async-done(((bf16[6,512,1,256]{3,0,2,1:T(8,128)(2,1)}), bf16[6,512,1,256]{3,0,2,1:T(8,128)(2,1)S(1)}, u32[]{:S(2)}, u32[]{:S(2)}) %all-to-all-start.4) | async-done | bytes 1572896 | tf_op jit(solution)/shard_map/all_to_all | solution.py:153
  683.2 90.6 %while.27 = (s32[]{:T(128)}, bf16[6,512,256]{1,2,0:T(8,128)(2,1)}, f32[6,1534,512]{1,2,0:T(8,128)}, bf16[6,1534,512]{1,2,0:T(8,128)(2,1)}, s32[6]{0:T(128)S(1)},...) while((s32[]{:T(128)}, bf16[6,512,256]{1,2,0:T(8,128)(2,1)}, ...), condition=%wide.region_15.16_spmd.clone, body=%wide.region_13.15_spmd.clone.sunk | while | flops 2032505856 | bytes 89080016 | solution.py:237
  773.8 22.6 %copy.274 = f32[6,1534,512]{2,0,1:T(8,128)} copy(f32[6,1534,512]{1,2,0:T(8,128)} %get-tuple-element.111) | data formatting | bytes 37699584 | tf_op jit(solution)/shard_map/while | solution.py:237
  860.0 21.1 %all-reduce.19.cloned.1.call-done = bf16[1020,1024]{1,0:T(8,128)(2,1)} async-done(((bf16[1020,1024]{1,0:T(8,128)(2,1)}), bf16[1020,1024]{1,0:T(8,128)(2,1)}) %all-reduce.19.cloned.1.call-update) | async-done | bytes 2088976 | tf_op jit(solution)/shard_map/psum | solution.py:271
  885.6 69.6 %reduce-scatter.20.cloned.1.call-done = bf16[1024,1024]{1,0:T(8,128)(2,1)} async-done(((bf16[1024,4096]{1,0:T(8,128)(2,1)}), bf16[1024,1024]{1,0:T(8,128)(2,1)}) %reduce-scatter.20.cloned.1.call-update) | async-done | bytes 2097168 | tf_op jit(solution)/shard_map/reduce_scatter | solution.py:182
  959.3 70.5 %reduce-scatter.22.cloned.1.call-done = bf16[1024,1024]{1,0:T(8,128)(2,1)} async-done(((bf16[4096,1024]{1,0:T(8,128)(2,1)}), bf16[1024,1024]{1,0:T(8,128)(2,1)}) %reduce-scatter.22.cloned.1.call-update) | async-done | bytes 2097168 | tf_op jit(solution)/shard_map/reduce_scatter | solution.py:185
  1044.0 24.4 %all-to-all-done.6 = bf16[6,512,1,256]{3,0,2,1:T(8,128)(2,1)} async-done(((bf16[6,512,1,256]{3,0,2,1:T(8,128)(2,1)}), bf16[6,512,1,256]{3,0,2,1:T(8,128)(2,1)}, u32[]{:S(2)}, u32[]{:S(2)}) %all-to-all-start.6) | async-done | bytes 1572896 | tf_op jit(solution)/shard_map/all_to_all | solution.py:290
  1109.4 22.7 %collective-permute-done.2 = bf16[1,512,512]{2,1,0:T(8,128)(2,1)S(1)} collective-permute-done((bf16[1,512,512]{2,1,0:T(8,128)(2,1)S(1)}, bf16[1,512,512]{2,1,0:T(8,128)(2,1)S(1)}, u32[]{:S(2)}, u32[]{:S(2)}) %collective-permute-start.2) | collective-permute-done | bytes 524320 | tf_op jit(solution)/shard_map/ppermute | solution.py:20
  1134.6 28.2 %all_to_all.145 = bf16[6,512,1,256]{3,0,2,1:T(8,128)(2,1)S(1)} all-to-all(bf16[6,512,1,256]{3,0,2,1:T(8,128)(2,1)S(1)} %copy.272), channel_id=1, replica_groups=mesh['head'=4,'blk'=8] {'head'}, dimensions={1} | all-to-all | bytes 3145728 | tf_op jit(solution)/shard_map/all_to_all | solution.py:296
  1172.4 28.4 %all_to_all.146 = bf16[6,512,1,256]{3,0,2,1:T(8,128)(2,1)S(1)} all-to-all(bf16[6,512,1,256]{3,0,2,1:T(8,128)(2,1)S(1)} %copy.270), channel_id=1, replica_groups=mesh['head'=4,'blk'=8] {'head'}, dimensions={1} | all-to-all | bytes 3145728 | tf_op jit(solution)/shard_map/all_to_all | solution.py:293
  1260.6 43.2 %all-reduce.12 = (f32[1024]{0:T(1024)S(1)}, f32[1024]{0:T(1024)S(1)}) all-reduce(f32[1024]{0:T(1024)S(1)} %get-tuple-element.218, f32[1024]{0:T(1024)S(1)} %copy-done.62), channel_id=10, replica_groups=mesh['head'=4,'blk'=8] {'head','blk'}, use_global_device_ids=true, to_apply=%region_28.29.clone | all-reduce | flops 2048 | bytes 16384
  1315.8 67.5 %reduce-scatter.18.cloned.1.call-done = f32[32,1024]{1,0:T(8,128)} async-done(((f32[1024,1024]{1,0:T(8,128)}), f32[32,1024]{1,0:T(8,128)}) %reduce-scatter.18.cloned.1.call-update) | async-done | bytes 131088 | tf_op jit(solution)/shard_map/reduce_scatter | solution.py:342
  1383.3 145.3 %reduce-scatter.12.cloned.1.call-done = f32[32,1024]{1,0:T(8,128)} async-done(((f32[1024,1024]{1,0:T(8,128)}), f32[32,1024]{1,0:T(8,128)}) %reduce-scatter.12.cloned.1.call-update) | async-done | bytes 131088 | tf_op jit(solution)/shard_map/reduce_scatter | solution.py:339
  1528.6 146.0 %reduce-scatter.16.cloned.1.call-done = f32[32,1024]{1,0:T(8,128)} async-done(((f32[1024,1024]{1,0:T(8,128)}), f32[32,1024]{1,0:T(8,128)}) %reduce-scatter.16.cloned.1.call-update) | async-done | bytes 131088 | tf_op jit(solution)/shard_map/reduce_scatter | solution.py:341
  1674.5 143.3 %reduce-scatter.14.cloned.1.call-done = f32[32,1024]{1,0:T(8,128)} async-done(((f32[1024,1024]{1,0:T(8,128)}), f32[32,1024]{1,0:T(8,128)}) %reduce-scatter.14.cloned.1.call-update) | async-done | bytes 131088 | tf_op jit(solution)/shard_map/reduce_scatter | solution.py:340
  (557 shorter events, 590.9 us)
Async XLA Ops:
  7.2 74.9 %all-gather.10.cloned.1.call-start = ((), (), s32[]{:S(2)}) async-start(), calls=%async_computation.19 | async-start | bytes 1769472 | tf_op jit(solution)/shard_map/all_gather | solution.py:82
  7.9 97.7 %all-gather.20.cloned.1.call-start = ((), (), s32[]{:S(2)}) async-start(), calls=%async_computation.25 | async-start | bytes 2359296 | tf_op jit(solution)/shard_map/all_gather | solution.py:80
  8.7 155.5 %all-gather.14.cloned.1.call-start = ((), (), s32[]{:S(2)}) async-start(), calls=%async_computation.22 | async-start | bytes 2162688 | tf_op jit(solution)/shard_map/all_gather | solution.py:73
  9.4 213.1 %all-gather.12.cloned.1.call-start = ((), (), s32[]{:S(2)}) async-start(), calls=%async_computation.21 | async-start | bytes 2162688 | tf_op jit(solution)/shard_map/all_gather | solution.py:72
  10.0 277.2 %all-reduce.17.cloned.1.call-start = ((), (), s32[]{:S(2)}) async-start(), calls=%async_computation.20 | async-start | bytes 4194304 | tf_op jit(solution)/shard_map/psum | solution.py:112
  87.2 261.8 %all-gather.16.cloned.1.call-start = ((), (), s32[]{:S(2)}) async-start(), calls=%async_computation.23 | async-start | bytes 2162688 | tf_op jit(solution)/shard_map/all_gather | solution.py:71
  87.8 311.4 %all-gather.24.cloned.1.call-start = ((), (), s32[]{:S(2)}) async-start(), calls=%async_computation.27 | async-start | bytes 2359296 | tf_op jit(solution)/shard_map/all_gather | solution.py:81
  88.5 516.1 %all-gather.18.cloned.1.call-start = ((), (), s32[]{:S(2)}) async-start(), calls=%async_computation.24 | async-start | bytes 2162688 | tf_op jit(solution)/shard_map/all_gather | solution.py:74
  89.3 521.4 %all-gather.22.cloned.1.call-start = ((), (), s32[]{:S(2)}) async-start(), calls=%async_computation.26 | async-start | bytes 10485760 | tf_op jit(solution)/shard_map/all_gather | solution.py:88
  170.1 61.2 %all-to-all-start.2 = ((bf16[6,128,4,256]{3,1,0,2:T(8,128)(2,1)}), bf16[6,128,4,256]{3,1,0,2:T(8,128)(2,1)S(1)}, u32[]{:S(2)}, u32[]{:S(2)}) async-start(bf16[6,128,4,256]{3,1,0,2:T(8,128)(2,1)} %copy.253), calls=%async_computation.2 | async-start | bytes 3145728 | tf_op jit(solution)/shard_map/all_to_all | solution.py:100
  231.3 129.5 %all-to-all-start.1 = ((bf16[6,128,4,256]{3,1,0,2:T(8,128)(2,1)}), bf16[6,128,4,256]{3,1,0,2:T(8,128)(2,1)S(1)}, u32[]{:S(2)}, u32[]{:S(2)}) async-start(bf16[6,128,4,256]{3,1,0,2:T(8,128)(2,1)} %copy.251), calls=%async_computation.1 | async-start | bytes 3145728 | tf_op jit(solution)/shard_map/all_to_all | solution.py:99
  301.5 109.6 %collective-permute-start = (bf16[4,170,512]{2,0,1:T(4,128)(2,1)}, bf16[4,170,512]{2,0,1:T(4,128)(2,1)}, u32[]{:S(2)}, u32[]{:S(2)}) collective-permute-start(bf16[4,170,512]{2,0,1:T(4,128)(2,1)} %copy.248), channel_id=1, source_target_pairs={{0,1},{1,2},{2,3},{3,4},{4,5},{5,6},{6,7},{8,9},{9,10},{10,11},{11... | collective-permute-start | bytes 2088968 | tf_op jit(solution)/shard_map/ppermute | solution.py:20
  360.8 53.5 %all-to-all-start.3 = ((bf16[6,128,4,256]{3,1,0,2:T(8,128)(2,1)}), bf16[6,128,4,256]{3,1,0,2:T(8,128)(2,1)}, u32[]{:S(2)}, u32[]{:S(2)}) async-start(bf16[6,128,4,256]{3,1,0,2:T(8,128)(2,1)} %copy.255), calls=%async_computation.3 | async-start | bytes 3145728 | tf_op jit(solution)/shard_map/all_to_all | solution.py:98
  365.2 258.5 %all-gather.26.cloned.1.call-start = ((), (), s32[]{:S(2)}) async-start(), calls=%async_computation.28 | async-start | bytes 10485760 | tf_op jit(solution)/shard_map/all_gather | solution.py:89
  661.7 219.3 %all-reduce.19.cloned.1.call-start = ((), (), s32[]{:S(2)}) async-start(), calls=%async_computation.29 | async-start | bytes 4194304 | tf_op jit(solution)/shard_map/psum | solution.py:271
  829.4 125.8 %reduce-scatter.20.cloned.1.call-start = ((), (), s32[]{:S(2)}) async-start(), calls=%async_computation.34 | async-start | bytes 10485760 | tf_op jit(solution)/shard_map/reduce_scatter | solution.py:182
  841.5 188.2 %reduce-scatter.22.cloned.1.call-start = ((), (), s32[]{:S(2)}) async-start(), calls=%async_computation.35 | async-start | bytes 10485760 | tf_op jit(solution)/shard_map/reduce_scatter | solution.py:185
  857.8 452.5 %reduce-scatter.26.cloned.1.call-start = ((), (), s32[]{:S(2)}) async-start(), calls=%async_computation.37 | async-start | bytes 1769472 | tf_op jit(solution)/shard_map/reduce_scatter | solution.py:334
  885.6 426.5 %reduce-scatter.28.cloned.1.call-start = ((), (), s32[]{:S(2)}) async-start(), calls=%async_computation.38 | async-start | bytes 2359296
  959.2 354.8 %reduce-scatter.24.cloned.1.call-start = ((), (), s32[]{:S(2)}) async-start(), calls=%async_computation.36 | async-start | bytes 2359296 | tf_op jit(solution)/shard_map/reduce_scatter | solution.py:331
  1029.8 353.5 %reduce-scatter.18.cloned.1.call-start = ((), (), s32[]{:S(2)}) async-start(), calls=%async_computation.33 | async-start | bytes 4325376 | tf_op jit(solution)/shard_map/reduce_scatter | solution.py:342
  1042.6 486.0 %reduce-scatter.12.cloned.1.call-start = ((), (), s32[]{:S(2)}) async-start(), calls=%async_computation.30 | async-start | bytes 4325376 | tf_op jit(solution)/shard_map/reduce_scatter | solution.py:339
  1076.6 598.0 %reduce-scatter.16.cloned.1.call-start = ((), (), s32[]{:S(2)}) async-start(), calls=%async_computation.32 | async-start | bytes 4325376 | tf_op jit(solution)/shard_map/reduce_scatter | solution.py:341
  1171.4 646.5 %reduce-scatter.14.cloned.1.call-start = ((), (), s32[]{:S(2)}) async-start(), calls=%async_computation.31 | async-start | bytes 4325376 | tf_op jit(solution)/shard_map/reduce_scatter | solution.py:340
  (86 other events, 1039.3 us)
Sparse Core Ops, SparseCore 0:
  10.2 44.3 all-gather.9
  56.6 48.9 all-gather.19
  108.6 55.4 all-gather.13
  166.9 55.5 all-gather.11
  224.7 62.3 all-reduce.16
  290.4 58.5 all-gather.15
  351.3 47.7 all-gather.23
  402.6 55.6 all-gather.17
  459.9 58.2 all-gather.21
  519.7 64.9 all-gather.25
  829.6 51.4 all-reduce.18
  883.4 71.7 reduce-scatter.19
  958.0 71.6 reduce-scatter.21
  1033.1 64.3 reduce-scatter.25
  1101.2 72.8 reduce-scatter.27
  1177.9 66.7 reduce-scatter.23
  1247.5 135.7 reduce-scatter.17
  1386.1 142.4 reduce-scatter.11
  1531.5 142.9 reduce-scatter.15
  1677.3 140.4 reduce-scatter.13
where the time goes:
time: 1850 us; the launch traced here: 1830 us
  waiting for transfers between devices  1040 us (56%)
  local copies, waits for them, and re-layouts  271 us (15%)
  matrix products  217 us (12%)
  blocking collectives  163 us (9%)
  other arithmetic  70.6 us (4%)
  starting transfers between devices  42.8 us (2%)
    reduce_scatter x1, waiting for transfers between devices, per_device(): lax.psum_scatter(grad_wv, ('head', 'blk'), scatter_dimension=0, tiled=True)  146 us
    reduce_scatter x1, waiting for transfers between devices, per_device(): lax.psum_scatter(grad_wq, ('head', 'blk'), scatter_dimension=0, tiled=True)  145 us
    reduce_scatter x1, waiting for transfers between devices, per_device(): lax.psum_scatter(grad_wk, ('head', 'blk'), scatter_dimension=0, tiled=True)  143 us
    unnamed x2, blocking collectives  82.8 us
    reduce_scatter x1, waiting for transfers between devices, per_device(): lax.psum_scatter(grad_down_full.astype(jnp.bfloat16), 'head', scatter_dim...  70.5 us
    reduce_scatter x1, waiting for transfers between devices, per_device(): lax.psum_scatter(grad_up_full.astype(jnp.bfloat16), 'head', scatter_dimen...  69.6 us
    reduce_scatter x1, waiting for transfers between devices, per_device(): lax.psum_scatter(grad_wo, ('head', 'blk'), scatter_dimension=0, tiled=True)  67.5 us
    concatenate x1, local copies, waits for them, and re-layouts, per_device(): pairs = jnp.concatenate(pieces + [mem_ext[:seg_count], own_pair], 1)  56.9 us
  transfers between devices with their start and end apart: 31, of which 20 were waited for; matrix products, arithmetic and copies ran while one was open for 21% of the time, Pallas kernels for 0%

commit v1 on v0

--- a/solution.py
+++ b/solution.py
@@ -127,7 +127,8 @@
     mem_ext = jnp.concatenate([recv_mem, own_pair], 0)
     pieces = [comp_ext[window - lag : window - lag + seg_count] for lag in range(CSEGS + 1, 1, -1)]
     pairs = jnp.concatenate(pieces + [mem_ext[:seg_count], own_pair], 1)
-    starts = jnp.cumsum(lengths) - lengths
+    order = jnp.arange(lengths.shape[0], dtype=jnp.int32)
+    starts = jnp.sum(jnp.where(order[None, :] < order[:, None], lengths[None, :], 0), axis=1)
     seg_ids = blk_index * seg_count + jnp.arange(seg_count, dtype=jnp.int32)
     seg_place = seg_ids - jnp.max(
         jnp.where(starts[None, :] <= seg_ids[:, None], starts[None, :], 0), axis=1

time: 1850 us -> 1850 us (level)
  no operation moved by 1% of the time
where the time goes in v1:
time: 1850 us; the launch traced here: 1830 us
  waiting for transfers between devices  1040 us (56%)
  local copies, waits for them, and re-layouts  271 us (15%)
  matrix products  217 us (12%)
  blocking collectives  163 us (9%)
  other arithmetic  70.6 us (4%)
  starting transfers between devices  42.8 us (2%)
    reduce_scatter x1, waiting for transfers between devices, per_device(): lax.psum_scatter(grad_wv, ('head', 'blk'), scatter_dimension=0, tiled=True)  146 us
    reduce_scatter x1, waiting for transfers between devices, per_device(): lax.psum_scatter(grad_wq, ('head', 'blk'), scatter_dimension=0, tiled=True)  145 us
    reduce_scatter x1, waiting for transfers between devices, per_device(): lax.psum_scatter(grad_wk, ('head', 'blk'), scatter_dimension=0, tiled=True)  143 us
    unnamed x2, blocking collectives  82.8 us
    reduce_scatter x1, waiting for transfers between devices, per_device(): lax.psum_scatter(grad_down_full.astype(jnp.bfloat16), 'head', scatter_dim...  70.5 us
    reduce_scatter x1, waiting for transfers between devices, per_device(): lax.psum_scatter(grad_up_full.astype(jnp.bfloat16), 'head', scatter_dimen...  69.6 us
    reduce_scatter x1, waiting for transfers between devices, per_device(): lax.psum_scatter(grad_wo, ('head', 'blk'), scatter_dimension=0, tiled=True)  67.5 us
    concatenate x1, local copies, waits for them, and re-layouts, per_device(): pairs = jnp.concatenate(pieces + [mem_ext[:seg_count], own_pair], 1)  56.9 us
  transfers between devices with their start and end apart: 31, of which 20 were waited for; matrix products, arithmetic and copies ran while one was open for 21% of the time, Pallas kernels for 0%

profile of v1, /device:TPU:24, one launch (start us, length us, event | category | flops | bytes accessed | tf_op | source)
XLA Modules:
  0.0 1825.2 jit_solution(17340873672018483946)
XLA Ops:
  11.7 39.6 %all-reduce.13 = (bf16[1024]{0:T(1024)(128)(2,1)S(1)}, bf16[1024]{0:T(1024)(128)(2,1)S(1)}) all-reduce(bf16[1024]{0:T(1024)(128)(2,1)S(1)} %dynamic-update-slice.2, bf16[1024]{0:T(1024)(128)(2,1)S(1)} %dynamic-update-slice.3), channel_id=1, replica_groups=mesh['head'=4,'blk'=8] {'head','blk'}, use_global_device_ids=true, to_apply=%add.8 | all-reduce | flops 2048 | bytes 8192
  54.9 23.4 %all_to_all.144 = bf16[6,128,4,256]{1,3,0,2:T(8,128)(2,1)S(1)} all-to-all(bf16[6,128,4,256]{1,3,0,2:T(8,128)(2,1)S(1)} %copy.245), channel_id=1, replica_groups=mesh['head'=4,'blk'=8] {'head'}, dimensions={2} | all-to-all | bytes 3145728 | tf_op jit(solution)/shard_map/all_to_all | solution.py:101
  110.1 54.0 %all-gather.14.cloned.1.call-done = bf16[1024,1024]{1,0:T(8,128)(2,1)} async-done(((bf16[32,1024]{1,0:T(8,128)(2,1)}), bf16[1024,1024]{1,0:T(8,128)(2,1)}) %all-gather.14.cloned.1.call-update) | async-done | bytes 2097168 | tf_op jit(solution)/shard_map/all_gather | solution.py:73
  174.3 48.2 %all-gather.12.cloned.1.call-done = bf16[1024,1024]{1,0:T(8,128)(2,1)} async-done(((bf16[32,1024]{1,0:T(8,128)(2,1)}), bf16[1024,1024]{1,0:T(8,128)(2,1)}) %all-gather.12.cloned.1.call-update) | async-done | bytes 2097168 | tf_op jit(solution)/shard_map/all_gather | solution.py:72
  235.1 52.1 %all-reduce.17.cloned.1.call-done = bf16[1020,1024]{1,0:T(8,128)(2,1)} async-done(((bf16[1020,1024]{1,0:T(8,128)(2,1)}), bf16[1020,1024]{1,0:T(8,128)(2,1)}) %all-reduce.17.cloned.1.call-update) | async-done | bytes 2088976 | tf_op jit(solution)/shard_map/psum | solution.py:112
  304.9 44.1 %all-gather.16.cloned.1.call-done = bf16[1024,1024]{1,0:T(8,128)(2,1)} async-done(((bf16[32,1024]{1,0:T(8,128)(2,1)}), bf16[1024,1024]{1,0:T(8,128)(2,1)}) %all-gather.16.cloned.1.call-update) | async-done | bytes 2097168 | tf_op jit(solution)/shard_map/all_gather | solution.py:71
  365.2 33.9 %all-gather.24.cloned.1.call-done = bf16[1024,1024]{1,0:T(8,128)(2,1)} async-done(((bf16[128,1024]{1,0:T(8,128)(2,1)}), bf16[1024,1024]{1,0:T(8,128)(2,1)}) %all-gather.24.cloned.1.call-update) | async-done | bytes 2097168 | tf_op jit(solution)/shard_map/all_gather | solution.py:81
  430.3 56.9 %concatenate.25 = bf16[6,1534,512]{2,1,0:T(8,128)(2,1)} concatenate(bf16[6,170,512]{2,1,0:T(8,128)(2,1)} %get-tuple-element.283, bf16[6,170,512]{2,1,0:T(8,128)(2,1)} %get-tuple-element.282, bf16[6,170,512]{2,1,0:T(8,128)(2,1)} %get-tuple-element.281, bf16[6,512,512]{2,1,0:T(8,128)(2,1)} %get-tuple-element.280, bf16[6,512,512]{2,1,0:T(8,128)(2,1)} %get-tuple-element.279), dimensions={1} | concatenate | bytes 18849792 | tf_op jit(solution)/shard_map/concatenate | solution.py:129
  500.1 59.5 %while.26 = (s32[]{:T(128)}, bf16[6,512,256]{1,2,0:T(8,128)(2,1)S(1)}, f32[6,2,512,1]{2,1,3,0:T(2,128)S(1)}, bf16[6,1534,512]{1,2,0:T(8,128)(2,1)}, s32[6]{0:T(1...) while((s32[]{:T(128)}, ...), condition=%wide.region_8.9_spmd.clone, body=%wide.region_5.8_spmd.clone.sunk | while | flops 823239168 | bytes 36185220 | solution.py:153
  566.5 32.3 %all-to-all-done.4 = bf16[6,512,1,256]{3,0,2,1:T(8,128)(2,1)S(1)} async-done(((bf16[6,512,1,256]{3,0,2,1:T(8,128)(2,1)}), bf16[6,512,1,256]{3,0,2,1:T(8,128)(2,1)S(1)}, u32[]{:S(2)}, u32[]{:S(2)}) %all-to-all-start.4) | async-done | bytes 1572896 | tf_op jit(solution)/shard_map/all_to_all | solution.py:154
  683.2 90.6 %while.27 = (s32[]{:T(128)}, bf16[6,512,256]{1,2,0:T(8,128)(2,1)}, f32[6,1534,512]{1,2,0:T(8,128)}, bf16[6,1534,512]{1,2,0:T(8,128)(2,1)}, s32[6]{0:T(128)S(1)},...) while((s32[]{:T(128)}, bf16[6,512,256]{1,2,0:T(8,128)(2,1)}, ...), condition=%wide.region_15.16_spmd.clone, body=%wide.region_13.15_spmd.clone.sunk | while | flops 2032505856 | bytes 89080016 | solution.py:238
  773.8 22.6 %copy.274 = f32[6,1534,512]{2,0,1:T(8,128)} copy(f32[6,1534,512]{1,2,0:T(8,128)} %get-tuple-element.111) | data formatting | bytes 37699584 | tf_op jit(solution)/shard_map/while | solution.py:238
  860.0 21.1 %all-reduce.19.cloned.1.call-done = bf16[1020,1024]{1,0:T(8,128)(2,1)} async-done(((bf16[1020,1024]{1,0:T(8,128)(2,1)}), bf16[1020,1024]{1,0:T(8,128)(2,1)}) %all-reduce.19.cloned.1.call-update) | async-done | bytes 2088976 | tf_op jit(solution)/shard_map/psum | solution.py:272
  885.6 69.6 %reduce-scatter.20.cloned.1.call-done = bf16[1024,1024]{1,0:T(8,128)(2,1)} async-done(((bf16[1024,4096]{1,0:T(8,128)(2,1)}), bf16[1024,1024]{1,0:T(8,128)(2,1)}) %reduce-scatter.20.cloned.1.call-update) | async-done | bytes 2097168 | tf_op jit(solution)/shard_map/reduce_scatter | solution.py:183
  959.3 70.5 %reduce-scatter.22.cloned.1.call-done = bf16[1024,1024]{1,0:T(8,128)(2,1)} async-done(((bf16[4096,1024]{1,0:T(8,128)(2,1)}), bf16[1024,1024]{1,0:T(8,128)(2,1)}) %reduce-scatter.22.cloned.1.call-update) | async-done | bytes 2097168 | tf_op jit(solution)/shard_map/reduce_scatter | solution.py:186
  1044.0 24.4 %all-to-all-done.6 = bf16[6,512,1,256]{3,0,2,1:T(8,128)(2,1)} async-done(((bf16[6,512,1,256]{3,0,2,1:T(8,128)(2,1)}), bf16[6,512,1,256]{3,0,2,1:T(8,128)(2,1)}, u32[]{:S(2)}, u32[]{:S(2)}) %all-to-all-start.6) | async-done | bytes 1572896 | tf_op jit(solution)/shard_map/all_to_all | solution.py:291
  1109.4 22.7 %collective-permute-done.2 = bf16[1,512,512]{2,1,0:T(8,128)(2,1)S(1)} collective-permute-done((bf16[1,512,512]{2,1,0:T(8,128)(2,1)S(1)}, bf16[1,512,512]{2,1,0:T(8,128)(2,1)S(1)}, u32[]{:S(2)}, u32[]{:S(2)}) %collective-permute-start.2) | collective-permute-done | bytes 524320 | tf_op jit(solution)/shard_map/ppermute | solution.py:20
  1134.6 28.2 %all_to_all.145 = bf16[6,512,1,256]{3,0,2,1:T(8,128)(2,1)S(1)} all-to-all(bf16[6,512,1,256]{3,0,2,1:T(8,128)(2,1)S(1)} %copy.272), channel_id=1, replica_groups=mesh['head'=4,'blk'=8] {'head'}, dimensions={1} | all-to-all | bytes 3145728 | tf_op jit(solution)/shard_map/all_to_all | solution.py:297
  1172.4 28.4 %all_to_all.146 = bf16[6,512,1,256]{3,0,2,1:T(8,128)(2,1)S(1)} all-to-all(bf16[6,512,1,256]{3,0,2,1:T(8,128)(2,1)S(1)} %copy.270), channel_id=1, replica_groups=mesh['head'=4,'blk'=8] {'head'}, dimensions={1} | all-to-all | bytes 3145728 | tf_op jit(solution)/shard_map/all_to_all | solution.py:294
  1260.6 43.2 %all-reduce.12 = (f32[1024]{0:T(1024)S(1)}, f32[1024]{0:T(1024)S(1)}) all-reduce(f32[1024]{0:T(1024)S(1)} %get-tuple-element.218, f32[1024]{0:T(1024)S(1)} %copy-done.62), channel_id=10, replica_groups=mesh['head'=4,'blk'=8] {'head','blk'}, use_global_device_ids=true, to_apply=%region_28.29.clone | all-reduce | flops 2048 | bytes 16384
  1315.8 67.5 %reduce-scatter.18.cloned.1.call-done = f32[32,1024]{1,0:T(8,128)} async-done(((f32[1024,1024]{1,0:T(8,128)}), f32[32,1024]{1,0:T(8,128)}) %reduce-scatter.18.cloned.1.call-update) | async-done | bytes 131088 | tf_op jit(solution)/shard_map/reduce_scatter | solution.py:343
  1383.3 145.3 %reduce-scatter.12.cloned.1.call-done = f32[32,1024]{1,0:T(8,128)} async-done(((f32[1024,1024]{1,0:T(8,128)}), f32[32,1024]{1,0:T(8,128)}) %reduce-scatter.12.cloned.1.call-update) | async-done | bytes 131088 | tf_op jit(solution)/shard_map/reduce_scatter | solution.py:340
  1528.6 146.0 %reduce-scatter.16.cloned.1.call-done = f32[32,1024]{1,0:T(8,128)} async-done(((f32[1024,1024]{1,0:T(8,128)}), f32[32,1024]{1,0:T(8,128)}) %reduce-scatter.16.cloned.1.call-update) | async-done | bytes 131088 | tf_op jit(solution)/shard_map/reduce_scatter | solution.py:342
  1674.5 143.3 %reduce-scatter.14.cloned.1.call-done = f32[32,1024]{1,0:T(8,128)} async-done(((f32[1024,1024]{1,0:T(8,128)}), f32[32,1024]{1,0:T(8,128)}) %reduce-scatter.14.cloned.1.call-update) | async-done | bytes 131088 | tf_op jit(solution)/shard_map/reduce_scatter | solution.py:341
  (556 shorter events, 590.8 us)
Async XLA Ops:
  7.2 74.9 %all-gather.10.cloned.1.call-start = ((), (), s32[]{:S(2)}) async-start(), calls=%async_computation.19 | async-start | bytes 1769472 | tf_op jit(solution)/shard_map/all_gather | solution.py:82
  7.9 97.7 %all-gather.20.cloned.1.call-start = ((), (), s32[]{:S(2)}) async-start(), calls=%async_computation.25 | async-start | bytes 2359296 | tf_op jit(solution)/shard_map/all_gather | solution.py:80
  8.7 155.5 %all-gather.14.cloned.1.call-start = ((), (), s32[]{:S(2)}) async-start(), calls=%async_computation.22 | async-start | bytes 2162688 | tf_op jit(solution)/shard_map/all_gather | solution.py:73
  9.4 213.1 %all-gather.12.cloned.1.call-start = ((), (), s32[]{:S(2)}) async-start(), calls=%async_computation.21 | async-start | bytes 2162688 | tf_op jit(solution)/shard_map/all_gather | solution.py:72
  10.0 277.2 %all-reduce.17.cloned.1.call-start = ((), (), s32[]{:S(2)}) async-start(), calls=%async_computation.20 | async-start | bytes 4194304 | tf_op jit(solution)/shard_map/psum | solution.py:112
  87.2 261.8 %all-gather.16.cloned.1.call-start = ((), (), s32[]{:S(2)}) async-start(), calls=%async_computation.23 | async-start | bytes 2162688 | tf_op jit(solution)/shard_map/all_gather | solution.py:71
  87.8 311.4 %all-gather.24.cloned.1.call-start = ((), (), s32[]{:S(2)}) async-start(), calls=%async_computation.27 | async-start | bytes 2359296 | tf_op jit(solution)/shard_map/all_gather | solution.py:81
  88.5 516.1 %all-gather.18.cloned.1.call-start = ((), (), s32[]{:S(2)}) async-start(), calls=%async_computation.24 | async-start | bytes 2162688 | tf_op jit(solution)/shard_map/all_gather | solution.py:74
  89.3 521.4 %all-gather.22.cloned.1.call-start = ((), (), s32[]{:S(2)}) async-start(), calls=%async_computation.26 | async-start | bytes 10485760 | tf_op jit(solution)/shard_map/all_gather | solution.py:88
  170.1 61.2 %all-to-all-start.2 = ((bf16[6,128,4,256]{3,1,0,2:T(8,128)(2,1)}), bf16[6,128,4,256]{3,1,0,2:T(8,128)(2,1)S(1)}, u32[]{:S(2)}, u32[]{:S(2)}) async-start(bf16[6,128,4,256]{3,1,0,2:T(8,128)(2,1)} %copy.253), calls=%async_computation.2 | async-start | bytes 3145728 | tf_op jit(solution)/shard_map/all_to_all | solution.py:100
  231.3 129.5 %all-to-all-start.1 = ((bf16[6,128,4,256]{3,1,0,2:T(8,128)(2,1)}), bf16[6,128,4,256]{3,1,0,2:T(8,128)(2,1)S(1)}, u32[]{:S(2)}, u32[]{:S(2)}) async-start(bf16[6,128,4,256]{3,1,0,2:T(8,128)(2,1)} %copy.251), calls=%async_computation.1 | async-start | bytes 3145728 | tf_op jit(solution)/shard_map/all_to_all | solution.py:99
  301.5 109.6 %collective-permute-start = (bf16[4,170,512]{2,0,1:T(4,128)(2,1)}, bf16[4,170,512]{2,0,1:T(4,128)(2,1)}, u32[]{:S(2)}, u32[]{:S(2)}) collective-permute-start(bf16[4,170,512]{2,0,1:T(4,128)(2,1)} %copy.248), channel_id=1, source_target_pairs={{0,1},{1,2},{2,3},{3,4},{4,5},{5,6},{6,7},{8,9},{9,10},{10,11},{11... | collective-permute-start | bytes 2088968 | tf_op jit(solution)/shard_map/ppermute | solution.py:20
  360.8 53.5 %all-to-all-start.3 = ((bf16[6,128,4,256]{3,1,0,2:T(8,128)(2,1)}), bf16[6,128,4,256]{3,1,0,2:T(8,128)(2,1)}, u32[]{:S(2)}, u32[]{:S(2)}) async-start(bf16[6,128,4,256]{3,1,0,2:T(8,128)(2,1)} %copy.255), calls=%async_computation.3 | async-start | bytes 3145728 | tf_op jit(solution)/shard_map/all_to_all | solution.py:98
  365.2 258.5 %all-gather.26.cloned.1.call-start = ((), (), s32[]{:S(2)}) async-start(), calls=%async_computation.28 | async-start | bytes 10485760 | tf_op jit(solution)/shard_map/all_gather | solution.py:89
  661.7 219.3 %all-reduce.19.cloned.1.call-start = ((), (), s32[]{:S(2)}) async-start(), calls=%async_computation.29 | async-start | bytes 4194304 | tf_op jit(solution)/shard_map/psum | solution.py:272
  829.4 125.8 %reduce-scatter.20.cloned.1.call-start = ((), (), s32[]{:S(2)}) async-start(), calls=%async_computation.34 | async-start | bytes 10485760 | tf_op jit(solution)/shard_map/reduce_scatter | solution.py:183
  841.5 188.2 %reduce-scatter.22.cloned.1.call-start = ((), (), s32[]{:S(2)}) async-start(), calls=%async_computation.35 | async-start | bytes 10485760 | tf_op jit(solution)/shard_map/reduce_scatter | solution.py:186
  857.8 452.5 %reduce-scatter.26.cloned.1.call-start = ((), (), s32[]{:S(2)}) async-start(), calls=%async_computation.37 | async-start | bytes 1769472 | tf_op jit(solution)/shard_map/reduce_scatter | solution.py:335
  885.6 426.5 %reduce-scatter.28.cloned.1.call-start = ((), (), s32[]{:S(2)}) async-start(), calls=%async_computation.38 | async-start | bytes 2359296
  959.2 354.8 %reduce-scatter.24.cloned.1.call-start = ((), (), s32[]{:S(2)}) async-start(), calls=%async_computation.36 | async-start | bytes 2359296 | tf_op jit(solution)/shard_map/reduce_scatter | solution.py:332
  1029.8 353.5 %reduce-scatter.18.cloned.1.call-start = ((), (), s32[]{:S(2)}) async-start(), calls=%async_computation.33 | async-start | bytes 4325376 | tf_op jit(solution)/shard_map/reduce_scatter | solution.py:343
  1042.6 486.0 %reduce-scatter.12.cloned.1.call-start = ((), (), s32[]{:S(2)}) async-start(), calls=%async_computation.30 | async-start | bytes 4325376 | tf_op jit(solution)/shard_map/reduce_scatter | solution.py:340
  1076.6 598.0 %reduce-scatter.16.cloned.1.call-start = ((), (), s32[]{:S(2)}) async-start(), calls=%async_computation.32 | async-start | bytes 4325376 | tf_op jit(solution)/shard_map/reduce_scatter | solution.py:342
  1171.4 646.5 %reduce-scatter.14.cloned.1.call-start = ((), (), s32[]{:S(2)}) async-start(), calls=%async_computation.31 | async-start | bytes 4325376 | tf_op jit(solution)/shard_map/reduce_scatter | solution.py:341
  (86 other events, 1039.4 us)
Sparse Core Ops, SparseCore 0:
  10.2 44.3 all-gather.9
  56.6 48.9 all-gather.19
  108.6 55.4 all-gather.13
  166.9 55.5 all-gather.11
  224.7 62.3 all-reduce.16
  290.4 58.5 all-gather.15
  351.3 47.7 all-gather.23
  402.6 55.6 all-gather.17
  459.9 58.2 all-gather.21
  519.7 64.9 all-gather.25
  829.6 51.4 all-reduce.18
  883.4 71.7 reduce-scatter.19
  958.0 71.6 reduce-scatter.21
  1033.1 64.3 reduce-scatter.25
  1101.2 72.8 reduce-scatter.27
  1177.9 66.7 reduce-scatter.23
  1247.5 135.7 reduce-scatter.17
  1386.1 142.4 reduce-scatter.11
  1531.5 142.9 reduce-scatter.15
  1677.3 140.4 reduce-scatter.13

commit v2 on v1

v2 whole, which is shorter than its diff:
```python
import jax
import jax.numpy as jnp
from jax import lax
from jax.sharding import PartitionSpec as P

HD = 128
RATE = 3
CSEGS = 3


EPS = 1e-05
NEG = -1e30
ROWS_IN = (((0,), (0,)), ((), ()))
COLS_IN = (((1,), (1,)), ((), ()))


def passed_along(value, axis, steps):
    count = lax.axis_size(axis)
    leading, last = (max(0, -steps), min(count, count - steps))
    return lax.ppermute(value, axis, [(source, source + steps) for source in range(leading, last)])


def layer_norm(values, gain):
    average = jnp.mean(values, axis=-1, keepdims=True)
    center = values - average
    variance = jnp.mean(center * center, axis=-1, keepdims=True)
    return center * lax.rsqrt(variance + EPS) * gain


def silu_slope(values):
    sig = jax.nn.sigmoid(values)
    return sig * (1.0 + values * (1.0 - sig))


def key_layout(seg_len, comp_rows, comp_segs, rate):
    groups = []
    places = []
    for lag in range(comp_segs + 1, 1, -1):
        groups.append(jnp.full((comp_rows,), lag, jnp.int32))
        places.append(rate * jnp.arange(comp_rows, dtype=jnp.int32) + rate // 2 - lag * seg_len)
    groups.append(jnp.full((seg_len,), 1, jnp.int32))
    places.append(jnp.arange(seg_len, dtype=jnp.int32) - seg_len)
    groups.append(jnp.zeros((seg_len,), jnp.int32))
    places.append(jnp.arange(seg_len, dtype=jnp.int32))
    return (jnp.concatenate(groups), jnp.concatenate(places))


def make_scores(query_heads, key_heads, group, place, seg_place, slopes):
    seg_len = query_heads.shape[0]
    positions = jnp.arange(seg_len, dtype=jnp.int32)
    allowed = (group[None, :] <= seg_place) & (place[None, :] <= positions[:, None])
    distance = (positions[:, None] - place[None, :]).astype(jnp.float32)
    raw = jnp.einsum("qhd,khd->hqk", query_heads, key_heads, preferred_element_type=jnp.float32)
    scores = raw * HD ** (-0.5) - slopes[:, None, None] * distance[None]
    return jnp.where(allowed[None], scores, NEG)


def head_swap(value, bit):
    count = lax.axis_size("head")
    return lax.ppermute(value, "head", [(source, source ^ bit) for source in range(count)])


def gather_over_head(value):
    seg_count, quarter, width = value.shape
    head_index = lax.axis_index("head")
    far = head_swap(value, 2)
    near = head_swap(value, 1)
    far_near = head_swap(far, 1)
    blocks = lax.axis_size("head")
    whole = jnp.zeros((seg_count, blocks, quarter, width), value.dtype)
    for block, held in ((0, value), (1, near), (2, far), (3, far_near)):
        whole = lax.dynamic_update_slice(
            whole, held[:, None], (0, jnp.bitwise_xor(head_index, block), 0, 0)
        )
    return whole.reshape(seg_count, blocks * quarter, width)


def scatter_over_head(pieces):
    head_index = lax.axis_index("head")

    def term(bits):
        return pieces(jnp.bitwise_xor(head_index, bits))

    sent = jnp.stack([term(1), term(3)]).astype(jnp.bfloat16)
    got = head_swap(sent, 1).astype(jnp.float32)
    far = (term(2) + got[1]).astype(jnp.bfloat16)
    return term(0) + got[0] + head_swap(far, 2).astype(jnp.float32)


def per_device(tokens, wq, wk, wv, wo, w_up, w_down, gain_one, gain_two, w_comp, lengths, grad_out):
    seg_count, quarter, width = tokens.shape
    head_groups = lax.axis_size("head")
    blk_count = lax.axis_size("blk")
    devices = head_groups * blk_count
    seg_len = quarter * head_groups
    head_cols = width // head_groups
    local_heads = head_cols // HD
    comp_rows = seg_len // RATE
    window = CSEGS + 1
    head_index = lax.axis_index("head")
    blk_index = lax.axis_index("blk")
    col_start = head_index * head_cols
    token_count = seg_count * quarter
    full_count = seg_count * seg_len
    comp_count = seg_count * comp_rows
    part = wq.shape[0]
    ff_part = w_down.shape[0]
    both = ("head", "blk")
    gains = jnp.pad(jnp.concatenate([gain_one, gain_two])[None], ((0, 7), (0, width - 2 * part)))
    first_pack = jnp.concatenate([wq, wk, wv, w_comp.reshape(RATE * part, width), gains], 0)
    second_pack = jnp.concatenate([wo, w_up.T, w_down], 0)
    first_all = lax.all_gather(first_pack, both, axis=0)
    second_all = lax.all_gather(second_pack, both, axis=0)
    full_tokens = gather_over_head(tokens)
    gain_first = first_all[:, 6 * part, :part].reshape(width).astype(jnp.float32)
    gain_second = first_all[:, 6 * part, part : 2 * part].reshape(width).astype(jnp.float32)
    mine = lax.dynamic_slice_in_dim(first_all[:, : 3 * part], col_start, head_cols, 2)
    wqkv = (
        mine.reshape(devices, 3, part, head_cols)
        .transpose(0, 2, 1, 3)
        .reshape(width, 3 * head_cols)
    )
    wkv = wqkv[:, head_cols:]
    comp_matrix = (
        first_all[:, 3 * part : 6 * part]
        .reshape(devices, RATE, part, width)
        .transpose(1, 0, 2, 3)
        .reshape(RATE * width, width)
    )
    wo_all = second_all[:, :part].reshape(width, width)
    up_all = second_all[:, part : part + ff_part].reshape(devices * ff_part, width)
    down_all = second_all[:, part + ff_part :].reshape(devices * ff_part, width)

    full_rows = full_tokens.reshape(full_count, width).astype(jnp.float32)
    normed = layer_norm(full_rows, gain_first).astype(jnp.bfloat16)
    heads = jnp.dot(normed, wqkv, preferred_element_type=jnp.float32).astype(jnp.bfloat16)
    heads = heads.reshape(seg_count, seg_len, 3 * head_cols)
    heads_q = heads[..., :head_cols]
    own_pair = heads[..., head_cols:]
    grouped = normed.reshape(seg_count, seg_len, width)[:, : RATE * comp_rows].reshape(
        comp_count, RATE * width
    )
    packed = jnp.dot(grouped, comp_matrix, preferred_element_type=jnp.float32).astype(jnp.bfloat16)
    comp_pair = (
        jnp.dot(packed, wkv, preferred_element_type=jnp.float32)
        .astype(jnp.bfloat16)
        .reshape(seg_count, comp_rows, 2 * head_cols)
    )
    compressed = lax.dynamic_slice_in_dim(packed, col_start, head_cols, 1).reshape(
        seg_count, comp_rows, head_cols
    )
    recv_mem, recv_comp = passed_along(
        (own_pair[seg_count - 1 :], comp_pair[seg_count - window :]), "blk", 1
    )
    comp_ext = jnp.concatenate([recv_comp, comp_pair], 0)
    mem_ext = jnp.concatenate([recv_mem, own_pair], 0)
    order = jnp.arange(lengths.shape[0], dtype=jnp.int32)
    starts = jnp.sum(jnp.where(order[None, :] < order[:, None], lengths[None, :], 0), axis=1)
    seg_ids = blk_index * seg_count + jnp.arange(seg_count, dtype=jnp.int32)
    seg_place = seg_ids - jnp.max(
        jnp.where(starts[None, :] <= seg_ids[:, None], starts[None, :], 0), axis=1
    )
    pieces = [comp_ext[window - lag : window - lag + seg_count] for lag in range(CSEGS + 1, 1, -1)]
    pairs = jnp.concatenate(pieces + [mem_ext[:seg_count], own_pair], 1)
    head_ids = head_index * local_heads + jnp.arange(local_heads, dtype=jnp.int32)
    slopes = jnp.exp2(-head_ids.astype(jnp.float32)) / 64.0
    group, place = key_layout(seg_len, comp_rows, CSEGS, RATE)

    def attend_fwd(args):
        query_seg, pair_seg, place_seg = args
        query_heads = query_seg.reshape(seg_len, local_heads, HD)
        key_heads = pair_seg[:, :head_cols].reshape(-1, local_heads, HD)
        value_heads = pair_seg[:, head_cols:].reshape(-1, local_heads, HD)
        scores = make_scores(query_heads, key_heads, group, place, place_seg, slopes)
        row_top = jnp.max(scores, axis=-1, keepdims=True)
        weights = jnp.exp(scores - row_top)
        total = jnp.sum(weights, axis=-1, keepdims=True)
        probs = (weights / total).astype(jnp.bfloat16)
        result = jnp.einsum("hqk,khd->qhd", probs, value_heads, preferred_element_type=jnp.float32)
        return (result.reshape(seg_len, head_cols).astype(jnp.bfloat16), row_top + jnp.log(total))

    attn_out, log_total = lax.map(attend_fwd, (heads_q, pairs, seg_place))
    mixed = lax.all_to_all(
        attn_out.reshape(seg_count, seg_len, 1, head_cols),
        "head",
        split_axis=1,
        concat_axis=2,
        tiled=True,
    ).reshape(token_count, width)
    token_rows = tokens.reshape(token_count, width).astype(jnp.float32)
    branch = jnp.dot(mixed, wo_all, preferred_element_type=jnp.float32)
    hidden = token_rows + branch
    normed_two = layer_norm(hidden, gain_second).astype(jnp.bfloat16)
    lifted = lax.dot_general(normed_two, up_all, COLS_IN, preferred_element_type=jnp.float32)
    active = jax.nn.silu(lifted).astype(jnp.bfloat16)
    ffn_term = jnp.dot(active, down_all, preferred_element_type=jnp.float32)
    out_tokens = (hidden + ffn_term).astype(jnp.bfloat16).reshape(tokens.shape)
    upstream = grad_out.reshape(token_count, width)
    grad_down = lax.dot_general(active, upstream, ROWS_IN, preferred_element_type=jnp.float32)
    grad_active = lax.dot_general(upstream, down_all, COLS_IN, preferred_element_type=jnp.float32)
    grad_lifted = (grad_active * silu_slope(lifted)).astype(jnp.bfloat16)
    grad_up = lax.dot_general(grad_lifted, normed_two, ROWS_IN, preferred_element_type=jnp.float32)
    grad_normed_two = jnp.dot(grad_lifted, up_all, preferred_element_type=jnp.float32)
    second_value, second_pull = jax.vjp(layer_norm, hidden, gain_second)
    grad_hidden_norm, grad_gain_two = second_pull(grad_normed_two)
    grad_hidden = upstream.astype(jnp.float32) + grad_hidden_norm
    grad_branch = grad_hidden.astype(jnp.bfloat16)
    grad_wo = lax.dot_general(mixed, grad_branch, ROWS_IN, preferred_element_type=jnp.float32)
    first_grads = jnp.concatenate(
        [
            grad_wo.astype(jnp.bfloat16).reshape(devices, part, width),
            grad_up.astype(jnp.bfloat16).reshape(devices, ff_part, width),
            grad_down.astype(jnp.bfloat16).reshape(devices, ff_part, width),
        ],
        1,
    )
    first_sum = lax.psum_scatter(first_grads, both, scatter_dimension=0).astype(jnp.float32)
    grad_mixed = lax.dot_general(
        grad_branch, wo_all, COLS_IN, preferred_element_type=jnp.float32
    ).astype(jnp.bfloat16)
    grad_heads = lax.all_to_all(
        grad_mixed.reshape(seg_count, quarter, head_groups, head_cols),
        "head",
        split_axis=2,
        concat_axis=1,
        tiled=True,
    ).reshape(seg_count, seg_len, head_cols)
    def attend_back(args):
        query_seg, pair_seg, place_seg, lse_seg, grad_seg = args
        query_heads = query_seg.reshape(seg_len, local_heads, HD)
        key_heads = pair_seg[:, :head_cols].reshape(-1, local_heads, HD)
        value_heads = pair_seg[:, head_cols:].reshape(-1, local_heads, HD)
        scores = make_scores(query_heads, key_heads, group, place, place_seg, slopes)
        probs = jnp.exp(scores - lse_seg)
        grad_seg_heads = grad_seg.reshape(seg_len, local_heads, HD)
        grad_probs = jnp.einsum(
            "qhd,khd->hqk", grad_seg_heads, value_heads, preferred_element_type=jnp.float32
        )
        grad_scores = (
            probs * (grad_probs - jnp.sum(probs * grad_probs, axis=-1, keepdims=True))
        ).astype(jnp.bfloat16)
        grad_query_seg = jnp.einsum(
            "hqk,khd->qhd", grad_scores, key_heads, preferred_element_type=jnp.float32
        ) * HD ** (-0.5)
        grad_key_seg = jnp.einsum(
            "hqk,qhd->khd", grad_scores, query_heads, preferred_element_type=jnp.float32
        ) * HD ** (-0.5)
        grad_value_seg = jnp.einsum(
            "hqk,qhd->khd",
            probs.astype(jnp.bfloat16),
            grad_seg_heads,
            preferred_element_type=jnp.float32,
        )
        key_count = pair_seg.shape[0]
        grad_pair_seg = jnp.concatenate(
            [
                grad_key_seg.reshape(key_count, head_cols),
                grad_value_seg.reshape(key_count, head_cols),
            ],
            1,
        )
        return (grad_query_seg.reshape(seg_len, head_cols).astype(jnp.bfloat16), grad_pair_seg)

    grad_query, grad_pairs = lax.map(
        attend_back, (heads_q, pairs, seg_place, log_total, grad_heads)
    )
    grad_comp_ext = jnp.zeros((window + seg_count, comp_rows, 2 * head_cols), jnp.float32)
    for piece_index in range(CSEGS):
        lag = CSEGS + 1 - piece_index
        piece = grad_pairs[:, piece_index * comp_rows : (piece_index + 1) * comp_rows]
        grad_comp_ext = grad_comp_ext + jnp.pad(piece, ((window - lag, lag), (0, 0), (0, 0)))
    mem_start = CSEGS * comp_rows
    grad_mem = grad_pairs[:, mem_start : mem_start + seg_len]
    grad_own = grad_pairs[:, mem_start + seg_len :]
    grad_mem_ext = jnp.pad(grad_mem, ((0, 1), (0, 0), (0, 0))) + jnp.pad(
        grad_own, ((1, 0), (0, 0), (0, 0))
    )
    back_mem = grad_mem_ext[:1]
    own_pair_grad = grad_mem_ext[1:]
    back_comp = grad_comp_ext[:window]
    comp_pair_grad = grad_comp_ext[window:]
    got_mem = passed_along(back_mem.astype(jnp.bfloat16), "blk", -1).astype(back_mem.dtype)
    got_comp = passed_along(back_comp.astype(jnp.bfloat16), "blk", -1).astype(back_comp.dtype)
    joined_mem = jnp.pad(got_mem, ((seg_count, 0), (0, 0), (0, 0)))
    own_pair_grad = own_pair_grad + joined_mem[1:]
    joined_comp = jnp.pad(got_comp, ((seg_count, 0), (0, 0), (0, 0)))
    comp_pair_grad = comp_pair_grad + joined_comp[window:]
    grad_qkv = jnp.concatenate([grad_query, own_pair_grad.astype(jnp.bfloat16)], 2).reshape(
        full_count, 3 * head_cols
    )
    comp_grad_rows = comp_pair_grad.reshape(comp_count, 2 * head_cols).astype(jnp.bfloat16)
    grad_packed_part = lax.dot_general(
        comp_grad_rows, wkv, COLS_IN, preferred_element_type=jnp.float32
    )
    grad_packed_mine = scatter_over_head(
        lambda block: lax.dynamic_slice_in_dim(grad_packed_part, block * head_cols, head_cols, 1)
    ).astype(jnp.bfloat16)
    grad_grouped = lax.dot_general(
        grad_packed_part.astype(jnp.bfloat16), comp_matrix, COLS_IN, preferred_element_type=jnp.float32
    ).astype(jnp.bfloat16)
    grad_sent = jnp.pad(
        grad_grouped.reshape(seg_count, RATE * comp_rows, width),
        ((0, 0), (0, seg_len - RATE * comp_rows), (0, 0)),
    )
    grad_normed_part = lax.dot_general(
        grad_qkv, wqkv, COLS_IN, preferred_element_type=jnp.float32
    ).reshape(seg_count, head_groups, quarter, width) + grad_sent.reshape(
        seg_count, head_groups, quarter, width
    ).astype(jnp.float32)
    average = jnp.mean(full_rows, axis=-1, keepdims=True)
    center = full_rows - average
    spread = lax.rsqrt(jnp.mean(center * center, axis=-1, keepdims=True) + EPS)
    grad_gain_one = jnp.sum(grad_normed_part.reshape(full_count, width) * (center * spread), axis=0)
    grad_normed = scatter_over_head(
        lambda block: lax.dynamic_slice_in_dim(grad_normed_part, block, 1, 1)
    ).reshape(token_count, width)
    first_value, first_pull = jax.vjp(lambda rows: layer_norm(rows, gain_first), token_rows)
    (grad_rows_norm,) = first_pull(grad_normed)
    grad_tokens = (grad_hidden + grad_rows_norm).astype(jnp.bfloat16).reshape(tokens.shape)
    comp_term = lax.dot_general(packed, comp_grad_rows, ROWS_IN, preferred_element_type=jnp.float32)
    grad_wqkv = lax.dot_general(normed, grad_qkv, ROWS_IN, preferred_element_type=jnp.float32)
    grad_wqkv = grad_wqkv + jnp.pad(comp_term, ((0, 0), (head_cols, 0)))
    grad_comp = lax.dot_general(
        grouped, grad_packed_mine, ROWS_IN, preferred_element_type=jnp.float32
    )

    def by_owner(value, kinds):
        return value.astype(jnp.bfloat16).reshape(
            kinds, head_groups, blk_count, part, head_cols
        ).transpose(2, 1, 0, 3, 4).reshape(blk_count, head_groups, kinds * part, head_cols)

    gain_rows = jnp.stack(
        [grad_gain_one.reshape(head_groups, blk_count, part), grad_gain_two.reshape(head_groups, blk_count, part)], 2
    ).transpose(1, 0, 2, 3).astype(jnp.bfloat16)
    second_grads = jnp.concatenate(
        [
            by_owner(jnp.concatenate([grad_wqkv[:, i * head_cols : (i + 1) * head_cols] for i in range(3)], 0), 3),
            by_owner(grad_comp, RATE),
            jnp.pad(gain_rows, ((0, 0), (0, 0), (0, 14), (0, head_cols - part))),
        ],
        2,
    )
    second_part = lax.psum_scatter(second_grads, "blk", scatter_dimension=0)
    second_sum = lax.all_to_all(second_part, "head", split_axis=0, concat_axis=0, tiled=True).astype(
        jnp.float32
    )
    gain_sum = jnp.sum(second_sum[:, 6 * part : 6 * part + 2, :part], axis=0)
    weight_sum = (
        second_sum[:, : 6 * part]
        .reshape(head_groups, 6, part, head_cols)
        .transpose(1, 2, 0, 3)
        .reshape(6, part, width)
    )
    return (
        out_tokens,
        compressed,
        grad_tokens,
        weight_sum[0],
        weight_sum[1],
        weight_sum[2],
        first_sum[:part],
        first_sum[part : part + ff_part].T,
        first_sum[part + ff_part :],
        gain_sum[0],
        gain_sum[1],
        weight_sum[3:],
    )


def solution(mesh):
    return jax.shard_map(
        per_device,
        mesh=mesh,
        in_specs=(
            P("blk", "head", None),
            P(("head", "blk"), None),
            P(("head", "blk"), None),
            P(("head", "blk"), None),
            P(("head", "blk"), None),
            P(None, ("head", "blk")),
            P(("head", "blk"), None),
            P(("head", "blk")),
            P(("head", "blk")),
            P(None, ("head", "blk"), None),
            P(),
            P("blk", "head", None),
        ),
        out_specs=(
            P("blk", "head", None),
            P("blk", None, "head"),
            P("blk", "head", None),
            P(("head", "blk"), None),
            P(("head", "blk"), None),
            P(("head", "blk"), None),
            P(("head", "blk"), None),
            P(None, ("head", "blk")),
            P(("head", "blk"), None),
            P(("head", "blk")),
            P(("head", "blk")),
            P(None, ("head", "blk"), None),
        ),
        check_vma=False,
    )
```

time: 1850 us -> 1020 us (0.55)
  waiting for transfers between devices: 1040 us -> 356 us
  blocking collectives: 163 us -> 0 us
  other arithmetic: 70.6 us -> 142 us
    reduce_scatter x8 -> x2, waiting for transfers between devices: 642 us -> 173 us  [the longest x1 173 us: per_device(): lax.psum_scatter(first_grads, both, scatter_dimension=0).astype(jnp.float32)]
    all_gather x9 -> x2, waiting for transfers between devices: 197 us -> 39.3 us  [the longest x1 39.3 us: per_device(): first_all = lax.all_gather(first_pack, both, axis=0)]
    unnamed x2 -> x0, blocking collectives: 82.8 us -> none
    ppermute x0 -> x7, waiting for transfers between devices: none -> 82.3 us  [head_swap(): lax.ppermute(value, 'head', [(source, source ^ bit) for source in range(c...]
    all_to_all x3 -> x0, blocking collectives: 80 us -> none  [the longest x1 28.4 us: per_device(): lax.all_to_all(grad_key_heads.reshape(back_shape), 'head', split_axis=1,...]
    psum x2 -> x0, waiting for transfers between devices: 73.2 us -> none  [the longest x1 52.1 us: per_device(): packed = lax.psum(packed_part.astype(jnp.bfloat16), 'head')]
    concatenate x1, local copies, waits for them, and re-layouts: 56.9 us -> 17.4 us  [per_device(): pairs = jnp.concatenate(pieces + [mem_ext[:seg_count], own_pair], 1)]
    ppermute x4, waiting for transfers between devices: 45.1 us -> 13.7 us  [passed_along(): lax.ppermute(value, axis, [(source, source + steps) for source in range(l...]
  transfers between devices with their start and end apart: 31 -> 18, of which waited for: 20 -> 11; matrix products, arithmetic and copies ran while one was open for 21% -> 31% of each run, Pallas kernels for 0% -> 0%
where the time goes in v2:
time: 1020 us; the launch traced here: 1010 us
  waiting for transfers between devices  356 us (35%)
  local copies, waits for them, and re-layouts  255 us (25%)
  matrix products  210 us (21%)
  other arithmetic  142 us (14%)
  starting transfers between devices  27.5 us (3%)
  between operations  15.3 us (2%)
    reduce_scatter x1, waiting for transfers between devices, per_device(): lax.psum_scatter(first_grads, both, scatter_dimension=0).astype(jnp.float32)  173 us
    ppermute x7, waiting for transfers between devices, head_swap(): lax.ppermute(value, 'head', [(source, source ^ bit) for source in range(c...  82.3 us
    while x2, local copies, waits for them, and re-layouts, per_device(): lax.map(attend_back, (heads_q, pairs, seg_place, log_total, grad_heads))  41.3 us
    all_gather x1, waiting for transfers between devices, per_device(): first_all = lax.all_gather(first_pack, both, axis=0)  39.3 us
    dot_general x12, matrix products, make_scores(): jnp.einsum('qhd,khd->hqk', query_heads, key_heads, preferred_element_type...  32.2 us
    unnamed x133, local copies, waits for them, and re-layouts  31.6 us
    all_to_all x1, waiting for transfers between devices, per_device(): lax.all_to_all(attn_out.reshape(seg_count, seg_len, 1, head_cols), 'head'...  25.6 us
    dynamic_slice x36, local copies, waits for them, and re-layouts, per_device(): attn_out, log_total = lax.map(attend_fwd, (heads_q, pairs, seg_place))  25.3 us
  transfers between devices with their start and end apart: 18, of which 11 were waited for; matrix products, arithmetic and copies ran while one was open for 31% of the time, Pallas kernels for 0%

profile of v2, /device:TPU:24, one launch (start us, length us, event | category | flops | bytes accessed | tf_op | source)
XLA Modules:
  0.0 1007.0 jit_solution(15073009721603157688)
XLA Ops:
  13.9 43.6 %collective-permute-done.1 = bf16[6,128,1024]{2,1,0:T(8,128)(2,1)S(1)} collective-permute-done((bf16[6,128,1024]{2,1,0:T(8,128)(2,1)}, bf16[6,128,1024]{2,1,0:T(8,128)(2,1)S(1)}, u32[]{:S(2)}, u32[]{:S(2)}) %collective-permute-start.1) | collective-permute-done | bytes 1572896 | tf_op jit(solution)/shard_map/ppermute | solution.py:60
  74.7 39.3 %all-gather.5.cloned.1.call-done = bf16[6400,1024]{1,0:T(8,128)(2,1)} async-done(((bf16[200,1024]{1,0:T(8,128)(2,1)}), bf16[6400,1024]{1,0:T(8,128)(2,1)}) %all-gather.5.cloned.1.call-update) | async-done | bytes 13107216 | tf_op jit(solution)/shard_map/all_gather | solution.py:112
  146.5 9.2 fusion.15
  162.9 10.6 %convolution_convert_fusion.6 = bf16[1020,1024]{1,0:T(8,128)(2,1)S(1)} fusion(bf16[1020,3072]{1,0:T(8,128)(2,1)} %reshape.609, bf16[3072,1024]{1,0:T(8,128)(2,1)} %bitcast.369), kind=kOutput, calls=%fused_computation.114 | convolution fusion | flops 6418329600 | bytes 14647296 | tf_op jit(solution)/shard_map/dot_general | solution.py:143
  198.5 10.1 collective-permute-done.3
  215.5 17.4 %concatenate.50 = bf16[6,1534,512]{1,2,0:T(8,128)(2,1)} concatenate(bf16[6,170,512]{1,2,0:T(8,128)(2,1)} %get-tuple-element.321, bf16[6,170,512]{1,2,0:T(8,128)(2,1)} %get-tuple-element.322, bf16[6,170,512]{1,2,0:T(8,128)(2,1)} %get-tuple-element.320, bf16[6,512,512]{1,2,0:T(8,128)(2,1)} %pad_maximum_fusion.2, bf16[6,512,512]{1,2,0:T(8,128)(2,1)S(1)} %copy.243), dimensions={1} | concatenate | bytes 18849792 | tf_op jit(solution)/shard_map/concatenate | solution.py:164
  232.9 66.9 %while.26 = (s32[]{:T(128)}, bf16[6,512,256]{1,2,0:T(8,128)(2,1)}, f32[6,2,512,1]{2,1,3,0:T(2,128)}, bf16[6,1534,512]{1,2,0:T(8,128)(2,1)}, s32[6]{0:T(128)S(1)}...) while((s32[]{:T(128)}, bf16[6,512,256]{1,2,0:T(8,128)(2,1)}, ...), condition=%wide.region_7.8_spmd.clone, body=%wide.region_4.7_spmd.clone.sunk | while | flops 823239168 | bytes 36185220 | solution.py:182
  308.1 25.6 %all-to-all-done = bf16[6,512,1,256]{3,0,2,1:T(8,128)(2,1)S(1)} async-done(((bf16[6,512,1,256]{3,0,2,1:T(8,128)(2,1)}), bf16[6,512,1,256]{3,0,2,1:T(8,128)(2,1)S(1)}, u32[]{:S(2)}, u32[]{:S(2)}) %all-to-all-start) | async-done | bytes 1572896 | tf_op jit(solution)/shard_map/all_to_all | solution.py:183
  338.3 11.1 %fusion.79 = (bf16[32,128,1024]{2,1,0:T(8,128)(2,1)}, bf16[32,128,1024]{2,1,0:T(8,128)(2,1)S(1)}) fusion(bf16[32,288,1024]{2,1,0:T(8,128)(2,1)} %bitcast.351), kind=kLoop, calls=%fused_computation.208 | loop fusion | bytes 33554432 | tf_op jit(solution)/shard_map/slice | solution.py:131
  351.8 14.3 %fusion.71 = f32[768,4096]{1,0:T(8,128)} fusion(bf16[4096,1024]{1,0:T(8,128)(2,1)} %bitcast.360, f32[768,1024]{1,0:T(8,128)S(1)} %get-tuple-element.344, f32[1024]{0:T(1024)S(1)} %reshape.641, f32[768]{0:T(1024)S(1)} %fusion.61, f32[768]{0:T(1024)S(1)} %broadcast_multiply_fusion.2), kind=kOutput, calls=%fused_computation.201 | convolution fusion | flops 6445596672 | bytes 24127488 | tf_op jit(solution)/shard_map/dot_general | solution.py:194
  366.1 13.4 %fusion.16 = bf16[768,4096]{1,0:T(8,128)(2,1)} fusion(f32[768,4096]{1,0:T(8,128)} %fusion.71, bf16[4096,1024]{1,0:T(8,128)(2,1)S(1)} %bitcast.358, bf16[768,1024]{1,0:T(8,128)(2,1)S(1)} %bitcast.374), kind=kOutput, calls=%fused_computation.44 | convolution fusion | flops 6470762496 | bytes 28835840 | tf_op jit(solution)/shard_map/dot_general | solution.py:200
  379.4 12.5 %multiply_reduce_fusion.3 = (bf16[1024]{0:T(1024)(128)(2,1)}, f32[768]{0:T(1024)S(1)}, f32[768,1024]{1,0:T(8,128)S(1)}) fusion(f32[768,1024]{1,0:T(8,128)S(1)} %get-tuple-element.344, f32[768]{0:T(1024)S(1)} %fusion.61, f32[768]{0:T(1024)S(1)} %broadcast_multiply_fusion.2, f32[1024]{0:T(1024)S(1)} %reshape.641, bf16[768,4096]{1,0:T(8,128)(2,1)} %fusion.16, ...), kind=kOutput, calls=%fused_computation.97 | convolution fusion | flops 6447953920 | bytes 20986880 | tf_op jit(solution)/shard_map/dot_general | solution.py:203
  404.0 20.0 %all-to-all-done.1 = bf16[6,128,4,256]{3,1,0,2:T(8,128)(2,1)S(1)} async-done(((bf16[6,128,4,256]{3,1,0,2:T(8,128)(2,1)}), bf16[6,128,4,256]{3,1,0,2:T(8,128)(2,1)S(1)}, u32[]{:S(2)}, u32[]{:S(2)}) %all-to-all-start.1) | async-done | bytes 1572896 | tf_op jit(solution)/shard_map/all_to_all | solution.py:221
  425.2 114.7 %while.27 = (s32[]{:T(128)}, bf16[6,512,256]{2,1,0:T(8,128)(2,1)}, f32[6,1534,512]{1,2,0:T(8,128)}, bf16[6,1534,512]{1,2,0:T(8,128)(2,1)}, s32[6]{0:T(128)S(1)},...) while((s32[]{:T(128)}, bf16[6,512,256]{2,1,0:T(8,128)(2,1)}, ...), condition=%wide.region_14.15_spmd.clone, body=%wide.region_12.14_spmd.clone.sunk | while | flops 2032505856 | bytes 77072536 | solution.py:264
  539.9 18.7 %copy.210 = f32[6,1534,512]{2,1,0:T(8,128)} copy(f32[6,1534,512]{1,2,0:T(8,128)} %get-tuple-element.111) | data formatting | bytes 37699584 | tf_op jit(solution)/shard_map/while | solution.py:264
  558.6 22.6 %copy.213 = f32[6,1534,512]{2,0,1:T(8,128)} copy(f32[6,1534,512]{1,2,0:T(8,128)} %get-tuple-element.111) | data formatting | bytes 37699584 | tf_op jit(solution)/shard_map/while | solution.py:264
  660.9 13.1 %multiply_reduce_fusion.1 = (bf16[1024]{0:T(1024)(128)(2,1)S(1)}, f32[6,4,128,1024]{3,2,1,0:T(8,128)}) fusion(bf16[6,4,128,1024]{3,2,1,0:T(8,128)(2,1)S(1)} %bitcast.337, f32[6,4,128]{2,1,0:T(4,128)S(1)} %copy-done.39, f32[6,4,128]{2,1,0:T(4,128)S(1)} %copy-done.37, bf16[6,4,128,1024]{3,2,1,0:T(8,128)(2,1)} %bitcast.373, ...), kind=kOutput, calls=%fused_computation.45 | convolution fusion | flops 4853857280 | bytes 31483904 | tf_op jit(solution)/shard_map/dot_general | solution.py:305
  686.0 12.7 %collective-permute-done.10 = bf16[1020,256]{1,0:T(8,128)(2,1)S(1)} collective-permute-done((bf16[1020,256]{1,0:T(8,128)(2,1)S(1)}, bf16[1020,256]{1,0:T(8,128)(2,1)S(1)}, u32[]{:S(2)}, u32[]{:S(2)}) %collective-permute-start.10) | collective-permute-done | bytes 522272 | tf_op jit(solution)/shard_map/ppermute | solution.py:60
  711.5 10.5 %convolution_convert_fusion.1 = bf16[4096,1024]{1,0:T(8,128)(2,1)S(1)} fusion(bf16[768,4096]{1,0:T(8,128)(2,1)} %fusion.16, f32[768,1024]{1,0:T(8,128)S(1)} %copy-done.12, f32[1024]{0:T(1024)S(1)} %copy-done.45, f32[768]{0:T(1024)S(1)} %copy-done.47, f32[768]{0:T(1024)S(1)} %copy-done.41), kind=kOutput, calls=%fused_computation.52 | convolution fusion | flops 6449790976 | bytes 17836032 | tf_op jit(solution)/shard_map/dot_general | solution.py:202
  722.0 10.3 %convolution_convert_fusion = bf16[4096,1024]{1,0:T(8,128)(2,1)S(1)} fusion(bf16[768,1024]{1,0:T(8,128)(2,1)S(1)} %bitcast.375, f32[768,4096]{1,0:T(8,128)} %fusion.71), kind=kOutput, calls=%fused_computation.51 | convolution fusion | flops 6462373888 | bytes 22544384 | tf_op jit(solution)/shard_map/dot_general | solution.py:199
  732.3 16.7 %pad_maximum_fusion = bf16[32,288,1024]{2,1,0:T(8,128)(2,1)} fusion(bf16[32,128,1024]{2,1,0:T(8,128)(2,1)S(1)} %bitcast.363, bf16[32,128,1024]{2,1,0:T(8,128)(2,1)S(1)} %bitcast.362, bf16[32,32,1024]{2,1,0:T(8,128)(2,1)S(1)} %bitcast.390), kind=kLoop, calls=%fused_computation.37 | loop fusion | flops 56623104 | bytes 37748736 | tf_op jit(solution)/shard_map/concatenate | solution.py:209
  766.3 13.5 %add_convert_fusion.1 = bf16[768,1024]{1,0:T(8,128)(2,1)} fusion(f32[768,1024]{1,0:T(8,128)S(1)} %copy-done.13, bf16[4096,1024]{1,0:T(8,128)(2,1)} %bitcast.359, f32[768,4096]{1,0:T(8,128)} %fusion.71), kind=kOutput, calls=%fused_computation.101 | convolution fusion | flops 6459752448 | bytes 25690112 | tf_op jit(solution)/shard_map/dot_general | solution.py:196
  779.8 22.3 %collective-permute-done.8 = bf16[6,1,128,1024]{3,2,1,0:T(8,128)(2,1)S(1)} collective-permute-done((bf16[6,1,128,1024]{3,2,1,0:T(8,128)(2,1)S(1)}, bf16[6,1,128,1024]{3,2,1,0:T(8,128)(2,1)S(1)}, u32[]{:S(2)}, u32[]{:S(2)}) %collective-permute-start.8) | collective-permute-done | bytes 1572896 | tf_op jit(solution)/shard_map/ppermute | solution.py:60
  823.5 173.0 %reduce-scatter.5.cloned.1.call-done = bf16[1,288,1024]{2,1,0:T(8,128)(2,1)} async-done(((bf16[32,288,1024]{2,1,0:T(8,128)(2,1)}), bf16[1,288,1024]{2,1,0:T(8,128)(2,1)}) %reduce-scatter.5.cloned.1.call-update) | async-done | bytes 589840 | tf_op jit(solution)/shard_map/reduce_scatter | solution.py:217
  (515 shorter events, 450.6 us)
Async XLA Ops:
  7.2 106.8 %all-gather.5.cloned.1.call-start = ((), (), s32[]{:S(2)}) async-start(), calls=%async_computation.7 | async-start | bytes 13516800 | tf_op jit(solution)/shard_map/all_gather | solution.py:112
  12.2 324.2 %all-gather.7.cloned.1.call-start = ((), (), s32[]{:S(2)}) async-start(), calls=%async_computation.8 | async-start | bytes 19464192 | tf_op jit(solution)/shard_map/all_gather | solution.py:113
  12.3 45.2 %collective-permute-start.1 = (bf16[6,128,1024]{2,1,0:T(8,128)(2,1)}, bf16[6,128,1024]{2,1,0:T(8,128)(2,1)S(1)}, u32[]{:S(2)}, u32[]{:S(2)}) collective-permute-start(bf16[6,128,1024]{2,1,0:T(8,128)(2,1)} %param.16), channel_id=1, source_target_pairs={{0,16},{8,24},{16,0},{24,8},{1,17},{9,25},{17,1},{25,9},{2,18},{10... | collective-permute-start | bytes 4718600 | tf_op jit(solution)/shard_map/ppermute | solution.py:60
  13.9 48.3 %collective-permute-start = (bf16[6,128,1024]{2,1,0:T(8,128)(2,1)}, bf16[6,128,1024]{2,1,0:T(8,128)(2,1)}, u32[]{:S(2)}, u32[]{:S(2)}) collective-permute-start(bf16[6,128,1024]{2,1,0:T(8,128)(2,1)} %param.16), channel_id=1, source_target_pairs={{0,8},{8,0},{16,24},{24,16},{1,9},{9,1},{17,25},{25,17},{2,10},{10... | collective-permute-start | bytes 4718600 | tf_op jit(solution)/shard_map/ppermute | solution.py:60
  57.5 6.5 collective-permute-start.2
  65.1 65.5 %copy-start.36 = (f32[6,4,128]{2,1,0:T(4,128)}, f32[6,4,128]{2,1,0:T(4,128)S(1)}, u32[]{:S(2)}) copy-start(f32[6,4,128]{2,1,0:T(4,128)S(1)} %get-tuple-element.334) | copy-start | bytes 36868
  67.3 63.3 %copy-start.38 = (f32[6,4,128]{2,1,0:T(4,128)}, f32[6,4,128]{2,1,0:T(4,128)S(1)}, u32[]{:S(2)}) copy-start(f32[6,4,128]{2,1,0:T(4,128)S(1)} %get-tuple-element.331) | copy-start | bytes 36868
  130.6 42.9 %copy-start.23 = (bf16[128,8,3,256]{3,1,2,0:T(8,128)(2,1)}, bf16[128,8,3,256]{3,1,2,0:T(8,128)(2,1)S(1)}, u32[]{:S(2)}) copy-start(bf16[128,8,3,256]{3,1,2,0:T(8,128)(2,1)S(1)} %copy.255) | copy-start | bytes 4718596
  143.0 52.6 %collective-permute-start.4 = (bf16[1,512,512]{1,2,0:T(8,128)(2,1)}, bf16[1,512,512]{1,2,0:T(8,128)(2,1)}, u32[]{:S(2)}, u32[]{:S(2)}) collective-permute-start(bf16[1,512,512]{1,2,0:T(8,128)(2,1)} %copy.242), channel_id=1, source_target_pairs={{0,1},{1,2},{2,3},{3,4},{4,5},{5,6},{6,7},{8,9},{9,10},{10,11},{11... | collective-permute-start | bytes 1572872 | tf_op jit(solution)/shard_map/ppermute | solution.py:20
  176.6 32.0 %collective-permute-start.3 = (bf16[4,170,512]{2,0,1:T(4,128)(2,1)}, bf16[4,170,512]{2,0,1:T(4,128)(2,1)}, u32[]{:S(2)}, u32[]{:S(2)}) collective-permute-start(bf16[4,170,512]{2,0,1:T(4,128)(2,1)} %copy.197), channel_id=1, source_target_pairs={{0,1},{1,2},{2,3},{3,4},{4,5},{5,6},{6,7},{8,9},{9,10},{10,11},{11... | collective-permute-start | bytes 2088968 | tf_op jit(solution)/shard_map/ppermute | solution.py:20
  304.3 29.4 %all-to-all-start = ((bf16[6,512,1,256]{3,0,2,1:T(8,128)(2,1)}), bf16[6,512,1,256]{3,0,2,1:T(8,128)(2,1)S(1)}, u32[]{:S(2)}, u32[]{:S(2)}) async-start(bf16[6,512,1,256]{3,0,2,1:T(8,128)(2,1)} %bitcast.357), calls=%async_computation | async-start | bytes 4194304 | tf_op jit(solution)/shard_map/all_to_all | solution.py:183
  308.1 83.8 %copy-start.44 = (f32[1024]{0:T(1024)}, f32[1024]{0:T(1024)S(1)}, u32[]{:S(2)}) copy-start(f32[1024]{0:T(1024)S(1)} %reshape.641) | copy-start | bytes 12292
  351.3 40.6 %copy-start.11 = (f32[768,1024]{1,0:T(8,128)}, f32[768,1024]{1,0:T(8,128)S(1)}, u32[]{:S(2)}) copy-start(f32[768,1024]{1,0:T(8,128)S(1)} %get-tuple-element.344) | copy-start | bytes 9437188
  351.3 40.6 %copy-start.40 = (f32[768]{0:T(1024)}, f32[768]{0:T(1024)S(1)}, u32[]{:S(2)}) copy-start(f32[768]{0:T(1024)S(1)} %broadcast_multiply_fusion.2) | copy-start | bytes 9220
  400.3 23.6 %all-to-all-start.1 = ((bf16[6,128,4,256]{3,1,0,2:T(8,128)(2,1)}), bf16[6,128,4,256]{3,1,0,2:T(8,128)(2,1)S(1)}, u32[]{:S(2)}, u32[]{:S(2)}) async-start(bf16[6,128,4,256]{3,1,0,2:T(8,128)(2,1)} %copy.207), calls=%async_computation.1 | async-start | bytes 3145728 | tf_op jit(solution)/shard_map/all_to_all | solution.py:221
  403.9 404.5 %reduce-scatter.3.cloned.1.call-start = ((), (), s32[]{:S(2)}) async-start(), calls=%async_computation.5 | async-start | bytes 3833856 | tf_op jit(solution)/shard_map/reduce_scatter | solution.py:343
  593.0 20.3 %collective-permute-start.5 = (bf16[1,512,512]{2,1,0:T(8,128)(2,1)}, bf16[1,512,512]{2,1,0:T(8,128)(2,1)}, u32[]{:S(2)}, u32[]{:S(2)}) collective-permute-start(bf16[1,512,512]{2,1,0:T(8,128)(2,1)} %fusion.50), channel_id=1, source_target_pairs={{1,0},{2,1},{3,2},{4,3},{5,4},{6,5},{7,6},{9,8},{10,9},{11,10},{12... | collective-permute-start | bytes 1572872 | tf_op jit(solution)/shard_map/ppermute | solution.py:20
  604.5 20.2 %collective-permute-start.6 = (bf16[4,170,512]{2,0,1:T(4,128)(2,1)}, bf16[4,170,512]{2,0,1:T(4,128)(2,1)}, u32[]{:S(2)}, u32[]{:S(2)}) collective-permute-start(bf16[4,170,512]{2,0,1:T(4,128)(2,1)} %slice.366), channel_id=1, source_target_pairs={{1,0},{2,1},{3,2},{4,3},{5,4},{6,5},{7,6},{9,8},{10,9},{11,10},{12... | collective-permute-start | bytes 2088968 | tf_op jit(solution)/shard_map/ppermute | solution.py:20
  660.7 20.1 %collective-permute-start.9 = (bf16[2,1020,256]{2,0,1:T(2,128)(2,1)S(1)}, bf16[2,1020,256]{2,0,1:T(2,128)(2,1)}, u32[]{:S(2)}, u32[]{:S(2)}) collective-permute-start(bf16[2,1020,256]{2,0,1:T(2,128)(2,1)S(1)} %copy.221), channel_id=1, source_target_pairs={{0,8},{8,0},{16,24},{24,16},{1,9},{9,1},{17,25},{25,17},{2,10},{10... | collective-permute-start | bytes 3133448 | tf_op jit(solution)/shard_map/ppermute | solution.py:60
  684.8 13.9 %collective-permute-start.10 = (bf16[1020,256]{1,0:T(8,128)(2,1)S(1)}, bf16[1020,256]{1,0:T(8,128)(2,1)S(1)}, u32[]{:S(2)}, u32[]{:S(2)}) collective-permute-start(bf16[1020,256]{1,0:T(8,128)(2,1)S(1)} %fusion.46), channel_id=1, source_target_pairs={{0,16},{8,24},{16,0},{24,8},{1,17},{9,25},{17,1},{25,9},{2,18},{10... | collective-permute-start | bytes 1566728 | tf_op jit(solution)/shard_map/ppermute | solution.py:60
  706.2 290.3 %reduce-scatter.5.cloned.1.call-start = ((), (), s32[]{:S(2)}) async-start(), calls=%async_computation.6 | async-start | bytes 19464192 | tf_op jit(solution)/shard_map/reduce_scatter | solution.py:217
  754.3 6.0 collective-permute-start.7
  765.6 36.5 %collective-permute-start.8 = (bf16[6,1,128,1024]{3,2,1,0:T(8,128)(2,1)S(1)}, bf16[6,1,128,1024]{3,2,1,0:T(8,128)(2,1)S(1)}, u32[]{:S(2)}, u32[]{:S(2)}) collective-permute-start(bf16[6,1,128,1024]{3,2,1,0:T(8,128)(2,1)S(1)} %fusion.27), channel_id=1, source_target_pairs={{0,16},{8,24},{16,0},{24,8},{1,17},{9,25},{17,1},{25,9},{2,18},{10... | collective-permute-start | bytes 4718600 | tf_op jit(solution)/shard_map/ppermute | solution.py:60
  808.4 11.3 %all-to-all-start.2 = ((bf16[4,208,256]{2,1,0:T(8,128)(2,1)}), bf16[4,208,256]{2,1,0:T(8,128)(2,1)S(1)}, u32[]{:S(2)}, u32[]{:S(2)}) async-start(bf16[4,208,256]{2,1,0:T(8,128)(2,1)} %bitcast.404), calls=%async_computation.3 | async-start | bytes 851968 | tf_op jit(solution)/shard_map/all_to_all | solution.py:344
  (64 other events, 475.3 us)
Sparse Core Ops, SparseCore 0:
  12.4 101.5 all-gather.4
  117.0 141.1 all-gather.6
  706.2 77.0 reduce-scatter.2
  790.7 205.7 reduce-scatter.4

commit v3 on v2

v3 whole, which is shorter than its diff:
```python
import jax
import jax.numpy as jnp
from jax import lax
from jax.experimental import pallas as pl
from jax.experimental.pallas import tpu as pltpu
from jax.sharding import PartitionSpec as P

HD = 128
RATE = 3
CSEGS = 3


EPS = 1e-05
NEG = -1e30
ROWS_IN = (((0,), (0,)), ((), ()))
COLS_IN = (((1,), (1,)), ((), ()))


def passed_along(value, axis, steps):
    count = lax.axis_size(axis)
    leading, last = (max(0, -steps), min(count, count - steps))
    return lax.ppermute(value, axis, [(source, source + steps) for source in range(leading, last)])


def layer_norm(values, gain):
    average = jnp.mean(values, axis=-1, keepdims=True)
    center = values - average
    variance = jnp.mean(center * center, axis=-1, keepdims=True)
    return center * lax.rsqrt(variance + EPS) * gain


def silu_slope(values):
    sig = jax.nn.sigmoid(values)
    return sig * (1.0 + values * (1.0 - sig))


LOG2E = 1.4426950408889634
PAD_ROWS = 176
VMEM_LIMIT = 56 * 1024 * 1024


def key_bias(rows, base, step, valid_rows, open_, slope):
    row = lax.broadcasted_iota(jnp.int32, (rows, 1), 0)
    place = (base + step * row).astype(jnp.float32)
    return jnp.where((row < valid_rows) & open_, place * slope, NEG)


def fwd_kernel(place_ref, slope_ref, q_ref, own_ref, prev_ref, recv_ref, comp_ref, out_ref, lse_ref):
    step = pl.program_id(0)
    place = place_ref[step]
    seg_len = q_ref.shape[1]
    half = seg_len // 2
    pad_rows = comp_ref.shape[1]
    local_heads = q_ref.shape[2] // HD
    values_at = local_heads * HD
    factor = HD ** (-0.5) * LOG2E
    lower = lax.broadcasted_iota(jnp.int32, (half, half), 0) <= lax.broadcasted_iota(
        jnp.int32, (half, half), 1
    )
    for h in range(local_heads):
        kc = slice(h * HD, (h + 1) * HD)
        vc = slice(values_at + h * HD, values_at + (h + 1) * HD)
        slope = slope_ref[h]
        parts = []
        for piece in range(CSEGS):
            lag = CSEGS + 1 - piece
            bias = key_bias(pad_rows, RATE // 2 - lag * seg_len, RATE, seg_len // RATE, place >= lag, slope)
            parts.append((comp_ref[step + piece, :, kc], comp_ref[step + piece, :, vc], bias))
        bias = key_bias(seg_len, -seg_len, 1, seg_len, place >= 1, slope)
        is_first = step == 0
        parts.append(
            (
                jnp.where(is_first, recv_ref[0, :, kc], prev_ref[0, :, kc]),
                jnp.where(is_first, recv_ref[0, :, vc], prev_ref[0, :, vc]),
                bias,
            )
        )
        own_bias = [
            key_bias(half, n * half, 1, half, place >= 0, slope) for n in range(2)
        ]
        for n in range(2):
            query = q_ref[0, n * half : (n + 1) * half, kc]
            group = list(parts)
            for m in range(n + 1):
                rows = slice(m * half, (m + 1) * half)
                group.append((own_ref[0, rows, kc], own_ref[0, rows, vc], own_bias[m]))
            scores = []
            top = None
            for index, (k, v, bias) in enumerate(group):
                raw = lax.dot_general(k, query, COLS_IN, preferred_element_type=jnp.float32)
                raw = raw * factor + bias
                if index == len(group) - 1:
                    raw = jnp.where(lower, raw, NEG)
                scores.append(raw)
                peak = jnp.max(raw, axis=0, keepdims=True)
                top = peak if top is None else jnp.maximum(top, peak)
            total = jnp.zeros_like(top)
            result = jnp.zeros((HD, half), jnp.float32)
            for raw, (k, v, bias) in zip(scores, group):
                weight = jnp.exp2(raw - top)
                total = total + jnp.sum(weight, axis=0, keepdims=True)
                result = result + lax.dot_general(
                    v, weight.astype(jnp.bfloat16), ROWS_IN, preferred_element_type=jnp.float32
                )
            result = result * (1.0 / total)
            out_ref[0, n * half : (n + 1) * half, kc] = result.T.astype(jnp.bfloat16)
            lse_ref[0, h : h + 1, n * half : (n + 1) * half] = top + jnp.log(total) * LOG2E


def bwd_kernel(
    place_ref, slope_ref, q_ref, own_ref, prev_ref, recv_ref, comp_ref, grad_ref, att_ref, lse_ref,
    gq_ref, gkv_ref, tail_ref, gcomp_ref,
):
    step = pl.program_id(0)
    place = place_ref[step]
    seg_len = q_ref.shape[1]
    half = seg_len // 2
    pad_rows = comp_ref.shape[1]
    local_heads = q_ref.shape[2] // HD
    values_at = local_heads * HD
    scale = HD ** (-0.5)
    factor = scale * LOG2E
    is_first = step == 0
    lower = lax.broadcasted_iota(jnp.int32, (half, half), 0) <= lax.broadcasted_iota(
        jnp.int32, (half, half), 1
    )

    @pl.when(is_first)
    def _():
        tail_ref[...] = jnp.zeros_like(tail_ref)
        gcomp_ref[...] = jnp.zeros_like(gcomp_ref)

    for h in range(local_heads):
        kc = slice(h * HD, (h + 1) * HD)
        vc = slice(values_at + h * HD, values_at + (h + 1) * HD)
        slope = slope_ref[h]
        query = q_ref[0, :, kc]
        grad = grad_ref[0, :, kc]
        lse = lse_ref[0, h : h + 1, :]
        product = grad.astype(jnp.float32) * att_ref[0, :, kc].astype(jnp.float32)
        delta = jnp.sum(product.T, axis=0, keepdims=True)

        def part(k, v, bias, cols, masked):
            raw = lax.dot_general(k, query[cols], COLS_IN, preferred_element_type=jnp.float32)
            raw = raw * factor + bias
            if masked:
                raw = jnp.where(lower, raw, NEG)
            prob = jnp.exp2(raw - lse[:, cols])
            grad_prob = lax.dot_general(v, grad[cols], COLS_IN, preferred_element_type=jnp.float32)
            grad_score = (prob * (grad_prob - delta[:, cols])).astype(jnp.bfloat16)
            gk = jnp.dot(grad_score, query[cols], preferred_element_type=jnp.float32) * scale
            gv = jnp.dot(prob.astype(jnp.bfloat16), grad[cols], preferred_element_type=jnp.float32)
            gq = lax.dot_general(k, grad_score, ROWS_IN, preferred_element_type=jnp.float32)
            return gk, gv, gq

        every = slice(0, seg_len)
        total = jnp.zeros((HD, seg_len), jnp.float32)
        for piece in range(CSEGS):
            lag = CSEGS + 1 - piece
            bias = key_bias(pad_rows, RATE // 2 - lag * seg_len, RATE, seg_len // RATE, place >= lag, slope)
            gk, gv, gq = part(comp_ref[step + piece, :, kc], comp_ref[step + piece, :, vc], bias, every, False)
            gcomp_ref[step + piece, :, kc] += gk
            gcomp_ref[step + piece, :, vc] += gv
            total = total + gq
        for n in range(2):
            rows = slice(n * half, (n + 1) * half)
            bias = key_bias(half, n * half - seg_len, 1, half, place >= 1, slope)
            k = jnp.where(is_first, recv_ref[0, rows, kc], prev_ref[0, rows, kc])
            v = jnp.where(is_first, recv_ref[0, rows, vc], prev_ref[0, rows, vc])
            gk, gv, gq = part(k, v, bias, every, False)
            gkv_ref[0, rows, kc] = (tail_ref[rows, kc] + gk).astype(jnp.bfloat16)
            gkv_ref[0, rows, vc] = (tail_ref[rows, vc] + gv).astype(jnp.bfloat16)
            total = total + gq
        lo, hi = slice(0, half), slice(half, seg_len)
        bias_lo = key_bias(half, 0, 1, half, place >= 0, slope)
        bias_hi = key_bias(half, half, 1, half, place >= 0, slope)
        gk0, gv0, gq0 = part(own_ref[0, lo, kc], own_ref[0, lo, vc], bias_lo, lo, True)
        gk1, gv1, gq1 = part(own_ref[0, lo, kc], own_ref[0, lo, vc], bias_lo, hi, False)
        gk2, gv2, gq2 = part(own_ref[0, hi, kc], own_ref[0, hi, vc], bias_hi, hi, True)
        tail_ref[lo, kc] = gk0 + gk1
        tail_ref[lo, vc] = gv0 + gv1
        tail_ref[hi, kc] = gk2
        tail_ref[hi, vc] = gv2
        gq_ref[0, lo, kc] = ((total[:, lo] + gq0) * scale).T.astype(jnp.bfloat16)
        gq_ref[0, hi, kc] = ((total[:, hi] + gq1 + gq2) * scale).T.astype(jnp.bfloat16)


def attention_specs(seg_len, head_cols, comp_shape):
    pair = 2 * head_cols
    return [
        pl.BlockSpec(memory_space=pltpu.SMEM),
        pl.BlockSpec(memory_space=pltpu.SMEM),
        pl.BlockSpec((1, seg_len, head_cols), lambda s: (s, 0, 2)),
        pl.BlockSpec((1, seg_len, pair), lambda s: (s, 0, 0)),
        pl.BlockSpec((1, seg_len, pair), lambda s: (jnp.maximum(s - 1, 0), 0, 0)),
        pl.BlockSpec((1, seg_len, pair), lambda s: (0, 0, 0)),
        pl.BlockSpec(comp_shape, lambda s: (0, 0, 0)),
    ]


def attend_fwd(place, slope, heads, recv_mem, comp_ext, head_cols):
    seg_count, seg_len, _ = heads.shape
    local_heads = head_cols // HD
    return pl.pallas_call(
        fwd_kernel,
        grid=(seg_count,),
        in_specs=attention_specs(seg_len, head_cols, comp_ext.shape),
        out_specs=[
            pl.BlockSpec((1, seg_len, head_cols), lambda s: (s, 0, 0)),
            pl.BlockSpec((1, local_heads, seg_len), lambda s: (s, 0, 0)),
        ],
        out_shape=[
            jax.ShapeDtypeStruct((seg_count, seg_len, head_cols), jnp.bfloat16),
            jax.ShapeDtypeStruct((seg_count, local_heads, seg_len), jnp.float32),
        ],
        compiler_params=pltpu.CompilerParams(vmem_limit_bytes=VMEM_LIMIT),
        cost_estimate=pl.CostEstimate(flops=5 * 10**9, bytes_accessed=16 * 10**6, transcendentals=10**7),
        name="attend_fwd",
    )(place, slope, heads, heads, heads, recv_mem, comp_ext)


def attend_bwd(place, slope, heads, recv_mem, comp_ext, grad_heads, attn_out, lse, head_cols):
    seg_count, seg_len, _ = heads.shape
    local_heads = head_cols // HD
    pair = 2 * head_cols
    blocks = seg_count + 1
    return pl.pallas_call(
        bwd_kernel,
        grid=(seg_count,),
        in_specs=attention_specs(seg_len, head_cols, comp_ext.shape)
        + [
            pl.BlockSpec((1, seg_len, head_cols), lambda s: (s, 0, 0)),
            pl.BlockSpec((1, seg_len, head_cols), lambda s: (s, 0, 0)),
            pl.BlockSpec((1, local_heads, seg_len), lambda s: (s, 0, 0)),
        ],
        out_specs=[
            pl.BlockSpec((1, seg_len, head_cols), lambda s: (s, 0, 0)),
            pl.BlockSpec((1, seg_len, pair), lambda s: (lax.rem(s + blocks - 1, blocks), 0, 0)),
            pl.BlockSpec((seg_len, pair), lambda s: (0, 0)),
            pl.BlockSpec(comp_ext.shape, lambda s: (0, 0, 0)),
        ],
        out_shape=[
            jax.ShapeDtypeStruct((seg_count, seg_len, head_cols), jnp.bfloat16),
            jax.ShapeDtypeStruct((blocks, seg_len, pair), jnp.bfloat16),
            jax.ShapeDtypeStruct((seg_len, pair), jnp.float32),
            jax.ShapeDtypeStruct(comp_ext.shape, jnp.float32),
        ],
        compiler_params=pltpu.CompilerParams(vmem_limit_bytes=VMEM_LIMIT),
        cost_estimate=pl.CostEstimate(flops=12 * 10**9, bytes_accessed=24 * 10**6, transcendentals=10**7),
        name="attend_bwd",
    )(place, slope, heads, heads, heads, recv_mem, comp_ext, grad_heads, attn_out, lse)


def head_swap(value, bit):
    count = lax.axis_size("head")
    return lax.ppermute(value, "head", [(source, source ^ bit) for source in range(count)])


def gather_over_head(value):
    seg_count, quarter, width = value.shape
    head_index = lax.axis_index("head")
    far = head_swap(value, 2)
    near = head_swap(value, 1)
    far_near = head_swap(far, 1)
    blocks = lax.axis_size("head")
    whole = jnp.zeros((seg_count, blocks, quarter, width), value.dtype)
    for block, held in ((0, value), (1, near), (2, far), (3, far_near)):
        whole = lax.dynamic_update_slice(
            whole, held[:, None], (0, jnp.bitwise_xor(head_index, block), 0, 0)
        )
    return whole.reshape(seg_count, blocks * quarter, width)


def scatter_over_head(pieces):
    head_index = lax.axis_index("head")

    def term(bits):
        return pieces(jnp.bitwise_xor(head_index, bits))

    sent = jnp.stack([term(1), term(3)]).astype(jnp.bfloat16)
    got = head_swap(sent, 1).astype(jnp.float32)
    far = (term(2) + got[1]).astype(jnp.bfloat16)
    return term(0) + got[0] + head_swap(far, 2).astype(jnp.float32)


def per_device(tokens, wq, wk, wv, wo, w_up, w_down, gain_one, gain_two, w_comp, lengths, grad_out):
    seg_count, quarter, width = tokens.shape
    head_groups = lax.axis_size("head")
    blk_count = lax.axis_size("blk")
    devices = head_groups * blk_count
    seg_len = quarter * head_groups
    head_cols = width // head_groups
    local_heads = head_cols // HD
    comp_rows = seg_len // RATE
    pad_rows = (comp_rows + 15) // 16 * 16
    window = CSEGS + 1
    head_index = lax.axis_index("head")
    blk_index = lax.axis_index("blk")
    col_start = head_index * head_cols
    token_count = seg_count * quarter
    full_count = seg_count * seg_len
    comp_count = seg_count * pad_rows
    part = wq.shape[0]
    ff_part = w_down.shape[0]
    both = ("head", "blk")
    gains = jnp.pad(jnp.concatenate([gain_one, gain_two])[None], ((0, 7), (0, width - 2 * part)))
    first_pack = jnp.concatenate([wk, wv, wq, w_comp.reshape(RATE * part, width), gains], 0)
    second_pack = jnp.concatenate([wo, w_up.T, w_down], 0)
    first_all = lax.all_gather(first_pack, both, axis=0)
    second_all = lax.all_gather(second_pack, both, axis=0)
    full_tokens = gather_over_head(tokens)
    gain_first = first_all[:, 6 * part, :part].reshape(width).astype(jnp.float32)
    gain_second = first_all[:, 6 * part, part : 2 * part].reshape(width).astype(jnp.float32)
    mine = lax.dynamic_slice_in_dim(first_all[:, : 3 * part], col_start, head_cols, 2)
    wkvq = (
        mine.reshape(devices, 3, part, head_cols)
        .transpose(0, 2, 1, 3)
        .reshape(width, 3 * head_cols)
    )
    wkv = wkvq[:, : 2 * head_cols]
    wq_mine = wkvq[:, 2 * head_cols :]
    comp_matrix = (
        first_all[:, 3 * part : 6 * part]
        .reshape(devices, RATE, part, width)
        .transpose(1, 0, 2, 3)
        .reshape(RATE * width, width)
    )
    wo_all = second_all[:, :part].reshape(width, width)
    up_all = second_all[:, part : part + ff_part].reshape(devices * ff_part, width)
    down_all = second_all[:, part + ff_part :].reshape(devices * ff_part, width)

    full_rows = full_tokens.reshape(full_count, width).astype(jnp.float32)
    normed = layer_norm(full_rows, gain_first).astype(jnp.bfloat16)
    heads = jnp.dot(normed, wkvq, preferred_element_type=jnp.float32).astype(jnp.bfloat16)
    heads = heads.reshape(seg_count, seg_len, 3 * head_cols)
    grouped = normed.reshape(seg_count, seg_len, width)[:, : RATE * comp_rows].reshape(
        seg_count, comp_rows, RATE * width
    )
    grouped = jnp.pad(grouped, ((0, 0), (0, pad_rows - comp_rows), (0, 0))).reshape(
        comp_count, RATE * width
    )
    packed = jnp.dot(grouped, comp_matrix, preferred_element_type=jnp.float32).astype(jnp.bfloat16)
    comp_pair = (
        jnp.dot(packed, wkv, preferred_element_type=jnp.float32)
        .astype(jnp.bfloat16)
        .reshape(seg_count, pad_rows, 2 * head_cols)
    )
    compressed = lax.dynamic_slice_in_dim(packed, col_start, head_cols, 1).reshape(
        seg_count, pad_rows, head_cols
    )[:, :comp_rows]
    recv_mem, recv_comp = passed_along(
        (heads[seg_count - 1 :, :, : 2 * head_cols], comp_pair[seg_count - window :]), "blk", 1
    )
    comp_ext = jnp.concatenate([recv_comp, comp_pair], 0)
    order = jnp.arange(lengths.shape[0], dtype=jnp.int32)
    starts = jnp.sum(jnp.where(order[None, :] < order[:, None], lengths[None, :], 0), axis=1)
    seg_ids = blk_index * seg_count + jnp.arange(seg_count, dtype=jnp.int32)
    seg_place = seg_ids - jnp.max(
        jnp.where(starts[None, :] <= seg_ids[:, None], starts[None, :], 0), axis=1
    )
    head_ids = head_index * local_heads + jnp.arange(local_heads, dtype=jnp.int32)
    slopes = jnp.exp2(-head_ids.astype(jnp.float32)) / 64.0 * LOG2E
    attn_out, lse = attend_fwd(seg_place, slopes, heads, recv_mem, comp_ext, head_cols)
    mixed = lax.all_to_all(
        attn_out.reshape(seg_count, seg_len, 1, head_cols),
        "head",
        split_axis=1,
        concat_axis=2,
        tiled=True,
    ).reshape(token_count, width)
    token_rows = tokens.reshape(token_count, width).astype(jnp.float32)
    branch = jnp.dot(mixed, wo_all, preferred_element_type=jnp.float32)
    hidden = token_rows + branch
    normed_two = layer_norm(hidden, gain_second).astype(jnp.bfloat16)
    lifted = lax.dot_general(normed_two, up_all, COLS_IN, preferred_element_type=jnp.float32)
    active = jax.nn.silu(lifted).astype(jnp.bfloat16)
    ffn_term = jnp.dot(active, down_all, preferred_element_type=jnp.float32)
    out_tokens = (hidden + ffn_term).astype(jnp.bfloat16).reshape(tokens.shape)
    upstream = grad_out.reshape(token_count, width)
    grad_down = lax.dot_general(active, upstream, ROWS_IN, preferred_element_type=jnp.float32)
    grad_active = lax.dot_general(upstream, down_all, COLS_IN, preferred_element_type=jnp.float32)
    grad_lifted = (grad_active * silu_slope(lifted)).astype(jnp.bfloat16)
    grad_up = lax.dot_general(grad_lifted, normed_two, ROWS_IN, preferred_element_type=jnp.float32)
    grad_normed_two = jnp.dot(grad_lifted, up_all, preferred_element_type=jnp.float32)
    second_value, second_pull = jax.vjp(layer_norm, hidden, gain_second)
    grad_hidden_norm, grad_gain_two = second_pull(grad_normed_two)
    grad_hidden = upstream.astype(jnp.float32) + grad_hidden_norm
    grad_branch = grad_hidden.astype(jnp.bfloat16)
    grad_wo = lax.dot_general(mixed, grad_branch, ROWS_IN, preferred_element_type=jnp.float32)
    first_grads = jnp.concatenate(
        [
            grad_wo.astype(jnp.bfloat16).reshape(devices, part, width),
            grad_up.astype(jnp.bfloat16).reshape(devices, ff_part, width),
            grad_down.astype(jnp.bfloat16).reshape(devices, ff_part, width),
        ],
        1,
    )
    grad_mixed = lax.dot_general(
        grad_branch, wo_all, COLS_IN, preferred_element_type=jnp.float32
    ).astype(jnp.bfloat16)
    grad_mixed, first_grads = lax.optimization_barrier((grad_mixed, first_grads))
    first_sum = lax.psum_scatter(first_grads, both, scatter_dimension=0).astype(jnp.float32)
    grad_heads = lax.all_to_all(
        grad_mixed.reshape(seg_count, quarter, head_groups, head_cols),
        "head",
        split_axis=2,
        concat_axis=1,
        tiled=True,
    ).reshape(seg_count, seg_len, head_cols)
    grad_query, grad_pair, tail, grad_comp_ext = attend_bwd(
        seg_place, slopes, heads, recv_mem, comp_ext, grad_heads, attn_out, lse, head_cols
    )
    got_mem, got_comp = passed_along(
        (grad_pair[seg_count], grad_comp_ext[:window].astype(jnp.bfloat16)), "blk", -1
    )
    last_pair = (tail + got_mem.astype(jnp.float32)).astype(jnp.bfloat16)
    grad_pair = lax.dynamic_update_slice(grad_pair, last_pair[None], (seg_count - 1, 0, 0))
    comp_pair_grad = grad_comp_ext[window:] + jnp.pad(
        got_comp.astype(jnp.float32), ((seg_count - window, 0), (0, 0), (0, 0))
    )
    grad_kv = grad_pair[:seg_count].reshape(full_count, 2 * head_cols)
    grad_q = grad_query.reshape(full_count, head_cols)
    comp_grad_rows = comp_pair_grad.reshape(comp_count, 2 * head_cols).astype(jnp.bfloat16)
    grad_packed_part = lax.dot_general(
        comp_grad_rows, wkv, COLS_IN, preferred_element_type=jnp.float32
    )
    grad_packed_mine = scatter_over_head(
        lambda block: lax.dynamic_slice_in_dim(grad_packed_part, block * head_cols, head_cols, 1)
    ).astype(jnp.bfloat16)
    grad_grouped = lax.dot_general(
        grad_packed_part.astype(jnp.bfloat16), comp_matrix, COLS_IN, preferred_element_type=jnp.float32
    ).astype(jnp.bfloat16)
    grad_sent = jnp.pad(
        grad_grouped.reshape(seg_count, pad_rows, RATE * width)[:, :comp_rows].reshape(
            seg_count, RATE * comp_rows, width
        ),
        ((0, 0), (0, seg_len - RATE * comp_rows), (0, 0)),
    )
    grad_normed_part = (
        lax.dot_general(grad_q, wq_mine, COLS_IN, preferred_element_type=jnp.float32)
        + lax.dot_general(grad_kv, wkv, COLS_IN, preferred_element_type=jnp.float32)
    ).reshape(seg_count, head_groups, quarter, width) + grad_sent.reshape(
        seg_count, head_groups, quarter, width
    ).astype(jnp.float32)
    average = jnp.mean(full_rows, axis=-1, keepdims=True)
    center = full_rows - average
    spread = lax.rsqrt(jnp.mean(center * center, axis=-1, keepdims=True) + EPS)
    grad_gain_one = jnp.sum(grad_normed_part.reshape(full_count, width) * (center * spread), axis=0)
    grad_normed = scatter_over_head(
        lambda block: lax.dynamic_slice_in_dim(grad_normed_part, block, 1, 1)
    ).reshape(token_count, width)
    first_value, first_pull = jax.vjp(lambda rows: layer_norm(rows, gain_first), token_rows)
    (grad_rows_norm,) = first_pull(grad_normed)
    grad_tokens = (grad_hidden + grad_rows_norm).astype(jnp.bfloat16).reshape(tokens.shape)
    comp_term = lax.dot_general(packed, comp_grad_rows, ROWS_IN, preferred_element_type=jnp.float32)
    grad_wq = lax.dot_general(normed, grad_q, ROWS_IN, preferred_element_type=jnp.float32)
    grad_wkv = lax.dot_general(normed, grad_kv, ROWS_IN, preferred_element_type=jnp.float32) + comp_term
    grad_comp = lax.dot_general(
        grouped, grad_packed_mine, ROWS_IN, preferred_element_type=jnp.float32
    )

    def by_owner(value, kinds):
        return value.astype(jnp.bfloat16).reshape(
            kinds, head_groups, blk_count, part, head_cols
        ).transpose(2, 1, 0, 3, 4).reshape(blk_count, head_groups, kinds * part, head_cols)

    gain_rows = jnp.stack(
        [grad_gain_one.reshape(head_groups, blk_count, part), grad_gain_two.reshape(head_groups, blk_count, part)], 2
    ).transpose(1, 0, 2, 3).astype(jnp.bfloat16)
    second_grads = jnp.concatenate(
        [
            by_owner(jnp.concatenate([grad_wq, grad_wkv[:, :head_cols], grad_wkv[:, head_cols:]], 0), 3),
            by_owner(grad_comp, RATE),
            jnp.pad(gain_rows, ((0, 0), (0, 0), (0, 14), (0, head_cols - part))),
        ],
        2,
    )
    second_part = lax.psum_scatter(second_grads, "blk", scatter_dimension=0)
    second_sum = lax.all_to_all(second_part, "head", split_axis=0, concat_axis=0, tiled=True).astype(
        jnp.float32
    )
    gain_sum = jnp.sum(second_sum[:, 6 * part : 6 * part + 2, :part], axis=0)
    weight_sum = (
        second_sum[:, : 6 * part]
        .reshape(head_groups, 6, part, head_cols)
        .transpose(1, 2, 0, 3)
        .reshape(6, part, width)
    )
    return (
        out_tokens,
        compressed,
        grad_tokens,
        weight_sum[0],
        weight_sum[1],
        weight_sum[2],
        first_sum[:part],
        first_sum[part : part + ff_part].T,
        first_sum[part + ff_part :],
        gain_sum[0],
        gain_sum[1],
        weight_sum[3:],
    )


def solution(mesh):
    return jax.shard_map(
        per_device,
        mesh=mesh,
        in_specs=(
            P("blk", "head", None),
            P(("head", "blk"), None),
            P(("head", "blk"), None),
            P(("head", "blk"), None),
            P(("head", "blk"), None),
            P(None, ("head", "blk")),
            P(("head", "blk"), None),
            P(("head", "blk")),
            P(("head", "blk")),
            P(None, ("head", "blk"), None),
            P(),
            P("blk", "head", None),
        ),
        out_specs=(
            P("blk", "head", None),
            P("blk", None, "head"),
            P("blk", "head", None),
            P(("head", "blk"), None),
            P(("head", "blk"), None),
            P(("head", "blk"), None),
            P(("head", "blk"), None),
            P(None, ("head", "blk")),
            P(("head", "blk"), None),
            P(("head", "blk")),
            P(("head", "blk")),
            P(None, ("head", "blk"), None),
        ),
        check_vma=False,
    )
```

time: 1020 us -> 884 us (0.87)
  local copies, waits for them, and re-layouts: 255 us -> 94.6 us
  waiting for transfers between devices: 356 us -> 447 us
  matrix products: 210 us -> 151 us
  other arithmetic: 142 us -> 84.9 us
  Pallas kernels: 0 us -> 56.9 us
    dot_general x45 -> x5, matrix products: 95 us -> 35.4 us  [the longest x1 13.3 us: per_device(): lax.dot_general(grad_q, wq_mine, COLS_IN, preferred_element_type=jnp.floa...]
    pallas_call x0 -> x2, Pallas kernels: none -> 56.9 us  [the longest x1 35.8 us: attend_bwd(): pl.pallas_call(bwd_kernel, grid=(seg_count,), in_specs=attention_specs(se...]
    ppermute x4, waiting for transfers between devices: 13.7 us -> 65 us  [passed_along(): lax.ppermute(value, axis, [(source, source + steps) for source in range(l...]
    while x27 -> x0, local copies, waits for them, and re-layouts: 45.7 us -> none  [the longest x2 41.3 us: per_device(): lax.map(attend_back, (heads_q, pairs, seg_place, log_total, grad_heads))]
    dynamic_slice x36 -> x0, local copies, waits for them, and re-layouts: 25.3 us -> none  [per_device(): attn_out, log_total = lax.map(attend_fwd, (heads_q, pairs, seg_place))]
    reduce_scatter x1, waiting for transfers between devices: 173 us -> 198 us  [per_device(): lax.psum_scatter(first_grads, both, scatter_dimension=0).astype(jnp.float32)]
    dynamic_update_slice x12 -> x1, other arithmetic: 23.4 us -> 0.2 us  [per_device(): lax.dynamic_update_slice(grad_pair, last_pair[None], (seg_count - 1, 0, 0))]
    slice x20 -> x5, local copies, waits for them, and re-layouts: 31.3 us -> 10.6 us  [the longest x1 8.63 us: per_device(): first_all[:, 3 * part:6 * part].reshape(devices, RATE, part, width)]
  transfers between devices with their start and end apart: 18 -> 18, of which waited for: 11 -> 14; matrix products, arithmetic and copies ran while one was open for 31% -> 20% of each run, Pallas kernels for 0% -> 2%
where the time goes in v3:
time: 884 us; the launch traced here: 876 us
  waiting for transfers between devices  447 us (51%)
  matrix products  151 us (17%)
  local copies, waits for them, and re-layouts  94.6 us (11%)
  other arithmetic  84.9 us (10%)
  Pallas kernels  56.9 us (6%)
  starting transfers between devices  27 us (3%)
  between operations  15.2 us (2%)
    reduce_scatter x1, waiting for transfers between devices, per_device(): lax.psum_scatter(first_grads, both, scatter_dimension=0).astype(jnp.float32)  198 us
    ppermute x7, waiting for transfers between devices, head_swap(): lax.ppermute(value, 'head', [(source, source ^ bit) for source in range(c...  81.3 us
    ppermute x4, waiting for transfers between devices, passed_along(): lax.ppermute(value, axis, [(source, source + steps) for source in range(l...  65 us
    all_gather x1, waiting for transfers between devices, per_device(): first_all = lax.all_gather(first_pack, both, axis=0)  36.9 us
    pallas_call x1, Pallas kernels, attend_bwd(): pl.pallas_call(bwd_kernel, grid=(seg_count,), in_specs=attention_specs(se...  35.8 us
    all_to_all x1, waiting for transfers between devices, per_device(): lax.all_to_all(attn_out.reshape(seg_count, seg_len, 1, head_cols), 'head'...  25.7 us
    pallas_call x1, Pallas kernels, attend_fwd(): pl.pallas_call(fwd_kernel, grid=(seg_count,), in_specs=attention_specs(se...  21.1 us
    all_to_all x1, waiting for transfers between devices, per_device(): lax.all_to_all(grad_mixed.reshape(seg_count, quarter, head_groups, head_c...  20 us
  transfers between devices with their start and end apart: 18, of which 14 were waited for; matrix products, arithmetic and copies ran while one was open for 20% of the time, Pallas kernels for 2%

profile of v3, /device:TPU:24, one launch (start us, length us, event | category | flops | bytes accessed | tf_op | source)
XLA Modules:
  0.0 876.2 jit_solution(12336677289349034300)
XLA Ops:
  16.9 43.4 %collective-permute-done.1 = bf16[6,128,1024]{2,1,0:T(8,128)(2,1)S(1)} collective-permute-done((bf16[6,128,1024]{2,1,0:T(8,128)(2,1)S(1)}, bf16[6,128,1024]{2,1,0:T(8,128)(2,1)S(1)}, u32[]{:S(2)}, u32[]{:S(2)}) %collective-permute-start.1) | collective-permute-done | bytes 1572896 | tf_op jit(solution)/shard_map/ppermute | solution.py:256
  77.4 36.9 %all-gather.5.cloned.1.call-done = bf16[6400,1024]{1,0:T(8,128)(2,1)} async-done(((bf16[200,1024]{1,0:T(8,128)(2,1)}), bf16[6400,1024]{1,0:T(8,128)(2,1)}) %all-gather.5.cloned.1.call-update) | async-done | bytes 13107216 | tf_op jit(solution)/shard_map/all_gather | solution.py:309
  130.8 9.2 %fusion.2 = bf16[6,510,1024]{2,1,0:T(8,128)(2,1)} fusion(f32[6,512,1024]{2,1,0:T(8,128)} %bitcast_convert_fusion.2, f32[1024]{0:T(1024)S(1)} %reshape.476, f32[6,510]{1,0:T(8,128)S(1)} %bitcast.338, f32[6,510]{1,0:T(8,128)S(1)} %bitcast.337), kind=kLoop, calls=%fused_computation.4 | loop fusion | flops 12533760 | bytes 18829216 | tf_op jit(solution)/shard_map/convert_element_type | solution.py:333
  152.0 11.4 %convolution_convert_fusion.5 = bf16[1056,1024]{1,0:T(8,128)(2,1)S(1)} fusion(bf16[1056,3072]{1,0:T(8,128)(2,1)S(1)} %bitcast.288, bf16[3072,1024]{1,0:T(8,128)(2,1)} %bitcast.293), kind=kOutput, calls=%fused_computation.29 | convolution fusion | flops 6644858880 | bytes 14942208 | tf_op jit(solution)/shard_map/dot_general | solution.py:342
  178.9 21.2 %collective-permute-done.4 = bf16[4,176,512]{2,1,0:T(8,128)(2,1)S(1)} collective-permute-done((bf16[4,176,512]{2,1,0:T(8,128)(2,1)S(1)}, bf16[4,176,512]{2,1,0:T(8,128)(2,1)S(1)}, u32[]{:S(2)}, u32[]{:S(2)}) %collective-permute-start.4) | collective-permute-done | bytes 720928 | tf_op jit(solution)/shard_map/ppermute | solution.py:22
  201.5 32.0 %collective-permute-done.3.recv_ref = bf16[1,512,512]{2,1,0:T(8,128)(2,1)S(1)} collective-permute-done((bf16[1,512,512]{2,1,0:T(8,128)(2,1)S(1)}, bf16[1,512,512]{2,1,0:T(8,128)(2,1)S(1)}, u32[]{:S(2)}, u32[]{:S(2)}) %collective-permute-start.3) | collective-permute-done | bytes 524320 | tf_op jit(solution)/shard_map/ppermute | solution.py:22
  234.3 21.1 %attend_fwd.1 = (bf16[6,512,256]{2,1,0:T(8,128)(2,1)}, f32[6,2,512]{2,1,0:T(2,128)}) custom-call(s32[6]{0:T(128)} %fusion.51.place_ref, f32[2]{0:T(128)} %exponential_multiply_fusion.slope_ref, bf16[6,512,768]{2,1,0:T(8,128)(2,1)} %bitcast.340, bf16[6,512,768]{2,1,0:T(8,128)(2,1)} %bitcast.341, bf16[6,512,768]{2,1,0:T(8,128)(2,1)} %bitcast.342, ...), custom_call_target="tpu_custom_call" | custom-call | flops 5000000000 | bytes 16000000 | tf_op jit(solution)/shard_map/attend_fwd/pallas_call | solution.py:204
  264.1 25.7 %all-to-all-done = bf16[6,512,1,256]{3,0,2,1:T(8,128)(2,1)} async-done(((bf16[6,512,1,256]{3,0,2,1:T(8,128)(2,1)}), bf16[6,512,1,256]{3,0,2,1:T(8,128)(2,1)}, u32[]{:S(2)}, u32[]{:S(2)}) %all-to-all-start) | async-done | bytes 1572896 | tf_op jit(solution)/shard_map/all_to_all | solution.py:364
  295.3 12.8 %fusion.58 = (bf16[32,128,1024]{2,1,0:T(8,128)(2,1)}, bf16[32,128,1024]{2,1,0:T(8,128)(2,1)}) fusion(bf16[32,288,1024]{2,1,0:T(8,128)(2,1)} %bitcast.272), kind=kLoop, calls=%fused_computation.154 | loop fusion | bytes 33554432 | tf_op jit(solution)/shard_map/slice | solution.py:329
  310.5 13.5 %fusion.55 = f32[768,4096]{1,0:T(8,128)} fusion(bf16[4096,1024]{1,0:T(8,128)(2,1)} %bitcast.286, f32[768,1024]{1,0:T(8,128)S(1)} %get-tuple-element.125, f32[1024]{0:T(1024)S(1)} %reshape.478, f32[768]{0:T(1024)S(1)} %fusion.49, f32[768]{0:T(1024)S(1)} %broadcast_multiply_fusion.2), kind=kOutput, calls=%fused_computation.152 | convolution fusion | flops 6445596672 | bytes 24127488 | tf_op jit(solution)/shard_map/dot_general | solution.py:375
  324.0 14.8 %convolution_convert_fusion.1 = bf16[4096,1024]{1,0:T(8,128)(2,1)} fusion(bf16[768,1024]{1,0:T(8,128)(2,1)S(1)} %bitcast.297, f32[768,4096]{1,0:T(8,128)} %fusion.55), kind=kOutput, calls=%fused_computation.18 | convolution fusion | flops 6462373888 | bytes 22544384 | tf_op jit(solution)/shard_map/dot_general | solution.py:380
  338.8 13.6 %fusion.6 = bf16[768,4096]{1,0:T(8,128)(2,1)} fusion(f32[768,4096]{1,0:T(8,128)} %fusion.55, bf16[4096,1024]{1,0:T(8,128)(2,1)S(1)} %bitcast.281, bf16[768,1024]{1,0:T(8,128)(2,1)S(1)} %bitcast.298), kind=kOutput, calls=%fused_computation.11 | convolution fusion | flops 6470762496 | bytes 28835840 | tf_op jit(solution)/shard_map/dot_general | solution.py:381
  352.3 11.5 %multiply_reduce_fusion.1 = (bf16[1024]{0:T(1024)(128)(2,1)S(1)}, f32[768]{0:T(1024)S(1)}, f32[768,1024]{1,0:T(8,128)S(1)}) fusion(f32[768,1024]{1,0:T(8,128)S(1)} %get-tuple-element.125, f32[768]{0:T(1024)S(1)} %fusion.49, f32[768]{0:T(1024)S(1)} %broadcast_multiply_fusion.2, f32[1024]{0:T(1024)S(1)} %reshape.478, bf16[768,4096]{1,0:T(8,128)(2,1)} %fusion.6, ...), kind=kOutput, calls=%fused_computation.57 | convolution fusion | flops 6447953920 | bytes 20986880 | tf_op jit(solution)/shard_map/dot_general | solution.py:384
  363.8 10.2 %convolution_convert_fusion.2 = bf16[4096,1024]{1,0:T(8,128)(2,1)S(1)} fusion(bf16[768,4096]{1,0:T(8,128)(2,1)} %fusion.6, f32[768,1024]{1,0:T(8,128)S(1)} %get-tuple-element.125, f32[1024]{0:T(1024)S(1)} %reshape.478, f32[768]{0:T(1024)S(1)} %fusion.49, f32[768]{0:T(1024)S(1)} %broadcast_multiply_fusion.2), kind=kOutput, calls=%fused_computation.19 | convolution fusion | flops 6449790976 | bytes 17836032 | tf_op jit(solution)/shard_map/dot_general | solution.py:383
  381.5 16.7 %pad_maximum_fusion = bf16[32,288,1024]{2,1,0:T(8,128)(2,1)} fusion(bf16[32,128,1024]{2,1,0:T(8,128)(2,1)S(1)} %bitcast.284, bf16[32,128,1024]{2,1,0:T(8,128)(2,1)S(1)} %bitcast.285, bf16[32,32,1024]{2,1,0:T(8,128)(2,1)S(1)} %bitcast.312), kind=kLoop, calls=%fused_computation | loop fusion | flops 56623104 | bytes 37748736 | tf_op jit(solution)/shard_map/concatenate | solution.py:390
  405.4 20.0 %all-to-all-done.1 = bf16[6,128,4,256]{3,1,0,2:T(8,128)(2,1)} async-done(((bf16[6,128,4,256]{3,1,0,2:T(8,128)(2,1)}), bf16[6,128,4,256]{3,1,0,2:T(8,128)(2,1)}, u32[]{:S(2)}, u32[]{:S(2)}) %all-to-all-start.1) | async-done | bytes 1572896 | tf_op jit(solution)/shard_map/all_to_all | solution.py:403
  428.1 35.8 %attend_bwd.1 = (bf16[6,512,256]{2,1,0:T(8,128)(2,1)}, bf16[7,512,512]{2,1,0:T(8,128)(2,1)}, f32[512,512]{1,0:T(8,128)}, f32[10,176,512]{2,1,0:T(8,128)}) custom-call(s32[6]{0:T(128)} %fusion.51.place_ref, f32[2]{0:T(128)} %exponential_multiply_fusion.slope_ref, bf16[6,512,768]{2,1,0:T(8,128)(2,1)} %bitcast.343, bf16[6,512,768]{2,1,0:T(8,128)(2,1)} %bitcast.344, ...), custom_call_target="tpu_custom_call" | custom-call | flops 12000000000 | bytes 24000000 | tf_op jit(solution)/shard_map/attend_bwd/pallas_call | solution.py:227
  527.8 13.3 %fusion.5 = (bf16[1024]{0:T(1024)(128)(2,1)S(1)}, f32[3072,1024]{1,0:T(8,128)}) fusion(f32[6,512,1024]{2,1,0:T(8,128)} %pad_convert_fusion, bf16[6,4,128,1024]{3,2,1,0:T(8,128)(2,1)S(1)} %bitcast.262, f32[3072]{0:T(1024)S(1)} %bitcast.336, f32[3072]{0:T(1024)S(1)} %bitcast.331, f32[3072,1024]{1,0:T(8,128)} %fusion.35, bf16[3072,256]{1,0:T(8,128)(2,1)} %bitcast.292, ...), kind=kOutput, calls=%fused_computation.8 | convolution fusion | flops 1632631808 | bytes 46163968 | tf_op jit(solution)/shard_map/dot_general | solution.py:440
  555.7 13.5 %collective-permute-done.10 = bf16[1056,256]{1,0:T(8,128)(2,1)} collective-permute-done((bf16[1056,256]{1,0:T(8,128)(2,1)S(1)}, bf16[1056,256]{1,0:T(8,128)(2,1)}, u32[]{:S(2)}, u32[]{:S(2)}) %collective-permute-start.10) | collective-permute-done | bytes 540704 | tf_op jit(solution)/shard_map/ppermute | solution.py:256
  577.7 10.0 %add.174 = f32[6,4,128,1024]{3,2,1,0:T(8,128)S(1)} add(f32[6,4,128,1024]{3,2,1,0:T(8,128)} %bitcast.269, f32[6,4,128,1024]{3,2,1,0:T(8,128)} %bitcast.263) | non-fusion elementwise | flops 3145728 | bytes 37748736 | tf_op jit(solution)/shard_map/add | solution.py:439
  596.3 13.9 %add_convert_fusion = bf16[768,1024]{1,0:T(8,128)(2,1)} fusion(f32[768,1024]{1,0:T(8,128)} %copy-done.6, bf16[4096,1024]{1,0:T(8,128)(2,1)} %bitcast.278, f32[768,4096]{1,0:T(8,128)} %fusion.55), kind=kOutput, calls=%fused_computation.60 | convolution fusion | flops 6459752448 | bytes 25690112 | tf_op jit(solution)/shard_map/dot_general | solution.py:377
  610.2 21.9 %collective-permute-done.8 = bf16[6,1,128,1024]{3,2,1,0:T(8,128)(2,1)S(1)} collective-permute-done((bf16[6,1,128,1024]{3,2,1,0:T(8,128)(2,1)S(1)}, bf16[6,1,128,1024]{3,2,1,0:T(8,128)(2,1)S(1)}, u32[]{:S(2)}, u32[]{:S(2)}) %collective-permute-start.8) | collective-permute-done | bytes 1572896 | tf_op jit(solution)/shard_map/ppermute | solution.py:256
  636.3 16.2 %reduce-scatter.3.cloned.1.call-done = bf16[1,4,208,256]{3,2,1,0:T(8,128)(2,1)} async-done(((bf16[8,4,208,256]{3,2,1,0:T(8,128)(2,1)}), bf16[1,4,208,256]{3,2,1,0:T(8,128)(2,1)}) %reduce-scatter.3.cloned.1.call-update) | async-done | bytes 426000 | tf_op jit(solution)/shard_map/reduce_scatter | solution.py:478
  667.5 198.1 %reduce-scatter.5.cloned.1.call-done = bf16[1,288,1024]{2,1,0:T(8,128)(2,1)} async-done(((bf16[32,288,1024]{2,1,0:T(8,128)(2,1)}), bf16[1,288,1024]{2,1,0:T(8,128)(2,1)}) %reduce-scatter.5.cloned.1.call-update) | async-done | bytes 589840 | tf_op jit(solution)/shard_map/reduce_scatter | solution.py:402
  (246 shorter events, 224.3 us)
Async XLA Ops:
  7.2 107.1 %all-gather.5.cloned.1.call-start = ((), (), s32[]{:S(2)}) async-start(), calls=%async_computation.7 | async-start | bytes 13516800 | tf_op jit(solution)/shard_map/all_gather | solution.py:309
  12.4 280.6 %all-gather.7.cloned.1.call-start = ((), (), s32[]{:S(2)}) async-start(), calls=%async_computation.8 | async-start | bytes 19464192 | tf_op jit(solution)/shard_map/all_gather | solution.py:310
  15.4 45.0 %collective-permute-start.1 = (bf16[6,128,1024]{2,1,0:T(8,128)(2,1)S(1)}, bf16[6,128,1024]{2,1,0:T(8,128)(2,1)S(1)}, u32[]{:S(2)}, u32[]{:S(2)}) collective-permute-start(bf16[6,128,1024]{2,1,0:T(8,128)(2,1)S(1)} %copy-done.2), channel_id=1, source_target_pairs={{0,16},{8,24},{16,0},{24,8},{1,17},{9,25},{17,1},{25,9},{2,18},{10... | collective-permute-start | bytes 4718600 | tf_op jit(solution)/shard_map/ppermute | solution.py:256
  16.9 45.7 %collective-permute-start = (bf16[6,128,1024]{2,1,0:T(8,128)(2,1)S(1)}, bf16[6,128,1024]{2,1,0:T(8,128)(2,1)}, u32[]{:S(2)}, u32[]{:S(2)}) collective-permute-start(bf16[6,128,1024]{2,1,0:T(8,128)(2,1)S(1)} %copy-done.2), channel_id=1, source_target_pairs={{0,8},{8,0},{16,24},{24,16},{1,9},{9,1},{17,25},{25,17},{2,10},{10... | collective-permute-start | bytes 4718600 | tf_op jit(solution)/shard_map/ppermute | solution.py:256
  60.4 4.1 collective-permute-start.2
  67.0 101.3 %copy-start.24 = (f32[6,4,128]{2,1,0:T(4,128)}, f32[6,4,128]{2,1,0:T(4,128)S(1)}, u32[]{:S(2)}) copy-start(f32[6,4,128]{2,1,0:T(4,128)S(1)} %get-tuple-element.113) | copy-start | bytes 36868
  69.4 99.0 %copy-start.29 = (f32[6,4,128]{2,1,0:T(4,128)}, f32[6,4,128]{2,1,0:T(4,128)S(1)}, u32[]{:S(2)}) copy-start(f32[6,4,128]{2,1,0:T(4,128)S(1)} %get-tuple-element.115) | copy-start | bytes 36868
  164.8 35.3 %collective-permute-start.4 = (bf16[4,176,512]{2,1,0:T(8,128)(2,1)S(1)}, bf16[4,176,512]{2,1,0:T(8,128)(2,1)S(1)}, u32[]{:S(2)}, u32[]{:S(2)}) collective-permute-start(bf16[4,176,512]{2,1,0:T(8,128)(2,1)S(1)} %bitcast.324), channel_id=1, source_target_pairs={{0,1},{1,2},{2,3},{3,4},{4,5},{5,6},{6,7},{8,9},{9,10},{10,11},{11... | collective-permute-start | bytes 2162696 | tf_op jit(solution)/shard_map/ppermute | solution.py:22
  176.2 57.4 %copy-start.31 = (bf16[3072,768]{1,0:T(8,128)(2,1)}, bf16[3072,768]{1,0:T(8,128)(2,1)S(1)}, u32[]{:S(2)}) copy-start(bf16[3072,768]{1,0:T(8,128)(2,1)S(1)} %convolution_convert_fusion.3) | copy-start | bytes 14155780
  176.2 57.3 %collective-permute-start.3 = (bf16[1,512,512]{2,1,0:T(8,128)(2,1)S(1)}, bf16[1,512,512]{2,1,0:T(8,128)(2,1)S(1)}, u32[]{:S(2)}, u32[]{:S(2)}) collective-permute-start(bf16[1,512,512]{2,1,0:T(8,128)(2,1)S(1)} %slice.168), channel_id=1, source_target_pairs={{0,1},{1,2},{2,3},{3,4},{4,5},{5,6},{6,7},{8,9},{9,10},{10,11},{11... | collective-permute-start | bytes 1572872 | tf_op jit(solution)/shard_map/ppermute | solution.py:22
  259.1 30.7 %all-to-all-start = ((bf16[6,512,1,256]{3,0,2,1:T(8,128)(2,1)}), bf16[6,512,1,256]{3,0,2,1:T(8,128)(2,1)}, u32[]{:S(2)}, u32[]{:S(2)}) async-start(bf16[6,512,1,256]{3,0,2,1:T(8,128)(2,1)} %copy.105), calls=%async_computation | async-start | bytes 4194304 | tf_op jit(solution)/shard_map/all_to_all | solution.py:364
  310.0 64.1 %copy-start.6 = (f32[768,1024]{1,0:T(8,128)}, f32[768,1024]{1,0:T(8,128)S(1)}, u32[]{:S(2)}) copy-start(f32[768,1024]{1,0:T(8,128)S(1)} %get-tuple-element.125) | copy-start | bytes 9437188
  400.7 71.1 %slice-start.4 = ((s8[6291456]{0:T(1024)(128)(4,1)}), s8[2097152]{0:T(1024)(128)(4,1)S(1)}, s32[]{:S(2)}) async-start(s8[6291456]{0:T(1024)(128)(4,1)} %bitcast.266), calls=%async_computation.13 | async-start | bytes 4194304
  400.7 24.7 %all-to-all-start.1 = ((bf16[6,128,4,256]{3,1,0,2:T(8,128)(2,1)}), bf16[6,128,4,256]{3,1,0,2:T(8,128)(2,1)}, u32[]{:S(2)}, u32[]{:S(2)}) async-start(bf16[6,128,4,256]{3,1,0,2:T(8,128)(2,1)} %copy.109), calls=%async_computation.1 | async-start | bytes 3145728 | tf_op jit(solution)/shard_map/all_to_all | solution.py:403
  405.2 247.2 %reduce-scatter.3.cloned.1.call-start = ((), (), s32[]{:S(2)}) async-start(), calls=%async_computation.5 | async-start | bytes 3833856 | tf_op jit(solution)/shard_map/reduce_scatter | solution.py:478
  428.1 43.8 %slice-start.5 = ((s8[6291456]{0:T(1024)(128)(4,1)}), s8[4194304]{0:T(1024)(128)(4,1)S(1)}, s32[]{:S(2)}) async-start(s8[6291456]{0:T(1024)(128)(4,1)} %bitcast.266), calls=%async_computation.14 | async-start | bytes 8388608
  465.0 16.7 %collective-permute-start.5 = (bf16[512,512]{1,0:T(8,128)(2,1)S(1)}, bf16[512,512]{1,0:T(8,128)(2,1)S(1)}, u32[]{:S(2)}, u32[]{:S(2)}) collective-permute-start(bf16[512,512]{1,0:T(8,128)(2,1)S(1)} %slice_bitcast_fusion.6), channel_id=1, source_target_pairs={{1,0},{2,1},{3,2},{4,3},{5,4},{6,5},{7,6},{9,8},{10,9},{11,10},{12... | collective-permute-start | bytes 1572872 | tf_op jit(solution)/shard_map/ppermute | solution.py:22
  468.4 27.4 %collective-permute-start.6 = (bf16[4,176,512]{2,1,0:T(8,128)(2,1)S(1)}, bf16[4,176,512]{2,1,0:T(8,128)(2,1)S(1)}, u32[]{:S(2)}, u32[]{:S(2)}) collective-permute-start(bf16[4,176,512]{2,1,0:T(8,128)(2,1)S(1)} %slice.253), channel_id=1, source_target_pairs={{1,0},{2,1},{3,2},{4,3},{5,4},{6,5},{7,6},{9,8},{10,9},{11,10},{12... | collective-permute-start | bytes 2162696 | tf_op jit(solution)/shard_map/ppermute | solution.py:22
  518.6 32.3 %collective-permute-start.9 = (bf16[2,1056,256]{2,1,0:T(8,128)(2,1)}, bf16[2,1056,256]{2,1,0:T(8,128)(2,1)}, u32[]{:S(2)}, u32[]{:S(2)}) collective-permute-start(bf16[2,1056,256]{2,1,0:T(8,128)(2,1)} %pad_maximum_fusion.4), channel_id=1, source_target_pairs={{0,8},{8,0},{16,24},{24,16},{1,9},{9,1},{17,25},{25,17},{2,10},{10... | collective-permute-start | bytes 3244040 | tf_op jit(solution)/shard_map/ppermute | solution.py:256
  554.6 14.7 %collective-permute-start.10 = (bf16[1056,256]{1,0:T(8,128)(2,1)S(1)}, bf16[1056,256]{1,0:T(8,128)(2,1)}, u32[]{:S(2)}, u32[]{:S(2)}) collective-permute-start(bf16[1056,256]{1,0:T(8,128)(2,1)S(1)} %fusion.29), channel_id=1, source_target_pairs={{0,16},{8,24},{16,0},{24,8},{1,17},{9,25},{17,1},{25,9},{2,18},{10... | collective-permute-start | bytes 1622024 | tf_op jit(solution)/shard_map/ppermute | solution.py:256
  577.2 288.5 %reduce-scatter.5.cloned.1.call-start = ((), (), s32[]{:S(2)}) async-start(), calls=%async_computation.6 | async-start | bytes 19464192 | tf_op jit(solution)/shard_map/reduce_scatter | solution.py:402
  588.6 5.7 collective-permute-start.7
  595.6 36.5 %collective-permute-start.8 = (bf16[6,1,128,1024]{3,2,1,0:T(8,128)(2,1)S(1)}, bf16[6,1,128,1024]{3,2,1,0:T(8,128)(2,1)S(1)}, u32[]{:S(2)}, u32[]{:S(2)}) collective-permute-start(bf16[6,1,128,1024]{3,2,1,0:T(8,128)(2,1)S(1)} %fusion.14), channel_id=1, source_target_pairs={{0,16},{8,24},{16,0},{24,8},{1,17},{9,25},{17,1},{25,9},{2,18},{10... | collective-permute-start | bytes 4718600 | tf_op jit(solution)/shard_map/ppermute | solution.py:256
  652.5 11.2 %all-to-all-start.2 = ((bf16[4,208,256]{2,1,0:T(8,128)(2,1)}), bf16[4,208,256]{2,1,0:T(8,128)(2,1)S(1)}, u32[]{:S(2)}, u32[]{:S(2)}) async-start(bf16[4,208,256]{2,1,0:T(8,128)(2,1)} %bitcast.329), calls=%async_computation.3 | async-start | bytes 851968 | tf_op jit(solution)/shard_map/all_to_all | solution.py:479
  (41 other events, 424.2 us)
Sparse Core Ops, SparseCore 0:
  12.5 101.7 all-gather.4
  117.3 141.6 all-gather.6
  577.3 75.1 reduce-scatter.2
  659.8 205.7 reduce-scatter.4

commit v4 on v3

--- a/solution.py
+++ b/solution.py
@@ -27,11 +27,6 @@
     center = values - average
     variance = jnp.mean(center * center, axis=-1, keepdims=True)
     return center * lax.rsqrt(variance + EPS) * gain
-
-
-def silu_slope(values):
-    sig = jax.nn.sigmoid(values)
-    return sig * (1.0 + values * (1.0 - sig))
 
 
 LOG2E = 1.4426950408889634
@@ -251,6 +246,131 @@
     )(place, slope, heads, heads, heads, recv_mem, comp_ext, grad_heads, attn_out, lse)
 
 
+def row_norm(values):
+    average = jnp.mean(values, axis=-1, keepdims=True)
+    center = values - average
+    spread = lax.rsqrt(jnp.mean(center * center, axis=-1, keepdims=True) + EPS)
+    return center * spread, spread
+
+
+def norm_back(grad, unit, spread, gain):
+    scaled = grad * gain
+    along = jnp.mean(scaled * unit, axis=-1, keepdims=True)
+    return spread * (scaled - jnp.mean(scaled, axis=-1, keepdims=True) - unit * along)
+
+
+def ffn_kernel(
+    up_ref, down_ref, wo_ref, mixed_ref, tokens_ref, grad_ref, gain_ref,
+    out_ref, pack_ref, g_hidden_ref, g_gain_ref, g_mixed_ref, g_wo_ref,
+    hidden, normed, result, g_normed,
+):
+    step = pl.program_id(0)
+    width = mixed_ref.shape[1]
+    ff_part = up_ref.shape[1]
+    block = up_ref.shape[0] * ff_part
+
+    @pl.when(step == 0)
+    def _():
+        branch = jnp.dot(
+            mixed_ref[...], wo_ref[...].reshape(width, width), preferred_element_type=jnp.float32
+        )
+        rows = tokens_ref[...].astype(jnp.float32) + branch
+        hidden[...] = rows
+        unit, spread = row_norm(rows)
+        normed[...] = (unit * gain_ref[...]).astype(jnp.bfloat16)
+        result[...] = rows
+        g_normed[...] = jnp.zeros_like(g_normed)
+
+    up = up_ref[...].reshape(block, width)
+    down = down_ref[...].reshape(block, width)
+    grad = grad_ref[...]
+    lifted = lax.dot_general(up, normed[...], COLS_IN, preferred_element_type=jnp.float32)
+    sig = 0.5 * jnp.tanh(0.5 * lifted) + 0.5
+    smooth = lifted * sig
+    active = smooth.astype(jnp.bfloat16)
+    g_active = lax.dot_general(down, grad, COLS_IN, preferred_element_type=jnp.float32)
+    g_lifted = (g_active * (sig + smooth * (1.0 - sig))).astype(jnp.bfloat16)
+    g_down = jnp.dot(active, grad, preferred_element_type=jnp.float32).astype(jnp.bfloat16)
+    g_up = jnp.dot(g_lifted, normed[...], preferred_element_type=jnp.float32).astype(jnp.bfloat16)
+    pack_ref[:, :ff_part] = g_up.reshape(up_ref.shape)
+    pack_ref[:, ff_part : 2 * ff_part] = g_down.reshape(up_ref.shape)
+    result[...] += lax.dot_general(active, down, ROWS_IN, preferred_element_type=jnp.float32)
+    g_normed[...] += lax.dot_general(g_lifted, up, ROWS_IN, preferred_element_type=jnp.float32)
+
+    @pl.when(step == pl.num_programs(0) - 1)
+    def _():
+        out_ref[...] = result[...].astype(jnp.bfloat16)
+        unit, spread = row_norm(hidden[...])
+        gn = g_normed[...]
+        g_gain_ref[...] = jnp.sum(gn * unit, axis=0, keepdims=True)
+        g_hidden = grad_ref[...].astype(jnp.float32) + norm_back(gn, unit, spread, gain_ref[...])
+        g_hidden_ref[...] = g_hidden
+        g_branch = g_hidden.astype(jnp.bfloat16)
+        g_mixed_ref[...] = lax.dot_general(
+            g_branch, wo_ref[...].reshape(width, width), COLS_IN, preferred_element_type=jnp.float32
+        ).astype(jnp.bfloat16)
+        g_wo_ref[...] = lax.dot_general(
+            mixed_ref[...], g_branch, ROWS_IN, preferred_element_type=jnp.float32
+        ).astype(jnp.bfloat16)
+
+
+def feed_forward(pack, wo_part, ff_part, mixed, tokens, grad, gain):
+    devices, pack_rows, width = pack.shape
+    rows = mixed.shape[0]
+    per_step = 512 // ff_part
+    steps = devices // per_step
+    if wo_part % 16 == 0:
+        wo, wo_spec = pack, pl.BlockSpec(
+            (devices, wo_part, width), lambda j: (0, 2 * ff_part // wo_part, 0)
+        )
+    else:
+        wo = pack[:, 2 * ff_part :].reshape(width, width)
+        wo_spec = pl.BlockSpec((width, width), lambda j: (0, 0))
+
+    def fixed(shape):
+        return pl.BlockSpec(shape, lambda j: (0,) * len(shape))
+
+    flat = (rows, width)
+    return pl.pallas_call(
+        ffn_kernel,
+        grid=(steps,),
+        in_specs=[
+            pl.BlockSpec((per_step, ff_part, width), lambda j: (j, 0, 0)),
+            pl.BlockSpec((per_step, ff_part, width), lambda j: (j, 1, 0)),
+            wo_spec,
+            fixed(flat),
+            fixed(flat),
+            fixed(flat),
+            fixed((1, width)),
+        ],
+        out_specs=[
+            fixed(flat),
+            pl.BlockSpec((per_step, pack_rows, width), lambda j: (j, 0, 0)),
+            fixed(flat),
+            fixed((1, width)),
+            fixed(flat),
+            fixed((width, width)),
+        ],
+        out_shape=[
+            jax.ShapeDtypeStruct(flat, jnp.bfloat16),
+            jax.ShapeDtypeStruct(pack.shape, jnp.bfloat16),
+            jax.ShapeDtypeStruct(flat, jnp.float32),
+            jax.ShapeDtypeStruct((1, width), jnp.float32),
+            jax.ShapeDtypeStruct(flat, jnp.bfloat16),
+            jax.ShapeDtypeStruct((width, width), jnp.bfloat16),
+        ],
+        scratch_shapes=[
+            pltpu.VMEM(flat, jnp.float32),
+            pltpu.VMEM(flat, jnp.bfloat16),
+            pltpu.VMEM(flat, jnp.float32),
+            pltpu.VMEM(flat, jnp.float32),
+        ],
+        compiler_params=pltpu.CompilerParams(vmem_limit_bytes=VMEM_LIMIT),
+        cost_estimate=pl.CostEstimate(flops=42 * 10**9, bytes_accessed=50 * 10**6, transcendentals=4 * 10**6),
+        name="feed_forward",
+    )(pack, pack, wo, mixed, tokens, grad, gain)
+
+
 def head_swap(value, bit):
     count = lax.axis_size("head")
     return lax.ppermute(value, "head", [(source, source ^ bit) for source in range(count)])
@@ -305,7 +425,7 @@
     both = ("head", "blk")
     gains = jnp.pad(jnp.concatenate([gain_one, gain_two])[None], ((0, 7), (0, width - 2 * part)))
     first_pack = jnp.concatenate([wk, wv, wq, w_comp.reshape(RATE * part, width), gains], 0)
-    second_pack = jnp.concatenate([wo, w_up.T, w_down], 0)
+    second_pack = jnp.concatenate([w_up.T, w_down, wo], 0)
     first_all = lax.all_gather(first_pack, both, axis=0)
     second_all = lax.all_gather(second_pack, both, axis=0)
     full_tokens = gather_over_head(tokens)
@@ -325,10 +445,6 @@
         .transpose(1, 0, 2, 3)
         .reshape(RATE * width, width)
     )
-    wo_all = second_all[:, :part].reshape(width, width)
-    up_all = second_all[:, part : part + ff_part].reshape(devices * ff_part, width)
-    down_all = second_all[:, part + ff_part :].reshape(devices * ff_part, width)
-
     full_rows = full_tokens.reshape(full_count, width).astype(jnp.float32)
     normed = layer_norm(full_rows, gain_first).astype(jnp.bfloat16)
     heads = jnp.dot(normed, wkvq, preferred_element_type=jnp.float32).astype(jnp.bfloat16)
@@ -369,37 +485,21 @@
         tiled=True,
     ).reshape(token_count, width)
     token_rows = tokens.reshape(token_count, width).astype(jnp.float32)
-    branch = jnp.dot(mixed, wo_all, preferred_element_type=jnp.float32)
-    hidden = token_rows + branch
-    normed_two = layer_norm(hidden, gain_second).astype(jnp.bfloat16)
-    lifted = lax.dot_general(normed_two, up_all, COLS_IN, preferred_element_type=jnp.float32)
-    active = jax.nn.silu(lifted).astype(jnp.bfloat16)
-    ffn_term = jnp.dot(active, down_all, preferred_element_type=jnp.float32)
-    out_tokens = (hidden + ffn_term).astype(jnp.bfloat16).reshape(tokens.shape)
-    upstream = grad_out.reshape(token_count, width)
-    grad_down = lax.dot_general(active, upstream, ROWS_IN, preferred_element_type=jnp.float32)
-    grad_active = lax.dot_general(upstream, down_all, COLS_IN, preferred_element_type=jnp.float32)
-    grad_lifted = (grad_active * silu_slope(lifted)).astype(jnp.bfloat16)
-    grad_up = lax.dot_general(grad_lifted, normed_two, ROWS_IN, preferred_element_type=jnp.float32)
-    grad_normed_two = jnp.dot(grad_lifted, up_all, preferred_element_type=jnp.float32)
-    second_value, second_pull = jax.vjp(layer_norm, hidden, gain_second)
-    grad_hidden_norm, grad_gain_two = second_pull(grad_normed_two)
-    grad_hidden = upstream.astype(jnp.float32) + grad_hidden_norm
-    grad_branch = grad_hidden.astype(jnp.bfloat16)
-    grad_wo = lax.dot_general(mixed, grad_branch, ROWS_IN, preferred_element_type=jnp.float32)
-    first_grads = jnp.concatenate(
-        [
-            grad_wo.astype(jnp.bfloat16).reshape(devices, part, width),
-            grad_up.astype(jnp.bfloat16).reshape(devices, ff_part, width),
-            grad_down.astype(jnp.bfloat16).reshape(devices, ff_part, width),
-        ],
-        1,
-    )
-    grad_mixed = lax.dot_general(
-        grad_branch, wo_all, COLS_IN, preferred_element_type=jnp.float32
-    ).astype(jnp.bfloat16)
+    result_rows, first_grads, grad_hidden, grad_gain_two, grad_mixed, grad_wo = feed_forward(
+        second_all,
+        part,
+        ff_part,
+        mixed,
+        tokens.reshape(token_count, width),
+        grad_out.reshape(token_count, width),
+        gain_second[None],
+    )
+    out_tokens = result_rows.reshape(tokens.shape)
+    first_grads = lax.dynamic_update_slice(
+        first_grads, grad_wo.reshape(devices, part, width), (0, 2 * ff_part, 0)
+    )
     grad_mixed, first_grads = lax.optimization_barrier((grad_mixed, first_grads))
-    first_sum = lax.psum_scatter(first_grads, both, scatter_dimension=0).astype(jnp.float32)
+    first_sum = lax.psum_scatter(first_grads, both, scatter_dimension=0)
     grad_heads = lax.all_to_all(
         grad_mixed.reshape(seg_count, quarter, head_groups, head_cols),
         "head",
@@ -475,6 +575,8 @@
         ],
         2,
     )
+    second_grads, first_sum = lax.optimization_barrier((second_grads, first_sum))
+    first_sum = first_sum.astype(jnp.float32)
     second_part = lax.psum_scatter(second_grads, "blk", scatter_dimension=0)
     second_sum = lax.all_to_all(second_part, "head", split_axis=0, concat_axis=0, tiled=True).astype(
         jnp.float32
@@ -493,9 +595,9 @@
         weight_sum[0],
         weight_sum[1],
         weight_sum[2],
-        first_sum[:part],
-        first_sum[part : part + ff_part].T,
-        first_sum[part + ff_part :],
+        first_sum[2 * ff_part :],
+        first_sum[:ff_part].T,
+        first_sum[ff_part : 2 * ff_part],
         gain_sum[0],
         gain_sum[1],
         weight_sum[3:],

time: 884 us -> 696 us (0.79)
  waiting for transfers between devices: 447 us -> 306 us
  matrix products: 151 us -> 62.2 us
  Pallas kernels: 56.9 us -> 116 us
  local copies, waits for them, and re-layouts: 94.6 us -> 83.8 us
  other arithmetic: 84.9 us -> 75.2 us
    reduce_scatter x1, waiting for transfers between devices: 198 us -> 27.4 us  [per_device(): first_sum = lax.psum_scatter(first_grads, both, scatter_dimension=0)]
    dot_general x9 -> x0, matrix products: 83 us -> none  [the longest x1 14.8 us: per_device(): lax.dot_general(active, upstream, ROWS_IN, preferred_element_type=jnp.flo...]
    pallas_call x0 -> x1, Pallas kernels: none -> 58.2 us  [feed_forward(): pl.pallas_call(ffn_kernel, grid=(steps,), in_specs=[pl.BlockSpec((per_ste...]
    ppermute x4, waiting for transfers between devices: 65 us -> 88 us  [passed_along(): lax.ppermute(value, axis, [(source, source + steps) for source in range(l...]
    concatenate x2 -> x1, other arithmetic: 18.5 us -> 1.84 us  [per_device(): second_pack = jnp.concatenate([w_up.T, w_down, wo], 0)]
    slice x4 -> x2, local copies, waits for them, and re-layouts: 16.7 us -> 1.51 us  [the longest x1 0.85 us: per_device(): first_sum[ff_part:2 * ff_part]]
    unnamed x108 -> x90, local copies, waits for them, and re-layouts: 17.1 us -> 20.1 us
  transfers between devices with their start and end apart: 18 -> 18, of which waited for: 14 -> 13; matrix products, arithmetic and copies ran while one was open for 20% -> 29% of each run, Pallas kernels for 2% -> 8%
where the time goes in v4:
time: 696 us; the launch traced here: 688 us
  waiting for transfers between devices  306 us (44%)
  Pallas kernels  116 us (17%)
  local copies, waits for them, and re-layouts  83.8 us (12%)
  other arithmetic  75.2 us (11%)
  matrix products  62.2 us (9%)
  starting transfers between devices  29.8 us (4%)
  between operations  15.2 us (2%)
    ppermute x4, waiting for transfers between devices, passed_along(): lax.ppermute(value, axis, [(source, source + steps) for source in range(l...  88 us
    ppermute x7, waiting for transfers between devices, head_swap(): lax.ppermute(value, 'head', [(source, source ^ bit) for source in range(c...  83.5 us
    pallas_call x1, Pallas kernels, feed_forward(): pl.pallas_call(ffn_kernel, grid=(steps,), in_specs=[pl.BlockSpec((per_ste...  58.2 us
    all_gather x1, waiting for transfers between devices, per_device(): first_all = lax.all_gather(first_pack, both, axis=0)  36.9 us
    pallas_call x1, Pallas kernels, attend_bwd(): pl.pallas_call(bwd_kernel, grid=(seg_count,), in_specs=attention_specs(se...  36.7 us
    reduce_scatter x1, waiting for transfers between devices, per_device(): first_sum = lax.psum_scatter(first_grads, both, scatter_dimension=0)  27.4 us
    reduce_scatter x1, waiting for transfers between devices, per_device(): second_part = lax.psum_scatter(second_grads, 'blk', scatter_dimension=0)  25 us
    all_to_all x1, waiting for transfers between devices, per_device(): lax.all_to_all(attn_out.reshape(seg_count, seg_len, 1, head_cols), 'head'...  24.9 us
  transfers between devices with their start and end apart: 18, of which 13 were waited for; matrix products, arithmetic and copies ran while one was open for 29% of the time, Pallas kernels for 8%

profile of v4, /device:TPU:24, one launch (start us, length us, event | category | flops | bytes accessed | tf_op | source)
XLA Modules:
  0.0 688.4 jit_solution(10655193192478489751)
XLA Ops:
  17.0 43.4 %collective-permute-done.1 = bf16[6,128,1024]{2,1,0:T(8,128)(2,1)S(1)} collective-permute-done((bf16[6,128,1024]{2,1,0:T(8,128)(2,1)S(1)}, bf16[6,128,1024]{2,1,0:T(8,128)(2,1)S(1)}, u32[]{:S(2)}, u32[]{:S(2)}) %collective-permute-start.1) | collective-permute-done | bytes 1572896 | tf_op jit(solution)/shard_map/ppermute | solution.py:376
  69.5 7.9 %bitcast_convert_fusion.2 = f32[6,512,1024]{2,1,0:T(8,128)} fusion(bf16[6,4,128,1024]{3,2,1,0:T(8,128)(2,1)S(1)} %bitcast_dynamic-update-slice_fusion), kind=kLoop, calls=%fused_computation.131 | loop fusion | flops 3145728 | bytes 18874368 | tf_op jit(solution)/shard_map/convert_element_type | solution.py:448
  77.4 36.9 %all-gather.7.cloned.1.call-done = bf16[6400,1024]{1,0:T(8,128)(2,1)} async-done(((bf16[200,1024]{1,0:T(8,128)(2,1)}), bf16[6400,1024]{1,0:T(8,128)(2,1)}) %all-gather.7.cloned.1.call-update) | async-done | bytes 13107216 | tf_op jit(solution)/shard_map/all_gather | solution.py:429
  115.4 8.6 %fusion.2 = bf16[6,510,1024]{2,1,0:T(8,128)(2,1)} fusion(f32[6,512,1024]{2,1,0:T(8,128)} %bitcast_convert_fusion.2, f32[1024]{0:T(1024)S(1)} %reshape.430, f32[6,510]{1,0:T(8,128)S(1)} %bitcast.295, f32[6,510]{1,0:T(8,128)S(1)} %bitcast.296), kind=kLoop, calls=%fused_computation.3 | loop fusion | flops 12533760 | bytes 18829216 | tf_op jit(solution)/shard_map/convert_element_type | solution.py:449
  124.0 8.3 %reshape.404 = bf16[6,170,3072]{2,1,0:T(8,128)(2,1)} reshape(bf16[6,510,1024]{2,1,0:T(8,128)(2,1)} %fusion.2) | data formatting | bytes 12533760 | tf_op jit(solution)/shard_map/reshape | solution.py:452
  135.9 7.9 %fusion.53 = (bf16[32,96,1024]{2,1,0:T(8,128)(2,1)S(1)}, bf16[32,96,1024]{2,1,0:T(8,128)(2,1)S(1)}) fusion(bf16[32,200,1024]{2,1,0:T(8,128)(2,1)} %bitcast.242), kind=kLoop, calls=%fused_computation.128 | loop fusion | bytes 25165824 | tf_op jit(solution)/shard_map/slice | solution.py:443
  175.0 16.4 %collective-permute-done.4 = bf16[4,176,512]{2,1,0:T(8,128)(2,1)S(1)} collective-permute-done((bf16[4,176,512]{2,1,0:T(8,128)(2,1)S(1)}, bf16[4,176,512]{2,1,0:T(8,128)(2,1)S(1)}, u32[]{:S(2)}, u32[]{:S(2)}) %collective-permute-start.4) | collective-permute-done | bytes 720928 | tf_op jit(solution)/shard_map/ppermute | solution.py:22
  192.8 29.9 %collective-permute-done.3.recv_ref = bf16[1,512,512]{2,1,0:T(8,128)(2,1)S(1)} collective-permute-done((bf16[1,512,512]{2,1,0:T(8,128)(2,1)S(1)}, bf16[1,512,512]{2,1,0:T(8,128)(2,1)S(1)}, u32[]{:S(2)}, u32[]{:S(2)}) %collective-permute-start.3) | collective-permute-done | bytes 524320 | tf_op jit(solution)/shard_map/ppermute | solution.py:22
  223.4 21.1 %attend_fwd.1 = (bf16[6,512,256]{2,1,0:T(8,128)(2,1)}, f32[6,2,512]{2,1,0:T(2,128)}) custom-call(s32[6]{0:T(128)} %fusion.48.place_ref, f32[2]{0:T(128)} %exponential_multiply_fusion.slope_ref, bf16[6,512,768]{2,1,0:T(8,128)(2,1)} %bitcast.298, bf16[6,512,768]{2,1,0:T(8,128)(2,1)} %bitcast.299, bf16[6,512,768]{2,1,0:T(8,128)(2,1)} %bitcast.300, ...), custom_call_target="tpu_custom_call" | custom-call | flops 5000000000 | bytes 16000000 | tf_op jit(solution)/shard_map/attend_fwd/pallas_call | solution.py:199
  252.5 24.9 %all-to-all-done = bf16[6,512,1,256]{3,0,2,1:T(8,128)(2,1)S(1)} async-done(((bf16[6,512,1,256]{3,0,2,1:T(8,128)(2,1)}), bf16[6,512,1,256]{3,0,2,1:T(8,128)(2,1)S(1)}, u32[]{:S(2)}, u32[]{:S(2)}) %all-to-all-start) | async-done | bytes 1572896 | tf_op jit(solution)/shard_map/all_to_all | solution.py:480
  280.2 58.2 %feed_forward.1 = (bf16[768,1024]{1,0:T(8,128)(2,1)}, bf16[32,288,1024]{2,1,0:T(8,128)(2,1)}, f32[768,1024]{1,0:T(8,128)}, f32[1,1024]{1,0:T(1,128)}, bf16[768,1...) custom-call(bf16[32,288,1024]{2,1,0:T(8,128)(2,1)} %bitcast.304, bf16[32,288,1024]{2,1,0:T(8,128)(2,1)} %bitcast.305, ...), custom_call_target="tpu_custom_call" | custom-call | flops 41999998976 | bytes 50000000 | tf_op jit(solution)/shard_map/feed_forward/pallas_call | solution.py:334
  349.7 19.8 %all-to-all-done.1 = bf16[6,128,4,256]{3,1,0,2:T(8,128)(2,1)S(1)} async-done(((bf16[6,128,4,256]{3,1,0,2:T(8,128)(2,1)}), bf16[6,128,4,256]{3,1,0,2:T(8,128)(2,1)S(1)}, u32[]{:S(2)}, u32[]{:S(2)}) %all-to-all-start.1) | async-done | bytes 1572896 | tf_op jit(solution)/shard_map/all_to_all | solution.py:503
  370.8 36.7 %attend_bwd.1 = (bf16[6,512,256]{2,1,0:T(8,128)(2,1)}, bf16[7,512,512]{2,1,0:T(8,128)(2,1)}, f32[512,512]{1,0:T(8,128)}, f32[10,176,512]{2,1,0:T(8,128)}) custom-call(s32[6]{0:T(128)} %fusion.48.place_ref, f32[2]{0:T(128)} %exponential_multiply_fusion.slope_ref, bf16[6,512,768]{2,1,0:T(8,128)(2,1)} %bitcast.301, bf16[6,512,768]{2,1,0:T(8,128)(2,1)} %bitcast.302, ...), custom_call_target="tpu_custom_call" | custom-call | flops 12000000000 | bytes 24000000 | tf_op jit(solution)/shard_map/attend_bwd/pallas_call | solution.py:222
  411.9 7.8 %collective-permute-start.5 = (bf16[512,512]{1,0:T(8,128)(2,1)S(1)}, bf16[512,512]{1,0:T(8,128)(2,1)S(1)}, u32[]{:S(2)}, u32[]{:S(2)}) collective-permute-start(bf16[512,512]{1,0:T(8,128)(2,1)S(1)} %slice_bitcast_fusion.5), channel_id=1, source_target_pairs={{1,0},{2,1},{3,2},{4,3},{5,4},{6,5},{7,6},{9,8},{10,9},{11,10},{12... | collective-permute-start | bytes 1572872 | tf_op jit(solution)/shard_map/ppermute | solution.py:22
  423.2 41.7 %collective-permute-done.5 = bf16[512,512]{1,0:T(8,128)(2,1)S(1)} collective-permute-done((bf16[512,512]{1,0:T(8,128)(2,1)S(1)}, bf16[512,512]{1,0:T(8,128)(2,1)S(1)}, u32[]{:S(2)}, u32[]{:S(2)}) %collective-permute-start.5) | collective-permute-done | bytes 524320 | tf_op jit(solution)/shard_map/ppermute | solution.py:22
  466.6 7.4 %fusion.33 = f32[3072,1024]{1,0:T(8,128)} fusion(bf16[3072,512]{1,0:T(8,128)(2,1)S(1)} %bitcast.239, bf16[1024,768]{1,0:T(8,128)(2,1)S(1)} %bitcast.268), kind=kOutput, calls=%fused_computation.74 | convolution fusion | flops 3221225472 | bytes 16777216 | tf_op jit(solution)/shard_map/dot_general | solution.py:541
  477.2 9.0 %convolution_convert_fusion = bf16[1056,3072]{1,0:T(8,128)(2,1)} fusion(bf16[3072,1024]{1,0:T(8,128)(2,1)S(1)} %bitcast.255, f32[1056,1024]{1,0:T(8,128)S(1)} %fusion.31), kind=kOutput, calls=%fused_computation.12 | convolution fusion | flops 6648102912 | bytes 17104896 | tf_op jit(solution)/shard_map/dot_general | solution.py:530
  486.2 8.4 %reshape.422 = bf16[6,510,1024]{2,1,0:T(8,128)(2,1)} reshape(bf16[6,170,3072]{2,1,0:T(8,128)(2,1)} %bitcast.249) | data formatting | bytes 12533760 | tf_op jit(solution)/shard_map/reshape | solution.py:534
  494.5 9.2 %pad_convert_fusion = f32[6,512,1024]{2,1,0:T(8,128)} fusion(bf16[6,510,1024]{2,1,0:T(8,128)(2,1)} %reshape.422), kind=kLoop, calls=%fused_computation.16 | loop fusion | flops 3145728 | bytes 18849792 | tf_op jit(solution)/shard_map/convert_element_type | solution.py:544
  503.7 13.6 %fusion.5 = (bf16[1024]{0:T(1024)(128)(2,1)S(1)}, f32[3072,1024]{1,0:T(8,128)}) fusion(f32[6,512,1024]{2,1,0:T(8,128)} %pad_convert_fusion, bf16[6,4,128,1024]{3,2,1,0:T(8,128)(2,1)S(1)} %bitcast.229, f32[3072]{0:T(1024)S(1)} %bitcast.294, f32[3072]{0:T(1024)S(1)} %bitcast.289, f32[3072,1024]{1,0:T(8,128)} %fusion.33, bf16[3072,256]{1,0:T(8,128)(2,1)} %bitcast.251, ...), kind=kOutput, calls=%fused_computation.7 | convolution fusion | flops 1632631808 | bytes 46163968 | tf_op jit(solution)/shard_map/dot_general | solution.py:540
  533.1 16.1 %add.143 = f32[6,4,128,1024]{3,2,1,0:T(8,128)} add(f32[6,4,128,1024]{3,2,1,0:T(8,128)} %bitcast.236, f32[6,4,128,1024]{3,2,1,0:T(8,128)} %bitcast.230) | non-fusion elementwise | flops 3145728 | bytes 37748736 | tf_op jit(solution)/shard_map/add | solution.py:539
  558.5 27.4 %reduce-scatter.3.cloned.1.call-done = bf16[1,288,1024]{2,1,0:T(8,128)(2,1)} async-done(((bf16[32,288,1024]{2,1,0:T(8,128)(2,1)}), bf16[1,288,1024]{2,1,0:T(8,128)(2,1)}) %reduce-scatter.3.cloned.1.call-update) | async-done | bytes 589840 | tf_op jit(solution)/shard_map/reduce_scatter | solution.py:502
  602.6 32.6 %collective-permute-done.8 = bf16[6,1,128,1024]{3,2,1,0:T(8,128)(2,1)S(1)} collective-permute-done((bf16[6,1,128,1024]{3,2,1,0:T(8,128)(2,1)S(1)}, bf16[6,1,128,1024]{3,2,1,0:T(8,128)(2,1)S(1)}, u32[]{:S(2)}, u32[]{:S(2)}) %collective-permute-start.8) | collective-permute-done | bytes 1572896 | tf_op jit(solution)/shard_map/ppermute | solution.py:376
  641.3 25.0 %reduce-scatter.5.cloned.1.call-done = bf16[1,4,208,256]{3,2,1,0:T(8,128)(2,1)} async-done(((bf16[8,4,208,256]{3,2,1,0:T(8,128)(2,1)}), bf16[1,4,208,256]{3,2,1,0:T(8,128)(2,1)}) %reduce-scatter.5.cloned.1.call-update) | async-done | bytes 426000 | tf_op jit(solution)/shard_map/reduce_scatter | solution.py:580
  (212 shorter events, 155.0 us)
Async XLA Ops:
  7.2 107.1 %all-gather.7.cloned.1.call-start = ((), (), s32[]{:S(2)}) async-start(), calls=%async_computation.8 | async-start | bytes 13516800 | tf_op jit(solution)/shard_map/all_gather | solution.py:429
  12.4 267.8 %all-gather.5.cloned.1.call-start = ((), (), s32[]{:S(2)}) async-start(), calls=%async_computation.7 | async-start | bytes 19464192 | tf_op jit(solution)/shard_map/all_gather | solution.py:430
  15.4 45.0 %collective-permute-start.1 = (bf16[6,128,1024]{2,1,0:T(8,128)(2,1)S(1)}, bf16[6,128,1024]{2,1,0:T(8,128)(2,1)S(1)}, u32[]{:S(2)}, u32[]{:S(2)}) collective-permute-start(bf16[6,128,1024]{2,1,0:T(8,128)(2,1)S(1)} %copy-done.2), channel_id=1, source_target_pairs={{0,16},{8,24},{16,0},{24,8},{1,17},{9,25},{17,1},{25,9},{2,18},{10... | collective-permute-start | bytes 4718600 | tf_op jit(solution)/shard_map/ppermute | solution.py:376
  17.0 45.7 %collective-permute-start = (bf16[6,128,1024]{2,1,0:T(8,128)(2,1)S(1)}, bf16[6,128,1024]{2,1,0:T(8,128)(2,1)}, u32[]{:S(2)}, u32[]{:S(2)}) collective-permute-start(bf16[6,128,1024]{2,1,0:T(8,128)(2,1)S(1)} %copy-done.2), channel_id=1, source_target_pairs={{0,8},{8,0},{16,24},{24,16},{1,9},{9,1},{17,25},{25,17},{2,10},{10... | collective-permute-start | bytes 4718600 | tf_op jit(solution)/shard_map/ppermute | solution.py:376
  60.4 4.1 collective-permute-start.2
  115.4 49.1 %copy-start.22 = (f32[1024]{0:T(1024)}, f32[1024]{0:T(1024)S(1)}, u32[]{:S(2)}) copy-start(f32[1024]{0:T(1024)S(1)} %reshape.430) | copy-start | bytes 12292
  161.2 30.2 %collective-permute-start.4 = (bf16[4,176,512]{2,1,0:T(8,128)(2,1)S(1)}, bf16[4,176,512]{2,1,0:T(8,128)(2,1)S(1)}, u32[]{:S(2)}, u32[]{:S(2)}) collective-permute-start(bf16[4,176,512]{2,1,0:T(8,128)(2,1)S(1)} %bitcast.282), channel_id=1, source_target_pairs={{0,1},{1,2},{2,3},{3,4},{4,5},{5,6},{6,7},{8,9},{9,10},{10,11},{11... | collective-permute-start | bytes 2162696 | tf_op jit(solution)/shard_map/ppermute | solution.py:22
  172.3 50.4 %copy-start.25 = (bf16[3072,768]{1,0:T(8,128)(2,1)}, bf16[3072,768]{1,0:T(8,128)(2,1)S(1)}, u32[]{:S(2)}) copy-start(bf16[3072,768]{1,0:T(8,128)(2,1)S(1)} %convolution_convert_fusion.1) | copy-start | bytes 14155780
  172.3 50.3 %collective-permute-start.3 = (bf16[1,512,512]{2,1,0:T(8,128)(2,1)S(1)}, bf16[1,512,512]{2,1,0:T(8,128)(2,1)S(1)}, u32[]{:S(2)}, u32[]{:S(2)}) collective-permute-start(bf16[1,512,512]{2,1,0:T(8,128)(2,1)S(1)} %slice.144), channel_id=1, source_target_pairs={{0,1},{1,2},{2,3},{3,4},{4,5},{5,6},{6,7},{8,9},{9,10},{10,11},{11... | collective-permute-start | bytes 1572872 | tf_op jit(solution)/shard_map/ppermute | solution.py:22
  248.1 29.3 %all-to-all-start = ((bf16[6,512,1,256]{3,0,2,1:T(8,128)(2,1)}), bf16[6,512,1,256]{3,0,2,1:T(8,128)(2,1)S(1)}, u32[]{:S(2)}, u32[]{:S(2)}) async-start(bf16[6,512,1,256]{3,0,2,1:T(8,128)(2,1)} %copy.104), calls=%async_computation | async-start | bytes 4194304 | tf_op jit(solution)/shard_map/all_to_all | solution.py:480
  251.8 334.1 %reduce-scatter.3.cloned.1.call-start = ((), (), s32[]{:S(2)}) async-start(), calls=%async_computation.5 | async-start | bytes 19464192 | tf_op jit(solution)/shard_map/reduce_scatter | solution.py:502
  345.9 23.6 %all-to-all-start.1 = ((bf16[6,128,4,256]{3,1,0,2:T(8,128)(2,1)}), bf16[6,128,4,256]{3,1,0,2:T(8,128)(2,1)S(1)}, u32[]{:S(2)}, u32[]{:S(2)}) async-start(bf16[6,128,4,256]{3,1,0,2:T(8,128)(2,1)} %copy.106), calls=%async_computation.1 | async-start | bytes 3145728 | tf_op jit(solution)/shard_map/all_to_all | solution.py:503
  349.4 316.9 %reduce-scatter.5.cloned.1.call-start = ((), (), s32[]{:S(2)}) async-start(), calls=%async_computation.6 | async-start | bytes 3833856 | tf_op jit(solution)/shard_map/reduce_scatter | solution.py:580
  369.5 50.3 %slice-start.4 = ((s8[6291456]{0:T(1024)(128)(4,1)}), s8[4194304]{0:T(1024)(128)(4,1)S(1)}, s32[]{:S(2)}) async-start(s8[6291456]{0:T(1024)(128)(4,1)} %bitcast.233), calls=%async_computation.13 | async-start | bytes 8388608
  370.8 49.0 %slice-start.5 = ((s8[6291456]{0:T(1024)(128)(4,1)}), s8[2097152]{0:T(1024)(128)(4,1)S(1)}, s32[]{:S(2)}) async-start(s8[6291456]{0:T(1024)(128)(4,1)} %bitcast.233), calls=%async_computation.14 | async-start | bytes 4194304
  408.9 65.1 %collective-permute-start.6 = (bf16[4,176,512]{2,1,0:T(8,128)(2,1)S(1)}, bf16[4,176,512]{2,1,0:T(8,128)(2,1)S(1)}, u32[]{:S(2)}, u32[]{:S(2)}) collective-permute-start(bf16[4,176,512]{2,1,0:T(8,128)(2,1)S(1)} %slice.224), channel_id=1, source_target_pairs={{1,0},{2,1},{3,2},{4,3},{5,4},{6,5},{7,6},{9,8},{10,9},{11,10},{12... | collective-permute-start | bytes 2162696 | tf_op jit(solution)/shard_map/ppermute | solution.py:22
  411.9 53.0 %collective-permute-start.5 = (bf16[512,512]{1,0:T(8,128)(2,1)S(1)}, bf16[512,512]{1,0:T(8,128)(2,1)S(1)}, u32[]{:S(2)}, u32[]{:S(2)}) collective-permute-start(bf16[512,512]{1,0:T(8,128)(2,1)S(1)} %slice_bitcast_fusion.5), channel_id=1, source_target_pairs={{1,0},{2,1},{3,2},{4,3},{5,4},{6,5},{7,6},{9,8},{10,9},{11,10},{12... | collective-permute-start | bytes 1572872 | tf_op jit(solution)/shard_map/ppermute | solution.py:22
  419.8 45.1 %copy-start.12 = (bf16[7,512,512]{2,1,0:T(8,128)(2,1)S(1)}, bf16[7,512,512]{2,1,0:T(8,128)(2,1)}, u32[]{:S(2)}) copy-start(bf16[7,512,512]{2,1,0:T(8,128)(2,1)} %get-tuple-element.37) | copy-start | bytes 11010052
  419.8 45.1 %copy-start.20 = (f32[512,512]{1,0:T(8,128)S(1)}, f32[512,512]{1,0:T(8,128)}, u32[]{:S(2)}) copy-start(f32[512,512]{1,0:T(8,128)} %get-tuple-element.38) | copy-start | bytes 3145732
  477.2 50.1 %collective-permute-start.9 = (bf16[2,1056,256]{2,1,0:T(8,128)(2,1)}, bf16[2,1056,256]{2,1,0:T(8,128)(2,1)}, u32[]{:S(2)}, u32[]{:S(2)}) collective-permute-start(bf16[2,1056,256]{2,1,0:T(8,128)(2,1)} %pad_maximum_fusion.3), channel_id=1, source_target_pairs={{0,8},{8,0},{16,24},{24,16},{1,9},{9,1},{17,25},{25,17},{2,10},{10... | collective-permute-start | bytes 3244040 | tf_op jit(solution)/shard_map/ppermute | solution.py:376
  530.8 20.2 %collective-permute-start.10 = (bf16[1056,256]{1,0:T(8,128)(2,1)S(1)}, bf16[1056,256]{1,0:T(8,128)(2,1)}, u32[]{:S(2)}, u32[]{:S(2)}) collective-permute-start(bf16[1056,256]{1,0:T(8,128)(2,1)S(1)} %fusion.27), channel_id=1, source_target_pairs={{0,16},{8,24},{16,0},{24,8},{1,17},{9,25},{17,1},{25,9},{2,18},{10... | collective-permute-start | bytes 1622024 | tf_op jit(solution)/shard_map/ppermute | solution.py:376
  589.5 5.7 collective-permute-start.7
  598.7 36.4 %collective-permute-start.8 = (bf16[6,1,128,1024]{3,2,1,0:T(8,128)(2,1)S(1)}, bf16[6,1,128,1024]{3,2,1,0:T(8,128)(2,1)S(1)}, u32[]{:S(2)}, u32[]{:S(2)}) collective-permute-start(bf16[6,1,128,1024]{3,2,1,0:T(8,128)(2,1)S(1)} %fusion.19), channel_id=1, source_target_pairs={{0,16},{8,24},{16,0},{24,8},{1,17},{9,25},{17,1},{25,9},{2,18},{10... | collective-permute-start | bytes 4718600 | tf_op jit(solution)/shard_map/ppermute | solution.py:376
  666.3 11.2 %all-to-all-start.2 = ((bf16[4,208,256]{2,1,0:T(8,128)(2,1)}), bf16[4,208,256]{2,1,0:T(8,128)(2,1)S(1)}, u32[]{:S(2)}, u32[]{:S(2)}) async-start(bf16[4,208,256]{2,1,0:T(8,128)(2,1)} %bitcast.287), calls=%async_computation.4 | async-start | bytes 851968 | tf_op jit(solution)/shard_map/all_to_all | solution.py:581
  (32 other events, 263.5 us)
Sparse Core Ops, SparseCore 0:
  12.5 101.7 all-gather.6
  117.9 140.1 all-gather.4
  341.8 243.9 reduce-scatter.2
  589.3 76.9 reduce-scatter.4

commit v5 on v3

v5 whole, which is shorter than its diff:
```python
import jax
import jax.numpy as jnp
from jax import lax
from jax.experimental import pallas as pl
from jax.experimental.pallas import tpu as pltpu
from jax.sharding import PartitionSpec as P

HD = 128
RATE = 3
CSEGS = 3


EPS = 1e-05
NEG = -1e30
ROWS_IN = (((0,), (0,)), ((), ()))
COLS_IN = (((1,), (1,)), ((), ()))


def passed_along(value, axis, steps):
    count = lax.axis_size(axis)
    leading, last = (max(0, -steps), min(count, count - steps))
    return lax.ppermute(value, axis, [(source, source + steps) for source in range(leading, last)])


LOG2E = 1.4426950408889634
PAD_ROWS = 176
VMEM_LIMIT = 56 * 1024 * 1024


def key_bias(rows, base, step, valid_rows, open_, slope):
    row = lax.broadcasted_iota(jnp.int32, (rows, 1), 0)
    place = (base + step * row).astype(jnp.float32)
    return jnp.where((row < valid_rows) & open_, place * slope, NEG)


def fwd_kernel(place_ref, slope_ref, q_ref, own_ref, prev_ref, recv_ref, comp_ref, out_ref, lse_ref):
    step = pl.program_id(0)
    place = place_ref[step]
    seg_len = q_ref.shape[1]
    half = seg_len // 2
    pad_rows = comp_ref.shape[1]
    local_heads = q_ref.shape[2] // HD
    values_at = local_heads * HD
    factor = HD ** (-0.5) * LOG2E
    lower = lax.broadcasted_iota(jnp.int32, (half, half), 0) <= lax.broadcasted_iota(
        jnp.int32, (half, half), 1
    )
    for h in range(local_heads):
        kc = slice(h * HD, (h + 1) * HD)
        vc = slice(values_at + h * HD, values_at + (h + 1) * HD)
        slope = slope_ref[h]
        parts = []
        for piece in range(CSEGS):
            lag = CSEGS + 1 - piece
            bias = key_bias(pad_rows, RATE // 2 - lag * seg_len, RATE, seg_len // RATE, place >= lag, slope)
            parts.append((comp_ref[step + piece, :, kc], comp_ref[step + piece, :, vc], bias))
        bias = key_bias(seg_len, -seg_len, 1, seg_len, place >= 1, slope)
        is_first = step == 0
        parts.append(
            (
                jnp.where(is_first, recv_ref[0, :, kc], prev_ref[0, :, kc]),
                jnp.where(is_first, recv_ref[0, :, vc], prev_ref[0, :, vc]),
                bias,
            )
        )
        own_bias = [
            key_bias(half, n * half, 1, half, place >= 0, slope) for n in range(2)
        ]
        for n in range(2):
            query = q_ref[0, n * half : (n + 1) * half, kc]
            group = list(parts)
            for m in range(n + 1):
                rows = slice(m * half, (m + 1) * half)
                group.append((own_ref[0, rows, kc], own_ref[0, rows, vc], own_bias[m]))
            scores = []
            top = None
            for index, (k, v, bias) in enumerate(group):
                raw = lax.dot_general(k, query, COLS_IN, preferred_element_type=jnp.float32)
                raw = raw * factor + bias
                if index == len(group) - 1:
                    raw = jnp.where(lower, raw, NEG)
                scores.append(raw)
                peak = jnp.max(raw, axis=0, keepdims=True)
                top = peak if top is None else jnp.maximum(top, peak)
            total = jnp.zeros_like(top)
            result = jnp.zeros((HD, half), jnp.float32)
            for raw, (k, v, bias) in zip(scores, group):
                weight = jnp.exp2(raw - top)
                total = total + jnp.sum(weight, axis=0, keepdims=True)
                result = result + lax.dot_general(
                    v, weight.astype(jnp.bfloat16), ROWS_IN, preferred_element_type=jnp.float32
                )
            result = result * (1.0 / total)
            out_ref[0, n * half : (n + 1) * half, kc] = result.T.astype(jnp.bfloat16)
            lse_ref[0, h : h + 1, n * half : (n + 1) * half] = top + jnp.log(total) * LOG2E


def bwd_kernel(
    place_ref, slope_ref, q_ref, own_ref, prev_ref, recv_ref, comp_ref, head_ref, g0, g1, g2, g3, att_ref, lse_ref,
    gq_ref, gkv_ref, tail_ref, gcomp_ref, grad_ref,
):
    step = pl.program_id(0)
    place = place_ref[step]
    seg_len = q_ref.shape[1]
    half = seg_len // 2
    pad_rows = comp_ref.shape[1]
    local_heads = q_ref.shape[2] // HD
    values_at = local_heads * HD
    scale = HD ** (-0.5)
    factor = scale * LOG2E
    is_first = step == 0
    lower = lax.broadcasted_iota(jnp.int32, (half, half), 0) <= lax.broadcasted_iota(
        jnp.int32, (half, half), 1
    )

    @pl.when(is_first)
    def _():
        tail_ref[...] = jnp.zeros_like(tail_ref)
        gcomp_ref[...] = jnp.zeros_like(gcomp_ref)

    place_rows(head_ref[0], (g0, g1, g2, g3), grad_ref)
    for h in range(local_heads):
        kc = slice(h * HD, (h + 1) * HD)
        vc = slice(values_at + h * HD, values_at + (h + 1) * HD)
        slope = slope_ref[h]
        query = q_ref[0, :, kc]
        grad = grad_ref[:, kc]
        lse = lse_ref[0, h : h + 1, :]
        product = grad.astype(jnp.float32) * att_ref[0, :, kc].astype(jnp.float32)
        delta = jnp.sum(product.T, axis=0, keepdims=True)

        def part(k, v, bias, cols, masked):
            raw = lax.dot_general(k, query[cols], COLS_IN, preferred_element_type=jnp.float32)
            raw = raw * factor + bias
            if masked:
                raw = jnp.where(lower, raw, NEG)
            prob = jnp.exp2(raw - lse[:, cols])
            grad_prob = lax.dot_general(v, grad[cols], COLS_IN, preferred_element_type=jnp.float32)
            grad_score = (prob * (grad_prob - delta[:, cols])).astype(jnp.bfloat16)
            gk = jnp.dot(grad_score, query[cols], preferred_element_type=jnp.float32) * scale
            gv = jnp.dot(prob.astype(jnp.bfloat16), grad[cols], preferred_element_type=jnp.float32)
            gq = lax.dot_general(k, grad_score, ROWS_IN, preferred_element_type=jnp.float32)
            return gk, gv, gq

        every = slice(0, seg_len)
        total = jnp.zeros((HD, seg_len), jnp.float32)
        for piece in range(CSEGS):
            lag = CSEGS + 1 - piece
            bias = key_bias(pad_rows, RATE // 2 - lag * seg_len, RATE, seg_len // RATE, place >= lag, slope)
            gk, gv, gq = part(comp_ref[step + piece, :, kc], comp_ref[step + piece, :, vc], bias, every, False)
            gcomp_ref[step + piece, :, kc] += gk
            gcomp_ref[step + piece, :, vc] += gv
            total = total + gq
        for n in range(2):
            rows = slice(n * half, (n + 1) * half)
            bias = key_bias(half, n * half - seg_len, 1, half, place >= 1, slope)
            k = jnp.where(is_first, recv_ref[0, rows, kc], prev_ref[0, rows, kc])
            v = jnp.where(is_first, recv_ref[0, rows, vc], prev_ref[0, rows, vc])
            gk, gv, gq = part(k, v, bias, every, False)
            gkv_ref[0, rows, kc] = (tail_ref[rows, kc] + gk).astype(jnp.bfloat16)
            gkv_ref[0, rows, vc] = (tail_ref[rows, vc] + gv).astype(jnp.bfloat16)
            total = total + gq
        lo, hi = slice(0, half), slice(half, seg_len)
        bias_lo = key_bias(half, 0, 1, half, place >= 0, slope)
        bias_hi = key_bias(half, half, 1, half, place >= 0, slope)
        gk0, gv0, gq0 = part(own_ref[0, lo, kc], own_ref[0, lo, vc], bias_lo, lo, True)
        gk1, gv1, gq1 = part(own_ref[0, lo, kc], own_ref[0, lo, vc], bias_lo, hi, False)
        gk2, gv2, gq2 = part(own_ref[0, hi, kc], own_ref[0, hi, vc], bias_hi, hi, True)
        tail_ref[lo, kc] = gk0 + gk1
        tail_ref[lo, vc] = gv0 + gv1
        tail_ref[hi, kc] = gk2
        tail_ref[hi, vc] = gv2
        gq_ref[0, lo, kc] = ((total[:, lo] + gq0) * scale).T.astype(jnp.bfloat16)
        gq_ref[0, hi, kc] = ((total[:, hi] + gq1 + gq2) * scale).T.astype(jnp.bfloat16)


def attention_specs(seg_len, head_cols, comp_shape):
    pair = 2 * head_cols
    return [
        pl.BlockSpec(memory_space=pltpu.SMEM),
        pl.BlockSpec(memory_space=pltpu.SMEM),
        pl.BlockSpec((1, seg_len, head_cols), lambda s: (s, 0, 2)),
        pl.BlockSpec((1, seg_len, pair), lambda s: (s, 0, 0)),
        pl.BlockSpec((1, seg_len, pair), lambda s: (jnp.maximum(s - 1, 0), 0, 0)),
        pl.BlockSpec((1, seg_len, pair), lambda s: (0, 0, 0)),
        pl.BlockSpec(comp_shape, lambda s: (0, 0, 0)),
    ]


def attend_fwd(place, slope, heads, recv_mem, comp_ext, head_cols):
    seg_count, seg_len, _ = heads.shape
    local_heads = head_cols // HD
    return pl.pallas_call(
        fwd_kernel,
        grid=(seg_count,),
        in_specs=attention_specs(seg_len, head_cols, comp_ext.shape),
        out_specs=[
            pl.BlockSpec((1, seg_len, head_cols), lambda s: (s, 0, 0)),
            pl.BlockSpec((1, local_heads, seg_len), lambda s: (s, 0, 0)),
        ],
        out_shape=[
            jax.ShapeDtypeStruct((seg_count, seg_len, head_cols), jnp.bfloat16),
            jax.ShapeDtypeStruct((seg_count, local_heads, seg_len), jnp.float32),
        ],
        compiler_params=pltpu.CompilerParams(vmem_limit_bytes=VMEM_LIMIT),
        cost_estimate=pl.CostEstimate(flops=5 * 10**9, bytes_accessed=16 * 10**6, transcendentals=10**7),
        name="attend_fwd",
    )(place, slope, heads, heads, heads, recv_mem, comp_ext)


def attend_bwd(head, place, slope, heads, recv_mem, comp_ext, grad_mixed, attn_out, lse, head_cols):
    seg_count, seg_len, _ = heads.shape
    local_heads = head_cols // HD
    pair = 2 * head_cols
    blocks = seg_count + 1
    return pl.pallas_call(
        bwd_kernel,
        grid=(seg_count,),
        in_specs=attention_specs(seg_len, head_cols, comp_ext.shape)
        + [pl.BlockSpec(memory_space=pltpu.SMEM)]
        + [by_segment(grad_mixed[0].shape[1:])] * 4
        + [by_segment((seg_len, head_cols)), by_segment((local_heads, seg_len))],
        out_specs=[
            pl.BlockSpec((1, seg_len, head_cols), lambda s: (s, 0, 0)),
            pl.BlockSpec((1, seg_len, pair), lambda s: (lax.rem(s + blocks - 1, blocks), 0, 0)),
            pl.BlockSpec((seg_len, pair), lambda s: (0, 0)),
            pl.BlockSpec(comp_ext.shape, lambda s: (0, 0, 0)),
        ],
        out_shape=[
            jax.ShapeDtypeStruct((seg_count, seg_len, head_cols), jnp.bfloat16),
            jax.ShapeDtypeStruct((blocks, seg_len, pair), jnp.bfloat16),
            jax.ShapeDtypeStruct((seg_len, pair), jnp.float32),
            jax.ShapeDtypeStruct(comp_ext.shape, jnp.float32),
        ],
        scratch_shapes=[pltpu.VMEM((seg_len, head_cols), jnp.bfloat16)],
        compiler_params=pltpu.CompilerParams(vmem_limit_bytes=VMEM_LIMIT),
        cost_estimate=pl.CostEstimate(flops=12 * 10**9, bytes_accessed=24 * 10**6, transcendentals=10**7),
        name="attend_bwd",
    )(place, slope, heads, heads, heads, recv_mem, comp_ext, head, *grad_mixed, attn_out, lse)


def row_norm(values):
    average = jnp.mean(values, axis=-1, keepdims=True)
    center = values - average
    spread = lax.rsqrt(jnp.mean(center * center, axis=-1, keepdims=True) + EPS)
    return center * spread, spread


def norm_back(grad, unit, spread, gain):
    scaled = grad * gain
    along = jnp.mean(scaled * unit, axis=-1, keepdims=True)
    return spread * (scaled - jnp.mean(scaled, axis=-1, keepdims=True) - unit * along)


def place_rows(head, pieces, target):
    for bits, piece in enumerate(pieces):
        rows = piece.shape[1]
        at = pl.multiple_of(jnp.bitwise_xor(head, bits) * rows, rows)
        target[pl.ds(at, rows), :] = piece[0].astype(target.dtype)


def hand_out(head, source, keep_ref, sent_ref):
    rows = keep_ref.shape[2]
    for bits, (ref, slot) in enumerate(
        ((keep_ref, 0), (sent_ref, 0), (keep_ref, 1), (sent_ref, 1))
    ):
        at = pl.multiple_of(jnp.bitwise_xor(head, bits) * rows, rows)
        ref[slot, 0] = source[pl.ds(at, rows), :].astype(ref.dtype)


def prep_kernel(
    head_ref, t0, t1, t2, t3, gain_ref, w_ref, heads_ref, normed_ref, grouped_ref, packed_ref, spread
):
    head = head_ref[0]
    quarter, width = t0.shape[1:]
    seg_len = heads_ref.shape[1]
    head_cols = w_ref.shape[2]
    pad_rows = grouped_ref.shape[1]
    tiles = width // 128
    for bits, piece in enumerate((t0, t1, t2, t3)):
        unit, _ = row_norm(piece[0].astype(jnp.float32))
        normed = (unit * gain_ref[...]).astype(jnp.bfloat16)
        at = pl.multiple_of(jnp.bitwise_xor(head, bits) * quarter, quarter)
        normed_ref[0, pl.ds(at, quarter), :] = normed
        wide = normed.astype(jnp.float32)
        for c in range(tiles):
            spread[c, pl.ds(at, quarter), :] = wide[:, c * 128 : (c + 1) * 128]
    last = spread[:, seg_len - 8 : seg_len, :]
    row = lax.broadcasted_iota(jnp.int32, last.shape, 1)
    spread[:, seg_len - 8 : seg_len, :] = jnp.where(row < 8 - seg_len % RATE, last, 0.0)
    spread[:, seg_len:, :] = jnp.zeros((tiles, spread.shape[1] - seg_len, 128), jnp.float32)
    rows = normed_ref[0]
    for n in range(3):
        heads_ref[0, :, n * head_cols : (n + 1) * head_cols] = jnp.dot(
            rows, w_ref[n], preferred_element_type=jnp.float32
        ).astype(jnp.bfloat16)
    total = jnp.zeros((pad_rows, head_cols), jnp.float32)
    for tap in range(RATE):
        for c in range(tiles):
            at = tap * width + c * 128
            grouped_ref[0, :, at : at + 128] = spread[
                c, pl.ds(tap, pad_rows, stride=RATE), :
            ].astype(jnp.bfloat16)
        total = total + jnp.dot(
            grouped_ref[0, :, tap * width : (tap + 1) * width],
            w_ref[3 + tap],
            preferred_element_type=jnp.float32,
        )
    packed_ref[0] = total.astype(jnp.bfloat16)


def fixed(shape):
    return pl.BlockSpec(shape, lambda s: (0,) * len(shape), pipeline_mode=pl.Buffered(1))


def by_segment(shape):
    return pl.BlockSpec((1,) + shape, lambda s: (s,) + (0,) * len(shape))


def piece_specs(quarter, width):
    spec = pl.BlockSpec((2, 1, quarter, width), lambda s: (0, s, 0, 0))
    return [spec, spec]


def piece_shapes(seg_count, quarter, width):
    shape = jax.ShapeDtypeStruct((2, seg_count, quarter, width), jnp.bfloat16)
    return [shape, shape]


def prepare(head, tokens, gain, weights, pad_rows):
    seg_count, quarter, width = tokens[0].shape
    seg_len = quarter * len(tokens)
    head_cols = weights.shape[2]
    bf16 = jnp.bfloat16
    return pl.pallas_call(
        prep_kernel,
        grid=(seg_count,),
        in_specs=[pl.BlockSpec(memory_space=pltpu.SMEM)]
        + [by_segment((quarter, width))] * 4
        + [fixed((1, width)), fixed(weights.shape)],
        out_specs=[
            by_segment((seg_len, 3 * head_cols)),
            by_segment((seg_len, width)),
            by_segment((pad_rows, RATE * width)),
            by_segment((pad_rows, head_cols)),
        ],
        out_shape=[
            jax.ShapeDtypeStruct((seg_count, seg_len, 3 * head_cols), bf16),
            jax.ShapeDtypeStruct((seg_count, seg_len, width), bf16),
            jax.ShapeDtypeStruct((seg_count, pad_rows, RATE * width), bf16),
            jax.ShapeDtypeStruct((seg_count, pad_rows, head_cols), bf16),
        ],
        scratch_shapes=[pltpu.VMEM((width // 128, RATE * pad_rows, 128), jnp.float32)],
        compiler_params=pltpu.CompilerParams(vmem_limit_bytes=VMEM_LIMIT),
        cost_estimate=pl.CostEstimate(flops=7 * 10**9, bytes_accessed=30 * 10**6, transcendentals=3072),
        name="prepare",
    )(head, *tokens, gain, weights)


def ffn_kernel(
    head_ref, a0, a1, a2, a3, o0, o1, o2, o3, t0, t1, t2, t3, g0, g1, g2, g3, gain_ref, up_ref, down_ref,
    f_keep, f_sent, n_keep, n_sent, hidden_ref, pack_ref,
    rows, grads, acc_up, acc_down,
):
    step = pl.program_id(0)
    head = head_ref[0]
    quarter, width = t0.shape[1:]
    ff_part = up_ref.shape[1]
    parts = up_ref.shape[0] // 2
    block = parts * ff_part

    @pl.when(step == 0)
    def _():
        acc_up[...] = jnp.zeros_like(acc_up)
        acc_down[...] = jnp.zeros_like(acc_down)

    place_rows(head, (t0, t1, t2, t3), rows)
    place_rows(head, (g0, g1, g2, g3), grads)
    hidden = rows[...]
    for a, o in ((a0, o0), (a1, o1), (a2, o2), (a3, o3)):
        hidden = hidden + jnp.dot(a[0], o[...], preferred_element_type=jnp.float32)
    rows[...] = hidden
    at = pl.multiple_of(head * quarter, quarter)
    hidden_ref[0] = rows[pl.ds(at, quarter), :]
    unit, _ = row_norm(hidden)
    normed = (unit * gain_ref[...]).astype(jnp.bfloat16)
    grad = grads[...]
    result = jnp.zeros(hidden.shape, jnp.float32)
    g_normed = jnp.zeros(hidden.shape, jnp.float32)
    for n in range(2):
        own = slice(n * parts, (n + 1) * parts)
        up = up_ref[own].reshape(block, width)
        down = down_ref[own].reshape(block, width)
        lifted = lax.dot_general(normed, up, COLS_IN, preferred_element_type=jnp.float32)
        sig = 0.5 * jnp.tanh(0.5 * lifted) + 0.5
        smooth = lifted * sig
        active = smooth.astype(jnp.bfloat16)
        g_active = lax.dot_general(grad, down, COLS_IN, preferred_element_type=jnp.float32)
        g_lifted = (g_active * (sig + smooth * (1.0 - sig))).astype(jnp.bfloat16)
        result = result + jnp.dot(active, down, preferred_element_type=jnp.float32)
        g_normed = g_normed + jnp.dot(g_lifted, up, preferred_element_type=jnp.float32)
        acc_down[n] += lax.dot_general(active, grad, ROWS_IN, preferred_element_type=jnp.float32)
        acc_up[n] += lax.dot_general(g_lifted, normed, ROWS_IN, preferred_element_type=jnp.float32)
    rows[...] = g_normed
    hand_out(head, rows, n_keep, n_sent)
    rows[...] = result
    hand_out(head, rows, f_keep, f_sent)

    @pl.when(step == pl.num_programs(0) - 1)
    def _():
        for n in range(2):
            own = slice(n * parts, (n + 1) * parts)
            shape = (parts, ff_part, width)
            pack_ref[own, :ff_part] = acc_up[n].astype(jnp.bfloat16).reshape(shape)
            pack_ref[own, ff_part:] = acc_down[n].astype(jnp.bfloat16).reshape(shape)


def feed_forward(head, attended, wo, tokens, grads, gain, pack, ff_part):
    seg_count, quarter, width = tokens[0].shape
    seg_len, head_cols = attended[0].shape[1:]
    blks = pack.shape[0]
    half = blks // 2 * ff_part
    pieces = piece_specs(quarter, width)
    shapes = piece_shapes(seg_count, quarter, width)

    def weight(index):
        return pl.BlockSpec(
            (blks, ff_part, width), lambda s: (0, index, 0), pipeline_mode=pl.Buffered(1)
        )

    return pl.pallas_call(
        ffn_kernel,
        grid=(seg_count,),
        in_specs=[pl.BlockSpec(memory_space=pltpu.SMEM)]
        + [by_segment((seg_len, head_cols))] * 4
        + [fixed((head_cols, width))] * 4
        + [by_segment((quarter, width))] * 8
        + [fixed((1, width)), weight(0), weight(1)],
        out_specs=pieces + pieces
        + [
            by_segment((quarter, width)),
            pl.BlockSpec((blks, 2 * ff_part, width), lambda s: (0, 0, 0)),
        ],
        out_shape=shapes + shapes
        + [
            jax.ShapeDtypeStruct((seg_count, quarter, width), jnp.float32),
            jax.ShapeDtypeStruct((blks, 2 * ff_part, width), jnp.bfloat16),
        ],
        scratch_shapes=[
            pltpu.VMEM((seg_len, width), jnp.float32),
            pltpu.VMEM((seg_len, width), jnp.bfloat16),
            pltpu.VMEM((2, half, width), jnp.float32),
            pltpu.VMEM((2, half, width), jnp.float32),
        ],
        compiler_params=pltpu.CompilerParams(vmem_limit_bytes=VMEM_LIMIT),
        cost_estimate=pl.CostEstimate(flops=45 * 10**9, bytes_accessed=60 * 10**6, transcendentals=4 * 10**6),
        name="feed_forward",
    )(head, *attended, *wo, *tokens, *grads, gain, pack, pack)


def g_normed_kernel(head_ref, gq_ref, gkv_ref, gp_ref, w_ref, keep_ref, sent_ref, spread, rows):
    head = head_ref[0]
    seg_len, head_cols = gq_ref.shape[1:]
    pad_rows = gp_ref.shape[1]
    width = w_ref.shape[1]
    total = lax.dot_general(gq_ref[0], w_ref[2], COLS_IN, preferred_element_type=jnp.float32)
    for n in range(2):
        part = gkv_ref[0, :, n * head_cols : (n + 1) * head_cols]
        total = total + lax.dot_general(part, w_ref[n], COLS_IN, preferred_element_type=jnp.float32)
    for tap in range(RATE):
        sent = lax.dot_general(gp_ref[0], w_ref[3 + tap], COLS_IN, preferred_element_type=jnp.float32)
        for c in range(width // 128):
            spread[c, pl.ds(tap, pad_rows, stride=RATE), :] = sent[:, c * 128 : (c + 1) * 128]
    for c in range(width // 128):
        own = slice(c * 128, (c + 1) * 128)
        rows[:, own] = total[:, own] + spread[c, :seg_len, :]
    hand_out(head, rows, keep_ref, sent_ref)


def g_normed_parts(head, grad_query, grad_pair, grad_packed, weights, quarter):
    seg_count, seg_len, head_cols = grad_query.shape
    width = weights.shape[1]
    pad_rows = grad_packed.shape[1]
    return pl.pallas_call(
        g_normed_kernel,
        grid=(seg_count,),
        in_specs=[
            pl.BlockSpec(memory_space=pltpu.SMEM),
            by_segment((seg_len, head_cols)),
            by_segment((seg_len, 2 * head_cols)),
            by_segment((pad_rows, head_cols)),
            fixed(weights.shape),
        ],
        out_specs=piece_specs(quarter, width),
        out_shape=piece_shapes(seg_count, quarter, width),
        scratch_shapes=[
            pltpu.VMEM((width // 128, RATE * pad_rows, 128), jnp.float32),
            pltpu.VMEM((seg_len, width), jnp.float32),
        ],
        compiler_params=pltpu.CompilerParams(vmem_limit_bytes=VMEM_LIMIT),
        cost_estimate=pl.CostEstimate(flops=7 * 10**9, bytes_accessed=20 * 10**6, transcendentals=0),
        name="g_normed",
    )(head, grad_query, grad_pair, grad_packed, weights)


def head_swap(value, bit):
    count = lax.axis_size("head")
    return lax.ppermute(value, "head", [(source, source ^ bit) for source in range(count)])


def to_all_heads(value):
    far = head_swap(value, 2)
    return value, head_swap(value, 1), far, head_swap(far, 1)


def sum_over_heads(keep, sent):
    got = head_swap(sent, 1).astype(jnp.float32)
    far = (keep[1].astype(jnp.float32) + got[1]).astype(jnp.bfloat16)
    return keep[0].astype(jnp.float32) + got[0] + head_swap(far, 2).astype(jnp.float32)


def per_device(tokens, wq, wk, wv, wo, w_up, w_down, gain_one, gain_two, w_comp, lengths, grad_out):
    seg_count, quarter, width = tokens.shape
    head_groups = lax.axis_size("head")
    blk_count = lax.axis_size("blk")
    seg_len = quarter * head_groups
    head_cols = width // head_groups
    local_heads = head_cols // HD
    comp_rows = seg_len // RATE
    pad_rows = (comp_rows + 15) // 16 * 16
    window = CSEGS + 1
    head_index = lax.axis_index("head")
    blk_index = lax.axis_index("blk")
    token_count = seg_count * quarter
    full_count = seg_count * seg_len
    comp_count = seg_count * pad_rows
    part = wq.shape[0]
    ff_part = w_down.shape[0]
    bf16 = jnp.bfloat16
    head = head_index[None].astype(jnp.int32)

    columns = (
        jnp.concatenate([wk, wv, wq, w_comp.reshape(RATE * part, width)], 0)
        .reshape(6 * part, head_groups, head_cols)
        .transpose(1, 0, 2)
    )
    gains = jnp.pad(
        jnp.concatenate([gain_one, gain_two])[None], ((0, 15), (0, head_cols - 2 * part))
    )
    columns = jnp.concatenate(
        [columns, jnp.broadcast_to(gains, (head_groups, 16, head_cols))], 1
    )
    columns = lax.all_to_all(columns, "head", split_axis=0, concat_axis=0, tiled=True)
    columns, tokens_held = lax.optimization_barrier((columns, tokens))
    first_all = lax.all_gather(columns, "blk", axis=0)
    second_all = lax.all_gather(jnp.concatenate([w_up.T, w_down, wo], 0), "blk", axis=0)
    token_pieces = to_all_heads(tokens_held)
    grad_held, tokens_far = lax.optimization_barrier((grad_out, token_pieces[2]))
    token_pieces = token_pieces[:2] + (tokens_far,) + token_pieces[3:]
    grad_pieces = to_all_heads(grad_held)
    gain_pair = first_all[:, :, 6 * part, : 2 * part].reshape(
        blk_count, head_groups, 2, part
    ).transpose(2, 1, 0, 3).reshape(2, 1, width).astype(jnp.float32)
    gain_first, gain_second = gain_pair[0], gain_pair[1]
    weights = (
        first_all[:, :, : 6 * part]
        .reshape(blk_count, head_groups, 6, part, head_cols)
        .transpose(2, 1, 0, 3, 4)
        .reshape(6, width, head_cols)
    )
    wkv = jnp.concatenate([weights[0], weights[1]], 1)
    wo_mine = second_all[:, 2 * ff_part :].reshape(head_cols, width)
    wo_pieces = to_all_heads(wo_mine)

    heads, normed, grouped, packed_mine = prepare(
        head, token_pieces, gain_first, weights, pad_rows
    )
    compressed = packed_mine[:, :comp_rows]
    packed = jnp.zeros((comp_count, width), bf16)
    for bits, piece in enumerate(to_all_heads(packed_mine.reshape(comp_count, head_cols))):
        packed = lax.dynamic_update_slice(
            packed, piece, (0, jnp.bitwise_xor(head_index, bits) * head_cols)
        )
    comp_pair = (
        jnp.dot(packed, wkv, preferred_element_type=jnp.float32)
        .astype(bf16)
        .reshape(seg_count, pad_rows, 2 * head_cols)
    )
    recv_mem, recv_comp = passed_along(
        (heads[seg_count - 1 :, :, : 2 * head_cols], comp_pair[seg_count - window :]), "blk", 1
    )
    comp_ext = jnp.concatenate([recv_comp, comp_pair], 0)
    order = jnp.arange(lengths.shape[0], dtype=jnp.int32)
    starts = jnp.sum(jnp.where(order[None, :] < order[:, None], lengths[None, :], 0), axis=1)
    seg_ids = blk_index * seg_count + jnp.arange(seg_count, dtype=jnp.int32)
    seg_place = seg_ids - jnp.max(
        jnp.where(starts[None, :] <= seg_ids[:, None], starts[None, :], 0), axis=1
    )
    head_ids = head_index * local_heads + jnp.arange(local_heads, dtype=jnp.int32)
    slopes = jnp.exp2(-head_ids.astype(jnp.float32)) / 64.0 * LOG2E
    attn_out, lse = attend_fwd(seg_place, slopes, heads, recv_mem, comp_ext, head_cols)

    attended = to_all_heads(attn_out)
    f_keep, f_sent, n_keep, n_sent, hidden, first_grads = feed_forward(
        head, attended, wo_pieces, token_pieces, grad_pieces, gain_second, second_all, ff_part
    )
    first_sum = lax.psum_scatter(first_grads, "blk", scatter_dimension=0)
    grad_normed_two = sum_over_heads(n_keep, n_sent).reshape(token_count, width)
    hidden = hidden.reshape(token_count, width)
    unit, spread = row_norm(hidden)
    grad_gain_two = jnp.sum(grad_normed_two * unit, axis=0)
    grad_hidden = grad_out.reshape(token_count, width).astype(jnp.float32) + norm_back(
        grad_normed_two, unit, spread, gain_second
    )
    grad_branch = grad_hidden.astype(bf16)
    grad_mixed = [
        head_swap(
            lax.dot_general(grad_branch, block, COLS_IN, preferred_element_type=jnp.float32)
            .astype(bf16)
            .reshape(seg_count, quarter, head_cols),
            bits,
        )
        if bits
        else lax.dot_general(grad_branch, block, COLS_IN, preferred_element_type=jnp.float32)
        .astype(bf16)
        .reshape(seg_count, quarter, head_cols)
        for bits, block in enumerate(wo_pieces)
    ]
    f_sent, grad_mixed = lax.optimization_barrier((f_sent, grad_mixed))
    out_tokens = (
        (hidden.reshape(tokens.shape) + sum_over_heads(f_keep, f_sent)).astype(bf16)
    )
    grad_wo = [
        lax.dot_general(
            lax.dynamic_slice_in_dim(block, head_index * quarter, quarter, 1).reshape(
                token_count, head_cols
            ),
            grad_branch,
            ROWS_IN,
            preferred_element_type=jnp.float32,
        ).astype(bf16)
        for block in attended
    ]
    grad_query, grad_pair, tail, grad_comp_ext = attend_bwd(
        head, seg_place, slopes, heads, recv_mem, comp_ext, grad_mixed, attn_out, lse, head_cols
    )
    got_mem, got_comp = passed_along(
        (grad_pair[seg_count], grad_comp_ext[:window].astype(bf16)), "blk", -1
    )
    last_pair = (tail + got_mem.astype(jnp.float32)).astype(bf16)
    grad_pair = lax.dynamic_update_slice(grad_pair, last_pair[None], (seg_count - 1, 0, 0))
    comp_pair_grad = grad_comp_ext[window:] + jnp.pad(
        got_comp.astype(jnp.float32), ((seg_count - window, 0), (0, 0), (0, 0))
    )
    comp_grad_rows = comp_pair_grad.reshape(comp_count, 2 * head_cols).astype(bf16)
    grad_packed_part = lax.dot_general(
        comp_grad_rows, wkv, COLS_IN, preferred_element_type=jnp.float32
    ).astype(bf16)

    def columns_of(bits):
        start = jnp.bitwise_xor(head_index, bits) * head_cols
        return lax.dynamic_slice_in_dim(grad_packed_part, start, head_cols, 1)

    grad_packed = sum_over_heads(
        (columns_of(0), columns_of(2)), jnp.stack([columns_of(1), columns_of(3)])
    ).astype(bf16)
    keep, sent = g_normed_parts(
        head,
        grad_query,
        grad_pair,
        grad_packed.reshape(seg_count, pad_rows, head_cols),
        weights,
        quarter,
    )
    grad_normed = sum_over_heads(keep, sent).reshape(token_count, width)
    unit_one, spread_one = row_norm(tokens.reshape(token_count, width).astype(jnp.float32))
    grad_tokens = (
        (grad_hidden + norm_back(grad_normed, unit_one, spread_one, gain_first))
        .astype(bf16)
        .reshape(tokens.shape)
    )
    normed = normed.reshape(full_count, width)
    grad_kv = grad_pair[:seg_count].reshape(full_count, 2 * head_cols)
    grad_wq = lax.dot_general(
        normed, grad_query.reshape(full_count, head_cols), ROWS_IN, preferred_element_type=jnp.float32
    )
    grad_wkv = lax.dot_general(normed, grad_kv, ROWS_IN, preferred_element_type=jnp.float32)
    comp_term = lax.dot_general(packed, comp_grad_rows, ROWS_IN, preferred_element_type=jnp.float32)
    grad_comp = lax.dot_general(
        grouped.reshape(comp_count, RATE * width),
        grad_packed,
        ROWS_IN,
        preferred_element_type=jnp.float32,
    ).reshape(RATE, width, head_cols)
    grad_gain_one = (
        jnp.sum(grad_wq * weights[2].astype(jnp.float32), axis=1)
        + jnp.sum(grad_wkv * wkv.astype(jnp.float32), axis=1)
        + jnp.sum(grad_comp * weights[3:].astype(jnp.float32), axis=(0, 2))
    ) / gain_first[0]
    grad_wkv = grad_wkv + comp_term
    grad_wo = sum_over_heads((grad_wo[0], grad_wo[2]), jnp.stack([grad_wo[1], grad_wo[3]]))

    def by_owner(value):
        return value.astype(bf16).reshape(
            head_groups, blk_count, part, value.shape[1]
        ).transpose(1, 0, 2, 3)

    gain_rows = (
        jnp.stack([grad_gain_one, grad_gain_two])
        .reshape(2, head_groups, blk_count, part)
        .transpose(2, 1, 0, 3)
        .astype(bf16)
    )
    second_grads = jnp.concatenate(
        [
            by_owner(grad_wq),
            by_owner(grad_wkv[:, :head_cols]),
            by_owner(grad_wkv[:, head_cols:]),
            by_owner(grad_comp[0]),
            by_owner(grad_comp[1]),
            by_owner(grad_comp[2]),
            jnp.pad(gain_rows, ((0, 0), (0, 0), (0, 14), (0, head_cols - part))),
            grad_wo.astype(bf16)
            .reshape(blk_count, part, head_groups, head_cols)
            .transpose(0, 2, 1, 3),
        ],
        2,
    )
    second_grads, first_sum = lax.optimization_barrier((second_grads, first_sum))
    first_sum = first_sum.astype(jnp.float32)
    own_rows = 6 * part + 16
    second_part = lax.psum_scatter(
        second_grads.reshape(-1, head_cols), "blk", scatter_dimension=0, tiled=True
    ).reshape(head_groups, own_rows + part, head_cols)
    second_sum = lax.all_to_all(
        second_part[:, :own_rows], "head", split_axis=0, concat_axis=0, tiled=True
    ).astype(jnp.float32)
    gain_sum = jnp.sum(second_sum[:, 6 * part : 6 * part + 2, :part], axis=0)
    weight_sum = (
        second_sum[:, : 6 * part]
        .reshape(head_groups, 6, part, head_cols)
        .transpose(1, 2, 0, 3)
        .reshape(6, part, width)
    )
    wo_sum = second_part[:, own_rows:].astype(jnp.float32).transpose(1, 0, 2).reshape(part, width)
    return (
        out_tokens,
        compressed,
        grad_tokens,
        weight_sum[0],
        weight_sum[1],
        weight_sum[2],
        wo_sum,
        first_sum[:ff_part].T,
        first_sum[ff_part:],
        gain_sum[0],
        gain_sum[1],
        weight_sum[3:],
    )


def solution(mesh):
    return jax.shard_map(
        per_device,
        mesh=mesh,
        in_specs=(
            P("blk", "head", None),
            P(("head", "blk"), None),
            P(("head", "blk"), None),
            P(("head", "blk"), None),
            P(("head", "blk"), None),
            P(None, ("head", "blk")),
            P(("head", "blk"), None),
            P(("head", "blk")),
            P(("head", "blk")),
            P(None, ("head", "blk"), None),
            P(),
            P("blk", "head", None),
        ),
        out_specs=(
            P("blk", "head", None),
            P("blk", None, "head"),
            P("blk", "head", None),
            P(("head", "blk"), None),
            P(("head", "blk"), None),
            P(("head", "blk"), None),
            P(("head", "blk"), None),
            P(None, ("head", "blk")),
            P(("head", "blk"), None),
            P(("head", "blk")),
            P(("head", "blk")),
            P(None, ("head", "blk"), None),
        ),
        check_vma=False,
    )
```

time: 884 us -> 646 us (0.73)
  waiting for transfers between devices: 447 us -> 292 us
  matrix products: 151 us -> 36.1 us
  Pallas kernels: 56.9 us -> 149 us
  local copies, waits for them, and re-layouts: 94.6 us -> 55.1 us
  other arithmetic: 84.9 us -> 51 us
  blocking collectives: 0 us -> 10.9 us
    reduce_scatter x2, waiting for transfers between devices: 214 us -> 12.6 us  [the longest x1 12.6 us: per_device(): lax.psum_scatter(second_grads.reshape(-1, head_cols), 'blk', scatter_dime...]
    dot_general x17 -> x11, matrix products: 140 us -> 29.7 us  [the longest x4 7.92 us: per_device(): lax.dot_general(lax.dynamic_slice_in_dim(block, head_index * quarter, qua...]
    ppermute x7 -> x28, waiting for transfers between devices: 81.3 us -> 190 us  [head_swap(): lax.ppermute(value, 'head', [(source, source ^ bit) for source in range(c...]
    pallas_call x0 -> x3, Pallas kernels: none -> 92.1 us  [the longest x1 61.3 us: feed_forward(): pl.pallas_call(ffn_kernel, grid=(seg_count,), in_specs=[pl.BlockSpec(memo...]
    all_to_all x3 -> x1, waiting for transfers between devices: 48.5 us -> 0.01 us  [per_device(): lax.all_to_all(second_part[:, :own_rows], 'head', split_axis=0, concat_ax...]
    reshape x6 -> x2, local copies, waits for them, and re-layouts: 22.9 us -> 2.89 us  [the longest x1 2.23 us: per_device(): second_grads = jnp.concatenate([by_owner(grad_wq), by_owner(grad_wkv[:, :...]
    concatenate x4 -> x2, other arithmetic: 20.5 us -> 1.12 us  [the longest x1 0.84 us: per_device(): jnp.concatenate([w_up.T, w_down, wo], 0)]
    slice x8 -> x11, local copies, waits for them, and re-layouts: 27.2 us -> 11.6 us  [the longest x1 2.1 us: per_device(): first_all[:, :, :6 * part]]
  transfers between devices with their start and end apart: 18 -> 37, of which waited for: 14 -> 20; matrix products, arithmetic and copies ran while one was open for 20% -> 19% of each run, Pallas kernels for 2% -> 14%
where the time goes in v5:
time: 646 us; the launch traced here: 640 us
  waiting for transfers between devices  292 us (45%)
  Pallas kernels  149 us (23%)
  local copies, waits for them, and re-layouts  55.1 us (9%)
  other arithmetic  51 us (8%)
  matrix products  36.1 us (6%)
  starting transfers between devices  30.4 us (5%)
  between operations  15 us (2%)
  blocking collectives  10.9 us (2%)
    ppermute x28, waiting for transfers between devices, head_swap(): lax.ppermute(value, 'head', [(source, source ^ bit) for source in range(c...  190 us
    ppermute x4, waiting for transfers between devices, passed_along(): lax.ppermute(value, axis, [(source, source + steps) for source in range(l...  64.3 us
    pallas_call x1, Pallas kernels, feed_forward(): pl.pallas_call(ffn_kernel, grid=(seg_count,), in_specs=[pl.BlockSpec(memo...  61.3 us
    pallas_call x1, Pallas kernels, attend_bwd(): pl.pallas_call(bwd_kernel, grid=(seg_count,), in_specs=attention_specs(se...  35.6 us
    all_gather x1, waiting for transfers between devices, per_device(): first_all = lax.all_gather(columns, 'blk', axis=0)  25.5 us
    pallas_call x1, Pallas kernels, attend_fwd(): pl.pallas_call(fwd_kernel, grid=(seg_count,), in_specs=attention_specs(se...  21.2 us
    unnamed x86, local copies, waits for them, and re-layouts  19 us
    pallas_call x1, Pallas kernels, prepare(): pl.pallas_call(prep_kernel, grid=(seg_count,), in_specs=[pl.BlockSpec(mem...  16.9 us
  transfers between devices with their start and end apart: 37, of which 20 were waited for; matrix products, arithmetic and copies ran while one was open for 19% of the time, Pallas kernels for 14%

profile of v5, /device:TPU:24, one launch (start us, length us, event | category | flops | bytes accessed | tf_op | source)
XLA Modules:
  0.0 639.6 jit_solution(4888905269605179425)
XLA Ops:
  12.4 10.9 %all_to_all.10 = bf16[4,208,256]{2,1,0:T(8,128)(2,1)} all-to-all(bf16[4,208,256]{2,1,0:T(8,128)(2,1)S(1)} %copy.240), channel_id=1, replica_groups=mesh['head'=4,'blk'=8] {'head'}, dimensions={0} | all-to-all | bytes 851968 | tf_op jit(solution)/shard_map/all_to_all | solution.py:553
  24.9 35.0 %collective-permute-done.1.t2 = bf16[6,128,1024]{2,1,0:T(8,128)(2,1)} collective-permute-done((bf16[6,128,1024]{2,1,0:T(8,128)(2,1)}, bf16[6,128,1024]{2,1,0:T(8,128)(2,1)}, u32[]{:S(2)}, u32[]{:S(2)}) %collective-permute-start.1) | collective-permute-done | bytes 1572896 | tf_op jit(solution)/shard_map/ppermute | solution.py:508
  60.0 25.5 %all-gather.5.cloned.1.call-done = bf16[32,208,256]{2,1,0:T(8,128)(2,1)} async-done(((bf16[4,208,256]{2,1,0:T(8,128)(2,1)}), bf16[32,208,256]{2,1,0:T(8,128)(2,1)}) %all-gather.5.cloned.1.call-update) | async-done | bytes 3407888 | tf_op jit(solution)/shard_map/all_gather | solution.py:555
  91.5 16.9 %prepare.1 = (bf16[6,512,768]{2,1,0:T(8,128)(2,1)}, bf16[6,512,1024]{2,1,0:T(8,128)(2,1)}, bf16[6,176,3072]{2,1,0:T(8,128)(2,1)}, bf16[6,176,256]{2,1,0:T(8,128)(2,1)}) custom-call(s32[1]{0:T(128)} %bitcast.head_ref, bf16[6,128,1024]{2,1,0:T(8,128)(2,1)} %t0.1, bf16[6,128,1024]{2,1,0:T(8,128)(2,1)} %collective-permute-done.t1, ...), custom_call_target="tpu_custom_call" | custom-call | flops 7000000000 | bytes 30000000 | tf_op jit(solution)/shard_map/prepare/pallas_call | solution.py:335
  111.1 11.8 %collective-permute-done.5 = bf16[1056,256]{1,0:T(8,128)(2,1)} collective-permute-done((bf16[1056,256]{1,0:T(8,128)(2,1)}, bf16[1056,256]{1,0:T(8,128)(2,1)}, u32[]{:S(2)}, u32[]{:S(2)}) %collective-permute-start.5) | collective-permute-done | bytes 540704 | tf_op jit(solution)/shard_map/ppermute | solution.py:508
  136.8 29.7 %collective-permute-done.7 = bf16[4,176,512]{2,1,0:T(8,128)(2,1)} collective-permute-done((bf16[4,176,512]{2,1,0:T(8,128)(2,1)}, bf16[4,176,512]{2,1,0:T(8,128)(2,1)}, u32[]{:S(2)}, u32[]{:S(2)}) %collective-permute-start.7) | collective-permute-done | bytes 720928 | tf_op jit(solution)/shard_map/ppermute | solution.py:22
  169.3 20.9 %collective-permute-done.3.recv_ref = bf16[1,512,512]{2,1,0:T(8,128)(2,1)S(1)} collective-permute-done((bf16[1,512,512]{2,1,0:T(8,128)(2,1)S(1)}, bf16[1,512,512]{2,1,0:T(8,128)(2,1)S(1)}, u32[]{:S(2)}, u32[]{:S(2)}) %collective-permute-start.3) | collective-permute-done | bytes 524320 | tf_op jit(solution)/shard_map/ppermute | solution.py:22
  191.0 21.2 %attend_fwd.1 = (bf16[6,512,256]{2,1,0:T(8,128)(2,1)}, f32[6,2,512]{2,1,0:T(2,128)}) custom-call(s32[6]{0:T(128)} %fusion.68.place_ref, f32[2]{0:T(128)} %exponential_multiply_fusion.slope_ref, bf16[6,512,768]{2,1,0:T(8,128)(2,1)} %get-tuple-element.44.q_ref.own_ref.prev_ref, bf16[6,512,768]{2,1,0:T(8,128)(2,1)} %get-tuple-element.44.q_ref.own_ref.prev_ref, ...), custom_call_target="tpu_custom_call" | custom-call | flops 5000000000 | bytes 16000000 | tf_op jit(solution)/shard_map/attend_fwd/pallas_call | solution.py:193
  214.2 34.7 %collective-permute-done.9.a2 = bf16[6,512,256]{2,1,0:T(8,128)(2,1)} collective-permute-done((bf16[6,512,256]{2,1,0:T(8,128)(2,1)}, bf16[6,512,256]{2,1,0:T(8,128)(2,1)}, u32[]{:S(2)}, u32[]{:S(2)}) %collective-permute-start.9) | collective-permute-done | bytes 1572896 | tf_op jit(solution)/shard_map/ppermute | solution.py:508
  252.5 13.0 %collective-permute-done.12.o2 = bf16[256,1024]{1,0:T(8,128)(2,1)} collective-permute-done((bf16[256,1024]{1,0:T(8,128)(2,1)}, bf16[256,1024]{1,0:T(8,128)(2,1)}, u32[]{:S(2)}, u32[]{:S(2)}) %collective-permute-start.12) | collective-permute-done | bytes 524320 | tf_op jit(solution)/shard_map/ppermute | solution.py:508
  267.7 61.3 %feed_forward.1 = (bf16[2,6,128,1024]{3,2,1,0:T(8,128)(2,1)}, bf16[2,6,128,1024]{3,2,1,0:T(8,128)(2,1)}, bf16[2,6,128,1024]{3,2,1,0:T(8,128)(2,1)}, bf16[2,6,128...) custom-call(s32[1]{0:T(128)} %bitcast.head_ref, ...), custom_call_target="tpu_custom_call" | custom-call | flops 44999999488 | bytes 60000000 | tf_op jit(solution)/shard_map/feed_forward/pallas_call | solution.py:431
  347.7 27.9 %collective-permute-done.18 = bf16[6,128,1024]{2,1,0:T(8,128)(2,1)} collective-permute-done((bf16[6,128,1024]{2,1,0:T(8,128)(2,1)}, bf16[6,128,1024]{2,1,0:T(8,128)(2,1)}, u32[]{:S(2)}, u32[]{:S(2)}) %collective-permute-start.18) | collective-permute-done | bytes 1572896 | tf_op jit(solution)/shard_map/ppermute | solution.py:508
  398.7 6.2 collective-permute-done.20.g2
  405.7 35.6 %attend_bwd.1 = (bf16[6,512,256]{2,1,0:T(8,128)(2,1)}, bf16[7,512,512]{2,1,0:T(8,128)(2,1)}, f32[512,512]{1,0:T(8,128)}, f32[10,176,512]{2,1,0:T(8,128)}) custom-call(s32[6]{0:T(128)} %fusion.68.place_ref, f32[2]{0:T(128)} %exponential_multiply_fusion.slope_ref, bf16[6,512,768]{2,1,0:T(8,128)(2,1)} %get-tuple-element.44.q_ref.own_ref.prev_ref, ...), custom_call_target="tpu_custom_call" | custom-call | flops 12000000000 | bytes 24000000 | tf_op jit(solution)/shard_map/attend_bwd/pallas_call | solution.py:216
  463.1 10.6 %collective-permute-done.25 = bf16[4,176,512]{2,1,0:T(8,128)(2,1)S(1)} collective-permute-done((bf16[4,176,512]{2,1,0:T(8,128)(2,1)S(1)}, bf16[4,176,512]{2,1,0:T(8,128)(2,1)S(1)}, u32[]{:S(2)}, u32[]{:S(2)}) %collective-permute-start.25) | collective-permute-done | bytes 720928 | tf_op jit(solution)/shard_map/ppermute | solution.py:22
  486.0 6.9 %collective-permute-done.31 = bf16[256,1024]{1,0:T(8,128)(2,1)S(1)} collective-permute-done((bf16[256,1024]{1,0:T(8,128)(2,1)S(1)}, bf16[256,1024]{1,0:T(8,128)(2,1)S(1)}, u32[]{:S(2)}, u32[]{:S(2)}) %collective-permute-start.31) | collective-permute-done | bytes 524320 | tf_op jit(solution)/shard_map/ppermute | solution.py:508
  497.5 5.8 collective-permute-done.27
  505.1 7.6 %fusion.24 = (f32[3072]{0:T(1024)S(1)}, bf16[3072,256]{1,0:T(8,128)(2,1)}) fusion(f32[3,4,8,32,256]{4,3,2,1,0:T(8,128)} %copy.255, bf16[1056,3072]{1,0:T(8,128)(2,1)} %bitcast.303, bf16[1056,256]{1,0:T(8,128)(2,1)S(1)} %fusion.54), kind=kOutput, calls=%fused_computation.34 | convolution fusion | flops 1663300608 | bytes 11759616 | tf_op jit(solution)/shard_map/dot_general | solution.py:689
  518.8 13.9 %g_normed.1 = (bf16[2,6,128,1024]{3,2,1,0:T(8,128)(2,1)}, bf16[2,6,128,1024]{3,2,1,0:T(8,128)(2,1)}) custom-call(s32[1]{0:T(128)} %bitcast.head_ref, bf16[6,512,256]{2,1,0:T(8,128)(2,1)} %get-tuple-element.59.gq_ref, bf16[7,512,512]{2,1,0:T(8,128)(2,1)} %copy-done.27, bf16[6,176,256]{2,1,0:T(8,128)(2,1)} %bitcast.275, bf16[6,1024,256]{2,1,0:T(8,128)(2,1)} %bitcast.255), custom_call_target="tpu_custom_call" | custom-call | flops 7000000000 | bytes 20000000 | tf_op jit(solution)/shard_map/g_normed/pallas_call | solution.py:484
  533.2 9.0 %collective-permute-done.28 = bf16[2,6,128,1024]{3,2,1,0:T(8,128)(2,1)S(1)} collective-permute-done((bf16[2,6,128,1024]{3,2,1,0:T(8,128)(2,1)}, bf16[2,6,128,1024]{3,2,1,0:T(8,128)(2,1)S(1)}, u32[]{:S(2)}, u32[]{:S(2)}) %collective-permute-start.28) | collective-permute-done | bytes 3145760 | tf_op jit(solution)/shard_map/ppermute | solution.py:508
  561.9 21.9 %collective-permute-done.29 = bf16[6,128,1024]{2,1,0:T(8,128)(2,1)} collective-permute-done((bf16[6,128,1024]{2,1,0:T(8,128)(2,1)}, bf16[6,128,1024]{2,1,0:T(8,128)(2,1)}, u32[]{:S(2)}, u32[]{:S(2)}) %collective-permute-start.29) | collective-permute-done | bytes 1572896 | tf_op jit(solution)/shard_map/ppermute | solution.py:508
  588.7 12.6 %reduce-scatter.5.cloned.1.call-done = bf16[960,256]{1,0:T(8,128)(2,1)} async-done(((bf16[7680,256]{1,0:T(8,128)(2,1)}), bf16[960,256]{1,0:T(8,128)(2,1)}) %reduce-scatter.5.cloned.1.call-update) | async-done | bytes 491536 | tf_op jit(solution)/shard_map/reduce_scatter | solution.py:732
  607.2 10.2 %collective-permute-done.23 = bf16[6,128,1024]{2,1,0:T(8,128)(2,1)} collective-permute-done((bf16[6,128,1024]{2,1,0:T(8,128)(2,1)}, bf16[6,128,1024]{2,1,0:T(8,128)(2,1)}, u32[]{:S(2)}, u32[]{:S(2)}) %collective-permute-start.23) | collective-permute-done | bytes 1572896 | tf_op jit(solution)/shard_map/ppermute | solution.py:508
  617.4 8.0 %fusion.8 = (bf16[6,128,1024]{2,1,0:T(8,128)(2,1)}, bf16[6,128,1024]{2,1,0:T(8,128)(2,1)}) fusion(bf16[6,128,1024]{2,1,0:T(8,128)(2,1)} %t0.1, f32[6,128,1024]{2,1,0:T(8,128)} %get-tuple-element.185, f32[6,128]{1,0:T(8,128)S(1)} %broadcast_multiply_fusion, f32[6,128]{1,0:T(8,128)S(1)} %broadcast_multiply_fusion.1, f32[6,128]{1,0:T(8,128)S(1)} %add_rsqrt_fusion, ...), kind=kLoop, calls=%fused_computation.11 | loop fusion | flops 18874368 | bytes 22048768 | tf_op jit(solution)/shard_map/convert_element_type | solution.py:679
  (261 shorter events, 167.5 us)
Async XLA Ops:
  7.2 78.3 %all-gather.5.cloned.1.call-start = ((), (), s32[]{:S(2)}) async-start(), calls=%async_computation.6 | async-start | bytes 3833856 | tf_op jit(solution)/shard_map/all_gather | solution.py:555
  23.3 225.7 %all-gather.7.cloned.1.call-start = ((), (), s32[]{:S(2)}) async-start(), calls=%async_computation.7 | async-start | bytes 5308416 | tf_op jit(solution)/shard_map/all_gather | solution.py:556
  23.3 36.6 %collective-permute-start.1 = (bf16[6,128,1024]{2,1,0:T(8,128)(2,1)}, bf16[6,128,1024]{2,1,0:T(8,128)(2,1)}, u32[]{:S(2)}, u32[]{:S(2)}) collective-permute-start(bf16[6,128,1024]{2,1,0:T(8,128)(2,1)} %t0.1), channel_id=1, source_target_pairs={{0,16},{8,24},{16,0},{24,8},{1,17},{9,25},{17,1},{25,9},{2,18},{10... | collective-permute-start | bytes 4718600 | tf_op jit(solution)/shard_map/ppermute | solution.py:508
  24.8 493.9 %reduce-scatter.3.cloned.1.call-start = ((), (), s32[]{:S(2)}) async-start(), calls=%async_computation.4 | async-start | bytes 4718592 | tf_op jit(solution)/shard_map/reduce_scatter | solution.py:607
  24.9 66.6 %collective-permute-start = (bf16[6,128,1024]{2,1,0:T(8,128)(2,1)}, bf16[6,128,1024]{2,1,0:T(8,128)(2,1)}, u32[]{:S(2)}, u32[]{:S(2)}) collective-permute-start(bf16[6,128,1024]{2,1,0:T(8,128)(2,1)} %t0.1), channel_id=1, source_target_pairs={{0,8},{8,0},{16,24},{24,16},{1,9},{9,1},{17,25},{25,17},{2,10},{10... | collective-permute-start | bytes 4718600 | tf_op jit(solution)/shard_map/ppermute | solution.py:508
  60.0 31.5 %collective-permute-start.2 = (bf16[6,128,1024]{2,1,0:T(8,128)(2,1)}, bf16[6,128,1024]{2,1,0:T(8,128)(2,1)}, u32[]{:S(2)}, u32[]{:S(2)}) collective-permute-start(bf16[6,128,1024]{2,1,0:T(8,128)(2,1)} %collective-permute-done.1.t2), channel_id=1, source_target_pairs={{0,8},{8,0},{16,24},{24,16},{1,9},{9,1},{17,25},{25,17},{2,10},{10... | collective-permute-start | bytes 4718600 | tf_op jit(solution)/shard_map/ppermute | solution.py:508
  128.3 38.2 %collective-permute-start.7 = (bf16[4,176,512]{2,1,0:T(8,128)(2,1)}, bf16[4,176,512]{2,1,0:T(8,128)(2,1)}, u32[]{:S(2)}, u32[]{:S(2)}) collective-permute-start(bf16[4,176,512]{2,1,0:T(8,128)(2,1)} %bitcast.12), channel_id=1, source_target_pairs={{0,1},{1,2},{2,3},{3,4},{4,5},{5,6},{6,7},{8,9},{9,10},{10,11},{11... | collective-permute-start | bytes 2162696 | tf_op jit(solution)/shard_map/ppermute | solution.py:22
  132.5 57.8 %collective-permute-start.3 = (bf16[1,512,512]{2,1,0:T(8,128)(2,1)S(1)}, bf16[1,512,512]{2,1,0:T(8,128)(2,1)S(1)}, u32[]{:S(2)}, u32[]{:S(2)}) collective-permute-start(bf16[1,512,512]{2,1,0:T(8,128)(2,1)S(1)} %slice.174), channel_id=1, source_target_pairs={{0,1},{1,2},{2,3},{3,4},{4,5},{5,6},{6,7},{8,9},{9,10},{10,11},{11... | collective-permute-start | bytes 1572872 | tf_op jit(solution)/shard_map/ppermute | solution.py:22
  135.3 78.4 %collective-permute-start.15 = (bf16[6,128,1024]{2,1,0:T(8,128)(2,1)}, bf16[6,128,1024]{2,1,0:T(8,128)(2,1)}, u32[]{:S(2)}, u32[]{:S(2)}) collective-permute-start(bf16[6,128,1024]{2,1,0:T(8,128)(2,1)} %g0), channel_id=1, source_target_pairs={{0,16},{8,24},{16,0},{24,8},{1,17},{9,25},{17,1},{25,9},{2,18},{10... | collective-permute-start | bytes 4718600 | tf_op jit(solution)/shard_map/ppermute | solution.py:508
  212.2 36.7 %collective-permute-start.9 = (bf16[6,512,256]{2,1,0:T(8,128)(2,1)}, bf16[6,512,256]{2,1,0:T(8,128)(2,1)}, u32[]{:S(2)}, u32[]{:S(2)}) collective-permute-start(bf16[6,512,256]{2,1,0:T(8,128)(2,1)} %get-tuple-element.46.a0.att_ref), channel_id=1, source_target_pairs={{0,16},{8,24},{16,0},{24,8},{1,17},{9,25},{17,1},{25,9},{2,18},{10... | collective-permute-start | bytes 4718600 | tf_op jit(solution)/shard_map/ppermute | solution.py:508
  213.7 38.6 %collective-permute-start.14 = (bf16[6,128,1024]{2,1,0:T(8,128)(2,1)}, bf16[6,128,1024]{2,1,0:T(8,128)(2,1)}, u32[]{:S(2)}, u32[]{:S(2)}) collective-permute-start(bf16[6,128,1024]{2,1,0:T(8,128)(2,1)} %g0), channel_id=1, source_target_pairs={{0,8},{8,0},{16,24},{24,16},{1,9},{9,1},{17,25},{25,17},{2,10},{10... | collective-permute-start | bytes 4718600 | tf_op jit(solution)/shard_map/ppermute | solution.py:508
  213.7 52.4 %collective-permute-start.16 = (bf16[6,128,1024]{2,1,0:T(8,128)(2,1)}, bf16[6,128,1024]{2,1,0:T(8,128)(2,1)}, u32[]{:S(2)}, u32[]{:S(2)}) collective-permute-start(bf16[6,128,1024]{2,1,0:T(8,128)(2,1)} %collective-permute-done.15.g2), channel_id=1, source_target_pairs={{0,8},{8,0},{16,24},{24,16},{1,9},{9,1},{17,25},{25,17},{2,10},{10... | collective-permute-start | bytes 4718600 | tf_op jit(solution)/shard_map/ppermute | solution.py:508
  214.2 53.5 %collective-permute-start.8 = (bf16[6,512,256]{2,1,0:T(8,128)(2,1)}, bf16[6,512,256]{2,1,0:T(8,128)(2,1)}, u32[]{:S(2)}, u32[]{:S(2)}) collective-permute-start(bf16[6,512,256]{2,1,0:T(8,128)(2,1)} %get-tuple-element.46.a0.att_ref), channel_id=1, source_target_pairs={{0,8},{8,0},{16,24},{24,16},{1,9},{9,1},{17,25},{25,17},{2,10},{10... | collective-permute-start | bytes 4718600 | tf_op jit(solution)/shard_map/ppermute | solution.py:508
  248.9 18.8 %collective-permute-start.10 = (bf16[6,512,256]{2,1,0:T(8,128)(2,1)}, bf16[6,512,256]{2,1,0:T(8,128)(2,1)}, u32[]{:S(2)}, u32[]{:S(2)}) collective-permute-start(bf16[6,512,256]{2,1,0:T(8,128)(2,1)} %collective-permute-done.9.a2), channel_id=1, source_target_pairs={{0,8},{8,0},{16,24},{24,16},{1,9},{9,1},{17,25},{25,17},{2,10},{10... | collective-permute-start | bytes 4718600 | tf_op jit(solution)/shard_map/ppermute | solution.py:508
  338.8 36.8 %collective-permute-start.18 = (bf16[6,128,1024]{2,1,0:T(8,128)(2,1)}, bf16[6,128,1024]{2,1,0:T(8,128)(2,1)}, u32[]{:S(2)}, u32[]{:S(2)}) collective-permute-start(bf16[6,128,1024]{2,1,0:T(8,128)(2,1)} %fusion.34), channel_id=1, source_target_pairs={{0,16},{8,24},{16,0},{24,8},{1,17},{9,25},{17,1},{25,9},{2,18},{10... | collective-permute-start | bytes 4718600 | tf_op jit(solution)/shard_map/ppermute | solution.py:508
  345.1 256.2 %reduce-scatter.5.cloned.1.call-start = ((), (), s32[]{:S(2)}) async-start(), calls=%async_computation.5 | async-start | bytes 4423680 | tf_op jit(solution)/shard_map/reduce_scatter | solution.py:732
  387.2 17.6 %collective-permute-start.20 = (bf16[6,128,256]{2,1,0:T(8,128)(2,1)S(1)}, bf16[6,128,256]{2,1,0:T(8,128)(2,1)S(1)}, u32[]{:S(2)}, u32[]{:S(2)}) collective-permute-start(bf16[6,128,256]{2,1,0:T(8,128)(2,1)S(1)} %bitcast.301), channel_id=1, source_target_pairs={{0,16},{8,24},{16,0},{24,8},{1,17},{9,25},{17,1},{25,9},{2,18},{10... | collective-permute-start | bytes 1179656 | tf_op jit(solution)/shard_map/ppermute | solution.py:508
  395.9 66.9 %collective-permute-start.30 = (bf16[2,256,1024]{2,1,0:T(8,128)(2,1)S(1)}, bf16[2,256,1024]{2,1,0:T(8,128)(2,1)S(1)}, u32[]{:S(2)}, u32[]{:S(2)}) collective-permute-start(bf16[2,256,1024]{2,1,0:T(8,128)(2,1)S(1)} %pad_maximum_fusion.3), channel_id=1, source_target_pairs={{0,8},{8,0},{16,24},{24,16},{1,9},{9,1},{17,25},{25,17},{2,10},{10... | collective-permute-start | bytes 3145736 | tf_op jit(solution)/shard_map/ppermute | solution.py:508
  442.4 16.7 %collective-permute-start.24 = (bf16[512,512]{1,0:T(8,128)(2,1)S(1)}, bf16[512,512]{1,0:T(8,128)(2,1)S(1)}, u32[]{:S(2)}, u32[]{:S(2)}) collective-permute-start(bf16[512,512]{1,0:T(8,128)(2,1)S(1)} %slice_bitcast_fusion.5), channel_id=1, source_target_pairs={{1,0},{2,1},{3,2},{4,3},{5,4},{6,5},{7,6},{9,8},{10,9},{11,10},{12... | collective-permute-start | bytes 1572872 | tf_op jit(solution)/shard_map/ppermute | solution.py:22
  445.8 27.9 %collective-permute-start.25 = (bf16[4,176,512]{2,1,0:T(8,128)(2,1)S(1)}, bf16[4,176,512]{2,1,0:T(8,128)(2,1)S(1)}, u32[]{:S(2)}, u32[]{:S(2)}) collective-permute-start(bf16[4,176,512]{2,1,0:T(8,128)(2,1)S(1)} %slice.335), channel_id=1, source_target_pairs={{1,0},{2,1},{3,2},{4,3},{5,4},{6,5},{7,6},{9,8},{10,9},{11,10},{12... | collective-permute-start | bytes 2162696 | tf_op jit(solution)/shard_map/ppermute | solution.py:22
  483.7 19.6 %collective-permute-start.27 = (bf16[1056,256]{1,0:T(8,128)(2,1)}, bf16[1056,256]{1,0:T(8,128)(2,1)}, u32[]{:S(2)}, u32[]{:S(2)}) collective-permute-start(bf16[1056,256]{1,0:T(8,128)(2,1)} %fusion.51), channel_id=1, source_target_pairs={{0,16},{8,24},{16,0},{24,8},{1,17},{9,25},{17,1},{25,9},{2,18},{10... | collective-permute-start | bytes 1622024 | tf_op jit(solution)/shard_map/ppermute | solution.py:508
  546.2 37.6 %collective-permute-start.29 = (bf16[6,128,1024]{2,1,0:T(8,128)(2,1)}, bf16[6,128,1024]{2,1,0:T(8,128)(2,1)}, u32[]{:S(2)}, u32[]{:S(2)}) collective-permute-start(bf16[6,128,1024]{2,1,0:T(8,128)(2,1)} %fusion.36), channel_id=1, source_target_pairs={{0,16},{8,24},{16,0},{24,8},{1,17},{9,25},{17,1},{25,9},{2,18},{10... | collective-permute-start | bytes 4718600 | tf_op jit(solution)/shard_map/ppermute | solution.py:508
  552.6 64.8 %collective-permute-start.23 = (bf16[6,128,1024]{2,1,0:T(8,128)(2,1)}, bf16[6,128,1024]{2,1,0:T(8,128)(2,1)}, u32[]{:S(2)}, u32[]{:S(2)}) collective-permute-start(bf16[6,128,1024]{2,1,0:T(8,128)(2,1)} %fusion.35), channel_id=1, source_target_pairs={{0,16},{8,24},{16,0},{24,8},{1,17},{9,25},{17,1},{25,9},{2,18},{10... | collective-permute-start | bytes 4718600 | tf_op jit(solution)/shard_map/ppermute | solution.py:508
  603.1 23.9 %all-to-all-start.1 = ((bf16[4,208,256]{2,1,0:T(8,128)(2,1)}), bf16[4,208,256]{2,1,0:T(8,128)(2,1)}, u32[]{:S(2)}, u32[]{:S(2)}) async-start(bf16[4,208,256]{2,1,0:T(8,128)(2,1)} %slice.249), calls=%async_computation.3 | async-start | bytes 851968 | tf_op jit(solution)/shard_map/all_to_all | solution.py:735
  (50 other events, 437.7 us)
Sparse Core Ops, SparseCore 0:
  23.4 62.0 all-gather.4
  87.7 91.2 all-gather.6
  345.2 85.8 reduce-scatter.2
  518.9 82.3 reduce-scatter.4

commit v6 on v5

--- a/solution.py
+++ b/solution.py
@@ -1,3 +1,5 @@
+import functools
+
 import jax
 import jax.numpy as jnp
 from jax import lax
@@ -33,8 +35,8 @@
     return jnp.where((row < valid_rows) & open_, place * slope, NEG)
 
 
-def fwd_kernel(place_ref, slope_ref, q_ref, own_ref, prev_ref, recv_ref, comp_ref, out_ref, lse_ref):
-    step = pl.program_id(0)
+def fwd_kernel(first, place_ref, slope_ref, q_ref, own_ref, prev_ref, recv_ref, comp_ref, out_ref, lse_ref):
+    step = pl.program_id(0) + first
     place = place_ref[step]
     seg_len = q_ref.shape[1]
     half = seg_len // 2
@@ -96,10 +98,10 @@
 
 
 def bwd_kernel(
-    place_ref, slope_ref, q_ref, own_ref, prev_ref, recv_ref, comp_ref, head_ref, g0, g1, g2, g3, att_ref, lse_ref,
+    first, place_ref, slope_ref, q_ref, own_ref, prev_ref, recv_ref, comp_ref, head_ref, g0, g1, g2, g3, att_ref, lse_ref, held_ref,
     gq_ref, gkv_ref, tail_ref, gcomp_ref, grad_ref,
 ):
-    step = pl.program_id(0)
+    step = pl.program_id(0) + first
     place = place_ref[step]
     seg_len = q_ref.shape[1]
     half = seg_len // 2
@@ -113,9 +115,11 @@
         jnp.int32, (half, half), 1
     )
 
-    @pl.when(is_first)
+    at_start = pl.program_id(0) == 0
+
+    @pl.when(at_start)
     def _():
-        tail_ref[...] = jnp.zeros_like(tail_ref)
+        tail_ref[...] = held_ref[...]
         gcomp_ref[...] = jnp.zeros_like(gcomp_ref)
 
     place_rows(head_ref[0], (g0, g1, g2, g3), grad_ref)
@@ -148,8 +152,8 @@
             lag = CSEGS + 1 - piece
             bias = key_bias(pad_rows, RATE // 2 - lag * seg_len, RATE, seg_len // RATE, place >= lag, slope)
             gk, gv, gq = part(comp_ref[step + piece, :, kc], comp_ref[step + piece, :, vc], bias, every, False)
-            gcomp_ref[step + piece, :, kc] += gk
-            gcomp_ref[step + piece, :, vc] += gv
+            gcomp_ref[step - first + piece, :, kc] += gk
+            gcomp_ref[step - first + piece, :, vc] += gv
             total = total + gq
         for n in range(2):
             rows = slice(n * half, (n + 1) * half)
@@ -174,69 +178,76 @@
         gq_ref[0, hi, kc] = ((total[:, hi] + gq1 + gq2) * scale).T.astype(jnp.bfloat16)
 
 
-def attention_specs(seg_len, head_cols, comp_shape):
+def attention_specs(first, seg_len, head_cols, comp_shape):
     pair = 2 * head_cols
     return [
         pl.BlockSpec(memory_space=pltpu.SMEM),
         pl.BlockSpec(memory_space=pltpu.SMEM),
-        pl.BlockSpec((1, seg_len, head_cols), lambda s: (s, 0, 2)),
-        pl.BlockSpec((1, seg_len, pair), lambda s: (s, 0, 0)),
-        pl.BlockSpec((1, seg_len, pair), lambda s: (jnp.maximum(s - 1, 0), 0, 0)),
-        pl.BlockSpec((1, seg_len, pair), lambda s: (0, 0, 0)),
-        pl.BlockSpec(comp_shape, lambda s: (0, 0, 0)),
+        pl.BlockSpec((1, seg_len, head_cols), lambda s: (s + first, 0, 2)),
+        pl.BlockSpec((1, seg_len, pair), lambda s: (s + first, 0, 0)),
+        pl.BlockSpec((1, seg_len, pair), lambda s: (jnp.maximum(s + first - 1, 0), 0, 0)),
+        fixed((1, seg_len, pair)),
+        fixed(comp_shape),
     ]
 
 
-def attend_fwd(place, slope, heads, recv_mem, comp_ext, head_cols):
-    seg_count, seg_len, _ = heads.shape
+def attend_fwd(first, count, place, slope, heads, recv_mem, comp_ext, head_cols):
+    seg_len = heads.shape[1]
     local_heads = head_cols // HD
     return pl.pallas_call(
-        fwd_kernel,
-        grid=(seg_count,),
-        in_specs=attention_specs(seg_len, head_cols, comp_ext.shape),
-        out_specs=[
-            pl.BlockSpec((1, seg_len, head_cols), lambda s: (s, 0, 0)),
-            pl.BlockSpec((1, local_heads, seg_len), lambda s: (s, 0, 0)),
-        ],
+        functools.partial(fwd_kernel, first),
+        grid=(count,),
+        in_specs=attention_specs(first, seg_len, head_cols, comp_ext.shape),
+        out_specs=[by_segment((seg_len, head_cols)), by_segment((local_heads, seg_len))],
         out_shape=[
-            jax.ShapeDtypeStruct((seg_count, seg_len, head_cols), jnp.bfloat16),
-            jax.ShapeDtypeStruct((seg_count, local_heads, seg_len), jnp.float32),
+            jax.ShapeDtypeStruct((count, seg_len, head_cols), jnp.bfloat16),
+            jax.ShapeDtypeStruct((count, local_heads, seg_len), jnp.float32),
         ],
         compiler_params=pltpu.CompilerParams(vmem_limit_bytes=VMEM_LIMIT),
-        cost_estimate=pl.CostEstimate(flops=5 * 10**9, bytes_accessed=16 * 10**6, transcendentals=10**7),
+        cost_estimate=pl.CostEstimate(
+            flops=count * 10**9, bytes_accessed=count * 3 * 10**6, transcendentals=count * 16 * 10**5
+        ),
         name="attend_fwd",
     )(place, slope, heads, heads, heads, recv_mem, comp_ext)
 
 
-def attend_bwd(head, place, slope, heads, recv_mem, comp_ext, grad_mixed, attn_out, lse, head_cols):
-    seg_count, seg_len, _ = heads.shape
+def attend_bwd(
+    first, head, place, slope, heads, recv_mem, comp_ext, grad_mixed, attn_out, lse, held, head_cols
+):
+    count, seg_len, _ = attn_out.shape
     local_heads = head_cols // HD
     pair = 2 * head_cols
-    blocks = seg_count + 1
+    window = (count + CSEGS - 1,) + comp_ext.shape[1:]
     return pl.pallas_call(
-        bwd_kernel,
-        grid=(seg_count,),
-        in_specs=attention_specs(seg_len, head_cols, comp_ext.shape)
+        functools.partial(bwd_kernel, first),
+        grid=(count,),
+        in_specs=attention_specs(first, seg_len, head_cols, comp_ext.shape)
         + [pl.BlockSpec(memory_space=pltpu.SMEM)]
         + [by_segment(grad_mixed[0].shape[1:])] * 4
-        + [by_segment((seg_len, head_cols)), by_segment((local_heads, seg_len))],
+        + [
+            by_segment((seg_len, head_cols)),
+            by_segment((local_heads, seg_len)),
+            fixed((seg_len, pair)),
+        ],
         out_specs=[
-            pl.BlockSpec((1, seg_len, head_cols), lambda s: (s, 0, 0)),
-            pl.BlockSpec((1, seg_len, pair), lambda s: (lax.rem(s + blocks - 1, blocks), 0, 0)),
+            by_segment((seg_len, head_cols)),
+            by_segment((seg_len, pair)),
             pl.BlockSpec((seg_len, pair), lambda s: (0, 0)),
-            pl.BlockSpec(comp_ext.shape, lambda s: (0, 0, 0)),
+            pl.BlockSpec(window, lambda s: (0, 0, 0)),
         ],
         out_shape=[
-            jax.ShapeDtypeStruct((seg_count, seg_len, head_cols), jnp.bfloat16),
-            jax.ShapeDtypeStruct((blocks, seg_len, pair), jnp.bfloat16),
+            jax.ShapeDtypeStruct((count, seg_len, head_cols), jnp.bfloat16),
+            jax.ShapeDtypeStruct((count, seg_len, pair), jnp.bfloat16),
             jax.ShapeDtypeStruct((seg_len, pair), jnp.float32),
-            jax.ShapeDtypeStruct(comp_ext.shape, jnp.float32),
+            jax.ShapeDtypeStruct(window, jnp.float32),
         ],
         scratch_shapes=[pltpu.VMEM((seg_len, head_cols), jnp.bfloat16)],
         compiler_params=pltpu.CompilerParams(vmem_limit_bytes=VMEM_LIMIT),
-        cost_estimate=pl.CostEstimate(flops=12 * 10**9, bytes_accessed=24 * 10**6, transcendentals=10**7),
+        cost_estimate=pl.CostEstimate(
+            flops=count * 2 * 10**9, bytes_accessed=count * 4 * 10**6, transcendentals=count * 16 * 10**5
+        ),
         name="attend_bwd",
-    )(place, slope, heads, heads, heads, recv_mem, comp_ext, head, *grad_mixed, attn_out, lse)
+    )(place, slope, heads, heads, heads, recv_mem, comp_ext, head, *grad_mixed, attn_out, lse, held)
 
 
 def row_norm(values):
@@ -358,8 +369,8 @@
 
 
 def ffn_kernel(
-    head_ref, a0, a1, a2, a3, o0, o1, o2, o3, t0, t1, t2, t3, g0, g1, g2, g3, gain_ref, up_ref, down_ref,
-    f_keep, f_sent, n_keep, n_sent, hidden_ref, pack_ref,
+    chained, head_ref, a0, a1, a2, a3, o0, o1, o2, o3, t0, t1, t2, t3, g0, g1, g2, g3, gain_ref,
+    up_ref, down_ref, earlier_ref, f_keep, f_sent, n_keep, n_sent, hidden_ref, pack_ref,
     rows, grads, acc_up, acc_down,
 ):
     step = pl.program_id(0)
@@ -371,14 +382,22 @@
 
     @pl.when(step == 0)
     def _():
-        acc_up[...] = jnp.zeros_like(acc_up)
-        acc_down[...] = jnp.zeros_like(acc_down)
+        if chained:
+            for n in range(2):
+                own = slice(n * parts, (n + 1) * parts)
+                acc_up[n] = earlier_ref[own, :ff_part].reshape(block, width).astype(jnp.float32)
+                acc_down[n] = earlier_ref[own, ff_part:].reshape(block, width).astype(jnp.float32)
+        else:
+            acc_up[...] = jnp.zeros_like(acc_up)
+            acc_down[...] = jnp.zeros_like(acc_down)
 
     place_rows(head, (t0, t1, t2, t3), rows)
     place_rows(head, (g0, g1, g2, g3), grads)
     hidden = rows[...]
     for a, o in ((a0, o0), (a1, o1), (a2, o2), (a3, o3)):
-        hidden = hidden + jnp.dot(a[0], o[...], preferred_element_type=jnp.float32)
+        hidden = hidden + jnp.dot(
+            a[0], o[...].reshape(a.shape[2], width), preferred_element_type=jnp.float32
+        )
     rows[...] = hidden
     at = pl.multiple_of(head * quarter, quarter)
     hidden_ref[0] = rows[pl.ds(at, quarter), :]
@@ -415,13 +434,39 @@
             pack_ref[own, ff_part:] = acc_down[n].astype(jnp.bfloat16).reshape(shape)
 
 
-def feed_forward(head, attended, wo, tokens, grads, gain, pack, ff_part):
-    seg_count, quarter, width = tokens[0].shape
-    seg_len, head_cols = attended[0].shape[1:]
+def wo_blocks(pack, part, ff_part, head_groups):
+    blks, _, width = pack.shape
+    start = 2 * ff_part
+    if part % 16 == 0:
+        specs = [
+            pl.BlockSpec(
+                (blks, part, width),
+                functools.partial(lambda index, s: (0, index, 0), start // part + n),
+                pipeline_mode=pl.Buffered(1),
+            )
+            for n in range(head_groups)
+        ]
+        return [pack] * head_groups, specs
+    blocks = [
+        pack[:, start + n * part : start + (n + 1) * part].reshape(blks * part, width)
+        for n in range(head_groups)
+    ]
+    return blocks, [fixed((blks * part, width))] * head_groups
+
+
+def feed_forward(first, head, attended, wo, wo_specs, tokens, grads, gain, pack, ff_part, earlier):
+    quarter, width = tokens[0].shape[1:]
+    count, seg_len, head_cols = attended[0].shape
     blks = pack.shape[0]
     half = blks // 2 * ff_part
+    grad_shape = (blks, 2 * ff_part, width)
     pieces = piece_specs(quarter, width)
-    shapes = piece_shapes(seg_count, quarter, width)
+    shapes = piece_shapes(count, quarter, width)
+    chained = earlier is not None
+    if not chained:
+        earlier, earlier_spec = head, pl.BlockSpec(memory_space=pltpu.SMEM)
+    else:
+        earlier_spec = fixed(grad_shape)
 
     def weight(index):
         return pl.BlockSpec(
@@ -429,22 +474,19 @@
         )
 
     return pl.pallas_call(
-        ffn_kernel,
-        grid=(seg_count,),
+        functools.partial(ffn_kernel, chained),
+        grid=(count,),
         in_specs=[pl.BlockSpec(memory_space=pltpu.SMEM)]
         + [by_segment((seg_len, head_cols))] * 4
-        + [fixed((head_cols, width))] * 4
-        + [by_segment((quarter, width))] * 8
-        + [fixed((1, width)), weight(0), weight(1)],
+        + wo_specs
+        + [pl.BlockSpec((1, quarter, width), lambda s: (s + first, 0, 0))] * 8
+        + [fixed((1, width)), weight(0), weight(1), earlier_spec],
         out_specs=pieces + pieces
-        + [
-            by_segment((quarter, width)),
-            pl.BlockSpec((blks, 2 * ff_part, width), lambda s: (0, 0, 0)),
-        ],
+        + [by_segment((quarter, width)), pl.BlockSpec(grad_shape, lambda s: (0, 0, 0))],
         out_shape=shapes + shapes
         + [
-            jax.ShapeDtypeStruct((seg_count, quarter, width), jnp.float32),
-            jax.ShapeDtypeStruct((blks, 2 * ff_part, width), jnp.bfloat16),
+            jax.ShapeDtypeStruct((count, quarter, width), jnp.float32),
+            jax.ShapeDtypeStruct(grad_shape, jnp.bfloat16),
         ],
         scratch_shapes=[
             pltpu.VMEM((seg_len, width), jnp.float32),
@@ -453,9 +495,72 @@
             pltpu.VMEM((2, half, width), jnp.float32),
         ],
         compiler_params=pltpu.CompilerParams(vmem_limit_bytes=VMEM_LIMIT),
-        cost_estimate=pl.CostEstimate(flops=45 * 10**9, bytes_accessed=60 * 10**6, transcendentals=4 * 10**6),
+        cost_estimate=pl.CostEstimate(
+            flops=count * 75 * 10**8, bytes_accessed=2 * 10**7 + count * 5 * 10**6, transcendentals=10**6
+        ),
         name="feed_forward",
-    )(head, *attended, *wo, *tokens, *grads, gain, pack, pack)
+    )(head, *attended, *wo, *tokens, *grads, gain, pack, pack, earlier)
+
+
+def middle_kernel(
+    keep_ref, got_ref, far_ref, hidden_ref, grad_ref, gain_ref, o0, o1, o2, o3,
+    g_hidden_ref, g_branch_ref, g_gain_ref, m0, m1, m2, m3,
+):
+    count, quarter, width = hidden_ref.shape
+    flat = (count * quarter, width)
+    gn = (
+        keep_ref[0].astype(jnp.float32)
+        + got_ref[0].astype(jnp.float32)
+        + far_ref[...].astype(jnp.float32)
+    ).reshape(flat)
+    unit, spread = row_norm(hidden_ref[...].reshape(flat))
+    g_gain_ref[...] = jnp.sum(gn * unit, axis=0, keepdims=True)
+    g_hidden = grad_ref[...].astype(jnp.float32).reshape(flat) + norm_back(
+        gn, unit, spread, gain_ref[...]
+    )
+    g_hidden_ref[...] = g_hidden.reshape(g_hidden_ref.shape)
+    g_branch = g_hidden.astype(jnp.bfloat16)
+    g_branch_ref[...] = g_branch.reshape(g_branch_ref.shape)
+    for o, m in ((o0, m0), (o1, m1), (o2, m2), (o3, m3)):
+        m[...] = (
+            lax.dot_general(
+                g_branch, o[...].reshape(m.shape[2], width), COLS_IN, preferred_element_type=jnp.float32
+            )
+            .astype(jnp.bfloat16)
+            .reshape(m.shape)
+        )
+
+
+def middle(first, keep, got, far, hidden, grad, gain, wo, wo_specs, head_cols):
+    count, quarter, width = hidden.shape
+    whole = (count, quarter, width)
+    piece = pl.BlockSpec((1,) + whole, lambda s: (0, 0, 0, 0))
+    block = pl.BlockSpec(whole, lambda s: (0, 0, 0))
+    mixed = (count, quarter, head_cols)
+    return pl.pallas_call(
+        middle_kernel,
+        grid=(1,),
+        in_specs=[
+            piece,
+            piece,
+            block,
+            block,
+            pl.BlockSpec(whole, lambda s: (first // count, 0, 0)),
+            fixed((1, width)),
+        ]
+        + wo_specs,
+        out_specs=[block, block, pl.BlockSpec((1, width), lambda s: (0, 0))]
+        + [pl.BlockSpec(mixed, lambda s: (0, 0, 0))] * 4,
+        out_shape=[
+            jax.ShapeDtypeStruct(whole, jnp.float32),
+            jax.ShapeDtypeStruct(whole, jnp.bfloat16),
+            jax.ShapeDtypeStruct((1, width), jnp.float32),
+        ]
+        + [jax.ShapeDtypeStruct(mixed, jnp.bfloat16)] * 4,
+        compiler_params=pltpu.CompilerParams(vmem_limit_bytes=VMEM_LIMIT),
+        cost_estimate=pl.CostEstimate(flops=count * 27 * 10**7, bytes_accessed=8 * 10**6, transcendentals=0),
+        name="middle",
+    )(keep, got, far, hidden, grad, gain, *wo)
 
 
 def g_normed_kernel(head_ref, gq_ref, gkv_ref, gp_ref, w_ref, keep_ref, sent_ref, spread, rows):
@@ -553,11 +658,14 @@
     columns = lax.all_to_all(columns, "head", split_axis=0, concat_axis=0, tiled=True)
     columns, tokens_held = lax.optimization_barrier((columns, tokens))
     first_all = lax.all_gather(columns, "blk", axis=0)
-    second_all = lax.all_gather(jnp.concatenate([w_up.T, w_down, wo], 0), "blk", axis=0)
+    second_all = lax.all_gather(
+        jnp.concatenate([w_up.T, w_down, *to_all_heads(wo)], 0), "blk", axis=0
+    )
     token_pieces = to_all_heads(tokens_held)
     grad_held, tokens_far = lax.optimization_barrier((grad_out, token_pieces[2]))
     token_pieces = token_pieces[:2] + (tokens_far,) + token_pieces[3:]
     grad_pieces = to_all_heads(grad_held)
+    token_pieces, grad_pieces = lax.optimization_barrier((token_pieces, grad_pieces))
     gain_pair = first_all[:, :, 6 * part, : 2 * part].reshape(
         blk_count, head_groups, 2, part
     ).transpose(2, 1, 0, 3).reshape(2, 1, width).astype(jnp.float32)
@@ -569,27 +677,33 @@
         .reshape(6, width, head_cols)
     )
     wkv = jnp.concatenate([weights[0], weights[1]], 1)
-    wo_mine = second_all[:, 2 * ff_part :].reshape(head_cols, width)
-    wo_pieces = to_all_heads(wo_mine)
+    wo_held, wo_specs = wo_blocks(second_all, part, ff_part, head_groups)
 
     heads, normed, grouped, packed_mine = prepare(
         head, token_pieces, gain_first, weights, pad_rows
     )
     compressed = packed_mine[:, :comp_rows]
-    packed = jnp.zeros((comp_count, width), bf16)
-    for bits, piece in enumerate(to_all_heads(packed_mine.reshape(comp_count, head_cols))):
-        packed = lax.dynamic_update_slice(
-            packed, piece, (0, jnp.bitwise_xor(head_index, bits) * head_cols)
+    recv_packed, recv_mem = passed_along(
+        (packed_mine[seg_count - window :], heads[seg_count - 1 :, :, : 2 * head_cols]), "blk", 1
+    )
+
+    def all_columns(value):
+        value = value.reshape(-1, head_cols)
+        whole = jnp.zeros((value.shape[0], width), bf16)
+        for bits, piece in enumerate(to_all_heads(value)):
+            start = jnp.bitwise_xor(head_index, bits) * head_cols
+            whole = lax.dynamic_update_slice(whole, piece, (0, start))
+        return whole
+
+    def comp_pairs(rows):
+        return (
+            jnp.dot(rows, wkv, preferred_element_type=jnp.float32)
+            .astype(bf16)
+            .reshape(-1, pad_rows, 2 * head_cols)
         )
-    comp_pair = (
-        jnp.dot(packed, wkv, preferred_element_type=jnp.float32)
-        .astype(bf16)
-        .reshape(seg_count, pad_rows, 2 * head_cols)
-    )
-    recv_mem, recv_comp = passed_along(
-        (heads[seg_count - 1 :, :, : 2 * head_cols], comp_pair[seg_count - window :]), "blk", 1
-    )
-    comp_ext = jnp.concatenate([recv_comp, comp_pair], 0)
+
+    packed = all_columns(packed_mine)
+    comp_ext = jnp.concatenate([comp_pairs(all_columns(recv_packed)), comp_pairs(packed)], 0)
     order = jnp.arange(lengths.shape[0], dtype=jnp.int32)
     starts = jnp.sum(jnp.where(order[None, :] < order[:, None], lengths[None, :], 0), axis=1)
     seg_ids = blk_index * seg_count + jnp.arange(seg_count, dtype=jnp.int32)
@@ -598,58 +712,123 @@
     )
     head_ids = head_index * local_heads + jnp.arange(local_heads, dtype=jnp.int32)
     slopes = jnp.exp2(-head_ids.astype(jnp.float32)) / 64.0 * LOG2E
-    attn_out, lse = attend_fwd(seg_place, slopes, heads, recv_mem, comp_ext, head_cols)
-
-    attended = to_all_heads(attn_out)
-    f_keep, f_sent, n_keep, n_sent, hidden, first_grads = feed_forward(
-        head, attended, wo_pieces, token_pieces, grad_pieces, gain_second, second_all, ff_part
-    )
+    size = 2 if seg_count % 2 == 0 else seg_count
+    firsts = range(0, seg_count, size)
+    attention = [
+        attend_fwd(first, size, seg_place, slopes, heads, recv_mem, comp_ext, head_cols)
+        for first in firsts
+    ]
+    attended = [to_all_heads(attn_out) for attn_out, _ in attention]
+    groups = len(firsts)
+    first_grads = None
+    f_keep, f_sent, hidden, far, summed = [], [], [], [], []
+    grad_hidden, grad_branch, grad_gain_two, mixed_all = [], [], 0.0, []
+    grad_query, grad_pair, grad_comp_parts = [], [], []
+    held = jnp.zeros((seg_len, 2 * head_cols), jnp.float32)
+
+    def run_middle(n):
+        g_hidden, g_branch, g_gain, *mixed = middle(
+            firsts[n], *summed[n], hidden[n], grad_out, gain_second, wo_held, wo_specs, head_cols
+        )
+        grad_hidden.append(g_hidden)
+        grad_branch.append(g_branch)
+        mixed_all.append(mixed[:1] + [head_swap(mixed[bits], bits) for bits in (1, 2, 3)])
+        return mixed[0], g_gain[0]
+
+    attended[0], attention = lax.optimization_barrier((attended[0], attention))
+    for n in range(groups):
+        pieces = attended[n]
+        if n >= 1:
+            pieces, far[n - 1] = lax.optimization_barrier((pieces, far[n - 1]))
+            summed[n - 1] = summed[n - 1] + (head_swap(far[n - 1], 2),)
+        if n >= 2:
+            first_mixed, g_gain = run_middle(n - 2)
+            grad_gain_two = grad_gain_two + g_gain
+            pieces, first_mixed = lax.optimization_barrier((pieces, first_mixed))
+            mixed_all[n - 2][0] = first_mixed
+        keep, sent, n_keep, n_sent, hidden_part, first_grads = feed_forward(
+            firsts[n], head, pieces, wo_held, wo_specs, token_pieces, grad_pieces, gain_second,
+            second_all, ff_part, first_grads,
+        )
+        f_keep.append(keep)
+        f_sent.append(sent)
+        hidden.append(hidden_part)
+        got = head_swap(n_sent, 1)
+        far.append((n_keep[1].astype(jnp.float32) + got[1].astype(jnp.float32)).astype(bf16))
+        summed.append((n_keep, got))
     first_sum = lax.psum_scatter(first_grads, "blk", scatter_dimension=0)
-    grad_normed_two = sum_over_heads(n_keep, n_sent).reshape(token_count, width)
-    hidden = hidden.reshape(token_count, width)
-    unit, spread = row_norm(hidden)
-    grad_gain_two = jnp.sum(grad_normed_two * unit, axis=0)
-    grad_hidden = grad_out.reshape(token_count, width).astype(jnp.float32) + norm_back(
-        grad_normed_two, unit, spread, gain_second
-    )
-    grad_branch = grad_hidden.astype(bf16)
-    grad_mixed = [
-        head_swap(
-            lax.dot_general(grad_branch, block, COLS_IN, preferred_element_type=jnp.float32)
-            .astype(bf16)
-            .reshape(seg_count, quarter, head_cols),
-            bits,
+    summed[-1] = summed[-1] + (head_swap(far[-1], 2),)
+    if groups == 2:
+        first_mixed, g_gain = run_middle(0)
+        grad_gain_two = grad_gain_two + g_gain
+    early = -(-window // size)
+
+    def comp_chunk(n):
+        total = grad_comp_parts[n][:size] if n < groups else 0.0
+        if n:
+            over = jnp.pad(
+                grad_comp_parts[n - 1][size:], ((0, max(size - CSEGS + 1, 0)), (0, 0), (0, 0))
+            )
+            total = total + over[:size]
+        return total
+
+    def comp_back():
+        return jnp.concatenate([comp_chunk(n) for n in range(early)], 0)[:window].astype(bf16)
+
+    for n in range(groups):
+        if n + 1 < groups:
+            first_mixed, g_gain = run_middle(n + 1)
+        elif groups == 1:
+            first_mixed, g_gain = run_middle(n)
+        mixed = mixed_all[n]
+        if n + 1 < groups or groups == 1:
+            grad_gain_two = grad_gain_two + g_gain
+            if n + 1 < groups:
+                mixed, first_mixed, far[-1] = lax.optimization_barrier((mixed, first_mixed, far[-1]))
+                mixed_all[n + 1][0] = first_mixed
+        if n == early and n < groups:
+            back, mixed = lax.optimization_barrier((comp_back(), mixed))
+        attn_out, lse = attention[n]
+        g_query, g_pair, held, g_comp = attend_bwd(
+            firsts[n], head, seg_place, slopes, heads, recv_mem, comp_ext, mixed, attn_out, lse, held,
+            head_cols,
         )
-        if bits
-        else lax.dot_general(grad_branch, block, COLS_IN, preferred_element_type=jnp.float32)
-        .astype(bf16)
-        .reshape(seg_count, quarter, head_cols)
-        for bits, block in enumerate(wo_pieces)
-    ]
-    f_sent, grad_mixed = lax.optimization_barrier((f_sent, grad_mixed))
+        grad_query.append(g_query)
+        grad_pair.append(g_pair)
+        grad_comp_parts.append(g_comp)
+    f_sent, mixed = lax.optimization_barrier((jnp.concatenate(f_sent, 1), mixed))
     out_tokens = (
-        (hidden.reshape(tokens.shape) + sum_over_heads(f_keep, f_sent)).astype(bf16)
-    )
+        jnp.concatenate(hidden, 0) + sum_over_heads(jnp.concatenate(f_keep, 1), f_sent)
+    ).astype(bf16)
+    grad_hidden = jnp.concatenate(grad_hidden, 0).reshape(token_count, width)
+    grad_branch = jnp.concatenate(grad_branch, 0).reshape(token_count, width)
     grad_wo = [
         lax.dot_general(
-            lax.dynamic_slice_in_dim(block, head_index * quarter, quarter, 1).reshape(
-                token_count, head_cols
-            ),
+            jnp.concatenate(
+                [
+                    lax.dynamic_slice_in_dim(pieces[bits], head_index * quarter, quarter, 1)
+                    for pieces in attended
+                ],
+                0,
+            ).reshape(token_count, head_cols),
             grad_branch,
             ROWS_IN,
             preferred_element_type=jnp.float32,
         ).astype(bf16)
-        for block in attended
+        for bits in range(head_groups)
     ]
-    grad_query, grad_pair, tail, grad_comp_ext = attend_bwd(
-        head, seg_place, slopes, heads, recv_mem, comp_ext, grad_mixed, attn_out, lse, head_cols
-    )
+    if early >= groups:
+        back = comp_back()
+    grad_comp_parts = [comp_chunk(n) for n in range(groups + 1)]
+    kept = jnp.concatenate(grad_comp_parts, 0)[window:]
+    kept = jnp.pad(kept, ((0, seg_count - kept.shape[0]), (0, 0), (0, 0)))
     got_mem, got_comp = passed_along(
-        (grad_pair[seg_count], grad_comp_ext[:window].astype(bf16)), "blk", -1
-    )
-    last_pair = (tail + got_mem.astype(jnp.float32)).astype(bf16)
-    grad_pair = lax.dynamic_update_slice(grad_pair, last_pair[None], (seg_count - 1, 0, 0))
-    comp_pair_grad = grad_comp_ext[window:] + jnp.pad(
+        (grad_pair[0][0], back), "blk", -1
+    )
+    last_pair = (held + got_mem.astype(jnp.float32)).astype(bf16)
+    grad_pair = jnp.concatenate([grad_pair[0][1:], *grad_pair[1:], last_pair[None]], 0)
+    grad_query = jnp.concatenate(grad_query, 0)
+    comp_pair_grad = kept + jnp.pad(
         got_comp.astype(jnp.float32), ((seg_count - window, 0), (0, 0), (0, 0))
     )
     comp_grad_rows = comp_pair_grad.reshape(comp_count, 2 * head_cols).astype(bf16)
@@ -680,7 +859,7 @@
         .reshape(tokens.shape)
     )
     normed = normed.reshape(full_count, width)
-    grad_kv = grad_pair[:seg_count].reshape(full_count, 2 * head_cols)
+    grad_kv = grad_pair.reshape(full_count, 2 * head_cols)
     grad_wq = lax.dot_general(
         normed, grad_query.reshape(full_count, head_cols), ROWS_IN, preferred_element_type=jnp.float32
     )
@@ -698,7 +877,7 @@
         + jnp.sum(grad_comp * weights[3:].astype(jnp.float32), axis=(0, 2))
     ) / gain_first[0]
     grad_wkv = grad_wkv + comp_term
-    grad_wo = sum_over_heads((grad_wo[0], grad_wo[2]), jnp.stack([grad_wo[1], grad_wo[3]]))
+    grad_wo = sum_over_heads((grad_wo[0], grad_wo[2]), jnp.stack([grad_wo[1], grad_wo[3]])).astype(bf16)
 
     def by_owner(value):
         return value.astype(bf16).reshape(
@@ -720,9 +899,7 @@
             by_owner(grad_comp[1]),
             by_owner(grad_comp[2]),
             jnp.pad(gain_rows, ((0, 0), (0, 0), (0, 14), (0, head_cols - part))),
-            grad_wo.astype(bf16)
-            .reshape(blk_count, part, head_groups, head_cols)
-            .transpose(0, 2, 1, 3),
+            grad_wo.reshape(blk_count, part, head_groups, head_cols).transpose(0, 2, 1, 3),
         ],
         2,
     )

time: 646 us -> 655 us (1.014)
  waiting for transfers between devices: 292 us -> 230 us
  Pallas kernels: 149 us -> 196 us
  local copies, waits for them, and re-layouts: 55.1 us -> 81.3 us
  starting transfers between devices: 30.4 us -> 41.8 us
  matrix products: 36.1 us -> 28.4 us
  other arithmetic: 51 us -> 44.1 us
    pallas_call x3 -> x12, Pallas kernels: 118 us -> 165 us  [the longest x3 79.3 us: feed_forward(): pl.pallas_call(functools.partial(ffn_kernel, chained), grid=(count,), in_...]
    ppermute x4, waiting for transfers between devices: 64.3 us -> 27.1 us  [passed_along(): lax.ppermute(value, axis, [(source, source + steps) for source in range(l...]
    all_gather x1, waiting for transfers between devices: 25.5 us -> 0.01 us  [per_device(): first_all = lax.all_gather(columns, 'blk', axis=0)]
    unnamed x86 -> x193, local copies, waits for them, and re-layouts: 19 us -> 34.4 us
    dynamic_slice x0 -> x11, local copies, waits for them, and re-layouts: none -> 14.8 us  [per_device(): lax.dynamic_slice_in_dim(pieces[bits], head_index * quarter, quarter, 1)]
    reduce_scatter x1, waiting for transfers between devices: 12.6 us -> 0.02 us  [per_device(): lax.psum_scatter(second_grads.reshape(-1, head_cols), 'blk', scatter_dime...]
    dot_general x9 -> x6, matrix products: 16.8 us -> 5.45 us  [the longest x4 3.25 us: per_device(): lax.dot_general(jnp.concatenate([lax.dynamic_slice_in_dim(pieces[bits], h...]
    ppermute x28 -> x47, starting transfers between devices: 15.8 us -> 26.4 us  [head_swap(): lax.ppermute(value, 'head', [(source, source ^ bit) for source in range(c...]
  transfers between devices with their start and end apart: 37 -> 56, of which waited for: 20 -> 20; matrix products, arithmetic and copies ran while one was open for 19% -> 19% of each run, Pallas kernels for 14% -> 18%
where the time goes in v6:
time: 655 us; the launch traced here: 649 us
  waiting for transfers between devices  230 us (35%)
  Pallas kernels  196 us (30%)
  local copies, waits for them, and re-layouts  81.3 us (12%)
  other arithmetic  44.1 us (7%)
  starting transfers between devices  41.8 us (6%)
  matrix products  28.4 us (4%)
  between operations  15.8 us (2%)
  blocking collectives  11.1 us (2%)
    ppermute x47, waiting for transfers between devices, head_swap(): lax.ppermute(value, 'head', [(source, source ^ bit) for source in range(c...  200 us
    pallas_call x3, Pallas kernels, feed_forward(): pl.pallas_call(functools.partial(ffn_kernel, chained), grid=(count,), in_...  79.3 us
    pallas_call x3, Pallas kernels, attend_bwd(): pl.pallas_call(functools.partial(bwd_kernel, first), grid=(count,), in_sp...  43.7 us
    unnamed x193, local copies, waits for them, and re-layouts  34.4 us
    ppermute x4, waiting for transfers between devices, passed_along(): lax.ppermute(value, axis, [(source, source + steps) for source in range(l...  27.1 us
    pallas_call x3, Pallas kernels, attend_fwd(): pl.pallas_call(functools.partial(fwd_kernel, first), grid=(count,), in_sp...  27.1 us
    ppermute x47, starting transfers between devices, head_swap(): lax.ppermute(value, 'head', [(source, source ^ bit) for source in range(c...  26.4 us
    pallas_call x1, Pallas kernels, prepare(): pl.pallas_call(prep_kernel, grid=(seg_count,), in_specs=[pl.BlockSpec(mem...  16.9 us
  transfers between devices with their start and end apart: 56, of which 20 were waited for; matrix products, arithmetic and copies ran while one was open for 19% of the time, Pallas kernels for 18%

profile of v6, /device:TPU:24, one launch (start us, length us, event | category | flops | bytes accessed | tf_op | source)
XLA Modules:
  0.0 648.8 jit_solution(9610672449519896422)
XLA Ops:
  12.4 11.1 %all_to_all.10 = bf16[4,208,256]{2,1,0:T(8,128)(2,1)} all-to-all(bf16[4,208,256]{2,1,0:T(8,128)(2,1)S(1)} %copy.241), channel_id=1, replica_groups=mesh['head'=4,'blk'=8] {'head'}, dimensions={0} | all-to-all | bytes 851968 | tf_op jit(solution)/shard_map/all_to_all | solution.py:658
  33.0 35.2 %collective-permute-done.1.t2 = bf16[6,128,1024]{2,1,0:T(8,128)(2,1)} collective-permute-done((bf16[6,128,1024]{2,1,0:T(8,128)(2,1)S(1)}, bf16[6,128,1024]{2,1,0:T(8,128)(2,1)}, u32[]{:S(2)}, u32[]{:S(2)}) %collective-permute-start.1) | collective-permute-done | bytes 1572896 | tf_op jit(solution)/shard_map/ppermute | solution.py:613
  70.2 33.9 %collective-permute-done.4.g2 = bf16[6,128,1024]{2,1,0:T(8,128)(2,1)} collective-permute-done((bf16[6,128,1024]{2,1,0:T(8,128)(2,1)S(1)}, bf16[6,128,1024]{2,1,0:T(8,128)(2,1)}, u32[]{:S(2)}, u32[]{:S(2)}) %collective-permute-start.4) | collective-permute-done | bytes 1572896 | tf_op jit(solution)/shard_map/ppermute | solution.py:613
  113.9 16.9 %prepare.1 = (bf16[6,512,768]{2,1,0:T(8,128)(2,1)}, bf16[6,512,1024]{2,1,0:T(8,128)(2,1)}, bf16[6,176,3072]{2,1,0:T(8,128)(2,1)}, bf16[6,176,256]{2,1,0:T(8,128)(2,1)}) custom-call(s32[1]{0:T(128)} %bitcast.head_ref.earlier_ref, bf16[6,128,1024]{2,1,0:T(8,128)(2,1)} %t0.3, bf16[6,128,1024]{2,1,0:T(8,128)(2,1)} %collective-permute-done.t1, ...), custom_call_target="tpu_custom_call" | custom-call | flops 7000000000 | bytes 30000000 | tf_op jit(solution)/shard_map/prepare/pallas_call | solution.py:346
  142.0 22.6 %collective-permute-done.7 = bf16[4,176,256]{2,1,0:T(8,128)(2,1)S(1)} collective-permute-done((bf16[4,176,256]{2,1,0:T(8,128)(2,1)S(1)}, bf16[4,176,256]{2,1,0:T(8,128)(2,1)S(1)}, u32[]{:S(2)}, u32[]{:S(2)}) %collective-permute-start.7) | collective-permute-done | bytes 360480 | tf_op jit(solution)/shard_map/ppermute | solution.py:24
  165.9 9.6 %collective-permute-done.9 = bf16[704,256]{1,0:T(8,128)(2,1)S(1)} collective-permute-done((bf16[704,256]{1,0:T(8,128)(2,1)S(1)}, bf16[704,256]{1,0:T(8,128)(2,1)S(1)}, u32[]{:S(2)}, u32[]{:S(2)}) %collective-permute-start.9) | collective-permute-done | bytes 360480 | tf_op jit(solution)/shard_map/ppermute | solution.py:613
  186.3 9.1 %attend_fwd.3 = (bf16[2,512,256]{2,1,0:T(8,128)(2,1)}, f32[2,2,512]{2,1,0:T(2,128)}) custom-call(s32[6]{0:T(128)} %fusion.73.place_ref, f32[2]{0:T(128)} %exponential_multiply_fusion.slope_ref, bf16[6,512,768]{2,1,0:T(8,128)(2,1)} %get-tuple-element.138.q_ref.own_ref.prev_ref, bf16[6,512,768]{2,1,0:T(8,128)(2,1)} %get-tuple-element.138.q_ref.own_ref.prev_ref, ...), custom_call_target="tpu_custom_call" | custom-call | flops 2000000000 | bytes 6000000 | tf_op jit(solution)/shard_map/attend_fwd/pallas_call | solution.py:197
  196.9 12.1 %collective-permute-done.15.a2 = bf16[2,512,256]{2,1,0:T(8,128)(2,1)} collective-permute-done((bf16[2,512,256]{2,1,0:T(8,128)(2,1)}, bf16[2,512,256]{2,1,0:T(8,128)(2,1)}, u32[]{:S(2)}, u32[]{:S(2)}) %collective-permute-start.15) | collective-permute-done | bytes 524320 | tf_op jit(solution)/shard_map/ppermute | solution.py:613
  209.7 9.0 %attend_fwd.5 = (bf16[2,512,256]{2,1,0:T(8,128)(2,1)}, f32[2,2,512]{2,1,0:T(2,128)}) custom-call(s32[6]{0:T(128)} %fusion.73.place_ref, f32[2]{0:T(128)} %exponential_multiply_fusion.slope_ref, bf16[6,512,768]{2,1,0:T(8,128)(2,1)} %get-tuple-element.138.q_ref.own_ref.prev_ref, bf16[6,512,768]{2,1,0:T(8,128)(2,1)} %get-tuple-element.138.q_ref.own_ref.prev_ref, ...), custom_call_target="tpu_custom_call" | custom-call | flops 2000000000 | bytes 6000000 | tf_op jit(solution)/shard_map/attend_fwd/pallas_call | solution.py:197
  218.7 9.0 %attend_fwd.4 = (bf16[2,512,256]{2,1,0:T(8,128)(2,1)}, f32[2,2,512]{2,1,0:T(2,128)}) custom-call(s32[6]{0:T(128)} %fusion.73.place_ref, f32[2]{0:T(128)} %exponential_multiply_fusion.slope_ref, bf16[6,512,768]{2,1,0:T(8,128)(2,1)} %get-tuple-element.138.q_ref.own_ref.prev_ref, bf16[6,512,768]{2,1,0:T(8,128)(2,1)} %get-tuple-element.138.q_ref.own_ref.prev_ref, ...), custom_call_target="tpu_custom_call" | custom-call | flops 2000000000 | bytes 6000000 | tf_op jit(solution)/shard_map/attend_fwd/pallas_call | solution.py:197
  227.7 25.8 %feed_forward.3 = (bf16[2,2,128,1024]{3,2,1,0:T(8,128)(2,1)}, bf16[2,2,128,1024]{3,2,1,0:T(8,128)(2,1)}, bf16[2,2,128,1024]{3,2,1,0:T(8,128)(2,1)}, bf16[2,2,128...) custom-call(s32[1]{0:T(128)} %bitcast.head_ref.earlier_ref, ...), custom_call_target="tpu_custom_call" | custom-call | flops 15000000512 | bytes 30000000 | tf_op jit(solution)/shard_map/feed_forward/pallas_call | solution.py:476
  255.4 12.5 %collective-permute-done.21.a2 = bf16[2,512,256]{2,1,0:T(8,128)(2,1)S(1)} collective-permute-done((bf16[2,512,256]{2,1,0:T(8,128)(2,1)S(1)}, bf16[2,512,256]{2,1,0:T(8,128)(2,1)S(1)}, u32[]{:S(2)}, u32[]{:S(2)}) %collective-permute-start.21) | collective-permute-done | bytes 524320 | tf_op jit(solution)/shard_map/ppermute | solution.py:613
  271.4 26.7 %feed_forward.4 = (bf16[2,2,128,1024]{3,2,1,0:T(8,128)(2,1)}, bf16[2,2,128,1024]{3,2,1,0:T(8,128)(2,1)}, bf16[2,2,128,1024]{3,2,1,0:T(8,128)(2,1)}, bf16[2,2,128...) custom-call(s32[1]{0:T(128)} %bitcast.head_ref.earlier_ref, ...), custom_call_target="tpu_custom_call" | custom-call | flops 15000000512 | bytes 30000000 | tf_op jit(solution)/shard_map/feed_forward/pallas_call | solution.py:476
  316.1 8.3 %collective-permute-done.28.far_ref = bf16[2,128,1024]{2,1,0:T(8,128)(2,1)S(1)} collective-permute-done((bf16[2,128,1024]{2,1,0:T(8,128)(2,1)}, bf16[2,128,1024]{2,1,0:T(8,128)(2,1)S(1)}, u32[]{:S(2)}, u32[]{:S(2)}) %collective-permute-start.28) | collective-permute-done | bytes 524320 | tf_op jit(solution)/shard_map/ppermute | solution.py:613
  333.1 26.8 %feed_forward.5 = (bf16[2,2,128,1024]{3,2,1,0:T(8,128)(2,1)}, bf16[2,2,128,1024]{3,2,1,0:T(8,128)(2,1)}, bf16[2,2,128,1024]{3,2,1,0:T(8,128)(2,1)}, bf16[2,2,128...) custom-call(s32[1]{0:T(128)} %bitcast.head_ref.earlier_ref, ...), custom_call_target="tpu_custom_call" | custom-call | flops 15000000512 | bytes 30000000 | tf_op jit(solution)/shard_map/feed_forward/pallas_call | solution.py:476
  389.8 14.7 %attend_bwd.3 = (bf16[2,512,256]{2,1,0:T(8,128)(2,1)}, bf16[2,512,512]{2,1,0:T(8,128)(2,1)}, f32[512,512]{1,0:T(8,128)}, f32[4,176,512]{2,1,0:T(8,128)}) custom-call(s32[6]{0:T(128)} %fusion.73.place_ref, f32[2]{0:T(128)} %exponential_multiply_fusion.slope_ref, bf16[6,512,768]{2,1,0:T(8,128)(2,1)} %get-tuple-element.138.q_ref.own_ref.prev_ref, ...), custom_call_target="tpu_custom_call" | custom-call | flops 4000000000 | bytes 8000000 | tf_op jit(solution)/shard_map/attend_bwd/pallas_call | solution.py:221
  416.3 14.5 %attend_bwd.4 = (bf16[2,512,256]{2,1,0:T(8,128)(2,1)}, bf16[2,512,512]{2,1,0:T(8,128)(2,1)}, f32[512,512]{1,0:T(8,128)}, f32[4,176,512]{2,1,0:T(8,128)}) custom-call(s32[6]{0:T(128)} %fusion.73.place_ref, f32[2]{0:T(128)} %exponential_multiply_fusion.slope_ref, bf16[6,512,768]{2,1,0:T(8,128)(2,1)} %get-tuple-element.138.q_ref.own_ref.prev_ref, ...), custom_call_target="tpu_custom_call" | custom-call | flops 4000000000 | bytes 8000000 | tf_op jit(solution)/shard_map/attend_bwd/pallas_call | solution.py:221
  445.1 14.5 %attend_bwd.5 = (bf16[2,512,256]{2,1,0:T(8,128)(2,1)}, bf16[2,512,512]{2,1,0:T(8,128)(2,1)}, f32[512,512]{1,0:T(8,128)}, f32[4,176,512]{2,1,0:T(8,128)}) custom-call(s32[6]{0:T(128)} %fusion.73.place_ref, f32[2]{0:T(128)} %exponential_multiply_fusion.slope_ref, bf16[6,512,768]{2,1,0:T(8,128)(2,1)} %get-tuple-element.138.q_ref.own_ref.prev_ref, ...), custom_call_target="tpu_custom_call" | custom-call | flops 4000000000 | bytes 8000000 | tf_op jit(solution)/shard_map/attend_bwd/pallas_call | solution.py:221
  461.3 7.4 %fusion.23 = (f32[1024]{0:T(1024)}, f32[1024,512,1]{1,0,2:T(8,128)S(1)}) fusion(bf16[1024,256]{1,0:T(8,128)(2,1)S(1)} %bitcast.262, bf16[1024,256]{1,0:T(8,128)(2,1)S(1)} %bitcast.266, bf16[6,512,1024]{2,1,0:T(8,128)(2,1)} %get-tuple-element.237, bf16[1,512,512]{2,1,0:T(8,128)(2,1)S(1)} %fusion.48, bf16[2,512,512]{2,1,0:T(8,128)(2,1)} %get-tuple-element.231, ...), kind=kOutput, calls=%fused_computation.38 | convolution fusion | flops 3229088768 | bytes 12587008 | tf_op jit(solution)/shard_map/dot_general | solution.py:866
  490.0 9.2 %collective-permute-done.50 = bf16[256,1024]{1,0:T(8,128)(2,1)S(1)} collective-permute-done((bf16[256,1024]{1,0:T(8,128)(2,1)S(1)}, bf16[256,1024]{1,0:T(8,128)(2,1)S(1)}, u32[]{:S(2)}, u32[]{:S(2)}) %collective-permute-start.50) | collective-permute-done | bytes 524320 | tf_op jit(solution)/shard_map/ppermute | solution.py:613
  503.1 6.9 %collective-permute-done.46 = bf16[1056,256]{1,0:T(8,128)(2,1)} collective-permute-done((bf16[1056,256]{1,0:T(8,128)(2,1)}, bf16[1056,256]{1,0:T(8,128)(2,1)}, u32[]{:S(2)}, u32[]{:S(2)}) %collective-permute-start.46) | collective-permute-done | bytes 540704 | tf_op jit(solution)/shard_map/ppermute | solution.py:613
  530.2 14.2 %g_normed.1 = (bf16[2,6,128,1024]{3,2,1,0:T(8,128)(2,1)}, bf16[2,6,128,1024]{3,2,1,0:T(8,128)(2,1)}) custom-call(s32[1]{0:T(128)} %bitcast.head_ref.earlier_ref, bf16[6,512,256]{2,1,0:T(8,128)(2,1)} %copy-done.73, bf16[6,512,512]{2,1,0:T(8,128)(2,1)} %pad_maximum_fusion.1.gkv_ref, bf16[6,176,256]{2,1,0:T(8,128)(2,1)} %bitcast.259, ...), custom_call_target="tpu_custom_call" | custom-call | flops 7000000000 | bytes 20000000 | tf_op jit(solution)/shard_map/g_normed/pallas_call | solution.py:589
  557.7 30.7 %collective-permute-done.42 = bf16[6,128,1024]{2,1,0:T(8,128)(2,1)} collective-permute-done((bf16[6,128,1024]{2,1,0:T(8,128)(2,1)}, bf16[6,128,1024]{2,1,0:T(8,128)(2,1)}, u32[]{:S(2)}, u32[]{:S(2)}) %collective-permute-start.42) | collective-permute-done | bytes 1572896 | tf_op jit(solution)/shard_map/ppermute | solution.py:613
  596.4 24.0 %collective-permute-done.48 = bf16[6,128,1024]{2,1,0:T(8,128)(2,1)} collective-permute-done((bf16[6,128,1024]{2,1,0:T(8,128)(2,1)}, bf16[6,128,1024]{2,1,0:T(8,128)(2,1)}, u32[]{:S(2)}, u32[]{:S(2)}) %collective-permute-start.48) | collective-permute-done | bytes 1572896 | tf_op jit(solution)/shard_map/ppermute | solution.py:613
  (428 shorter events, 228.2 us)
Async XLA Ops:
  7.2 100.8 %all-gather.5.cloned.1.call-start = ((), (), s32[]{:S(2)}) async-start(), calls=%async_computation.6 | async-start | bytes 3833856 | tf_op jit(solution)/shard_map/all_gather | solution.py:660
  23.6 204.1 %all-gather.7.cloned.1.call-start = ((), (), s32[]{:S(2)}) async-start(), calls=%async_computation.7 | async-start | bytes 7077888 | tf_op jit(solution)/shard_map/all_gather | solution.py:661
  31.2 493.3 %reduce-scatter.3.cloned.1.call-start = ((), (), s32[]{:S(2)}) async-start(), calls=%async_computation.4 | async-start | bytes 4718592 | tf_op jit(solution)/shard_map/reduce_scatter | solution.py:759
  31.2 36.9 %collective-permute-start.1 = (bf16[6,128,1024]{2,1,0:T(8,128)(2,1)S(1)}, bf16[6,128,1024]{2,1,0:T(8,128)(2,1)}, u32[]{:S(2)}, u32[]{:S(2)}) collective-permute-start(bf16[6,128,1024]{2,1,0:T(8,128)(2,1)S(1)} %copy-done), channel_id=1, source_target_pairs={{0,16},{8,24},{16,0},{24,8},{1,17},{9,25},{17,1},{25,9},{2,18},{10... | collective-permute-start | bytes 4718600 | tf_op jit(solution)/shard_map/ppermute | solution.py:613
  68.2 36.0 %collective-permute-start.4 = (bf16[6,128,1024]{2,1,0:T(8,128)(2,1)S(1)}, bf16[6,128,1024]{2,1,0:T(8,128)(2,1)}, u32[]{:S(2)}, u32[]{:S(2)}) collective-permute-start(bf16[6,128,1024]{2,1,0:T(8,128)(2,1)S(1)} %copy-done.2), channel_id=1, source_target_pairs={{0,16},{8,24},{16,0},{24,8},{1,17},{9,25},{17,1},{25,9},{2,18},{10... | collective-permute-start | bytes 4718600 | tf_op jit(solution)/shard_map/ppermute | solution.py:613
  69.7 35.8 %collective-permute-start = (bf16[6,128,1024]{2,1,0:T(8,128)(2,1)S(1)}, bf16[6,128,1024]{2,1,0:T(8,128)(2,1)}, u32[]{:S(2)}, u32[]{:S(2)}) collective-permute-start(bf16[6,128,1024]{2,1,0:T(8,128)(2,1)S(1)} %copy-done), channel_id=1, source_target_pairs={{0,8},{8,0},{16,24},{24,16},{1,9},{9,1},{17,25},{25,17},{2,10},{10... | collective-permute-start | bytes 4718600 | tf_op jit(solution)/shard_map/ppermute | solution.py:613
  69.7 35.8 %collective-permute-start.3 = (bf16[6,128,1024]{2,1,0:T(8,128)(2,1)S(1)}, bf16[6,128,1024]{2,1,0:T(8,128)(2,1)}, u32[]{:S(2)}, u32[]{:S(2)}) collective-permute-start(bf16[6,128,1024]{2,1,0:T(8,128)(2,1)S(1)} %copy-done.2), channel_id=1, source_target_pairs={{0,8},{8,0},{16,24},{24,16},{1,9},{9,1},{17,25},{25,17},{2,10},{10... | collective-permute-start | bytes 4718600 | tf_op jit(solution)/shard_map/ppermute | solution.py:613
  70.2 35.3 %collective-permute-start.2 = (bf16[6,128,1024]{2,1,0:T(8,128)(2,1)}, bf16[6,128,1024]{2,1,0:T(8,128)(2,1)}, u32[]{:S(2)}, u32[]{:S(2)}) collective-permute-start(bf16[6,128,1024]{2,1,0:T(8,128)(2,1)} %collective-permute-done.1.t2), channel_id=1, source_target_pairs={{0,8},{8,0},{16,24},{24,16},{1,9},{9,1},{17,25},{25,17},{2,10},{10... | collective-permute-start | bytes 4718600 | tf_op jit(solution)/shard_map/ppermute | solution.py:613
  130.8 35.0 %collective-permute-start.11 = (bf16[1056,256]{1,0:T(8,128)(2,1)}, bf16[1056,256]{1,0:T(8,128)(2,1)S(1)}, u32[]{:S(2)}, u32[]{:S(2)}) collective-permute-start(bf16[1056,256]{1,0:T(8,128)(2,1)} %bitcast.251), channel_id=1, source_target_pairs={{0,8},{8,0},{16,24},{24,16},{1,9},{9,1},{17,25},{25,17},{2,10},{10... | collective-permute-start | bytes 1622024 | tf_op jit(solution)/shard_map/ppermute | solution.py:613
  131.1 34.4 %collective-permute-start.12 = (bf16[1056,256]{1,0:T(8,128)(2,1)}, bf16[1056,256]{1,0:T(8,128)(2,1)S(1)}, u32[]{:S(2)}, u32[]{:S(2)}) collective-permute-start(bf16[1056,256]{1,0:T(8,128)(2,1)} %bitcast.252), channel_id=1, source_target_pairs={{0,16},{8,24},{16,0},{24,8},{1,17},{9,25},{17,1},{25,9},{2,18},{10... | collective-permute-start | bytes 1622024 | tf_op jit(solution)/shard_map/ppermute | solution.py:613
  133.6 31.0 %collective-permute-start.7 = (bf16[4,176,256]{2,1,0:T(8,128)(2,1)S(1)}, bf16[4,176,256]{2,1,0:T(8,128)(2,1)S(1)}, u32[]{:S(2)}, u32[]{:S(2)}) collective-permute-start(bf16[4,176,256]{2,1,0:T(8,128)(2,1)S(1)} %slice.188), channel_id=1, source_target_pairs={{0,1},{1,2},{2,3},{3,4},{4,5},{5,6},{6,7},{8,9},{9,10},{10,11},{11... | collective-permute-start | bytes 1081352 | tf_op jit(solution)/shard_map/ppermute | solution.py:24
  139.3 46.2 %collective-permute-start.6 = (bf16[1,512,512]{2,1,0:T(8,128)(2,1)S(1)}, bf16[1,512,512]{2,1,0:T(8,128)(2,1)S(1)}, u32[]{:S(2)}, u32[]{:S(2)}) collective-permute-start(bf16[1,512,512]{2,1,0:T(8,128)(2,1)S(1)} %slice.187), channel_id=1, source_target_pairs={{0,1},{1,2},{2,3},{3,4},{4,5},{5,6},{6,7},{8,9},{9,10},{10,11},{11... | collective-permute-start | bytes 1572872 | tf_op jit(solution)/shard_map/ppermute | solution.py:24
  196.9 30.7 %collective-permute-start.14 = (bf16[2,512,256]{2,1,0:T(8,128)(2,1)}, bf16[2,512,256]{2,1,0:T(8,128)(2,1)}, u32[]{:S(2)}, u32[]{:S(2)}) collective-permute-start(bf16[2,512,256]{2,1,0:T(8,128)(2,1)} %get-tuple-element.195.a0.att_ref), channel_id=1, source_target_pairs={{0,8},{8,0},{16,24},{24,16},{1,9},{9,1},{17,25},{25,17},{2,10},{10... | collective-permute-start | bytes 1572872 | tf_op jit(solution)/shard_map/ppermute | solution.py:613
  298.1 32.1 %collective-permute-start.27 = (bf16[2,2,128,1024]{3,2,1,0:T(8,128)(2,1)}, bf16[2,2,128,1024]{3,2,1,0:T(8,128)(2,1)}, u32[]{:S(2)}, u32[]{:S(2)}) collective-permute-start(bf16[2,2,128,1024]{3,2,1,0:T(8,128)(2,1)} %get-tuple-element.164), channel_id=1, source_target_pairs={{0,8},{8,0},{16,24},{24,16},{1,9},{9,1},{17,25},{25,17},{2,10},{10... | collective-permute-start | bytes 3145736 | tf_op jit(solution)/shard_map/ppermute | solution.py:613
  359.9 25.2 %collective-permute-start.33 = (bf16[2,2,128,1024]{3,2,1,0:T(8,128)(2,1)}, bf16[2,2,128,1024]{3,2,1,0:T(8,128)(2,1)S(1)}, u32[]{:S(2)}, u32[]{:S(2)}) collective-permute-start(bf16[2,2,128,1024]{3,2,1,0:T(8,128)(2,1)} %get-tuple-element.190), channel_id=1, source_target_pairs={{0,8},{8,0},{16,24},{24,16},{1,9},{9,1},{17,25},{25,17},{2,10},{10... | collective-permute-start | bytes 3145736 | tf_op jit(solution)/shard_map/ppermute | solution.py:613
  372.6 252.4 %reduce-scatter.5.cloned.1.call-start = ((), (), s32[]{:S(2)}) async-start(), calls=%async_computation.5 | async-start | bytes 4423680 | tf_op jit(solution)/shard_map/reduce_scatter | solution.py:909
  383.9 31.6 %collective-permute-start.34 = (bf16[2,128,256]{2,1,0:T(8,128)(2,1)}, bf16[2,128,256]{2,1,0:T(8,128)(2,1)S(1)}, u32[]{:S(2)}, u32[]{:S(2)}) collective-permute-start(bf16[2,128,256]{2,1,0:T(8,128)(2,1)} %get-tuple-element.199), channel_id=1, source_target_pairs={{0,8},{8,0},{16,24},{24,16},{1,9},{9,1},{17,25},{25,17},{2,10},{10... | collective-permute-start | bytes 393224 | tf_op jit(solution)/shard_map/ppermute | solution.py:613
  385.1 30.5 %collective-permute-start.35 = (bf16[2,128,256]{2,1,0:T(8,128)(2,1)}, bf16[2,128,256]{2,1,0:T(8,128)(2,1)S(1)}, u32[]{:S(2)}, u32[]{:S(2)}) collective-permute-start(bf16[2,128,256]{2,1,0:T(8,128)(2,1)} %get-tuple-element.200), channel_id=1, source_target_pairs={{0,16},{8,24},{16,0},{24,8},{1,17},{9,25},{17,1},{25,9},{2,18},{10... | collective-permute-start | bytes 393224 | tf_op jit(solution)/shard_map/ppermute | solution.py:613
  386.8 28.8 %collective-permute-start.36 = (bf16[2,128,256]{2,1,0:T(8,128)(2,1)S(1)}, bf16[2,128,256]{2,1,0:T(8,128)(2,1)S(1)}, u32[]{:S(2)}, u32[]{:S(2)}) collective-permute-start(bf16[2,128,256]{2,1,0:T(8,128)(2,1)S(1)} %copy-done.83), channel_id=1, source_target_pairs={{0,24},{8,16},{16,8},{24,0},{1,25},{9,17},{17,9},{25,1},{2,26},{10... | collective-permute-start | bytes 393224 | tf_op jit(solution)/shard_map/ppermute | solution.py:613
  407.8 51.9 %collective-permute-start.43 = (bf16[512,512]{1,0:T(8,128)(2,1)}, bf16[512,512]{1,0:T(8,128)(2,1)}, u32[]{:S(2)}, u32[]{:S(2)}) collective-permute-start(bf16[512,512]{1,0:T(8,128)(2,1)} %get-tuple-element.378), channel_id=1, source_target_pairs={{1,0},{2,1},{3,2},{4,3},{5,4},{6,5},{7,6},{9,8},{10,9},{11,10},{12... | collective-permute-start | bytes 1572872 | tf_op jit(solution)/shard_map/ppermute | solution.py:24
  436.6 45.7 %collective-permute-start.49 = (bf16[2,256,1024]{2,1,0:T(8,128)(2,1)}, bf16[2,256,1024]{2,1,0:T(8,128)(2,1)}, u32[]{:S(2)}, u32[]{:S(2)}) collective-permute-start(bf16[2,256,1024]{2,1,0:T(8,128)(2,1)} %pad_maximum_fusion.5), channel_id=1, source_target_pairs={{0,8},{8,0},{16,24},{24,16},{1,9},{9,1},{17,25},{25,17},{2,10},{10... | collective-permute-start | bytes 3145736 | tf_op jit(solution)/shard_map/ppermute | solution.py:613
  440.9 35.0 %collective-permute-start.44 = (bf16[4,176,512]{2,1,0:T(8,128)(2,1)S(1)}, bf16[4,176,512]{2,1,0:T(8,128)(2,1)S(1)}, u32[]{:S(2)}, u32[]{:S(2)}) collective-permute-start(bf16[4,176,512]{2,1,0:T(8,128)(2,1)S(1)} %pad_maximum_fusion.6), channel_id=1, source_target_pairs={{1,0},{2,1},{3,2},{4,3},{5,4},{6,5},{7,6},{9,8},{10,9},{11,10},{12... | collective-permute-start | bytes 2162696 | tf_op jit(solution)/shard_map/ppermute | solution.py:24
  550.8 37.6 %collective-permute-start.42 = (bf16[6,128,1024]{2,1,0:T(8,128)(2,1)}, bf16[6,128,1024]{2,1,0:T(8,128)(2,1)}, u32[]{:S(2)}, u32[]{:S(2)}) collective-permute-start(bf16[6,128,1024]{2,1,0:T(8,128)(2,1)} %fusion.24), channel_id=1, source_target_pairs={{0,16},{8,24},{16,0},{24,8},{1,17},{9,25},{17,1},{25,9},{2,18},{10... | collective-permute-start | bytes 4718600 | tf_op jit(solution)/shard_map/ppermute | solution.py:613
  555.0 65.4 %collective-permute-start.48 = (bf16[6,128,1024]{2,1,0:T(8,128)(2,1)}, bf16[6,128,1024]{2,1,0:T(8,128)(2,1)}, u32[]{:S(2)}, u32[]{:S(2)}) collective-permute-start(bf16[6,128,1024]{2,1,0:T(8,128)(2,1)} %fusion.25), channel_id=1, source_target_pairs={{0,16},{8,24},{16,0},{24,8},{1,17},{9,25},{17,1},{25,9},{2,18},{10... | collective-permute-start | bytes 4718600 | tf_op jit(solution)/shard_map/ppermute | solution.py:613
  (117 other events, 1216.4 us)
Sparse Core Ops, SparseCore 0:
  23.7 62.0 all-gather.4
  88.5 116.0 all-gather.6
  372.7 106.2 reduce-scatter.2
  524.7 82.1 reduce-scatter.4

commit v7 on v6

--- a/solution.py
+++ b/solution.py
@@ -35,7 +35,7 @@
     return jnp.where((row < valid_rows) & open_, place * slope, NEG)
 
 
-def fwd_kernel(first, place_ref, slope_ref, q_ref, own_ref, prev_ref, recv_ref, comp_ref, out_ref, lse_ref):
+def fwd_kernel(first, shift, place_ref, slope_ref, q_ref, own_ref, prev_ref, recv_ref, comp_ref, out_ref, lse_ref):
     step = pl.program_id(0) + first
     place = place_ref[step]
     seg_len = q_ref.shape[1]
@@ -55,16 +55,20 @@
         for piece in range(CSEGS):
             lag = CSEGS + 1 - piece
             bias = key_bias(pad_rows, RATE // 2 - lag * seg_len, RATE, seg_len // RATE, place >= lag, slope)
-            parts.append((comp_ref[step + piece, :, kc], comp_ref[step + piece, :, vc], bias))
+            at = step + piece - shift
+            parts.append((comp_ref[at, :, kc], comp_ref[at, :, vc], bias))
         bias = key_bias(seg_len, -seg_len, 1, seg_len, place >= 1, slope)
-        is_first = step == 0
-        parts.append(
-            (
-                jnp.where(is_first, recv_ref[0, :, kc], prev_ref[0, :, kc]),
-                jnp.where(is_first, recv_ref[0, :, vc], prev_ref[0, :, vc]),
-                bias,
+        if first:
+            parts.append((prev_ref[0, :, kc], prev_ref[0, :, vc], bias))
+        else:
+            is_first = step == 0
+            parts.append(
+                (
+                    jnp.where(is_first, recv_ref[0, :, kc], prev_ref[0, :, kc]),
+                    jnp.where(is_first, recv_ref[0, :, vc], prev_ref[0, :, vc]),
+                    bias,
+                )
             )
-        )
         own_bias = [
             key_bias(half, n * half, 1, half, place >= 0, slope) for n in range(2)
         ]
@@ -191,11 +195,11 @@
     ]
 
 
-def attend_fwd(first, count, place, slope, heads, recv_mem, comp_ext, head_cols):
+def attend_fwd(first, shift, count, place, slope, heads, recv_mem, comp_ext, head_cols):
     seg_len = heads.shape[1]
     local_heads = head_cols // HD
     return pl.pallas_call(
-        functools.partial(fwd_kernel, first),
+        functools.partial(fwd_kernel, first, shift),
         grid=(count,),
         in_specs=attention_specs(first, seg_len, head_cols, comp_ext.shape),
         out_specs=[by_segment((seg_len, head_cols)), by_segment((local_heads, seg_len))],
@@ -212,9 +216,9 @@
 
 
 def attend_bwd(
-    first, head, place, slope, heads, recv_mem, comp_ext, grad_mixed, attn_out, lse, held, head_cols
+    first, count, head, place, slope, heads, recv_mem, comp_ext, grad_mixed, attn_out, lse, held, head_cols
 ):
-    count, seg_len, _ = attn_out.shape
+    seg_len = attn_out.shape[1]
     local_heads = head_cols // HD
     pair = 2 * head_cols
     window = (count + CSEGS - 1,) + comp_ext.shape[1:]
@@ -223,10 +227,10 @@
         grid=(count,),
         in_specs=attention_specs(first, seg_len, head_cols, comp_ext.shape)
         + [pl.BlockSpec(memory_space=pltpu.SMEM)]
-        + [by_segment(grad_mixed[0].shape[1:])] * 4
+        + [by_segment(grad_mixed[0].shape[1:], first)] * 4
         + [
-            by_segment((seg_len, head_cols)),
-            by_segment((local_heads, seg_len)),
+            by_segment((seg_len, head_cols), first),
+            by_segment((local_heads, seg_len), first),
             fixed((seg_len, pair)),
         ],
         out_specs=[
@@ -324,8 +328,8 @@
     return pl.BlockSpec(shape, lambda s: (0,) * len(shape), pipeline_mode=pl.Buffered(1))
 
 
-def by_segment(shape):
-    return pl.BlockSpec((1,) + shape, lambda s: (s,) + (0,) * len(shape))
+def by_segment(shape, first=0):
+    return pl.BlockSpec((1,) + shape, lambda s: (s + first,) + (0,) * len(shape))
 
 
 def piece_specs(quarter, width):
@@ -369,8 +373,8 @@
 
 
 def ffn_kernel(
-    chained, head_ref, a0, a1, a2, a3, o0, o1, o2, o3, t0, t1, t2, t3, g0, g1, g2, g3, gain_ref,
-    up_ref, down_ref, earlier_ref, f_keep, f_sent, n_keep, n_sent, hidden_ref, pack_ref,
+    head_ref, a0, a1, a2, a3, o0, o1, o2, o3, t0, t1, t2, t3, g0, g1, g2, g3, gain_ref,
+    up_ref, down_ref, f_keep, f_sent, n_keep, n_sent, hidden_ref, pack_ref,
     rows, grads, acc_up, acc_down,
 ):
     step = pl.program_id(0)
@@ -382,14 +386,8 @@
 
     @pl.when(step == 0)
     def _():
-        if chained:
-            for n in range(2):
-                own = slice(n * parts, (n + 1) * parts)
-                acc_up[n] = earlier_ref[own, :ff_part].reshape(block, width).astype(jnp.float32)
-                acc_down[n] = earlier_ref[own, ff_part:].reshape(block, width).astype(jnp.float32)
-        else:
-            acc_up[...] = jnp.zeros_like(acc_up)
-            acc_down[...] = jnp.zeros_like(acc_down)
+        acc_up[...] = jnp.zeros_like(acc_up)
+        acc_down[...] = jnp.zeros_like(acc_down)
 
     place_rows(head, (t0, t1, t2, t3), rows)
     place_rows(head, (g0, g1, g2, g3), grads)
@@ -454,7 +452,7 @@
     return blocks, [fixed((blks * part, width))] * head_groups
 
 
-def feed_forward(first, head, attended, wo, wo_specs, tokens, grads, gain, pack, ff_part, earlier):
+def feed_forward(head, attended, wo, wo_specs, tokens, grads, gain, pack, ff_part):
     quarter, width = tokens[0].shape[1:]
     count, seg_len, head_cols = attended[0].shape
     blks = pack.shape[0]
@@ -462,11 +460,6 @@
     grad_shape = (blks, 2 * ff_part, width)
     pieces = piece_specs(quarter, width)
     shapes = piece_shapes(count, quarter, width)
-    chained = earlier is not None
-    if not chained:
-        earlier, earlier_spec = head, pl.BlockSpec(memory_space=pltpu.SMEM)
-    else:
-        earlier_spec = fixed(grad_shape)
 
     def weight(index):
         return pl.BlockSpec(
@@ -474,13 +467,13 @@
         )
 
     return pl.pallas_call(
-        functools.partial(ffn_kernel, chained),
+        ffn_kernel,
         grid=(count,),
         in_specs=[pl.BlockSpec(memory_space=pltpu.SMEM)]
         + [by_segment((seg_len, head_cols))] * 4
         + wo_specs
-        + [pl.BlockSpec((1, quarter, width), lambda s: (s + first, 0, 0))] * 8
-        + [fixed((1, width)), weight(0), weight(1), earlier_spec],
+        + [by_segment((quarter, width))] * 8
+        + [fixed((1, width)), weight(0), weight(1)],
         out_specs=pieces + pieces
         + [by_segment((quarter, width)), pl.BlockSpec(grad_shape, lambda s: (0, 0, 0))],
         out_shape=shapes + shapes
@@ -499,7 +492,7 @@
             flops=count * 75 * 10**8, bytes_accessed=2 * 10**7 + count * 5 * 10**6, transcendentals=10**6
         ),
         name="feed_forward",
-    )(head, *attended, *wo, *tokens, *grads, gain, pack, pack, earlier)
+    )(head, *attended, *wo, *tokens, *grads, gain, pack, pack)
 
 
 def middle_kernel(
@@ -514,7 +507,13 @@
         + far_ref[...].astype(jnp.float32)
     ).reshape(flat)
     unit, spread = row_norm(hidden_ref[...].reshape(flat))
-    g_gain_ref[...] = jnp.sum(gn * unit, axis=0, keepdims=True)
+    gain_part = jnp.sum(gn * unit, axis=0, keepdims=True)
+
+    @pl.when(pl.program_id(0) == 0)
+    def _():
+        g_gain_ref[...] = jnp.zeros_like(g_gain_ref)
+
+    g_gain_ref[...] += gain_part
     g_hidden = grad_ref[...].astype(jnp.float32).reshape(flat) + norm_back(
         gn, unit, spread, gain_ref[...]
     )
@@ -531,34 +530,26 @@
         )
 
 
-def middle(first, keep, got, far, hidden, grad, gain, wo, wo_specs, head_cols):
+def middle(keep, got, far, hidden, grad, gain, wo, wo_specs, head_cols):
     count, quarter, width = hidden.shape
-    whole = (count, quarter, width)
-    piece = pl.BlockSpec((1,) + whole, lambda s: (0, 0, 0, 0))
-    block = pl.BlockSpec(whole, lambda s: (0, 0, 0))
-    mixed = (count, quarter, head_cols)
+    size = 2 if count % 2 == 0 else 1
+    piece = pl.BlockSpec((1, size, quarter, width), lambda s: (0, s, 0, 0))
+    block = pl.BlockSpec((size, quarter, width), lambda s: (s, 0, 0))
+    mixed = jax.ShapeDtypeStruct((count, quarter, head_cols), jnp.bfloat16)
     return pl.pallas_call(
         middle_kernel,
-        grid=(1,),
-        in_specs=[
-            piece,
-            piece,
-            block,
-            block,
-            pl.BlockSpec(whole, lambda s: (first // count, 0, 0)),
-            fixed((1, width)),
-        ]
-        + wo_specs,
+        grid=(count // size,),
+        in_specs=[piece, piece, block, block, block, fixed((1, width))] + wo_specs,
         out_specs=[block, block, pl.BlockSpec((1, width), lambda s: (0, 0))]
-        + [pl.BlockSpec(mixed, lambda s: (0, 0, 0))] * 4,
+        + [pl.BlockSpec((size, quarter, head_cols), lambda s: (s, 0, 0))] * 4,
         out_shape=[
-            jax.ShapeDtypeStruct(whole, jnp.float32),
-            jax.ShapeDtypeStruct(whole, jnp.bfloat16),
+            jax.ShapeDtypeStruct(hidden.shape, jnp.float32),
+            jax.ShapeDtypeStruct(hidden.shape, jnp.bfloat16),
             jax.ShapeDtypeStruct((1, width), jnp.float32),
         ]
-        + [jax.ShapeDtypeStruct(mixed, jnp.bfloat16)] * 4,
+        + [mixed] * 4,
         compiler_params=pltpu.CompilerParams(vmem_limit_bytes=VMEM_LIMIT),
-        cost_estimate=pl.CostEstimate(flops=count * 27 * 10**7, bytes_accessed=8 * 10**6, transcendentals=0),
+        cost_estimate=pl.CostEstimate(flops=count * 27 * 10**7, bytes_accessed=24 * 10**6, transcendentals=0),
         name="middle",
     )(keep, got, far, hidden, grad, gain, *wo)
 
@@ -664,8 +655,7 @@
     token_pieces = to_all_heads(tokens_held)
     grad_held, tokens_far = lax.optimization_barrier((grad_out, token_pieces[2]))
     token_pieces = token_pieces[:2] + (tokens_far,) + token_pieces[3:]
-    grad_pieces = to_all_heads(grad_held)
-    token_pieces, grad_pieces = lax.optimization_barrier((token_pieces, grad_pieces))
+    grad_far = head_swap(grad_held, 2)
     gain_pair = first_all[:, :, 6 * part, : 2 * part].reshape(
         blk_count, head_groups, 2, part
     ).transpose(2, 1, 0, 3).reshape(2, 1, width).astype(jnp.float32)
@@ -702,8 +692,12 @@
             .reshape(-1, pad_rows, 2 * head_cols)
         )
 
+    grad_far, grad_held, packed_mine = lax.optimization_barrier((grad_far, grad_held, packed_mine))
+    grad_pieces = (grad_held, head_swap(grad_held, 1), grad_far, head_swap(grad_far, 1))
     packed = all_columns(packed_mine)
-    comp_ext = jnp.concatenate([comp_pairs(all_columns(recv_packed)), comp_pairs(packed)], 0)
+    comp_pair = comp_pairs(packed)
+    comp_pair, grad_pieces = lax.optimization_barrier((comp_pair, grad_pieces))
+    comp_ext = jnp.concatenate([comp_pairs(all_columns(recv_packed)), comp_pair], 0)
     order = jnp.arange(lengths.shape[0], dtype=jnp.int32)
     starts = jnp.sum(jnp.where(order[None, :] < order[:, None], lengths[None, :], 0), axis=1)
     seg_ids = blk_index * seg_count + jnp.arange(seg_count, dtype=jnp.int32)
@@ -712,129 +706,79 @@
     )
     head_ids = head_index * local_heads + jnp.arange(local_heads, dtype=jnp.int32)
     slopes = jnp.exp2(-head_ids.astype(jnp.float32)) / 64.0 * LOG2E
-    size = 2 if seg_count % 2 == 0 else seg_count
-    firsts = range(0, seg_count, size)
+    late = attend_fwd(
+        window, window, seg_count - window, seg_place, slopes, heads, heads[:1, :, : 2 * head_cols],
+        comp_pair, head_cols,
+    )
+    comp_ext, late = lax.optimization_barrier((comp_ext, late))
+    cuts = [0, window // 2, window]
     attention = [
-        attend_fwd(first, size, seg_place, slopes, heads, recv_mem, comp_ext, head_cols)
-        for first in firsts
-    ]
-    attended = [to_all_heads(attn_out) for attn_out, _ in attention]
-    groups = len(firsts)
-    first_grads = None
-    f_keep, f_sent, hidden, far, summed = [], [], [], [], []
-    grad_hidden, grad_branch, grad_gain_two, mixed_all = [], [], 0.0, []
-    grad_query, grad_pair, grad_comp_parts = [], [], []
-    held = jnp.zeros((seg_len, 2 * head_cols), jnp.float32)
-
-    def run_middle(n):
-        g_hidden, g_branch, g_gain, *mixed = middle(
-            firsts[n], *summed[n], hidden[n], grad_out, gain_second, wo_held, wo_specs, head_cols
-        )
-        grad_hidden.append(g_hidden)
-        grad_branch.append(g_branch)
-        mixed_all.append(mixed[:1] + [head_swap(mixed[bits], bits) for bits in (1, 2, 3)])
-        return mixed[0], g_gain[0]
-
-    attended[0], attention = lax.optimization_barrier((attended[0], attention))
-    for n in range(groups):
-        pieces = attended[n]
-        if n >= 1:
-            pieces, far[n - 1] = lax.optimization_barrier((pieces, far[n - 1]))
-            summed[n - 1] = summed[n - 1] + (head_swap(far[n - 1], 2),)
-        if n >= 2:
-            first_mixed, g_gain = run_middle(n - 2)
-            grad_gain_two = grad_gain_two + g_gain
-            pieces, first_mixed = lax.optimization_barrier((pieces, first_mixed))
-            mixed_all[n - 2][0] = first_mixed
-        keep, sent, n_keep, n_sent, hidden_part, first_grads = feed_forward(
-            firsts[n], head, pieces, wo_held, wo_specs, token_pieces, grad_pieces, gain_second,
-            second_all, ff_part, first_grads,
-        )
-        f_keep.append(keep)
-        f_sent.append(sent)
-        hidden.append(hidden_part)
-        got = head_swap(n_sent, 1)
-        far.append((n_keep[1].astype(jnp.float32) + got[1].astype(jnp.float32)).astype(bf16))
-        summed.append((n_keep, got))
+        attend_fwd(a, 0, b - a, seg_place, slopes, heads, recv_mem, comp_ext, head_cols)
+        for a, b in zip(cuts, cuts[1:])
+    ] + [late]
+    attn_out = jnp.concatenate([out for out, _ in attention], 0)
+    lse = jnp.concatenate([total for _, total in attention], 0)
+    far = jnp.concatenate([head_swap(out, 2) for out, _ in attention], 0)
+    attended = (attn_out, head_swap(attn_out, 1), far, head_swap(far, 1))
+    f_keep, f_sent, n_keep, n_sent, hidden, first_grads = feed_forward(
+        head, attended, wo_held, wo_specs, token_pieces, grad_pieces, gain_second, second_all, ff_part
+    )
     first_sum = lax.psum_scatter(first_grads, "blk", scatter_dimension=0)
-    summed[-1] = summed[-1] + (head_swap(far[-1], 2),)
-    if groups == 2:
-        first_mixed, g_gain = run_middle(0)
-        grad_gain_two = grad_gain_two + g_gain
-    early = -(-window // size)
-
-    def comp_chunk(n):
-        total = grad_comp_parts[n][:size] if n < groups else 0.0
-        if n:
-            over = jnp.pad(
-                grad_comp_parts[n - 1][size:], ((0, max(size - CSEGS + 1, 0)), (0, 0), (0, 0))
-            )
-            total = total + over[:size]
-        return total
-
-    def comp_back():
-        return jnp.concatenate([comp_chunk(n) for n in range(early)], 0)[:window].astype(bf16)
-
-    for n in range(groups):
-        if n + 1 < groups:
-            first_mixed, g_gain = run_middle(n + 1)
-        elif groups == 1:
-            first_mixed, g_gain = run_middle(n)
-        mixed = mixed_all[n]
-        if n + 1 < groups or groups == 1:
-            grad_gain_two = grad_gain_two + g_gain
-            if n + 1 < groups:
-                mixed, first_mixed, far[-1] = lax.optimization_barrier((mixed, first_mixed, far[-1]))
-                mixed_all[n + 1][0] = first_mixed
-        if n == early and n < groups:
-            back, mixed = lax.optimization_barrier((comp_back(), mixed))
-        attn_out, lse = attention[n]
-        g_query, g_pair, held, g_comp = attend_bwd(
-            firsts[n], head, seg_place, slopes, heads, recv_mem, comp_ext, mixed, attn_out, lse, held,
+    got = head_swap(n_sent, 1)
+    far = (n_keep[1].astype(jnp.float32) + got[1].astype(jnp.float32)).astype(bf16)
+    grad_hidden, grad_branch, grad_gain_two, *mixed = middle(
+        n_keep, got, head_swap(far, 2), hidden, grad_out, gain_second, wo_held, wo_specs, head_cols
+    )
+    grad_gain_two = grad_gain_two[0]
+    mixed = mixed[:1] + [head_swap(mixed[bits], bits) for bits in (1, 2, 3)]
+    f_sent, mixed = lax.optimization_barrier((f_sent, mixed))
+
+    def backward(a, b, held, mixed):
+        return attend_bwd(
+            a, b - a, head, seg_place, slopes, heads, recv_mem, comp_ext, mixed, attn_out, lse, held,
             head_cols,
         )
-        grad_query.append(g_query)
-        grad_pair.append(g_pair)
-        grad_comp_parts.append(g_comp)
-    f_sent, mixed = lax.optimization_barrier((jnp.concatenate(f_sent, 1), mixed))
-    out_tokens = (
-        jnp.concatenate(hidden, 0) + sum_over_heads(jnp.concatenate(f_keep, 1), f_sent)
+
+    held = jnp.zeros((seg_len, 2 * head_cols), jnp.float32)
+    query_one, pair_one, held, comp_one = backward(0, window, held, mixed)
+    mem_back, comp_back = pair_one[0], comp_one[:window].astype(bf16)
+    mem_back, comp_back, mixed, held = lax.optimization_barrier((mem_back, comp_back, mixed, held))
+    got_mem, got_comp = passed_along((mem_back, comp_back), "blk", -1)
+    query_two, pair_two, held, comp_two = backward(window, seg_count, held, mixed)
+    f_sum = sum_over_heads(f_keep, f_sent)
+    query_two, f_sum, first_sum = lax.optimization_barrier((query_two, f_sum, first_sum))
+    out_tokens = (hidden + f_sum).astype(bf16)
+    grad_hidden = grad_hidden.reshape(token_count, width)
+    grad_branch = grad_branch.reshape(token_count, width)
+    over = comp_one.shape[0] - window
+    kept = jnp.concatenate([comp_one[window:] + comp_two[:over], comp_two[over:]], 0)
+    kept = jnp.pad(kept, ((0, seg_count - kept.shape[0]), (0, 0), (0, 0)))
+    grad_pairs = [pair_one[1:], pair_two]
+    last_pair = (held + got_mem.astype(jnp.float32)).astype(bf16)
+    grad_pair = jnp.concatenate([*grad_pairs, last_pair[None]], 0)
+    grad_query = jnp.concatenate([query_one, query_two], 0)
+    comp_pair_grad = kept + jnp.pad(
+        got_comp.astype(jnp.float32), ((seg_count - window, 0), (0, 0), (0, 0))
+    )
+    comp_grad_rows = comp_pair_grad.reshape(comp_count, 2 * head_cols).astype(bf16)
+    grad_packed_part = lax.dot_general(
+        comp_grad_rows, wkv, COLS_IN, preferred_element_type=jnp.float32
     ).astype(bf16)
-    grad_hidden = jnp.concatenate(grad_hidden, 0).reshape(token_count, width)
-    grad_branch = jnp.concatenate(grad_branch, 0).reshape(token_count, width)
+
+    grad_packed_part, grad_query, grad_pair, grad_branch = lax.optimization_barrier(
+        (grad_packed_part, grad_query, grad_pair, grad_branch)
+    )
     grad_wo = [
         lax.dot_general(
-            jnp.concatenate(
-                [
-                    lax.dynamic_slice_in_dim(pieces[bits], head_index * quarter, quarter, 1)
-                    for pieces in attended
-                ],
-                0,
-            ).reshape(token_count, head_cols),
+            lax.dynamic_slice_in_dim(block, head_index * quarter, quarter, 1).reshape(
+                token_count, head_cols
+            ),
             grad_branch,
             ROWS_IN,
             preferred_element_type=jnp.float32,
         ).astype(bf16)
-        for bits in range(head_groups)
+        for block in attended
     ]
-    if early >= groups:
-        back = comp_back()
-    grad_comp_parts = [comp_chunk(n) for n in range(groups + 1)]
-    kept = jnp.concatenate(grad_comp_parts, 0)[window:]
-    kept = jnp.pad(kept, ((0, seg_count - kept.shape[0]), (0, 0), (0, 0)))
-    got_mem, got_comp = passed_along(
-        (grad_pair[0][0], back), "blk", -1
-    )
-    last_pair = (held + got_mem.astype(jnp.float32)).astype(bf16)
-    grad_pair = jnp.concatenate([grad_pair[0][1:], *grad_pair[1:], last_pair[None]], 0)
-    grad_query = jnp.concatenate(grad_query, 0)
-    comp_pair_grad = kept + jnp.pad(
-        got_comp.astype(jnp.float32), ((seg_count - window, 0), (0, 0), (0, 0))
-    )
-    comp_grad_rows = comp_pair_grad.reshape(comp_count, 2 * head_cols).astype(bf16)
-    grad_packed_part = lax.dot_general(
-        comp_grad_rows, wkv, COLS_IN, preferred_element_type=jnp.float32
-    ).astype(bf16)
 
     def columns_of(bits):
         start = jnp.bitwise_xor(head_index, bits) * head_cols

time: 655 us -> 638 us (0.974)
  waiting for transfers between devices: 230 us -> 270 us
  Pallas kernels: 196 us -> 167 us
  local copies, waits for them, and re-layouts: 81.3 us -> 62.9 us
  starting transfers between devices: 41.8 us -> 33.8 us
    pallas_call x9 -> x5, Pallas kernels: 122 us -> 97.5 us  [the longest x1 61.4 us: feed_forward(): pl.pallas_call(ffn_kernel, grid=(count,), in_specs=[pl.BlockSpec(memory_s...]
    reduce_scatter x1, waiting for transfers between devices: 0.02 us -> 19.1 us  [per_device(): lax.psum_scatter(second_grads.reshape(-1, head_cols), 'blk', scatter_dime...]
    all_gather x1, waiting for transfers between devices: 0.01 us -> 16.9 us  [per_device(): first_all = lax.all_gather(columns, 'blk', axis=0)]
    unnamed x193 -> x121, local copies, waits for them, and re-layouts: 34.4 us -> 22.8 us
    ppermute x4, waiting for transfers between devices: 27.1 us -> 37.4 us  [passed_along(): lax.ppermute(value, axis, [(source, source + steps) for source in range(l...]
    dynamic_slice x11 -> x3, local copies, waits for them, and re-layouts: 14.8 us -> 4.88 us  [per_device(): lax.dynamic_slice_in_dim(block, head_index * quarter, quarter, 1)]
    ppermute x47 -> x33, starting transfers between devices: 26.4 us -> 18.5 us  [head_swap(): lax.ppermute(value, 'head', [(source, source ^ bit) for source in range(c...]
    ppermute x47 -> x33, waiting for transfers between devices: 200 us -> 194 us  [head_swap(): lax.ppermute(value, 'head', [(source, source ^ bit) for source in range(c...]
  transfers between devices with their start and end apart: 56 -> 42, of which waited for: 20 -> 22; matrix products, arithmetic and copies ran while one was open for 19% -> 15% of each run, Pallas kernels for 18% -> 17%
where the time goes in v7:
time: 638 us; the launch traced here: 629 us
  waiting for transfers between devices  270 us (42%)
  Pallas kernels  167 us (26%)
  local copies, waits for them, and re-layouts  62.9 us (10%)
  other arithmetic  45.4 us (7%)
  starting transfers between devices  33.8 us (5%)
  matrix products  23.2 us (4%)
  between operations  15.5 us (2%)
  blocking collectives  10.9 us (2%)
    ppermute x33, waiting for transfers between devices, head_swap(): lax.ppermute(value, 'head', [(source, source ^ bit) for source in range(c...  194 us
    pallas_call x1, Pallas kernels, feed_forward(): pl.pallas_call(ffn_kernel, grid=(count,), in_specs=[pl.BlockSpec(memory_s...  61.4 us
    pallas_call x2, Pallas kernels, attend_bwd(): pl.pallas_call(functools.partial(bwd_kernel, first), grid=(count,), in_sp...  38.9 us
    ppermute x4, waiting for transfers between devices, passed_along(): lax.ppermute(value, axis, [(source, source + steps) for source in range(l...  37.4 us
    pallas_call x3, Pallas kernels, attend_fwd(): pl.pallas_call(functools.partial(fwd_kernel, first, shift), grid=(count,)...  26.8 us
    unnamed x121, local copies, waits for them, and re-layouts  22.8 us
    reduce_scatter x1, waiting for transfers between devices, per_device(): lax.psum_scatter(second_grads.reshape(-1, head_cols), 'blk', scatter_dime...  19.1 us
    ppermute x33, starting transfers between devices, head_swap(): lax.ppermute(value, 'head', [(source, source ^ bit) for source in range(c...  18.5 us
  transfers between devices with their start and end apart: 42, of which 22 were waited for; matrix products, arithmetic and copies ran while one was open for 15% of the time, Pallas kernels for 17%

profile of v7, /device:TPU:24, one launch (start us, length us, event | category | flops | bytes accessed | tf_op | source)
XLA Modules:
  0.0 628.8 jit_solution(16418159979643578766)
XLA Ops:
  12.4 10.9 %all_to_all.10 = bf16[4,208,256]{2,1,0:T(8,128)(2,1)} all-to-all(bf16[4,208,256]{2,1,0:T(8,128)(2,1)S(1)} %copy.209), channel_id=1, replica_groups=mesh['head'=4,'blk'=8] {'head'}, dimensions={0} | all-to-all | bytes 851968 | tf_op jit(solution)/shard_map/all_to_all | solution.py:649
  30.4 36.4 %collective-permute-done.1.t2 = bf16[6,128,1024]{2,1,0:T(8,128)(2,1)} collective-permute-done((bf16[6,128,1024]{2,1,0:T(8,128)(2,1)}, bf16[6,128,1024]{2,1,0:T(8,128)(2,1)}, u32[]{:S(2)}, u32[]{:S(2)}) %collective-permute-start.1) | collective-permute-done | bytes 1572896 | tf_op jit(solution)/shard_map/ppermute | solution.py:604
  68.6 16.9 %all-gather.5.cloned.1.call-done = bf16[32,208,256]{2,1,0:T(8,128)(2,1)} async-done(((bf16[4,208,256]{2,1,0:T(8,128)(2,1)}), bf16[32,208,256]{2,1,0:T(8,128)(2,1)}) %all-gather.5.cloned.1.call-update) | async-done | bytes 3407888 | tf_op jit(solution)/shard_map/all_gather | solution.py:651
  91.5 16.8 %prepare.1 = (bf16[6,512,768]{2,1,0:T(8,128)(2,1)}, bf16[6,512,1024]{2,1,0:T(8,128)(2,1)}, bf16[6,176,3072]{2,1,0:T(8,128)(2,1)}, bf16[6,176,256]{2,1,0:T(8,128)(2,1)}) custom-call(s32[1]{0:T(128)} %bitcast.head_ref, bf16[6,128,1024]{2,1,0:T(8,128)(2,1)} %t0.1, bf16[6,128,1024]{2,1,0:T(8,128)(2,1)} %collective-permute-done.t1, ...), custom_call_target="tpu_custom_call" | custom-call | flops 7000000000 | bytes 30000000 | tf_op jit(solution)/shard_map/prepare/pallas_call | solution.py:350
  117.9 14.1 %collective-permute-done.4 = bf16[4,176,256]{2,1,0:T(8,128)(2,1)S(1)} collective-permute-done((bf16[4,176,256]{2,1,0:T(8,128)(2,1)S(1)}, bf16[4,176,256]{2,1,0:T(8,128)(2,1)S(1)}, u32[]{:S(2)}, u32[]{:S(2)}) %collective-permute-start.4) | collective-permute-done | bytes 360480 | tf_op jit(solution)/shard_map/ppermute | solution.py:24
  134.4 7.8 %collective-permute-done.6 = bf16[704,256]{1,0:T(8,128)(2,1)S(1)} collective-permute-done((bf16[704,256]{1,0:T(8,128)(2,1)S(1)}, bf16[704,256]{1,0:T(8,128)(2,1)S(1)}, u32[]{:S(2)}, u32[]{:S(2)}) %collective-permute-start.6) | collective-permute-done | bytes 360480 | tf_op jit(solution)/shard_map/ppermute | solution.py:604
  148.5 8.7 %attend_fwd.3 = (bf16[2,512,256]{2,1,0:T(8,128)(2,1)}, f32[2,2,512]{2,1,0:T(2,128)}) custom-call(s32[6]{0:T(128)} %fusion.41.place_ref, f32[2]{0:T(128)} %exponential_multiply_fusion.slope_ref, bf16[6,512,768]{2,1,0:T(8,128)(2,1)} %get-tuple-element.84.q_ref.own_ref.prev_ref, bf16[6,512,768]{2,1,0:T(8,128)(2,1)} %get-tuple-element.84.q_ref.own_ref.prev_ref, ...), custom_call_target="tpu_custom_call" | custom-call | flops 2000000000 | bytes 6000000 | tf_op jit(solution)/shard_map/attend_fwd/pallas_call | solution.py:201
  157.2 23.2 %collective-permute-done.3.recv_ref = bf16[1,512,512]{2,1,0:T(8,128)(2,1)S(1)} collective-permute-done((bf16[1,512,512]{2,1,0:T(8,128)(2,1)}, bf16[1,512,512]{2,1,0:T(8,128)(2,1)S(1)}, u32[]{:S(2)}, u32[]{:S(2)}) %collective-permute-start.3) | collective-permute-done | bytes 524320 | tf_op jit(solution)/shard_map/ppermute | solution.py:24
  181.2 9.2 %attend_fwd.4 = (bf16[2,512,256]{2,1,0:T(8,128)(2,1)}, f32[2,2,512]{2,1,0:T(2,128)}) custom-call(s32[6]{0:T(128)} %fusion.41.place_ref, f32[2]{0:T(128)} %exponential_multiply_fusion.slope_ref, bf16[6,512,768]{2,1,0:T(8,128)(2,1)} %get-tuple-element.84.q_ref.own_ref.prev_ref, bf16[6,512,768]{2,1,0:T(8,128)(2,1)} %get-tuple-element.84.q_ref.own_ref.prev_ref, ...), custom_call_target="tpu_custom_call" | custom-call | flops 2000000000 | bytes 6000000 | tf_op jit(solution)/shard_map/attend_fwd/pallas_call | solution.py:201
  192.0 8.9 %attend_fwd.5 = (bf16[2,512,256]{2,1,0:T(8,128)(2,1)}, f32[2,2,512]{2,1,0:T(2,128)}) custom-call(s32[6]{0:T(128)} %fusion.41.place_ref, f32[2]{0:T(128)} %exponential_multiply_fusion.slope_ref, bf16[6,512,768]{2,1,0:T(8,128)(2,1)} %get-tuple-element.84.q_ref.own_ref.prev_ref, bf16[6,512,768]{2,1,0:T(8,128)(2,1)} %get-tuple-element.84.q_ref.own_ref.prev_ref, ...), custom_call_target="tpu_custom_call" | custom-call | flops 2000000000 | bytes 6000000 | tf_op jit(solution)/shard_map/attend_fwd/pallas_call | solution.py:201
  207.3 9.4 %collective-permute-done.16 = bf16[2,512,256]{2,1,0:T(8,128)(2,1)S(1)} collective-permute-done((bf16[2,512,256]{2,1,0:T(8,128)(2,1)}, bf16[2,512,256]{2,1,0:T(8,128)(2,1)S(1)}, u32[]{:S(2)}, u32[]{:S(2)}) %collective-permute-start.16) | collective-permute-done | bytes 524320 | tf_op jit(solution)/shard_map/ppermute | solution.py:604
  217.5 9.3 %collective-permute-done.17 = bf16[2,512,256]{2,1,0:T(8,128)(2,1)S(1)} collective-permute-done((bf16[2,512,256]{2,1,0:T(8,128)(2,1)S(1)}, bf16[2,512,256]{2,1,0:T(8,128)(2,1)S(1)}, u32[]{:S(2)}, u32[]{:S(2)}) %collective-permute-start.17) | collective-permute-done | bytes 524320 | tf_op jit(solution)/shard_map/ppermute | solution.py:604
  231.4 61.4 %feed_forward.1 = (bf16[2,6,128,1024]{3,2,1,0:T(8,128)(2,1)}, bf16[2,6,128,1024]{3,2,1,0:T(8,128)(2,1)}, bf16[2,6,128,1024]{3,2,1,0:T(8,128)(2,1)}, bf16[2,6,128...) custom-call(s32[1]{0:T(128)} %bitcast.head_ref, ...), custom_call_target="tpu_custom_call" | custom-call | flops 44999999488 | bytes 50000000 | tf_op jit(solution)/shard_map/feed_forward/pallas_call | solution.py:469
  303.0 35.0 %collective-permute-done.23.far_ref = bf16[6,128,1024]{2,1,0:T(8,128)(2,1)S(1)} collective-permute-done((bf16[6,128,1024]{2,1,0:T(8,128)(2,1)S(1)}, bf16[6,128,1024]{2,1,0:T(8,128)(2,1)S(1)}, u32[]{:S(2)}, u32[]{:S(2)}) %collective-permute-start.23) | collective-permute-done | bytes 1572896 | tf_op jit(solution)/shard_map/ppermute | solution.py:604
  339.2 9.3 %middle.1 = (f32[6,128,1024]{2,1,0:T(8,128)}, bf16[6,128,1024]{2,1,0:T(8,128)(2,1)}, f32[1,1024]{1,0:T(1,128)}, bf16[6,128,256]{2,1,0:T(8,128)(2,1)}, bf16[6,128...) custom-call(bf16[2,6,128,1024]{3,2,1,0:T(8,128)(2,1)} %get-tuple-element.103.keep_ref, ...), custom_call_target="tpu_custom_call" | custom-call | flops 1620000000 | bytes 24000000 | tf_op jit(solution)/shard_map/middle/pallas_call | solution.py:539
  350.6 10.2 %collective-permute-done.25.g2 = bf16[6,128,256]{2,1,0:T(8,128)(2,1)} collective-permute-done((bf16[6,128,256]{2,1,0:T(8,128)(2,1)}, bf16[6,128,256]{2,1,0:T(8,128)(2,1)}, u32[]{:S(2)}, u32[]{:S(2)}) %collective-permute-start.25) | collective-permute-done | bytes 393248 | tf_op jit(solution)/shard_map/ppermute | solution.py:604
  379.9 24.5 %attend_bwd.2 = (bf16[4,512,256]{2,1,0:T(8,128)(2,1)}, bf16[4,512,512]{2,1,0:T(8,128)(2,1)}, f32[512,512]{1,0:T(8,128)}, f32[6,176,512]{2,1,0:T(8,128)}) custom-call(s32[6]{0:T(128)} %fusion.41.place_ref, f32[2]{0:T(128)} %exponential_multiply_fusion.slope_ref, bf16[6,512,768]{2,1,0:T(8,128)(2,1)} %get-tuple-element.84.q_ref.own_ref.prev_ref, ...), custom_call_target="tpu_custom_call" | custom-call | flops 8000000000 | bytes 16000000 | tf_op jit(solution)/shard_map/attend_bwd/pallas_call | solution.py:225
  422.4 14.4 %attend_bwd.3 = (bf16[2,512,256]{2,1,0:T(8,128)(2,1)}, bf16[2,512,512]{2,1,0:T(8,128)(2,1)}, f32[512,512]{1,0:T(8,128)}, f32[4,176,512]{2,1,0:T(8,128)}) custom-call(s32[6]{0:T(128)} %fusion.41.place_ref, f32[2]{0:T(128)} %exponential_multiply_fusion.slope_ref, bf16[6,512,768]{2,1,0:T(8,128)(2,1)} %get-tuple-element.84.q_ref.own_ref.prev_ref, ...), custom_call_target="tpu_custom_call" | custom-call | flops 4000000000 | bytes 8000000 | tf_op jit(solution)/shard_map/attend_bwd/pallas_call | solution.py:225
  446.1 10.9 %collective-permute-done.28 = bf16[6,128,1024]{2,1,0:T(8,128)(2,1)} collective-permute-done((bf16[6,128,1024]{2,1,0:T(8,128)(2,1)}, bf16[6,128,1024]{2,1,0:T(8,128)(2,1)}, u32[]{:S(2)}, u32[]{:S(2)}) %collective-permute-start.28) | collective-permute-done | bytes 1572896 | tf_op jit(solution)/shard_map/ppermute | solution.py:604
  485.1 10.8 %collective-permute-done.36 = bf16[256,1024]{1,0:T(8,128)(2,1)S(1)} collective-permute-done((bf16[256,1024]{1,0:T(8,128)(2,1)S(1)}, bf16[256,1024]{1,0:T(8,128)(2,1)S(1)}, u32[]{:S(2)}, u32[]{:S(2)}) %collective-permute-start.36) | collective-permute-done | bytes 524320 | tf_op jit(solution)/shard_map/ppermute | solution.py:604
  496.5 9.2 %collective-permute-done.32 = bf16[1056,256]{1,0:T(8,128)(2,1)} collective-permute-done((bf16[1056,256]{1,0:T(8,128)(2,1)}, bf16[1056,256]{1,0:T(8,128)(2,1)}, u32[]{:S(2)}, u32[]{:S(2)}) %collective-permute-start.32) | collective-permute-done | bytes 540704 | tf_op jit(solution)/shard_map/ppermute | solution.py:604
  518.6 14.1 %g_normed.1 = (bf16[2,6,128,1024]{3,2,1,0:T(8,128)(2,1)}, bf16[2,6,128,1024]{3,2,1,0:T(8,128)(2,1)}) custom-call(s32[1]{0:T(128)} %bitcast.head_ref, bf16[6,512,256]{2,1,0:T(8,128)(2,1)} %copy-done.15, bf16[6,512,512]{2,1,0:T(8,128)(2,1)} %pad_maximum_fusion.gkv_ref, bf16[6,176,256]{2,1,0:T(8,128)(2,1)} %bitcast.220, bf16[6,1024,256]{2,1,0:T(8,128)(2,1)} %bitcast.197), custom_call_target="tpu_custom_call" | custom-call | flops 7000000000 | bytes 20000000 | tf_op jit(solution)/shard_map/g_normed/pallas_call | solution.py:580
  551.6 27.6 %collective-permute-done.34 = bf16[6,128,1024]{2,1,0:T(8,128)(2,1)} collective-permute-done((bf16[6,128,1024]{2,1,0:T(8,128)(2,1)S(1)}, bf16[6,128,1024]{2,1,0:T(8,128)(2,1)}, u32[]{:S(2)}, u32[]{:S(2)}) %collective-permute-start.34) | collective-permute-done | bytes 1572896 | tf_op jit(solution)/shard_map/ppermute | solution.py:604
  583.1 19.1 %reduce-scatter.5.cloned.1.call-done = bf16[960,256]{1,0:T(8,128)(2,1)} async-done(((bf16[7680,256]{1,0:T(8,128)(2,1)}), bf16[960,256]{1,0:T(8,128)(2,1)}) %reduce-scatter.5.cloned.1.call-update) | async-done | bytes 491536 | tf_op jit(solution)/shard_map/reduce_scatter | solution.py:853
  (315 shorter events, 195.2 us)
Async XLA Ops:
  7.2 78.4 %all-gather.5.cloned.1.call-start = ((), (), s32[]{:S(2)}) async-start(), calls=%async_computation.6 | async-start | bytes 3833856 | tf_op jit(solution)/shard_map/all_gather | solution.py:651
  23.3 208.1 %all-gather.7.cloned.1.call-start = ((), (), s32[]{:S(2)}) async-start(), calls=%async_computation.7 | async-start | bytes 7077888 | tf_op jit(solution)/shard_map/all_gather | solution.py:652
  29.9 431.2 %reduce-scatter.3.cloned.1.call-start = ((), (), s32[]{:S(2)}) async-start(), calls=%async_computation.4 | async-start | bytes 4718592 | tf_op jit(solution)/shard_map/reduce_scatter | solution.py:726
  30.0 36.8 %collective-permute-start.1 = (bf16[6,128,1024]{2,1,0:T(8,128)(2,1)}, bf16[6,128,1024]{2,1,0:T(8,128)(2,1)}, u32[]{:S(2)}, u32[]{:S(2)}) collective-permute-start(bf16[6,128,1024]{2,1,0:T(8,128)(2,1)} %t0.1), channel_id=1, source_target_pairs={{0,16},{8,24},{16,0},{24,8},{1,17},{9,25},{17,1},{25,9},{2,18},{10... | collective-permute-start | bytes 4718600 | tf_op jit(solution)/shard_map/ppermute | solution.py:604
  30.4 61.1 %collective-permute-start = (bf16[6,128,1024]{2,1,0:T(8,128)(2,1)}, bf16[6,128,1024]{2,1,0:T(8,128)(2,1)}, u32[]{:S(2)}, u32[]{:S(2)}) collective-permute-start(bf16[6,128,1024]{2,1,0:T(8,128)(2,1)} %t0.1), channel_id=1, source_target_pairs={{0,8},{8,0},{16,24},{24,16},{1,9},{9,1},{17,25},{25,17},{2,10},{10... | collective-permute-start | bytes 4718600 | tf_op jit(solution)/shard_map/ppermute | solution.py:604
  66.8 24.7 %collective-permute-start.2 = (bf16[6,128,1024]{2,1,0:T(8,128)(2,1)}, bf16[6,128,1024]{2,1,0:T(8,128)(2,1)}, u32[]{:S(2)}, u32[]{:S(2)}) collective-permute-start(bf16[6,128,1024]{2,1,0:T(8,128)(2,1)} %collective-permute-done.1.t2), channel_id=1, source_target_pairs={{0,8},{8,0},{16,24},{24,16},{1,9},{9,1},{17,25},{25,17},{2,10},{10... | collective-permute-start | bytes 4718600 | tf_op jit(solution)/shard_map/ppermute | solution.py:604
  66.8 41.5 %collective-permute-start.8 = (bf16[6,128,1024]{2,1,0:T(8,128)(2,1)}, bf16[6,128,1024]{2,1,0:T(8,128)(2,1)}, u32[]{:S(2)}, u32[]{:S(2)}) collective-permute-start(bf16[6,128,1024]{2,1,0:T(8,128)(2,1)} %grad_ref.1), channel_id=1, source_target_pairs={{0,16},{8,24},{16,0},{24,8},{1,17},{9,25},{17,1},{25,9},{2,18},{10... | collective-permute-start | bytes 4718600 | tf_op jit(solution)/shard_map/ppermute | solution.py:604
  108.3 25.4 %collective-permute-start.9 = (bf16[1056,256]{1,0:T(8,128)(2,1)}, bf16[1056,256]{1,0:T(8,128)(2,1)S(1)}, u32[]{:S(2)}, u32[]{:S(2)}) collective-permute-start(bf16[1056,256]{1,0:T(8,128)(2,1)} %bitcast.213), channel_id=1, source_target_pairs={{0,8},{8,0},{16,24},{24,16},{1,9},{9,1},{17,25},{25,17},{2,10},{10... | collective-permute-start | bytes 1622024 | tf_op jit(solution)/shard_map/ppermute | solution.py:604
  108.4 25.4 %collective-permute-start.10 = (bf16[1056,256]{1,0:T(8,128)(2,1)}, bf16[1056,256]{1,0:T(8,128)(2,1)S(1)}, u32[]{:S(2)}, u32[]{:S(2)}) collective-permute-start(bf16[1056,256]{1,0:T(8,128)(2,1)} %bitcast.214), channel_id=1, source_target_pairs={{0,16},{8,24},{16,0},{24,8},{1,17},{9,25},{17,1},{25,9},{2,18},{10... | collective-permute-start | bytes 1622024 | tf_op jit(solution)/shard_map/ppermute | solution.py:604
  112.3 34.7 %collective-permute-start.12 = (bf16[6,128,1024]{2,1,0:T(8,128)(2,1)}, bf16[6,128,1024]{2,1,0:T(8,128)(2,1)}, u32[]{:S(2)}, u32[]{:S(2)}) collective-permute-start(bf16[6,128,1024]{2,1,0:T(8,128)(2,1)} %grad_ref.1), channel_id=1, source_target_pairs={{0,8},{8,0},{16,24},{24,16},{1,9},{9,1},{17,25},{25,17},{2,10},{10... | collective-permute-start | bytes 4718600 | tf_op jit(solution)/shard_map/ppermute | solution.py:604
  112.5 34.5 %collective-permute-start.13 = (bf16[6,128,1024]{2,1,0:T(8,128)(2,1)}, bf16[6,128,1024]{2,1,0:T(8,128)(2,1)}, u32[]{:S(2)}, u32[]{:S(2)}) collective-permute-start(bf16[6,128,1024]{2,1,0:T(8,128)(2,1)} %collective-permute-done.8.g2), channel_id=1, source_target_pairs={{0,8},{8,0},{16,24},{24,16},{1,9},{9,1},{17,25},{25,17},{2,10},{10... | collective-permute-start | bytes 4718600 | tf_op jit(solution)/shard_map/ppermute | solution.py:604
  112.9 19.2 %collective-permute-start.4 = (bf16[4,176,256]{2,1,0:T(8,128)(2,1)S(1)}, bf16[4,176,256]{2,1,0:T(8,128)(2,1)S(1)}, u32[]{:S(2)}, u32[]{:S(2)}) collective-permute-start(bf16[4,176,256]{2,1,0:T(8,128)(2,1)S(1)} %slice.172), channel_id=1, source_target_pairs={{0,1},{1,2},{2,3},{3,4},{4,5},{5,6},{6,7},{8,9},{9,10},{10,11},{11... | collective-permute-start | bytes 1081352 | tf_op jit(solution)/shard_map/ppermute | solution.py:24
  142.4 38.1 %collective-permute-start.3 = (bf16[1,512,512]{2,1,0:T(8,128)(2,1)}, bf16[1,512,512]{2,1,0:T(8,128)(2,1)S(1)}, u32[]{:S(2)}, u32[]{:S(2)}) collective-permute-start(bf16[1,512,512]{2,1,0:T(8,128)(2,1)} %get-tuple-element.264), channel_id=1, source_target_pairs={{0,1},{1,2},{2,3},{3,4},{4,5},{5,6},{6,7},{8,9},{9,10},{10,11},{11... | collective-permute-start | bytes 1572872 | tf_op jit(solution)/shard_map/ppermute | solution.py:24
  201.4 25.4 %collective-permute-start.17 = (bf16[2,512,256]{2,1,0:T(8,128)(2,1)S(1)}, bf16[2,512,256]{2,1,0:T(8,128)(2,1)S(1)}, u32[]{:S(2)}, u32[]{:S(2)}) collective-permute-start(bf16[2,512,256]{2,1,0:T(8,128)(2,1)S(1)} %copy-done.33), channel_id=1, source_target_pairs={{0,16},{8,24},{16,0},{24,8},{1,17},{9,25},{17,1},{25,9},{2,18},{10... | collective-permute-start | bytes 1572872 | tf_op jit(solution)/shard_map/ppermute | solution.py:604
  206.4 21.9 %collective-permute-start.14 = (bf16[6,512,256]{2,1,0:T(8,128)(2,1)}, bf16[6,512,256]{2,1,0:T(8,128)(2,1)}, u32[]{:S(2)}, u32[]{:S(2)}) collective-permute-start(bf16[6,512,256]{2,1,0:T(8,128)(2,1)} %constant_dynamic-update-slice_fusion.a0.att_ref), channel_id=1, source_target_pairs={{0,8},{8,0},{16,24},{24,16},{1,9},{9,1},{17,25},{25,17},{2,10},{10... | collective-permute-start | bytes 4718600 | tf_op jit(solution)/shard_map/ppermute | solution.py:604
  293.0 309.2 %reduce-scatter.5.cloned.1.call-start = ((), (), s32[]{:S(2)}) async-start(), calls=%async_computation.5 | async-start | bytes 4423680 | tf_op jit(solution)/shard_map/reduce_scatter | solution.py:853
  301.5 36.5 %collective-permute-start.23 = (bf16[6,128,1024]{2,1,0:T(8,128)(2,1)S(1)}, bf16[6,128,1024]{2,1,0:T(8,128)(2,1)S(1)}, u32[]{:S(2)}, u32[]{:S(2)}) collective-permute-start(bf16[6,128,1024]{2,1,0:T(8,128)(2,1)S(1)} %fusion.22), channel_id=1, source_target_pairs={{0,16},{8,24},{16,0},{24,8},{1,17},{9,25},{17,1},{25,9},{2,18},{10... | collective-permute-start | bytes 4718600 | tf_op jit(solution)/shard_map/ppermute | solution.py:604
  350.1 18.3 %collective-permute-start.26 = (bf16[6,128,256]{2,1,0:T(8,128)(2,1)}, bf16[6,128,256]{2,1,0:T(8,128)(2,1)}, u32[]{:S(2)}, u32[]{:S(2)}) collective-permute-start(bf16[6,128,256]{2,1,0:T(8,128)(2,1)} %get-tuple-element.108), channel_id=1, source_target_pairs={{0,24},{8,16},{16,8},{24,0},{1,25},{9,17},{17,9},{25,1},{2,26},{10... | collective-permute-start | bytes 1179656 | tf_op jit(solution)/shard_map/ppermute | solution.py:604
  368.4 48.1 %collective-permute-start.27 = (bf16[2,6,128,1024]{3,2,1,0:T(8,128)(2,1)}, bf16[2,6,128,1024]{3,2,1,0:T(8,128)(2,1)}, u32[]{:S(2)}, u32[]{:S(2)}) collective-permute-start(bf16[2,6,128,1024]{3,2,1,0:T(8,128)(2,1)} %get-tuple-element.126), channel_id=1, source_target_pairs={{0,8},{8,0},{16,24},{24,16},{1,9},{9,1},{17,25},{25,17},{2,10},{10... | collective-permute-start | bytes 9437192 | tf_op jit(solution)/shard_map/ppermute | solution.py:604
  410.1 28.6 %collective-permute-start.30 = (bf16[512,512]{1,0:T(8,128)(2,1)}, bf16[512,512]{1,0:T(8,128)(2,1)}, u32[]{:S(2)}, u32[]{:S(2)}) collective-permute-start(bf16[512,512]{1,0:T(8,128)(2,1)} %slice_bitcast_fusion.5), channel_id=1, source_target_pairs={{1,0},{2,1},{3,2},{4,3},{5,4},{6,5},{7,6},{9,8},{10,9},{11,10},{12... | collective-permute-start | bytes 1572872 | tf_op jit(solution)/shard_map/ppermute | solution.py:24
  412.3 29.7 %collective-permute-start.29 = (bf16[4,176,512]{2,1,0:T(8,128)(2,1)}, bf16[4,176,512]{2,1,0:T(8,128)(2,1)}, u32[]{:S(2)}, u32[]{:S(2)}) collective-permute-start(bf16[4,176,512]{2,1,0:T(8,128)(2,1)} %slice.316), channel_id=1, source_target_pairs={{1,0},{2,1},{3,2},{4,3},{5,4},{6,5},{7,6},{9,8},{10,9},{11,10},{12... | collective-permute-start | bytes 2162696 | tf_op jit(solution)/shard_map/ppermute | solution.py:24
  420.9 36.2 %collective-permute-start.28 = (bf16[6,128,1024]{2,1,0:T(8,128)(2,1)}, bf16[6,128,1024]{2,1,0:T(8,128)(2,1)}, u32[]{:S(2)}, u32[]{:S(2)}) collective-permute-start(bf16[6,128,1024]{2,1,0:T(8,128)(2,1)} %fusion.23), channel_id=1, source_target_pairs={{0,16},{8,24},{16,0},{24,8},{1,17},{9,25},{17,1},{25,9},{2,18},{10... | collective-permute-start | bytes 4718600 | tf_op jit(solution)/shard_map/ppermute | solution.py:604
  483.6 22.1 %collective-permute-start.32 = (bf16[1056,256]{1,0:T(8,128)(2,1)}, bf16[1056,256]{1,0:T(8,128)(2,1)}, u32[]{:S(2)}, u32[]{:S(2)}) collective-permute-start(bf16[1056,256]{1,0:T(8,128)(2,1)} %fusion.32), channel_id=1, source_target_pairs={{0,16},{8,24},{16,0},{24,8},{1,17},{9,25},{17,1},{25,9},{2,18},{10... | collective-permute-start | bytes 1622024 | tf_op jit(solution)/shard_map/ppermute | solution.py:604
  542.6 36.6 %collective-permute-start.34 = (bf16[6,128,1024]{2,1,0:T(8,128)(2,1)S(1)}, bf16[6,128,1024]{2,1,0:T(8,128)(2,1)}, u32[]{:S(2)}, u32[]{:S(2)}) collective-permute-start(bf16[6,128,1024]{2,1,0:T(8,128)(2,1)S(1)} %fusion.24), channel_id=1, source_target_pairs={{0,16},{8,24},{16,0},{24,8},{1,17},{9,25},{17,1},{25,9},{2,18},{10... | collective-permute-start | bytes 4718600 | tf_op jit(solution)/shard_map/ppermute | solution.py:604
  (67 other events, 504.6 us)
Sparse Core Ops, SparseCore 0:
  23.4 62.0 all-gather.4
  87.7 111.9 all-gather.6
  293.1 86.9 reduce-scatter.2
  518.7 83.4 reduce-scatter.4

commit v8 on v7

--- a/solution.py
+++ b/solution.py
@@ -102,9 +102,10 @@
 
 
 def bwd_kernel(
-    first, place_ref, slope_ref, q_ref, own_ref, prev_ref, recv_ref, comp_ref, head_ref, g0, g1, g2, g3, att_ref, lse_ref, held_ref,
-    gq_ref, gkv_ref, tail_ref, gcomp_ref, grad_ref,
+    first, place_ref, slope_ref, q_ref, own_ref, prev_ref, recv_ref, comp_ref, head_ref, g0, g1, g2, g3,
+    att_ref, lse_ref, held_ref, over_ref, gq_ref, gkv_ref, tail_ref, rest_ref, back_ref, grad_ref, gcomp_ref,
 ):
+    opening = first == 0
     step = pl.program_id(0) + first
     place = place_ref[step]
     seg_len = q_ref.shape[1]
@@ -123,8 +124,12 @@
 
     @pl.when(at_start)
     def _():
-        tail_ref[...] = held_ref[...]
         gcomp_ref[...] = jnp.zeros_like(gcomp_ref)
+        if opening:
+            tail_ref[...] = jnp.zeros_like(tail_ref)
+        else:
+            tail_ref[...] = held_ref[...]
+            gcomp_ref[: CSEGS - 1] = over_ref[...]
 
     place_rows(head_ref[0], (g0, g1, g2, g3), grad_ref)
     for h in range(local_heads):
@@ -162,11 +167,24 @@
         for n in range(2):
             rows = slice(n * half, (n + 1) * half)
             bias = key_bias(half, n * half - seg_len, 1, half, place >= 1, slope)
-            k = jnp.where(is_first, recv_ref[0, rows, kc], prev_ref[0, rows, kc])
-            v = jnp.where(is_first, recv_ref[0, rows, vc], prev_ref[0, rows, vc])
+            k, v = prev_ref[0, rows, kc], prev_ref[0, rows, vc]
+            if opening:
+                k = jnp.where(is_first, recv_ref[0, rows, kc], k)
+                v = jnp.where(is_first, recv_ref[0, rows, vc], v)
             gk, gv, gq = part(k, v, bias, every, False)
-            gkv_ref[0, rows, kc] = (tail_ref[rows, kc] + gk).astype(jnp.bfloat16)
-            gkv_ref[0, rows, vc] = (tail_ref[rows, vc] + gv).astype(jnp.bfloat16)
+            gk = (tail_ref[rows, kc] + gk).astype(jnp.bfloat16)
+            gv = (tail_ref[rows, vc] + gv).astype(jnp.bfloat16)
+            gkv_ref[0, rows, kc] = gk
+            gkv_ref[0, rows, vc] = gv
+            if opening:
+                at = (CSEGS + 1) * pad_rows + n * half
+                send = slice(at, at + half)
+
+                @pl.when(is_first)
+                def _(gk=gk, gv=gv, send=send):
+                    back_ref[send, kc] = gk
+                    back_ref[send, vc] = gv
+
             total = total + gq
         lo, hi = slice(0, half), slice(half, seg_len)
         bias_lo = key_bias(half, 0, 1, half, place >= 0, slope)
@@ -181,6 +199,17 @@
         gq_ref[0, lo, kc] = ((total[:, lo] + gq0) * scale).T.astype(jnp.bfloat16)
         gq_ref[0, hi, kc] = ((total[:, hi] + gq1 + gq2) * scale).T.astype(jnp.bfloat16)
 
+    @pl.when(pl.program_id(0) == pl.num_programs(0) - 1)
+    def _():
+        if opening:
+            for entry in range(CSEGS + 1):
+                rows = slice(entry * pad_rows, (entry + 1) * pad_rows)
+                back_ref[rows, :] = gcomp_ref[entry].astype(jnp.bfloat16)
+            rest_ref[...] = gcomp_ref[CSEGS + 1 :]
+        else:
+            rest_ref[...] = gcomp_ref[...]
+            back_ref[...] = jnp.zeros_like(back_ref)
+
 
 def attention_specs(first, seg_len, head_cols, comp_shape):
     pair = 2 * head_cols
@@ -216,12 +245,24 @@
 
 
 def attend_bwd(
-    first, count, head, place, slope, heads, recv_mem, comp_ext, grad_mixed, attn_out, lse, held, head_cols
+    first, count, head, place, slope, heads, recv_mem, comp_ext, grad_mixed, attn_out, lse, held, over, head_cols
 ):
     seg_len = attn_out.shape[1]
     local_heads = head_cols // HD
     pair = 2 * head_cols
-    window = (count + CSEGS - 1,) + comp_ext.shape[1:]
+    pad_rows = comp_ext.shape[1]
+    entries = count + CSEGS - 1
+    opening = first == 0
+    done = count - 1 if opening else count
+    rest = entries - CSEGS - 1 if opening else entries
+    back = ((CSEGS + 1) * pad_rows + seg_len, pair) if opening else (16, pair)
+
+    def pair_block(s):
+        return (jnp.maximum(s - 1, 0) if opening else s, 0, 0)
+
+    def stays(shape):
+        return pl.BlockSpec(shape, lambda s: (0,) * len(shape))
+
     return pl.pallas_call(
         functools.partial(bwd_kernel, first),
         grid=(count,),
@@ -231,27 +272,33 @@
         + [
             by_segment((seg_len, head_cols), first),
             by_segment((local_heads, seg_len), first),
-            fixed((seg_len, pair)),
+            fixed(held.shape),
+            fixed(over.shape),
         ],
         out_specs=[
             by_segment((seg_len, head_cols)),
-            by_segment((seg_len, pair)),
-            pl.BlockSpec((seg_len, pair), lambda s: (0, 0)),
-            pl.BlockSpec(window, lambda s: (0, 0, 0)),
+            pl.BlockSpec((1, seg_len, pair), pair_block),
+            stays((seg_len, pair)),
+            stays((rest, pad_rows, pair)),
+            stays(back),
         ],
         out_shape=[
             jax.ShapeDtypeStruct((count, seg_len, head_cols), jnp.bfloat16),
-            jax.ShapeDtypeStruct((count, seg_len, pair), jnp.bfloat16),
+            jax.ShapeDtypeStruct((done, seg_len, pair), jnp.bfloat16),
             jax.ShapeDtypeStruct((seg_len, pair), jnp.float32),
-            jax.ShapeDtypeStruct(window, jnp.float32),
-        ],
-        scratch_shapes=[pltpu.VMEM((seg_len, head_cols), jnp.bfloat16)],
+            jax.ShapeDtypeStruct((rest, pad_rows, pair), jnp.float32),
+            jax.ShapeDtypeStruct(back, jnp.bfloat16),
+        ],
+        scratch_shapes=[
+            pltpu.VMEM((seg_len, head_cols), jnp.bfloat16),
+            pltpu.VMEM((entries, pad_rows, pair), jnp.float32),
+        ],
         compiler_params=pltpu.CompilerParams(vmem_limit_bytes=VMEM_LIMIT),
         cost_estimate=pl.CostEstimate(
             flops=count * 2 * 10**9, bytes_accessed=count * 4 * 10**6, transcendentals=count * 16 * 10**5
         ),
         name="attend_bwd",
-    )(place, slope, heads, heads, heads, recv_mem, comp_ext, head, *grad_mixed, attn_out, lse, held)
+    )(place, slope, heads, heads, heads, recv_mem, comp_ext, head, *grad_mixed, attn_out, lse, held, over)
 
 
 def row_norm(values):
@@ -696,7 +743,7 @@
     grad_pieces = (grad_held, head_swap(grad_held, 1), grad_far, head_swap(grad_far, 1))
     packed = all_columns(packed_mine)
     comp_pair = comp_pairs(packed)
-    comp_pair, grad_pieces = lax.optimization_barrier((comp_pair, grad_pieces))
+    comp_pair, grad_pieces, recv_mem = lax.optimization_barrier((comp_pair, grad_pieces, recv_mem))
     comp_ext = jnp.concatenate([comp_pairs(all_columns(recv_packed)), comp_pair], 0)
     order = jnp.arange(lengths.shape[0], dtype=jnp.int32)
     starts = jnp.sum(jnp.where(order[None, :] < order[:, None], lengths[None, :], 0), axis=1)
@@ -711,14 +758,18 @@
         comp_pair, head_cols,
     )
     comp_ext, late = lax.optimization_barrier((comp_ext, late))
-    cuts = [0, window // 2, window]
-    attention = [
-        attend_fwd(a, 0, b - a, seg_place, slopes, heads, recv_mem, comp_ext, head_cols)
-        for a, b in zip(cuts, cuts[1:])
-    ] + [late]
+    middle_seg = window // 2
+
+    def early(a, b, comp_ext):
+        return attend_fwd(a, 0, b - a, seg_place, slopes, heads, recv_mem, comp_ext, head_cols)
+
+    first = early(0, middle_seg, comp_ext)
+    late_far = head_swap(late[0], 2)
+    late_far, first, comp_ext = lax.optimization_barrier((late_far, first, comp_ext))
+    attention = [first, early(middle_seg, window, comp_ext), late]
     attn_out = jnp.concatenate([out for out, _ in attention], 0)
     lse = jnp.concatenate([total for _, total in attention], 0)
-    far = jnp.concatenate([head_swap(out, 2) for out, _ in attention], 0)
+    far = jnp.concatenate([head_swap(out, 2) for out, _ in attention[:2]] + [late_far], 0)
     attended = (attn_out, head_swap(attn_out, 1), far, head_swap(far, 1))
     f_keep, f_sent, n_keep, n_sent, hidden, first_grads = feed_forward(
         head, attended, wo_held, wo_specs, token_pieces, grad_pieces, gain_second, second_all, ff_part
@@ -731,55 +782,51 @@
     )
     grad_gain_two = grad_gain_two[0]
     mixed = mixed[:1] + [head_swap(mixed[bits], bits) for bits in (1, 2, 3)]
-    f_sent, mixed = lax.optimization_barrier((f_sent, mixed))
-
-    def backward(a, b, held, mixed):
-        return attend_bwd(
-            a, b - a, head, seg_place, slopes, heads, recv_mem, comp_ext, mixed, attn_out, lse, held,
-            head_cols,
-        )
-
-    held = jnp.zeros((seg_len, 2 * head_cols), jnp.float32)
-    query_one, pair_one, held, comp_one = backward(0, window, held, mixed)
-    mem_back, comp_back = pair_one[0], comp_one[:window].astype(bf16)
-    mem_back, comp_back, mixed, held = lax.optimization_barrier((mem_back, comp_back, mixed, held))
-    got_mem, got_comp = passed_along((mem_back, comp_back), "blk", -1)
-    query_two, pair_two, held, comp_two = backward(window, seg_count, held, mixed)
-    f_sum = sum_over_heads(f_keep, f_sent)
-    query_two, f_sum, first_sum = lax.optimization_barrier((query_two, f_sum, first_sum))
-    out_tokens = (hidden + f_sum).astype(bf16)
-    grad_hidden = grad_hidden.reshape(token_count, width)
-    grad_branch = grad_branch.reshape(token_count, width)
-    over = comp_one.shape[0] - window
-    kept = jnp.concatenate([comp_one[window:] + comp_two[:over], comp_two[over:]], 0)
-    kept = jnp.pad(kept, ((0, seg_count - kept.shape[0]), (0, 0), (0, 0)))
-    grad_pairs = [pair_one[1:], pair_two]
-    last_pair = (held + got_mem.astype(jnp.float32)).astype(bf16)
-    grad_pair = jnp.concatenate([*grad_pairs, last_pair[None]], 0)
-    grad_query = jnp.concatenate([query_one, query_two], 0)
-    comp_pair_grad = kept + jnp.pad(
-        got_comp.astype(jnp.float32), ((seg_count - window, 0), (0, 0), (0, 0))
-    )
-    comp_grad_rows = comp_pair_grad.reshape(comp_count, 2 * head_cols).astype(bf16)
-    grad_packed_part = lax.dot_general(
-        comp_grad_rows, wkv, COLS_IN, preferred_element_type=jnp.float32
-    ).astype(bf16)
-
-    grad_packed_part, grad_query, grad_pair, grad_branch = lax.optimization_barrier(
-        (grad_packed_part, grad_query, grad_pair, grad_branch)
-    )
     grad_wo = [
         lax.dot_general(
             lax.dynamic_slice_in_dim(block, head_index * quarter, quarter, 1).reshape(
                 token_count, head_cols
             ),
-            grad_branch,
+            grad_branch.reshape(token_count, width),
             ROWS_IN,
             preferred_element_type=jnp.float32,
         ).astype(bf16)
         for block in attended
     ]
-
+    f_got = head_swap(f_sent, 1)
+    f_far = (f_keep[1].astype(jnp.float32) + f_got[1].astype(jnp.float32)).astype(bf16)
+    wo_sent = jnp.stack([grad_wo[1], grad_wo[3]])
+    f_far, wo_sent, mixed = lax.optimization_barrier((f_far, wo_sent, mixed))
+
+    def backward(a, b, held, over, mixed):
+        return attend_bwd(
+            a, b - a, head, seg_place, slopes, heads, recv_mem, comp_ext, mixed, attn_out, lse, held,
+            over, head_cols,
+        )
+
+    held = jnp.zeros((16, 2 * head_cols), jnp.float32)
+    query_one, pair_one, held, over, back = backward(0, window, held, held, mixed)
+    wo_got = head_swap(wo_sent, 1).astype(jnp.float32)
+    wo_far = (grad_wo[2].astype(jnp.float32) + wo_got[1]).astype(bf16)
+    back, wo_far, held = lax.optimization_barrier((back, wo_far, held))
+    got_back = passed_along(back, "blk", -1).astype(jnp.float32)
+    query_two, pair_two, held, rest, _ = backward(window, seg_count, held, over, mixed)
+    grad_hidden = grad_hidden.reshape(token_count, width)
+    last_pair = (held + got_back[window * pad_rows :]).astype(bf16)
+    grad_pair = jnp.concatenate([pair_one, pair_two, last_pair[None]], 0)
+    grad_query = jnp.concatenate([query_one, query_two], 0)
+    got_comp = got_back[: window * pad_rows].reshape(window, pad_rows, 2 * head_cols)
+    comp_pair_grad = jnp.pad(rest, ((0, seg_count - rest.shape[0]), (0, 0), (0, 0))) + jnp.pad(
+        got_comp, ((seg_count - window, 0), (0, 0), (0, 0))
+    )
+    comp_grad_rows = comp_pair_grad.reshape(comp_count, 2 * head_cols).astype(bf16)
+    grad_packed_part = lax.dot_general(
+        comp_grad_rows, wkv, COLS_IN, preferred_element_type=jnp.float32
+    ).astype(bf16)
+
+    grad_packed_part, grad_query, grad_pair = lax.optimization_barrier(
+        (grad_packed_part, grad_query, grad_pair)
+    )
     def columns_of(bits):
         start = jnp.bitwise_xor(head_index, bits) * head_cols
         return lax.dynamic_slice_in_dim(grad_packed_part, start, head_cols, 1)
@@ -787,6 +834,14 @@
     grad_packed = sum_over_heads(
         (columns_of(0), columns_of(2)), jnp.stack([columns_of(1), columns_of(3)])
     ).astype(bf16)
+    f_far, wo_far = head_swap(f_far, 2), head_swap(wo_far, 2)
+    grad_packed, f_far, first_sum, wo_far = lax.optimization_barrier(
+        (grad_packed, f_far, first_sum, wo_far)
+    )
+    out_tokens = (
+        hidden + f_keep[0].astype(jnp.float32) + f_got[0].astype(jnp.float32) + f_far.astype(jnp.float32)
+    ).astype(bf16)
+    grad_wo = (grad_wo[0].astype(jnp.float32) + wo_got[0] + wo_far.astype(jnp.float32)).astype(bf16)
     keep, sent = g_normed_parts(
         head,
         grad_query,
@@ -821,7 +876,6 @@
         + jnp.sum(grad_comp * weights[3:].astype(jnp.float32), axis=(0, 2))
     ) / gain_first[0]
     grad_wkv = grad_wkv + comp_term
-    grad_wo = sum_over_heads((grad_wo[0], grad_wo[2]), jnp.stack([grad_wo[1], grad_wo[3]])).astype(bf16)
 
     def by_owner(value):
         return value.astype(bf16).reshape(

time: 638 us -> 600 us (0.940)
  waiting for transfers between devices: 270 us -> 248 us
  local copies, waits for them, and re-layouts: 62.9 us -> 48.2 us
    ppermute x33, waiting for transfers between devices: 194 us -> 159 us  [head_swap(): lax.ppermute(value, 'head', [(source, source ^ bit) for source in range(c...]
    ppermute x4 -> x3, waiting for transfers between devices: 37.4 us -> 49 us  [passed_along(): lax.ppermute(value, axis, [(source, source + steps) for source in range(l...]
    convert_element_type x2 -> x4, other arithmetic: 1.94 us -> 11.6 us  [the longest x1 5.91 us: per_device(): out_tokens = (hidden + f_keep[0].astype(jnp.float32) + f_got[0].astype(jn...]
  transfers between devices with their start and end apart: 42 -> 41, of which waited for: 22 -> 21; matrix products, arithmetic and copies ran while one was open for 15% -> 14% of each run, Pallas kernels for 17% -> 19%
where the time goes in v8:
time: 600 us; the launch traced here: 591 us
  waiting for transfers between devices  248 us (41%)
  Pallas kernels  171 us (28%)
  local copies, waits for them, and re-layouts  48.2 us (8%)
  other arithmetic  42.5 us (7%)
  starting transfers between devices  29.1 us (5%)
  matrix products  25.6 us (4%)
  between operations  15.3 us (3%)
  blocking collectives  10.9 us (2%)
    ppermute x33, waiting for transfers between devices, head_swap(): lax.ppermute(value, 'head', [(source, source ^ bit) for source in range(c...  159 us
    pallas_call x1, Pallas kernels, feed_forward(): pl.pallas_call(ffn_kernel, grid=(count,), in_specs=[pl.BlockSpec(memory_s...  61.4 us
    ppermute x3, waiting for transfers between devices, passed_along(): lax.ppermute(value, axis, [(source, source + steps) for source in range(l...  49 us
    pallas_call x2, Pallas kernels, attend_bwd(): pl.pallas_call(functools.partial(bwd_kernel, first), grid=(count,), in_sp...  43.4 us
    pallas_call x3, Pallas kernels, attend_fwd(): pl.pallas_call(functools.partial(fwd_kernel, first, shift), grid=(count,)...  26.5 us
    reduce_scatter x1, waiting for transfers between devices, per_device(): lax.psum_scatter(second_grads.reshape(-1, head_cols), 'blk', scatter_dime...  21.6 us
    unnamed x121, local copies, waits for them, and re-layouts  20.1 us
    ppermute x33, starting transfers between devices, head_swap(): lax.ppermute(value, 'head', [(source, source ^ bit) for source in range(c...  19 us
  transfers between devices with their start and end apart: 41, of which 21 were waited for; matrix products, arithmetic and copies ran while one was open for 14% of the time, Pallas kernels for 19%

profile of v8, /device:TPU:24, one launch (start us, length us, event | category | flops | bytes accessed | tf_op | source)
XLA Modules:
  0.0 590.7 jit_solution(18420912910775675105)
XLA Ops:
  12.4 10.9 %all_to_all.10 = bf16[4,208,256]{2,1,0:T(8,128)(2,1)} all-to-all(bf16[4,208,256]{2,1,0:T(8,128)(2,1)S(1)} %copy.246), channel_id=1, replica_groups=mesh['head'=4,'blk'=8] {'head'}, dimensions={0} | all-to-all | bytes 851968 | tf_op jit(solution)/shard_map/all_to_all | solution.py:696
  30.4 36.4 %collective-permute-done.1.t2 = bf16[6,128,1024]{2,1,0:T(8,128)(2,1)} collective-permute-done((bf16[6,128,1024]{2,1,0:T(8,128)(2,1)}, bf16[6,128,1024]{2,1,0:T(8,128)(2,1)}, u32[]{:S(2)}, u32[]{:S(2)}) %collective-permute-start.1) | collective-permute-done | bytes 1572896 | tf_op jit(solution)/shard_map/ppermute | solution.py:651
  68.5 17.0 %all-gather.5.cloned.1.call-done = bf16[32,208,256]{2,1,0:T(8,128)(2,1)} async-done(((bf16[4,208,256]{2,1,0:T(8,128)(2,1)}), bf16[32,208,256]{2,1,0:T(8,128)(2,1)}) %all-gather.5.cloned.1.call-update) | async-done | bytes 3407888 | tf_op jit(solution)/shard_map/all_gather | solution.py:698
  91.5 16.8 %prepare.1 = (bf16[6,512,768]{2,1,0:T(8,128)(2,1)}, bf16[6,512,1024]{2,1,0:T(8,128)(2,1)}, bf16[6,176,3072]{2,1,0:T(8,128)(2,1)}, bf16[6,176,256]{2,1,0:T(8,128)(2,1)}) custom-call(s32[1]{0:T(128)} %bitcast.head_ref, bf16[6,128,1024]{2,1,0:T(8,128)(2,1)} %t0.1, bf16[6,128,1024]{2,1,0:T(8,128)(2,1)} %collective-permute-done.t1, ...), custom_call_target="tpu_custom_call" | custom-call | flops 7000000000 | bytes 30000000 | tf_op jit(solution)/shard_map/prepare/pallas_call | solution.py:397
  117.8 14.3 %collective-permute-done.3 = bf16[4,176,256]{2,1,0:T(8,128)(2,1)S(1)} collective-permute-done((bf16[4,176,256]{2,1,0:T(8,128)(2,1)S(1)}, bf16[4,176,256]{2,1,0:T(8,128)(2,1)S(1)}, u32[]{:S(2)}, u32[]{:S(2)}) %collective-permute-start.3) | collective-permute-done | bytes 360480 | tf_op jit(solution)/shard_map/ppermute | solution.py:24
  146.4 27.2 %collective-permute-done.13.recv_ref = bf16[1,512,512]{2,1,0:T(8,128)(2,1)S(1)} collective-permute-done((bf16[1,512,512]{2,1,0:T(8,128)(2,1)S(1)}, bf16[1,512,512]{2,1,0:T(8,128)(2,1)S(1)}, u32[]{:S(2)}, u32[]{:S(2)}) %collective-permute-start.13) | collective-permute-done | bytes 524320 | tf_op jit(solution)/shard_map/ppermute | solution.py:24
  175.0 8.7 %attend_fwd.3 = (bf16[2,512,256]{2,1,0:T(8,128)(2,1)}, f32[2,2,512]{2,1,0:T(2,128)}) custom-call(s32[6]{0:T(128)} %fusion.51.place_ref, f32[2]{0:T(128)} %exponential_multiply_fusion.slope_ref, bf16[6,512,768]{2,1,0:T(8,128)(2,1)} %get-tuple-element.92.q_ref.own_ref.prev_ref, bf16[6,512,768]{2,1,0:T(8,128)(2,1)} %get-tuple-element.92.q_ref.own_ref.prev_ref, ...), custom_call_target="tpu_custom_call" | custom-call | flops 2000000000 | bytes 6000000 | tf_op jit(solution)/shard_map/attend_fwd/pallas_call | solution.py:230
  185.0 8.9 %attend_fwd.4 = (bf16[2,512,256]{2,1,0:T(8,128)(2,1)}, f32[2,2,512]{2,1,0:T(2,128)}) custom-call(s32[6]{0:T(128)} %fusion.51.place_ref, f32[2]{0:T(128)} %exponential_multiply_fusion.slope_ref, bf16[6,512,768]{2,1,0:T(8,128)(2,1)} %get-tuple-element.92.q_ref.own_ref.prev_ref, bf16[6,512,768]{2,1,0:T(8,128)(2,1)} %get-tuple-element.92.q_ref.own_ref.prev_ref, ...), custom_call_target="tpu_custom_call" | custom-call | flops 2000000000 | bytes 6000000 | tf_op jit(solution)/shard_map/attend_fwd/pallas_call | solution.py:230
  199.1 8.9 %attend_fwd.5 = (bf16[2,512,256]{2,1,0:T(8,128)(2,1)}, f32[2,2,512]{2,1,0:T(2,128)}) custom-call(s32[6]{0:T(128)} %fusion.51.place_ref, f32[2]{0:T(128)} %exponential_multiply_fusion.slope_ref, bf16[6,512,768]{2,1,0:T(8,128)(2,1)} %get-tuple-element.92.q_ref.own_ref.prev_ref, bf16[6,512,768]{2,1,0:T(8,128)(2,1)} %get-tuple-element.92.q_ref.own_ref.prev_ref, ...), custom_call_target="tpu_custom_call" | custom-call | flops 2000000000 | bytes 6000000 | tf_op jit(solution)/shard_map/attend_fwd/pallas_call | solution.py:230
  213.1 9.0 %collective-permute-done.17 = bf16[2,512,256]{2,1,0:T(8,128)(2,1)S(1)} collective-permute-done((bf16[2,512,256]{2,1,0:T(8,128)(2,1)}, bf16[2,512,256]{2,1,0:T(8,128)(2,1)S(1)}, u32[]{:S(2)}, u32[]{:S(2)}) %collective-permute-start.17) | collective-permute-done | bytes 524320 | tf_op jit(solution)/shard_map/ppermute | solution.py:651
  227.5 61.4 %feed_forward.1 = (bf16[2,6,128,1024]{3,2,1,0:T(8,128)(2,1)}, bf16[2,6,128,1024]{3,2,1,0:T(8,128)(2,1)}, bf16[2,6,128,1024]{3,2,1,0:T(8,128)(2,1)}, bf16[2,6,128...) custom-call(s32[1]{0:T(128)} %bitcast.head_ref, ...), custom_call_target="tpu_custom_call" | custom-call | flops 44999999488 | bytes 50000000 | tf_op jit(solution)/shard_map/feed_forward/pallas_call | solution.py:516
  289.4 8.5 %collective-permute-done.23.got_ref = bf16[2,6,128,1024]{3,2,1,0:T(8,128)(2,1)S(1)} collective-permute-done((bf16[2,6,128,1024]{3,2,1,0:T(8,128)(2,1)}, bf16[2,6,128,1024]{3,2,1,0:T(8,128)(2,1)S(1)}, u32[]{:S(2)}, u32[]{:S(2)}) %collective-permute-start.23) | collective-permute-done | bytes 3145760 | tf_op jit(solution)/shard_map/ppermute | solution.py:651
  307.9 31.2 %collective-permute-done.24.far_ref = bf16[6,128,1024]{2,1,0:T(8,128)(2,1)} collective-permute-done((bf16[6,128,1024]{2,1,0:T(8,128)(2,1)}, bf16[6,128,1024]{2,1,0:T(8,128)(2,1)}, u32[]{:S(2)}, u32[]{:S(2)}) %collective-permute-start.24) | collective-permute-done | bytes 1572896 | tf_op jit(solution)/shard_map/ppermute | solution.py:651
  339.1 9.2 %middle.1 = (f32[6,128,1024]{2,1,0:T(8,128)}, bf16[6,128,1024]{2,1,0:T(8,128)(2,1)}, f32[1,1024]{1,0:T(1,128)}, bf16[6,128,256]{2,1,0:T(8,128)(2,1)}, bf16[6,128...) custom-call(bf16[2,6,128,1024]{3,2,1,0:T(8,128)(2,1)} %get-tuple-element.112.keep_ref, ...), custom_call_target="tpu_custom_call" | custom-call | flops 1620000000 | bytes 24000000 | tf_op jit(solution)/shard_map/middle/pallas_call | solution.py:586
  354.2 6.4 %collective-permute-done.26.g2 = bf16[6,128,256]{2,1,0:T(8,128)(2,1)S(1)} collective-permute-done((bf16[6,128,256]{2,1,0:T(8,128)(2,1)}, bf16[6,128,256]{2,1,0:T(8,128)(2,1)S(1)}, u32[]{:S(2)}, u32[]{:S(2)}) %collective-permute-start.26) | collective-permute-done | bytes 393248 | tf_op jit(solution)/shard_map/ppermute | solution.py:651
  360.6 7.5 %collective-permute-done.27.g3 = bf16[6,128,256]{2,1,0:T(8,128)(2,1)S(1)} collective-permute-done((bf16[6,128,256]{2,1,0:T(8,128)(2,1)}, bf16[6,128,256]{2,1,0:T(8,128)(2,1)S(1)}, u32[]{:S(2)}, u32[]{:S(2)}) %collective-permute-start.27) | collective-permute-done | bytes 393248 | tf_op jit(solution)/shard_map/ppermute | solution.py:651
  369.8 28.0 %attend_bwd.2 = (bf16[4,512,256]{2,1,0:T(8,128)(2,1)}, bf16[3,512,512]{2,1,0:T(8,128)(2,1)}, f32[512,512]{1,0:T(8,128)}, f32[2,176,512]{2,1,0:T(8,128)}, bf16[1216,512]{1,0:T(8,128)(2,1)}) custom-call(s32[6]{0:T(128)} %fusion.51.place_ref, f32[2]{0:T(128)} %exponential_multiply_fusion.slope_ref, ...), custom_call_target="tpu_custom_call" | custom-call | flops 8000000000 | bytes 16000000 | tf_op jit(solution)/shard_map/attend_bwd/pallas_call | solution.py:266
  408.5 15.4 %attend_bwd.3 = (bf16[2,512,256]{2,1,0:T(8,128)(2,1)}, bf16[2,512,512]{2,1,0:T(8,128)(2,1)}, f32[512,512]{1,0:T(8,128)}, f32[4,176,512]{2,1,0:T(8,128)}, bf16[16,512]{1,0:T(8,128)(2,1)}) custom-call(s32[6]{0:T(128)} %fusion.51.place_ref, f32[2]{0:T(128)} %exponential_multiply_fusion.slope_ref, bf16[6,512,768]{2,1,0:T(8,128)(2,1)} %get-tuple-element.92.q_ref.own_ref.prev_ref, ...), custom_call_target="tpu_custom_call" | custom-call | flops 4000000000 | bytes 8000000 | tf_op jit(solution)/shard_map/attend_bwd/pallas_call | solution.py:266
  425.2 7.5 %collective-permute-done.29 = bf16[1216,512]{1,0:T(8,128)(2,1)} collective-permute-done((bf16[1216,512]{1,0:T(8,128)(2,1)}, bf16[1216,512]{1,0:T(8,128)(2,1)}, u32[]{:S(2)}, u32[]{:S(2)}) %collective-permute-start.29) | collective-permute-done | bytes 1245216 | tf_op jit(solution)/shard_map/ppermute | solution.py:24
  454.2 11.7 %collective-permute-done.31 = bf16[1056,256]{1,0:T(8,128)(2,1)S(1)} collective-permute-done((bf16[1056,256]{1,0:T(8,128)(2,1)S(1)}, bf16[1056,256]{1,0:T(8,128)(2,1)S(1)}, u32[]{:S(2)}, u32[]{:S(2)}) %collective-permute-start.31) | collective-permute-done | bytes 540704 | tf_op jit(solution)/shard_map/ppermute | solution.py:651
  469.5 6.4 %fusion.16 = (f32[3072]{0:T(1024)S(1)}, bf16[3072,256]{1,0:T(8,128)(2,1)S(1)}) fusion(f32[3,4,8,32,256]{4,3,2,1,0:T(8,128)} %copy.264, bf16[1056,3072]{1,0:T(8,128)(2,1)} %bitcast.265, bf16[1056,256]{1,0:T(8,128)(2,1)S(1)} %copy-done.24), kind=kOutput, calls=%fused_computation.25 | convolution fusion | flops 1663300608 | bytes 11759616 | tf_op jit(solution)/shard_map/dot_general | solution.py:867
  481.1 13.8 %g_normed.1 = (bf16[2,6,128,1024]{3,2,1,0:T(8,128)(2,1)}, bf16[2,6,128,1024]{3,2,1,0:T(8,128)(2,1)}) custom-call(s32[1]{0:T(128)} %bitcast.head_ref, bf16[6,512,256]{2,1,0:T(8,128)(2,1)} %copy-done.14, bf16[6,512,512]{2,1,0:T(8,128)(2,1)} %copy-done.8, bf16[6,176,256]{2,1,0:T(8,128)(2,1)} %bitcast.239, bf16[6,1024,256]{2,1,0:T(8,128)(2,1)} %bitcast.220), custom_call_target="tpu_custom_call" | custom-call | flops 7000000000 | bytes 20000000 | tf_op jit(solution)/shard_map/g_normed/pallas_call | solution.py:627
  518.1 23.3 %collective-permute-done.35 = bf16[6,128,1024]{2,1,0:T(8,128)(2,1)} collective-permute-done((bf16[6,128,1024]{2,1,0:T(8,128)(2,1)}, bf16[6,128,1024]{2,1,0:T(8,128)(2,1)}, u32[]{:S(2)}, u32[]{:S(2)}) %collective-permute-start.35) | collective-permute-done | bytes 1572896 | tf_op jit(solution)/shard_map/ppermute | solution.py:651
  545.3 21.6 %reduce-scatter.5.cloned.1.call-done = bf16[960,256]{1,0:T(8,128)(2,1)} async-done(((bf16[7680,256]{1,0:T(8,128)(2,1)}), bf16[960,256]{1,0:T(8,128)(2,1)}) %reduce-scatter.5.cloned.1.call-update) | async-done | bytes 491536 | tf_op jit(solution)/shard_map/reduce_scatter | solution.py:907
  (306 shorter events, 165.3 us)
Async XLA Ops:
  7.2 78.4 %all-gather.5.cloned.1.call-start = ((), (), s32[]{:S(2)}) async-start(), calls=%async_computation.6 | async-start | bytes 3833856 | tf_op jit(solution)/shard_map/all_gather | solution.py:698
  23.3 204.2 %all-gather.7.cloned.1.call-start = ((), (), s32[]{:S(2)}) async-start(), calls=%async_computation.7 | async-start | bytes 7077888 | tf_op jit(solution)/shard_map/all_gather | solution.py:699
  30.0 437.0 %reduce-scatter.3.cloned.1.call-start = ((), (), s32[]{:S(2)}) async-start(), calls=%async_computation.4 | async-start | bytes 4718592 | tf_op jit(solution)/shard_map/reduce_scatter | solution.py:777
  30.0 36.8 %collective-permute-start.1 = (bf16[6,128,1024]{2,1,0:T(8,128)(2,1)}, bf16[6,128,1024]{2,1,0:T(8,128)(2,1)}, u32[]{:S(2)}, u32[]{:S(2)}) collective-permute-start(bf16[6,128,1024]{2,1,0:T(8,128)(2,1)} %t0.1), channel_id=1, source_target_pairs={{0,16},{8,24},{16,0},{24,8},{1,17},{9,25},{17,1},{25,9},{2,18},{10... | collective-permute-start | bytes 4718600 | tf_op jit(solution)/shard_map/ppermute | solution.py:651
  30.4 61.1 %collective-permute-start = (bf16[6,128,1024]{2,1,0:T(8,128)(2,1)}, bf16[6,128,1024]{2,1,0:T(8,128)(2,1)}, u32[]{:S(2)}, u32[]{:S(2)}) collective-permute-start(bf16[6,128,1024]{2,1,0:T(8,128)(2,1)} %t0.1), channel_id=1, source_target_pairs={{0,8},{8,0},{16,24},{24,16},{1,9},{9,1},{17,25},{25,17},{2,10},{10... | collective-permute-start | bytes 4718600 | tf_op jit(solution)/shard_map/ppermute | solution.py:651
  66.9 24.6 %collective-permute-start.2 = (bf16[6,128,1024]{2,1,0:T(8,128)(2,1)}, bf16[6,128,1024]{2,1,0:T(8,128)(2,1)}, u32[]{:S(2)}, u32[]{:S(2)}) collective-permute-start(bf16[6,128,1024]{2,1,0:T(8,128)(2,1)} %collective-permute-done.1.t2), channel_id=1, source_target_pairs={{0,8},{8,0},{16,24},{24,16},{1,9},{9,1},{17,25},{25,17},{2,10},{10... | collective-permute-start | bytes 4718600 | tf_op jit(solution)/shard_map/ppermute | solution.py:651
  66.9 41.5 %collective-permute-start.7 = (bf16[6,128,1024]{2,1,0:T(8,128)(2,1)}, bf16[6,128,1024]{2,1,0:T(8,128)(2,1)}, u32[]{:S(2)}, u32[]{:S(2)}) collective-permute-start(bf16[6,128,1024]{2,1,0:T(8,128)(2,1)} %grad_ref.1), channel_id=1, source_target_pairs={{0,16},{8,24},{16,0},{24,8},{1,17},{9,25},{17,1},{25,9},{2,18},{10... | collective-permute-start | bytes 4718600 | tf_op jit(solution)/shard_map/ppermute | solution.py:651
  108.4 25.4 %collective-permute-start.8 = (bf16[1056,256]{1,0:T(8,128)(2,1)}, bf16[1056,256]{1,0:T(8,128)(2,1)S(1)}, u32[]{:S(2)}, u32[]{:S(2)}) collective-permute-start(bf16[1056,256]{1,0:T(8,128)(2,1)} %bitcast.232), channel_id=1, source_target_pairs={{0,8},{8,0},{16,24},{24,16},{1,9},{9,1},{17,25},{25,17},{2,10},{10... | collective-permute-start | bytes 1622024 | tf_op jit(solution)/shard_map/ppermute | solution.py:651
  108.4 25.5 %collective-permute-start.9 = (bf16[1056,256]{1,0:T(8,128)(2,1)}, bf16[1056,256]{1,0:T(8,128)(2,1)S(1)}, u32[]{:S(2)}, u32[]{:S(2)}) collective-permute-start(bf16[1056,256]{1,0:T(8,128)(2,1)} %bitcast.233), channel_id=1, source_target_pairs={{0,16},{8,24},{16,0},{24,8},{1,17},{9,25},{17,1},{25,9},{2,18},{10... | collective-permute-start | bytes 1622024 | tf_op jit(solution)/shard_map/ppermute | solution.py:651
  112.3 61.2 %collective-permute-start.11 = (bf16[6,128,1024]{2,1,0:T(8,128)(2,1)}, bf16[6,128,1024]{2,1,0:T(8,128)(2,1)}, u32[]{:S(2)}, u32[]{:S(2)}) collective-permute-start(bf16[6,128,1024]{2,1,0:T(8,128)(2,1)} %grad_ref.1), channel_id=1, source_target_pairs={{0,8},{8,0},{16,24},{24,16},{1,9},{9,1},{17,25},{25,17},{2,10},{10... | collective-permute-start | bytes 4718600 | tf_op jit(solution)/shard_map/ppermute | solution.py:651
  112.6 61.0 %collective-permute-start.12 = (bf16[6,128,1024]{2,1,0:T(8,128)(2,1)}, bf16[6,128,1024]{2,1,0:T(8,128)(2,1)}, u32[]{:S(2)}, u32[]{:S(2)}) collective-permute-start(bf16[6,128,1024]{2,1,0:T(8,128)(2,1)} %collective-permute-done.7.g2), channel_id=1, source_target_pairs={{0,8},{8,0},{16,24},{24,16},{1,9},{9,1},{17,25},{25,17},{2,10},{10... | collective-permute-start | bytes 4718600 | tf_op jit(solution)/shard_map/ppermute | solution.py:651
  112.9 19.2 %collective-permute-start.3 = (bf16[4,176,256]{2,1,0:T(8,128)(2,1)S(1)}, bf16[4,176,256]{2,1,0:T(8,128)(2,1)S(1)}, u32[]{:S(2)}, u32[]{:S(2)}) collective-permute-start(bf16[4,176,256]{2,1,0:T(8,128)(2,1)S(1)} %slice.158), channel_id=1, source_target_pairs={{0,1},{1,2},{2,3},{3,4},{4,5},{5,6},{6,7},{8,9},{9,10},{10,11},{11... | collective-permute-start | bytes 1081352 | tf_op jit(solution)/shard_map/ppermute | solution.py:24
  133.9 39.6 %collective-permute-start.13 = (bf16[1,512,512]{2,1,0:T(8,128)(2,1)S(1)}, bf16[1,512,512]{2,1,0:T(8,128)(2,1)S(1)}, u32[]{:S(2)}, u32[]{:S(2)}) collective-permute-start(bf16[1,512,512]{2,1,0:T(8,128)(2,1)S(1)} %get-tuple-element.270), channel_id=1, source_target_pairs={{0,1},{1,2},{2,3},{3,4},{4,5},{5,6},{6,7},{8,9},{9,10},{10,11},{11... | collective-permute-start | bytes 1572872 | tf_op jit(solution)/shard_map/ppermute | solution.py:24
  197.7 14.5 %collective-permute-start.16 = (bf16[2,512,256]{2,1,0:T(8,128)(2,1)}, bf16[2,512,256]{2,1,0:T(8,128)(2,1)S(1)}, u32[]{:S(2)}, u32[]{:S(2)}) collective-permute-start(bf16[2,512,256]{2,1,0:T(8,128)(2,1)} %get-tuple-element.101), channel_id=1, source_target_pairs={{0,16},{8,24},{16,0},{24,8},{1,17},{9,25},{17,1},{25,9},{2,18},{10... | collective-permute-start | bytes 1572872 | tf_op jit(solution)/shard_map/ppermute | solution.py:651
  289.1 15.0 %collective-permute-start.22 = (bf16[2,6,128,1024]{3,2,1,0:T(8,128)(2,1)}, bf16[2,6,128,1024]{3,2,1,0:T(8,128)(2,1)}, u32[]{:S(2)}, u32[]{:S(2)}) collective-permute-start(bf16[2,6,128,1024]{3,2,1,0:T(8,128)(2,1)} %get-tuple-element.111), channel_id=1, source_target_pairs={{0,8},{8,0},{16,24},{24,16},{1,9},{9,1},{17,25},{25,17},{2,10},{10... | collective-permute-start | bytes 9437192 | tf_op jit(solution)/shard_map/ppermute | solution.py:651
  302.3 36.8 %collective-permute-start.24 = (bf16[6,128,1024]{2,1,0:T(8,128)(2,1)}, bf16[6,128,1024]{2,1,0:T(8,128)(2,1)}, u32[]{:S(2)}, u32[]{:S(2)}) collective-permute-start(bf16[6,128,1024]{2,1,0:T(8,128)(2,1)} %fusion.20), channel_id=1, source_target_pairs={{0,16},{8,24},{16,0},{24,8},{1,17},{9,25},{17,1},{25,9},{2,18},{10... | collective-permute-start | bytes 4718600 | tf_op jit(solution)/shard_map/ppermute | solution.py:651
  304.0 262.8 %reduce-scatter.5.cloned.1.call-start = ((), (), s32[]{:S(2)}) async-start(), calls=%async_computation.5 | async-start | bytes 4423680 | tf_op jit(solution)/shard_map/reduce_scatter | solution.py:907
  350.2 17.9 %collective-permute-start.27 = (bf16[6,128,256]{2,1,0:T(8,128)(2,1)}, bf16[6,128,256]{2,1,0:T(8,128)(2,1)S(1)}, u32[]{:S(2)}, u32[]{:S(2)}) collective-permute-start(bf16[6,128,256]{2,1,0:T(8,128)(2,1)} %get-tuple-element.118), channel_id=1, source_target_pairs={{0,24},{8,16},{16,8},{24,0},{1,25},{9,17},{17,9},{25,1},{2,26},{10... | collective-permute-start | bytes 1179656 | tf_op jit(solution)/shard_map/ppermute | solution.py:651
  368.9 29.0 %collective-permute-start.28 = (bf16[2,256,1024]{2,1,0:T(8,128)(2,1)S(1)}, bf16[2,256,1024]{2,1,0:T(8,128)(2,1)S(1)}, u32[]{:S(2)}, u32[]{:S(2)}) collective-permute-start(bf16[2,256,1024]{2,1,0:T(8,128)(2,1)S(1)} %pad_maximum_fusion.5), channel_id=1, source_target_pairs={{0,8},{8,0},{16,24},{24,16},{1,9},{9,1},{17,25},{25,17},{2,10},{10... | collective-permute-start | bytes 3145736 | tf_op jit(solution)/shard_map/ppermute | solution.py:651
  400.9 31.7 %collective-permute-start.29 = (bf16[1216,512]{1,0:T(8,128)(2,1)}, bf16[1216,512]{1,0:T(8,128)(2,1)}, u32[]{:S(2)}, u32[]{:S(2)}) collective-permute-start(bf16[1216,512]{1,0:T(8,128)(2,1)} %get-tuple-element.132), channel_id=1, source_target_pairs={{1,0},{2,1},{3,2},{4,3},{5,4},{6,5},{7,6},{9,8},{10,9},{11,10},{12... | collective-permute-start | bytes 3735560 | tf_op jit(solution)/shard_map/ppermute | solution.py:24
  406.5 60.4 %collective-permute-start.32 = (bf16[6,128,1024]{2,1,0:T(8,128)(2,1)S(1)}, bf16[6,128,1024]{2,1,0:T(8,128)(2,1)}, u32[]{:S(2)}, u32[]{:S(2)}) collective-permute-start(bf16[6,128,1024]{2,1,0:T(8,128)(2,1)S(1)} %copy-done.15), channel_id=1, source_target_pairs={{0,16},{8,24},{16,0},{24,8},{1,17},{9,25},{17,1},{25,9},{2,18},{10... | collective-permute-start | bytes 4718600 | tf_op jit(solution)/shard_map/ppermute | solution.py:651
  408.2 58.7 %collective-permute-start.33 = (bf16[256,1024]{1,0:T(8,128)(2,1)}, bf16[256,1024]{1,0:T(8,128)(2,1)}, u32[]{:S(2)}, u32[]{:S(2)}) collective-permute-start(bf16[256,1024]{1,0:T(8,128)(2,1)} %fusion.31), channel_id=1, source_target_pairs={{0,16},{8,24},{16,0},{24,8},{1,17},{9,25},{17,1},{25,9},{2,18},{10... | collective-permute-start | bytes 1572872 | tf_op jit(solution)/shard_map/ppermute | solution.py:651
  449.8 16.1 %collective-permute-start.31 = (bf16[1056,256]{1,0:T(8,128)(2,1)S(1)}, bf16[1056,256]{1,0:T(8,128)(2,1)S(1)}, u32[]{:S(2)}, u32[]{:S(2)}) collective-permute-start(bf16[1056,256]{1,0:T(8,128)(2,1)S(1)} %fusion.36), channel_id=1, source_target_pairs={{0,16},{8,24},{16,0},{24,8},{1,17},{9,25},{17,1},{25,9},{2,18},{10... | collective-permute-start | bytes 1622024 | tf_op jit(solution)/shard_map/ppermute | solution.py:651
  504.6 36.8 %collective-permute-start.35 = (bf16[6,128,1024]{2,1,0:T(8,128)(2,1)}, bf16[6,128,1024]{2,1,0:T(8,128)(2,1)}, u32[]{:S(2)}, u32[]{:S(2)}) collective-permute-start(bf16[6,128,1024]{2,1,0:T(8,128)(2,1)} %fusion.21), channel_id=1, source_target_pairs={{0,16},{8,24},{16,0},{24,8},{1,17},{9,25},{17,1},{25,9},{2,18},{10... | collective-permute-start | bytes 4718600 | tf_op jit(solution)/shard_map/ppermute | solution.py:651
  (66 other events, 651.2 us)
Sparse Core Ops, SparseCore 0:
  23.4 62.0 all-gather.4
  87.7 112.0 all-gather.6
  304.1 86.0 reduce-scatter.2
  481.2 85.5 reduce-scatter.4

commit v9 on v8

--- a/solution.py
+++ b/solution.py
@@ -422,7 +422,7 @@
 def ffn_kernel(
     head_ref, a0, a1, a2, a3, o0, o1, o2, o3, t0, t1, t2, t3, g0, g1, g2, g3, gain_ref,
     up_ref, down_ref, f_keep, f_sent, n_keep, n_sent, hidden_ref, pack_ref,
-    rows, grads, acc_up, acc_down,
+    acc_up, acc_down,
 ):
     step = pl.program_id(0)
     head = head_ref[0]
@@ -436,19 +436,19 @@
         acc_up[...] = jnp.zeros_like(acc_up)
         acc_down[...] = jnp.zeros_like(acc_down)
 
-    place_rows(head, (t0, t1, t2, t3), rows)
-    place_rows(head, (g0, g1, g2, g3), grads)
-    hidden = rows[...]
+    starts = [
+        pl.multiple_of(jnp.bitwise_xor(head, bits) * quarter, quarter) for bits in range(4)
+    ]
+    hidden = jnp.concatenate([t[0] for t in (t0, t1, t2, t3)], 0).astype(jnp.float32)
     for a, o in ((a0, o0), (a1, o1), (a2, o2), (a3, o3)):
+        part = jnp.concatenate([a[0, pl.ds(at, quarter), :] for at in starts], 0)
         hidden = hidden + jnp.dot(
-            a[0], o[...].reshape(a.shape[2], width), preferred_element_type=jnp.float32
+            part, o[...].reshape(a.shape[2], width), preferred_element_type=jnp.float32
         )
-    rows[...] = hidden
-    at = pl.multiple_of(head * quarter, quarter)
-    hidden_ref[0] = rows[pl.ds(at, quarter), :]
+    hidden_ref[0] = hidden[:quarter]
     unit, _ = row_norm(hidden)
     normed = (unit * gain_ref[...]).astype(jnp.bfloat16)
-    grad = grads[...]
+    grad = jnp.concatenate([g[0] for g in (g0, g1, g2, g3)], 0)
     result = jnp.zeros(hidden.shape, jnp.float32)
     g_normed = jnp.zeros(hidden.shape, jnp.float32)
     for n in range(2):
@@ -465,10 +465,10 @@
         g_normed = g_normed + jnp.dot(g_lifted, up, preferred_element_type=jnp.float32)
         acc_down[n] += lax.dot_general(active, grad, ROWS_IN, preferred_element_type=jnp.float32)
         acc_up[n] += lax.dot_general(g_lifted, normed, ROWS_IN, preferred_element_type=jnp.float32)
-    rows[...] = g_normed
-    hand_out(head, rows, n_keep, n_sent)
-    rows[...] = result
-    hand_out(head, rows, f_keep, f_sent)
+    for value, keep, sent in ((g_normed, n_keep, n_sent), (result, f_keep, f_sent)):
+        value = value.astype(jnp.bfloat16)
+        for bits, (ref, slot) in enumerate(((keep, 0), (sent, 0), (keep, 1), (sent, 1))):
+            ref[slot, 0] = value[bits * quarter : (bits + 1) * quarter]
 
     @pl.when(step == pl.num_programs(0) - 1)
     def _():
@@ -529,8 +529,6 @@
             jax.ShapeDtypeStruct(grad_shape, jnp.bfloat16),
         ],
         scratch_shapes=[
-            pltpu.VMEM((seg_len, width), jnp.float32),
-            pltpu.VMEM((seg_len, width), jnp.bfloat16),
             pltpu.VMEM((2, half, width), jnp.float32),
             pltpu.VMEM((2, half, width), jnp.float32),
         ],
@@ -720,9 +718,19 @@
         head, token_pieces, gain_first, weights, pad_rows
     )
     compressed = packed_mine[:, :comp_rows]
-    recv_packed, recv_mem = passed_along(
-        (packed_mine[seg_count - window :], heads[seg_count - 1 :, :, : 2 * head_cols]), "blk", 1
-    )
+    pair = 2 * head_cols
+    tail_rows = packed_mine[seg_count - window :].reshape(window * pad_rows, head_cols)
+    half_rows = window * pad_rows // 2
+    onward = jnp.concatenate(
+        [
+            heads[seg_count - 1, :, :pair],
+            jnp.concatenate([tail_rows[:half_rows], tail_rows[half_rows:]], 1),
+        ],
+        0,
+    )
+    recv = passed_along(onward, "blk", 1)
+    recv_mem = recv[None, :seg_len]
+    recv_packed = jnp.concatenate([recv[seg_len:, :head_cols], recv[seg_len:, head_cols:]], 0)
 
     def all_columns(value):
         value = value.reshape(-1, head_cols)
@@ -743,7 +751,7 @@
     grad_pieces = (grad_held, head_swap(grad_held, 1), grad_far, head_swap(grad_far, 1))
     packed = all_columns(packed_mine)
     comp_pair = comp_pairs(packed)
-    comp_pair, grad_pieces, recv_mem = lax.optimization_barrier((comp_pair, grad_pieces, recv_mem))
+    comp_pair, grad_pieces = lax.optimization_barrier((comp_pair, grad_pieces))
     comp_ext = jnp.concatenate([comp_pairs(all_columns(recv_packed)), comp_pair], 0)
     order = jnp.arange(lengths.shape[0], dtype=jnp.int32)
     starts = jnp.sum(jnp.where(order[None, :] < order[:, None], lengths[None, :], 0), axis=1)
@@ -809,12 +817,36 @@
     wo_got = head_swap(wo_sent, 1).astype(jnp.float32)
     wo_far = (grad_wo[2].astype(jnp.float32) + wo_got[1]).astype(bf16)
     back, wo_far, held = lax.optimization_barrier((back, wo_far, held))
-    got_back = passed_along(back, "blk", -1).astype(jnp.float32)
+    got_back = passed_along(back, "blk", -1)
     query_two, pair_two, held, rest, _ = backward(window, seg_count, held, over, mixed)
     grad_hidden = grad_hidden.reshape(token_count, width)
+    grad_query = jnp.concatenate([query_one, query_two], 0)
+    normed = normed.reshape(full_count, width)
+    grad_wq = lax.dot_general(
+        normed, grad_query.reshape(full_count, head_cols), ROWS_IN, preferred_element_type=jnp.float32
+    )
+    wo_far = head_swap(wo_far, 2).astype(jnp.float32)
+    grad_wo = (grad_wo[0].astype(jnp.float32) + wo_got[0] + wo_far).astype(bf16)
+
+    def by_owner(value):
+        return value.astype(bf16).reshape(
+            head_groups, blk_count, part, value.shape[1]
+        ).transpose(1, 0, 2, 3)
+
+    query_grads = jnp.concatenate(
+        [
+            by_owner(grad_wq),
+            grad_wo.reshape(blk_count, part, head_groups, head_cols).transpose(0, 2, 1, 3),
+        ],
+        2,
+    )
+    query_grads, first_sum, got_back = lax.optimization_barrier((query_grads, first_sum, got_back))
+    got_back = got_back.astype(jnp.float32)
+    query_part = lax.psum_scatter(
+        query_grads.reshape(-1, head_cols), "blk", scatter_dimension=0, tiled=True
+    ).reshape(head_groups, 2 * part, head_cols)
     last_pair = (held + got_back[window * pad_rows :]).astype(bf16)
     grad_pair = jnp.concatenate([pair_one, pair_two, last_pair[None]], 0)
-    grad_query = jnp.concatenate([query_one, query_two], 0)
     got_comp = got_back[: window * pad_rows].reshape(window, pad_rows, 2 * head_cols)
     comp_pair_grad = jnp.pad(rest, ((0, seg_count - rest.shape[0]), (0, 0), (0, 0))) + jnp.pad(
         got_comp, ((seg_count - window, 0), (0, 0), (0, 0))
@@ -824,9 +856,8 @@
         comp_grad_rows, wkv, COLS_IN, preferred_element_type=jnp.float32
     ).astype(bf16)
 
-    grad_packed_part, grad_query, grad_pair = lax.optimization_barrier(
-        (grad_packed_part, grad_query, grad_pair)
-    )
+    grad_packed_part, grad_pair = lax.optimization_barrier((grad_packed_part, grad_pair))
+
     def columns_of(bits):
         start = jnp.bitwise_xor(head_index, bits) * head_cols
         return lax.dynamic_slice_in_dim(grad_packed_part, start, head_cols, 1)
@@ -834,14 +865,11 @@
     grad_packed = sum_over_heads(
         (columns_of(0), columns_of(2)), jnp.stack([columns_of(1), columns_of(3)])
     ).astype(bf16)
-    f_far, wo_far = head_swap(f_far, 2), head_swap(wo_far, 2)
-    grad_packed, f_far, first_sum, wo_far = lax.optimization_barrier(
-        (grad_packed, f_far, first_sum, wo_far)
-    )
+    f_far = head_swap(f_far, 2)
+    grad_packed, f_far = lax.optimization_barrier((grad_packed, f_far))
     out_tokens = (
         hidden + f_keep[0].astype(jnp.float32) + f_got[0].astype(jnp.float32) + f_far.astype(jnp.float32)
     ).astype(bf16)
-    grad_wo = (grad_wo[0].astype(jnp.float32) + wo_got[0] + wo_far.astype(jnp.float32)).astype(bf16)
     keep, sent = g_normed_parts(
         head,
         grad_query,
@@ -857,11 +885,7 @@
         .astype(bf16)
         .reshape(tokens.shape)
     )
-    normed = normed.reshape(full_count, width)
     grad_kv = grad_pair.reshape(full_count, 2 * head_cols)
-    grad_wq = lax.dot_general(
-        normed, grad_query.reshape(full_count, head_cols), ROWS_IN, preferred_element_type=jnp.float32
-    )
     grad_wkv = lax.dot_general(normed, grad_kv, ROWS_IN, preferred_element_type=jnp.float32)
     comp_term = lax.dot_general(packed, comp_grad_rows, ROWS_IN, preferred_element_type=jnp.float32)
     grad_comp = lax.dot_general(
@@ -877,11 +901,6 @@
     ) / gain_first[0]
     grad_wkv = grad_wkv + comp_term
 
-    def by_owner(value):
-        return value.astype(bf16).reshape(
-            head_groups, blk_count, part, value.shape[1]
-        ).transpose(1, 0, 2, 3)
-
     gain_rows = (
         jnp.stack([grad_gain_one, grad_gain_two])
         .reshape(2, head_groups, blk_count, part)
@@ -890,47 +909,48 @@
     )
     second_grads = jnp.concatenate(
         [
-            by_owner(grad_wq),
             by_owner(grad_wkv[:, :head_cols]),
             by_owner(grad_wkv[:, head_cols:]),
             by_owner(grad_comp[0]),
             by_owner(grad_comp[1]),
             by_owner(grad_comp[2]),
             jnp.pad(gain_rows, ((0, 0), (0, 0), (0, 14), (0, head_cols - part))),
-            grad_wo.reshape(blk_count, part, head_groups, head_cols).transpose(0, 2, 1, 3),
         ],
         2,
     )
-    second_grads, first_sum = lax.optimization_barrier((second_grads, first_sum))
+    second_grads, query_part = lax.optimization_barrier((second_grads, query_part))
     first_sum = first_sum.astype(jnp.float32)
-    own_rows = 6 * part + 16
+    own_rows = 5 * part + 16
     second_part = lax.psum_scatter(
         second_grads.reshape(-1, head_cols), "blk", scatter_dimension=0, tiled=True
-    ).reshape(head_groups, own_rows + part, head_cols)
+    ).reshape(head_groups, own_rows, head_cols)
     second_sum = lax.all_to_all(
-        second_part[:, :own_rows], "head", split_axis=0, concat_axis=0, tiled=True
+        second_part, "head", split_axis=0, concat_axis=0, tiled=True
     ).astype(jnp.float32)
-    gain_sum = jnp.sum(second_sum[:, 6 * part : 6 * part + 2, :part], axis=0)
+    query_sum = lax.all_to_all(
+        query_part[:, :part], "head", split_axis=0, concat_axis=0, tiled=True
+    ).astype(jnp.float32)
+    gain_sum = jnp.sum(second_sum[:, 5 * part : 5 * part + 2, :part], axis=0)
     weight_sum = (
-        second_sum[:, : 6 * part]
-        .reshape(head_groups, 6, part, head_cols)
+        second_sum[:, : 5 * part]
+        .reshape(head_groups, 5, part, head_cols)
         .transpose(1, 2, 0, 3)
-        .reshape(6, part, width)
-    )
-    wo_sum = second_part[:, own_rows:].astype(jnp.float32).transpose(1, 0, 2).reshape(part, width)
+        .reshape(5, part, width)
+    )
+    wo_sum = query_part[:, part:].astype(jnp.float32).transpose(1, 0, 2).reshape(part, width)
     return (
         out_tokens,
         compressed,
         grad_tokens,
+        query_sum.transpose(1, 0, 2).reshape(part, width),
         weight_sum[0],
         weight_sum[1],
-        weight_sum[2],
         wo_sum,
         first_sum[:ff_part].T,
         first_sum[ff_part:],
         gain_sum[0],
         gain_sum[1],
-        weight_sum[3:],
+        weight_sum[2:],
     )
 
 

time: 600 us -> 612 us (1.020)
  local copies, waits for them, and re-layouts: 48.2 us -> 55.1 us
    ppermute x33, waiting for transfers between devices: 159 us -> 124 us  [head_swap(): lax.ppermute(value, 'head', [(source, source ^ bit) for source in range(c...]
    reduce_scatter x0 -> x1, waiting for transfers between devices: none -> 24.7 us  [per_device(): lax.psum_scatter(query_grads.reshape(-1, head_cols), 'blk', scatter_dimen...]
    all_to_all x1 -> x2, waiting for transfers between devices: 1.51 us -> 22.1 us  [the longest x1 18.8 us: per_device(): lax.all_to_all(query_part[:, :part], 'head', split_axis=0, concat_axis=0,...]
    ppermute x3 -> x2, waiting for transfers between devices: 49 us -> 37.1 us  [passed_along(): lax.ppermute(value, axis, [(source, source + steps) for source in range(l...]
    reduce_scatter x1, waiting for transfers between devices: 21.6 us -> 27.9 us  [per_device(): lax.psum_scatter(second_grads.reshape(-1, head_cols), 'blk', scatter_dime...]
    unnamed x121 -> x120, local copies, waits for them, and re-layouts: 20.1 us -> 25.5 us
  transfers between devices with their start and end apart: 41 -> 42, of which waited for: 21 -> 21; matrix products, arithmetic and copies ran while one was open for 14% -> 17% of each run, Pallas kernels for 19% -> 18%
where the time goes in v9:
time: 612 us; the launch traced here: 602 us
  waiting for transfers between devices  253 us (41%)
  Pallas kernels  170 us (28%)
  local copies, waits for them, and re-layouts  55.1 us (9%)
  other arithmetic  39.4 us (6%)
  starting transfers between devices  29.6 us (5%)
  matrix products  28.5 us (5%)
  between operations  15.4 us (3%)
  blocking collectives  10.9 us (2%)
    ppermute x33, waiting for transfers between devices, head_swap(): lax.ppermute(value, 'head', [(source, source ^ bit) for source in range(c...  124 us
    pallas_call x1, Pallas kernels, feed_forward(): pl.pallas_call(ffn_kernel, grid=(count,), in_specs=[pl.BlockSpec(memory_s...  59.5 us
    pallas_call x2, Pallas kernels, attend_bwd(): pl.pallas_call(functools.partial(bwd_kernel, first), grid=(count,), in_sp...  43.2 us
    ppermute x2, waiting for transfers between devices, passed_along(): lax.ppermute(value, axis, [(source, source + steps) for source in range(l...  37.1 us
    reduce_scatter x1, waiting for transfers between devices, per_device(): lax.psum_scatter(second_grads.reshape(-1, head_cols), 'blk', scatter_dime...  27.9 us
    pallas_call x3, Pallas kernels, attend_fwd(): pl.pallas_call(functools.partial(fwd_kernel, first, shift), grid=(count,)...  26.8 us
    unnamed x120, local copies, waits for them, and re-layouts  25.5 us
    reduce_scatter x1, waiting for transfers between devices, per_device(): lax.psum_scatter(query_grads.reshape(-1, head_cols), 'blk', scatter_dimen...  24.7 us
  transfers between devices with their start and end apart: 42, of which 21 were waited for; matrix products, arithmetic and copies ran while one was open for 17% of the time, Pallas kernels for 18%

profile of v9, /device:TPU:24, one launch (start us, length us, event | category | flops | bytes accessed | tf_op | source)
XLA Modules:
  0.0 601.6 jit_solution(16697165583037822649)
XLA Ops:
  12.4 10.9 %all_to_all.15 = bf16[4,208,256]{2,1,0:T(8,128)(2,1)} all-to-all(bf16[4,208,256]{2,1,0:T(8,128)(2,1)S(1)} %copy.240), channel_id=1, replica_groups=mesh['head'=4,'blk'=8] {'head'}, dimensions={0} | all-to-all | bytes 851968 | tf_op jit(solution)/shard_map/all_to_all | solution.py:694
  30.4 36.4 %collective-permute-done.1.t2 = bf16[6,128,1024]{2,1,0:T(8,128)(2,1)} collective-permute-done((bf16[6,128,1024]{2,1,0:T(8,128)(2,1)}, bf16[6,128,1024]{2,1,0:T(8,128)(2,1)}, u32[]{:S(2)}, u32[]{:S(2)}) %collective-permute-start.1) | collective-permute-done | bytes 1572896 | tf_op jit(solution)/shard_map/ppermute | solution.py:649
  68.5 17.0 %all-gather.5.cloned.1.call-done = bf16[32,208,256]{2,1,0:T(8,128)(2,1)} async-done(((bf16[4,208,256]{2,1,0:T(8,128)(2,1)}), bf16[32,208,256]{2,1,0:T(8,128)(2,1)}) %all-gather.5.cloned.1.call-update) | async-done | bytes 3407888 | tf_op jit(solution)/shard_map/all_gather | solution.py:696
  91.5 16.8 %prepare.1 = (bf16[6,512,768]{2,1,0:T(8,128)(2,1)}, bf16[6,512,1024]{2,1,0:T(8,128)(2,1)}, bf16[6,176,3072]{2,1,0:T(8,128)(2,1)}, bf16[6,176,256]{2,1,0:T(8,128)(2,1)}) custom-call(s32[1]{0:T(128)} %bitcast.head_ref, bf16[6,128,1024]{2,1,0:T(8,128)(2,1)} %t0.1, bf16[6,128,1024]{2,1,0:T(8,128)(2,1)} %collective-permute-done.t1, ...), custom_call_target="tpu_custom_call" | custom-call | flops 7000000000 | bytes 30000000 | tf_op jit(solution)/shard_map/prepare/pallas_call | solution.py:397
  123.5 34.7 %collective-permute-done.3 = bf16[864,512]{1,0:T(8,128)(2,1)S(1)} collective-permute-done((bf16[864,512]{1,0:T(8,128)(2,1)S(1)}, bf16[864,512]{1,0:T(8,128)(2,1)S(1)}, u32[]{:S(2)}, u32[]{:S(2)}) %collective-permute-start.3) | collective-permute-done | bytes 884768 | tf_op jit(solution)/shard_map/ppermute | solution.py:24
  162.4 7.0 %collective-permute-done.5 = bf16[704,256]{1,0:T(8,128)(2,1)S(1)} collective-permute-done((bf16[704,256]{1,0:T(8,128)(2,1)S(1)}, bf16[704,256]{1,0:T(8,128)(2,1)S(1)}, u32[]{:S(2)}, u32[]{:S(2)}) %collective-permute-start.5) | collective-permute-done | bytes 360480 | tf_op jit(solution)/shard_map/ppermute | solution.py:649
  171.2 8.9 %attend_fwd.3 = (bf16[2,512,256]{2,1,0:T(8,128)(2,1)}, f32[2,2,512]{2,1,0:T(2,128)}) custom-call(s32[6]{0:T(128)} %fusion.51.place_ref, f32[2]{0:T(128)} %exponential_multiply_fusion.slope_ref, bf16[6,512,768]{2,1,0:T(8,128)(2,1)} %get-tuple-element.86.q_ref.own_ref.prev_ref, bf16[6,512,768]{2,1,0:T(8,128)(2,1)} %get-tuple-element.86.q_ref.own_ref.prev_ref, ...), custom_call_target="tpu_custom_call" | custom-call | flops 2000000000 | bytes 6000000 | tf_op jit(solution)/shard_map/attend_fwd/pallas_call | solution.py:230
  185.0 8.9 %attend_fwd.4 = (bf16[2,512,256]{2,1,0:T(8,128)(2,1)}, f32[2,2,512]{2,1,0:T(2,128)}) custom-call(s32[6]{0:T(128)} %fusion.51.place_ref, f32[2]{0:T(128)} %exponential_multiply_fusion.slope_ref, bf16[6,512,768]{2,1,0:T(8,128)(2,1)} %get-tuple-element.86.q_ref.own_ref.prev_ref, bf16[6,512,768]{2,1,0:T(8,128)(2,1)} %get-tuple-element.86.q_ref.own_ref.prev_ref, ...), custom_call_target="tpu_custom_call" | custom-call | flops 2000000000 | bytes 6000000 | tf_op jit(solution)/shard_map/attend_fwd/pallas_call | solution.py:230
  198.5 8.9 %attend_fwd.5 = (bf16[2,512,256]{2,1,0:T(8,128)(2,1)}, f32[2,2,512]{2,1,0:T(2,128)}) custom-call(s32[6]{0:T(128)} %fusion.51.place_ref, f32[2]{0:T(128)} %exponential_multiply_fusion.slope_ref, bf16[6,512,768]{2,1,0:T(8,128)(2,1)} %get-tuple-element.86.q_ref.own_ref.prev_ref, bf16[6,512,768]{2,1,0:T(8,128)(2,1)} %get-tuple-element.86.q_ref.own_ref.prev_ref, ...), custom_call_target="tpu_custom_call" | custom-call | flops 2000000000 | bytes 6000000 | tf_op jit(solution)/shard_map/attend_fwd/pallas_call | solution.py:230
  212.8 9.3 %collective-permute-done.16 = bf16[2,512,256]{2,1,0:T(8,128)(2,1)S(1)} collective-permute-done((bf16[2,512,256]{2,1,0:T(8,128)(2,1)}, bf16[2,512,256]{2,1,0:T(8,128)(2,1)S(1)}, u32[]{:S(2)}, u32[]{:S(2)}) %collective-permute-start.16) | collective-permute-done | bytes 524320 | tf_op jit(solution)/shard_map/ppermute | solution.py:649
  227.5 59.5 %feed_forward.1 = (bf16[2,6,128,1024]{3,2,1,0:T(8,128)(2,1)}, bf16[2,6,128,1024]{3,2,1,0:T(8,128)(2,1)}, bf16[2,6,128,1024]{3,2,1,0:T(8,128)(2,1)}, bf16[2,6,128...) custom-call(s32[1]{0:T(128)} %bitcast.head_ref, ...), custom_call_target="tpu_custom_call" | custom-call | flops 44999999488 | bytes 50000000 | tf_op jit(solution)/shard_map/feed_forward/pallas_call | solution.py:516
  287.7 5.4 collective-permute-done.22.got_ref
  307.4 26.2 %collective-permute-done.23.far_ref = bf16[6,128,1024]{2,1,0:T(8,128)(2,1)} collective-permute-done((bf16[6,128,1024]{2,1,0:T(8,128)(2,1)}, bf16[6,128,1024]{2,1,0:T(8,128)(2,1)}, u32[]{:S(2)}, u32[]{:S(2)}) %collective-permute-start.23) | collective-permute-done | bytes 1572896 | tf_op jit(solution)/shard_map/ppermute | solution.py:649
  333.6 9.3 %middle.1 = (f32[6,128,1024]{2,1,0:T(8,128)}, bf16[6,128,1024]{2,1,0:T(8,128)(2,1)}, f32[1,1024]{1,0:T(1,128)}, bf16[6,128,256]{2,1,0:T(8,128)(2,1)}, bf16[6,128...) custom-call(bf16[2,6,128,1024]{3,2,1,0:T(8,128)(2,1)} %get-tuple-element.110.keep_ref, ...), custom_call_target="tpu_custom_call" | custom-call | flops 1620000000 | bytes 24000000 | tf_op jit(solution)/shard_map/middle/pallas_call | solution.py:584
  349.8 5.4 collective-permute-done.25.g2
  355.2 7.5 %collective-permute-done.26.g3 = bf16[6,128,256]{2,1,0:T(8,128)(2,1)S(1)} collective-permute-done((bf16[6,128,256]{2,1,0:T(8,128)(2,1)}, bf16[6,128,256]{2,1,0:T(8,128)(2,1)S(1)}, u32[]{:S(2)}, u32[]{:S(2)}) %collective-permute-start.26) | collective-permute-done | bytes 393248 | tf_op jit(solution)/shard_map/ppermute | solution.py:649
  366.3 27.8 %attend_bwd.2 = (bf16[4,512,256]{2,1,0:T(8,128)(2,1)}, bf16[3,512,512]{2,1,0:T(8,128)(2,1)}, f32[512,512]{1,0:T(8,128)}, f32[2,176,512]{2,1,0:T(8,128)}, bf16[1216,512]{1,0:T(8,128)(2,1)}) custom-call(s32[6]{0:T(128)} %fusion.51.place_ref, f32[2]{0:T(128)} %exponential_multiply_fusion.slope_ref, ...), custom_call_target="tpu_custom_call" | custom-call | flops 8000000000 | bytes 16000000 | tf_op jit(solution)/shard_map/attend_bwd/pallas_call | solution.py:266
  399.9 15.4 %attend_bwd.3 = (bf16[2,512,256]{2,1,0:T(8,128)(2,1)}, bf16[2,512,512]{2,1,0:T(8,128)(2,1)}, f32[512,512]{1,0:T(8,128)}, f32[4,176,512]{2,1,0:T(8,128)}, bf16[16,512]{1,0:T(8,128)(2,1)}) custom-call(s32[6]{0:T(128)} %fusion.51.place_ref, f32[2]{0:T(128)} %exponential_multiply_fusion.slope_ref, bf16[6,512,768]{2,1,0:T(8,128)(2,1)} %get-tuple-element.86.q_ref.own_ref.prev_ref, ...), custom_call_target="tpu_custom_call" | custom-call | flops 4000000000 | bytes 8000000 | tf_op jit(solution)/shard_map/attend_bwd/pallas_call | solution.py:266
  446.7 10.2 %collective-permute-done.31 = bf16[1056,256]{1,0:T(8,128)(2,1)} collective-permute-done((bf16[1056,256]{1,0:T(8,128)(2,1)}, bf16[1056,256]{1,0:T(8,128)(2,1)}, u32[]{:S(2)}, u32[]{:S(2)}) %collective-permute-start.31) | collective-permute-done | bytes 540704 | tf_op jit(solution)/shard_map/ppermute | solution.py:649
  458.3 6.5 %fusion.16 = (f32[3072]{0:T(1024)S(1)}, bf16[3072,256]{1,0:T(8,128)(2,1)}) fusion(f32[3,4,8,32,256]{4,3,2,1,0:T(8,128)S(1)} %copy-done.5, bf16[1056,3072]{1,0:T(8,128)(2,1)} %bitcast.274, bf16[1056,256]{1,0:T(8,128)(2,1)S(1)} %fusion.39), kind=kOutput, calls=%fused_computation.25 | convolution fusion | flops 1663300608 | bytes 11759616 | tf_op jit(solution)/shard_map/dot_general | solution.py:891
  465.0 13.9 %g_normed.1 = (bf16[2,6,128,1024]{3,2,1,0:T(8,128)(2,1)}, bf16[2,6,128,1024]{3,2,1,0:T(8,128)(2,1)}) custom-call(s32[1]{0:T(128)} %bitcast.head_ref, bf16[6,512,256]{2,1,0:T(8,128)(2,1)} %copy-done.21, bf16[6,512,512]{2,1,0:T(8,128)(2,1)} %copy-done.7, bf16[6,176,256]{2,1,0:T(8,128)(2,1)} %bitcast.252, bf16[6,1024,256]{2,1,0:T(8,128)(2,1)} %bitcast.229), custom_call_target="tpu_custom_call" | custom-call | flops 7000000000 | bytes 20000000 | tf_op jit(solution)/shard_map/g_normed/pallas_call | solution.py:625
  482.4 24.7 %reduce-scatter.6.cloned.1.call-done = bf16[256,256]{1,0:T(8,128)(2,1)} async-done(((bf16[2048,256]{1,0:T(8,128)(2,1)}), bf16[256,256]{1,0:T(8,128)(2,1)}) %reduce-scatter.6.cloned.1.call-update) | async-done | bytes 131088 | tf_op jit(solution)/shard_map/reduce_scatter | solution.py:845
  529.7 18.8 %all-to-all-done.1 = bf16[4,32,256]{2,1,0:T(8,128)(2,1)S(1)} async-done(((bf16[4,32,256]{2,1,0:T(8,128)(2,1)}), bf16[4,32,256]{2,1,0:T(8,128)(2,1)S(1)}, u32[]{:S(2)}, u32[]{:S(2)}) %all-to-all-start.1) | async-done | bytes 65568 | tf_op jit(solution)/shard_map/all_to_all | solution.py:930
  553.1 27.9 %reduce-scatter.8.cloned.1.call-done = bf16[704,256]{1,0:T(8,128)(2,1)} async-done(((bf16[5632,256]{1,0:T(8,128)(2,1)}), bf16[704,256]{1,0:T(8,128)(2,1)}) %reduce-scatter.8.cloned.1.call-update) | async-done | bytes 360464 | tf_op jit(solution)/shard_map/reduce_scatter | solution.py:924
  (312 shorter events, 168.7 us)
Async XLA Ops:
  7.2 78.4 %all-gather.5.cloned.1.call-start = ((), (), s32[]{:S(2)}) async-start(), calls=%async_computation.9 | async-start | bytes 3833856 | tf_op jit(solution)/shard_map/all_gather | solution.py:696
  23.3 204.2 %all-gather.7.cloned.1.call-start = ((), (), s32[]{:S(2)}) async-start(), calls=%async_computation.10 | async-start | bytes 7077888 | tf_op jit(solution)/shard_map/all_gather | solution.py:697
  29.9 398.9 %reduce-scatter.4.cloned.1.call-start = ((), (), s32[]{:S(2)}) async-start(), calls=%async_computation.6 | async-start | bytes 4718592 | tf_op jit(solution)/shard_map/reduce_scatter | solution.py:785
  29.9 36.8 %collective-permute-start.1 = (bf16[6,128,1024]{2,1,0:T(8,128)(2,1)}, bf16[6,128,1024]{2,1,0:T(8,128)(2,1)}, u32[]{:S(2)}, u32[]{:S(2)}) collective-permute-start(bf16[6,128,1024]{2,1,0:T(8,128)(2,1)} %t0.1), channel_id=1, source_target_pairs={{0,16},{8,24},{16,0},{24,8},{1,17},{9,25},{17,1},{25,9},{2,18},{10... | collective-permute-start | bytes 4718600 | tf_op jit(solution)/shard_map/ppermute | solution.py:649
  30.4 61.1 %collective-permute-start = (bf16[6,128,1024]{2,1,0:T(8,128)(2,1)}, bf16[6,128,1024]{2,1,0:T(8,128)(2,1)}, u32[]{:S(2)}, u32[]{:S(2)}) collective-permute-start(bf16[6,128,1024]{2,1,0:T(8,128)(2,1)} %t0.1), channel_id=1, source_target_pairs={{0,8},{8,0},{16,24},{24,16},{1,9},{9,1},{17,25},{25,17},{2,10},{10... | collective-permute-start | bytes 4718600 | tf_op jit(solution)/shard_map/ppermute | solution.py:649
  66.8 24.7 %collective-permute-start.2 = (bf16[6,128,1024]{2,1,0:T(8,128)(2,1)}, bf16[6,128,1024]{2,1,0:T(8,128)(2,1)}, u32[]{:S(2)}, u32[]{:S(2)}) collective-permute-start(bf16[6,128,1024]{2,1,0:T(8,128)(2,1)} %collective-permute-done.1.t2), channel_id=1, source_target_pairs={{0,8},{8,0},{16,24},{24,16},{1,9},{9,1},{17,25},{25,17},{2,10},{10... | collective-permute-start | bytes 4718600 | tf_op jit(solution)/shard_map/ppermute | solution.py:649
  66.8 41.5 %collective-permute-start.7 = (bf16[6,128,1024]{2,1,0:T(8,128)(2,1)}, bf16[6,128,1024]{2,1,0:T(8,128)(2,1)}, u32[]{:S(2)}, u32[]{:S(2)}) collective-permute-start(bf16[6,128,1024]{2,1,0:T(8,128)(2,1)} %grad_ref.1), channel_id=1, source_target_pairs={{0,16},{8,24},{16,0},{24,8},{1,17},{9,25},{17,1},{25,9},{2,18},{10... | collective-permute-start | bytes 4718600 | tf_op jit(solution)/shard_map/ppermute | solution.py:649
  108.3 15.0 %collective-permute-start.8 = (bf16[1056,256]{1,0:T(8,128)(2,1)}, bf16[1056,256]{1,0:T(8,128)(2,1)S(1)}, u32[]{:S(2)}, u32[]{:S(2)}) collective-permute-start(bf16[1056,256]{1,0:T(8,128)(2,1)} %bitcast.243), channel_id=1, source_target_pairs={{0,8},{8,0},{16,24},{24,16},{1,9},{9,1},{17,25},{25,17},{2,10},{10... | collective-permute-start | bytes 1622024 | tf_op jit(solution)/shard_map/ppermute | solution.py:649
  113.2 45.0 %collective-permute-start.3 = (bf16[864,512]{1,0:T(8,128)(2,1)S(1)}, bf16[864,512]{1,0:T(8,128)(2,1)S(1)}, u32[]{:S(2)}, u32[]{:S(2)}) collective-permute-start(bf16[864,512]{1,0:T(8,128)(2,1)S(1)} %maximum_maximum_fusion), channel_id=1, source_target_pairs={{0,1},{1,2},{2,3},{3,4},{4,5},{5,6},{6,7},{8,9},{9,10},{10,11},{11... | collective-permute-start | bytes 2654216 | tf_op jit(solution)/shard_map/ppermute | solution.py:24
  116.9 52.6 %collective-permute-start.11 = (bf16[6,128,1024]{2,1,0:T(8,128)(2,1)}, bf16[6,128,1024]{2,1,0:T(8,128)(2,1)S(1)}, u32[]{:S(2)}, u32[]{:S(2)}) collective-permute-start(bf16[6,128,1024]{2,1,0:T(8,128)(2,1)} %grad_ref.1), channel_id=1, source_target_pairs={{0,8},{8,0},{16,24},{24,16},{1,9},{9,1},{17,25},{25,17},{2,10},{10... | collective-permute-start | bytes 4718600 | tf_op jit(solution)/shard_map/ppermute | solution.py:649
  117.0 52.6 %collective-permute-start.12 = (bf16[6,128,1024]{2,1,0:T(8,128)(2,1)}, bf16[6,128,1024]{2,1,0:T(8,128)(2,1)S(1)}, u32[]{:S(2)}, u32[]{:S(2)}) collective-permute-start(bf16[6,128,1024]{2,1,0:T(8,128)(2,1)} %collective-permute-done.7.g2), channel_id=1, source_target_pairs={{0,8},{8,0},{16,24},{24,16},{1,9},{9,1},{17,25},{25,17},{2,10},{10... | collective-permute-start | bytes 4718600 | tf_op jit(solution)/shard_map/ppermute | solution.py:649
  123.3 36.7 %collective-permute-start.10 = (bf16[1056,256]{1,0:T(8,128)(2,1)S(1)}, bf16[1056,256]{1,0:T(8,128)(2,1)S(1)}, u32[]{:S(2)}, u32[]{:S(2)}) collective-permute-start(bf16[1056,256]{1,0:T(8,128)(2,1)S(1)} %collective-permute-done.9), channel_id=1, source_target_pairs={{0,8},{8,0},{16,24},{24,16},{1,9},{9,1},{17,25},{25,17},{2,10},{10... | collective-permute-start | bytes 1622024 | tf_op jit(solution)/shard_map/ppermute | solution.py:649
  287.3 219.9 %reduce-scatter.6.cloned.1.call-start = ((), (), s32[]{:S(2)}) async-start(), calls=%async_computation.7 | async-start | bytes 1179648 | tf_op jit(solution)/shard_map/reduce_scatter | solution.py:845
  287.3 15.9 %collective-permute-start.21 = (bf16[2,6,128,1024]{3,2,1,0:T(8,128)(2,1)}, bf16[2,6,128,1024]{3,2,1,0:T(8,128)(2,1)}, u32[]{:S(2)}, u32[]{:S(2)}) collective-permute-start(bf16[2,6,128,1024]{3,2,1,0:T(8,128)(2,1)} %get-tuple-element.109), channel_id=1, source_target_pairs={{0,8},{8,0},{16,24},{24,16},{1,9},{9,1},{17,25},{25,17},{2,10},{10... | collective-permute-start | bytes 9437192 | tf_op jit(solution)/shard_map/ppermute | solution.py:649
  296.9 36.8 %collective-permute-start.23 = (bf16[6,128,1024]{2,1,0:T(8,128)(2,1)}, bf16[6,128,1024]{2,1,0:T(8,128)(2,1)}, u32[]{:S(2)}, u32[]{:S(2)}) collective-permute-start(bf16[6,128,1024]{2,1,0:T(8,128)(2,1)} %fusion.20), channel_id=1, source_target_pairs={{0,16},{8,24},{16,0},{24,8},{1,17},{9,25},{17,1},{25,9},{2,18},{10... | collective-permute-start | bytes 4718600 | tf_op jit(solution)/shard_map/ppermute | solution.py:649
  344.4 18.3 %collective-permute-start.26 = (bf16[6,128,256]{2,1,0:T(8,128)(2,1)}, bf16[6,128,256]{2,1,0:T(8,128)(2,1)S(1)}, u32[]{:S(2)}, u32[]{:S(2)}) collective-permute-start(bf16[6,128,256]{2,1,0:T(8,128)(2,1)} %get-tuple-element.116), channel_id=1, source_target_pairs={{0,24},{8,16},{16,8},{24,0},{1,25},{9,17},{17,9},{25,1},{2,26},{10... | collective-permute-start | bytes 1179656 | tf_op jit(solution)/shard_map/ppermute | solution.py:649
  363.5 31.9 %collective-permute-start.27 = (bf16[2,256,1024]{2,1,0:T(8,128)(2,1)}, bf16[2,256,1024]{2,1,0:T(8,128)(2,1)S(1)}, u32[]{:S(2)}, u32[]{:S(2)}) collective-permute-start(bf16[2,256,1024]{2,1,0:T(8,128)(2,1)} %pad_maximum_fusion.4), channel_id=1, source_target_pairs={{0,8},{8,0},{16,24},{24,16},{1,9},{9,1},{17,25},{25,17},{2,10},{10... | collective-permute-start | bytes 3145736 | tf_op jit(solution)/shard_map/ppermute | solution.py:649
  364.3 94.0 %collective-permute-start.32 = (bf16[6,128,1024]{2,1,0:T(8,128)(2,1)}, bf16[6,128,1024]{2,1,0:T(8,128)(2,1)}, u32[]{:S(2)}, u32[]{:S(2)}) collective-permute-start(bf16[6,128,1024]{2,1,0:T(8,128)(2,1)} %fusion.19), channel_id=1, source_target_pairs={{0,16},{8,24},{16,0},{24,8},{1,17},{9,25},{17,1},{25,9},{2,18},{10... | collective-permute-start | bytes 4718600 | tf_op jit(solution)/shard_map/ppermute | solution.py:649
  397.3 25.2 %collective-permute-start.28 = (bf16[256,1024]{1,0:T(8,128)(2,1)S(1)}, bf16[256,1024]{1,0:T(8,128)(2,1)}, u32[]{:S(2)}, u32[]{:S(2)}) collective-permute-start(bf16[256,1024]{1,0:T(8,128)(2,1)S(1)} %fusion.31), channel_id=1, source_target_pairs={{0,16},{8,24},{16,0},{24,8},{1,17},{9,25},{17,1},{25,9},{2,18},{10... | collective-permute-start | bytes 1572872 | tf_op jit(solution)/shard_map/ppermute | solution.py:649
  398.0 30.8 %collective-permute-start.29 = (bf16[1216,512]{1,0:T(8,128)(2,1)}, bf16[1216,512]{1,0:T(8,128)(2,1)S(1)}, u32[]{:S(2)}, u32[]{:S(2)}) collective-permute-start(bf16[1216,512]{1,0:T(8,128)(2,1)} %get-tuple-element.135), channel_id=1, source_target_pairs={{1,0},{2,1},{3,2},{4,3},{5,4},{6,5},{7,6},{9,8},{10,9},{11,10},{12... | collective-permute-start | bytes 3735560 | tf_op jit(solution)/shard_map/ppermute | solution.py:24
  444.7 136.4 %reduce-scatter.8.cloned.1.call-start = ((), (), s32[]{:S(2)}) async-start(), calls=%async_computation.8 | async-start | bytes 3244032 | tf_op jit(solution)/shard_map/reduce_scatter | solution.py:924
  478.9 30.0 %collective-permute-start.33 = (bf16[2,6,128,1024]{3,2,1,0:T(8,128)(2,1)}, bf16[2,6,128,1024]{3,2,1,0:T(8,128)(2,1)S(1)}, u32[]{:S(2)}, u32[]{:S(2)}) collective-permute-start(bf16[2,6,128,1024]{3,2,1,0:T(8,128)(2,1)} %get-tuple-element.147), channel_id=1, source_target_pairs={{0,8},{8,0},{16,24},{24,16},{1,9},{9,1},{17,25},{25,17},{2,10},{10... | collective-permute-start | bytes 9437192 | tf_op jit(solution)/shard_map/ppermute | solution.py:649
  512.9 36.2 %collective-permute-start.34 = (bf16[6,128,1024]{2,1,0:T(8,128)(2,1)}, bf16[6,128,1024]{2,1,0:T(8,128)(2,1)}, u32[]{:S(2)}, u32[]{:S(2)}) collective-permute-start(bf16[6,128,1024]{2,1,0:T(8,128)(2,1)} %fusion.21), channel_id=1, source_target_pairs={{0,16},{8,24},{16,0},{24,8},{1,17},{9,25},{17,1},{25,9},{2,18},{10... | collective-permute-start | bytes 4718600 | tf_op jit(solution)/shard_map/ppermute | solution.py:649
  520.8 27.6 %all-to-all-start.1 = ((bf16[4,32,256]{2,1,0:T(8,128)(2,1)}), bf16[4,32,256]{2,1,0:T(8,128)(2,1)S(1)}, u32[]{:S(2)}, u32[]{:S(2)}) async-start(bf16[4,32,256]{2,1,0:T(8,128)(2,1)} %get-tuple-element.292), calls=%async_computation.3 | async-start | bytes 131072 | tf_op jit(solution)/shard_map/all_to_all | solution.py:930
  (67 other events, 620.0 us)
Sparse Core Ops, SparseCore 0:
  23.4 62.0 all-gather.4
  87.7 108.4 all-gather.6
  287.4 87.2 reduce-scatter.3
  444.8 62.2 reduce-scatter.5
  510.5 70.5 reduce-scatter.7

commit v10 on v9

--- a/solution.py
+++ b/solution.py
@@ -729,9 +729,6 @@
         0,
     )
     recv = passed_along(onward, "blk", 1)
-    recv_mem = recv[None, :seg_len]
-    recv_packed = jnp.concatenate([recv[seg_len:, :head_cols], recv[seg_len:, head_cols:]], 0)
-
     def all_columns(value):
         value = value.reshape(-1, head_cols)
         whole = jnp.zeros((value.shape[0], width), bf16)
@@ -752,7 +749,6 @@
     packed = all_columns(packed_mine)
     comp_pair = comp_pairs(packed)
     comp_pair, grad_pieces = lax.optimization_barrier((comp_pair, grad_pieces))
-    comp_ext = jnp.concatenate([comp_pairs(all_columns(recv_packed)), comp_pair], 0)
     order = jnp.arange(lengths.shape[0], dtype=jnp.int32)
     starts = jnp.sum(jnp.where(order[None, :] < order[:, None], lengths[None, :], 0), axis=1)
     seg_ids = blk_index * seg_count + jnp.arange(seg_count, dtype=jnp.int32)
@@ -765,7 +761,10 @@
         window, window, seg_count - window, seg_place, slopes, heads, heads[:1, :, : 2 * head_cols],
         comp_pair, head_cols,
     )
-    comp_ext, late = lax.optimization_barrier((comp_ext, late))
+    recv, late = lax.optimization_barrier((recv, late))
+    recv_mem = recv[None, :seg_len]
+    recv_packed = jnp.concatenate([recv[seg_len:, :head_cols], recv[seg_len:, head_cols:]], 0)
+    comp_ext = jnp.concatenate([comp_pairs(all_columns(recv_packed)), comp_pair], 0)
     middle_seg = window // 2
 
     def early(a, b, comp_ext):
@@ -804,28 +803,24 @@
     f_got = head_swap(f_sent, 1)
     f_far = (f_keep[1].astype(jnp.float32) + f_got[1].astype(jnp.float32)).astype(bf16)
     wo_sent = jnp.stack([grad_wo[1], grad_wo[3]])
-    f_far, wo_sent, mixed = lax.optimization_barrier((f_far, wo_sent, mixed))
-
-    def backward(a, b, held, over, mixed):
-        return attend_bwd(
-            a, b - a, head, seg_place, slopes, heads, recv_mem, comp_ext, mixed, attn_out, lse, held,
-            over, head_cols,
-        )
-
-    held = jnp.zeros((16, 2 * head_cols), jnp.float32)
-    query_one, pair_one, held, over, back = backward(0, window, held, held, mixed)
     wo_got = head_swap(wo_sent, 1).astype(jnp.float32)
     wo_far = (grad_wo[2].astype(jnp.float32) + wo_got[1]).astype(bf16)
-    back, wo_far, held = lax.optimization_barrier((back, wo_far, held))
+    f_far, wo_far, mixed = lax.optimization_barrier((f_far, wo_far, mixed))
+    wo_far = head_swap(wo_far, 2).astype(jnp.float32)
+
+    none = jnp.zeros((16, 2 * head_cols), jnp.float32)
+    grad_query, pair_done, held, rest, back = attend_bwd(
+        0, seg_count, head, seg_place, slopes, heads, recv_mem, comp_ext, mixed, attn_out, lse, none,
+        none, head_cols,
+    )
+    back, f_far = lax.optimization_barrier((back, f_far))
     got_back = passed_along(back, "blk", -1)
-    query_two, pair_two, held, rest, _ = backward(window, seg_count, held, over, mixed)
+    f_far = head_swap(f_far, 2)
     grad_hidden = grad_hidden.reshape(token_count, width)
-    grad_query = jnp.concatenate([query_one, query_two], 0)
     normed = normed.reshape(full_count, width)
     grad_wq = lax.dot_general(
         normed, grad_query.reshape(full_count, head_cols), ROWS_IN, preferred_element_type=jnp.float32
     )
-    wo_far = head_swap(wo_far, 2).astype(jnp.float32)
     grad_wo = (grad_wo[0].astype(jnp.float32) + wo_got[0] + wo_far).astype(bf16)
 
     def by_owner(value):
@@ -833,20 +828,12 @@
             head_groups, blk_count, part, value.shape[1]
         ).transpose(1, 0, 2, 3)
 
-    query_grads = jnp.concatenate(
-        [
-            by_owner(grad_wq),
-            grad_wo.reshape(blk_count, part, head_groups, head_cols).transpose(0, 2, 1, 3),
-        ],
-        2,
-    )
-    query_grads, first_sum, got_back = lax.optimization_barrier((query_grads, first_sum, got_back))
+    wq_rows = by_owner(grad_wq)
+    wo_rows = grad_wo.reshape(blk_count, part, head_groups, head_cols).transpose(0, 2, 1, 3)
+    wq_rows, wo_rows, got_back = lax.optimization_barrier((wq_rows, wo_rows, got_back))
     got_back = got_back.astype(jnp.float32)
-    query_part = lax.psum_scatter(
-        query_grads.reshape(-1, head_cols), "blk", scatter_dimension=0, tiled=True
-    ).reshape(head_groups, 2 * part, head_cols)
     last_pair = (held + got_back[window * pad_rows :]).astype(bf16)
-    grad_pair = jnp.concatenate([pair_one, pair_two, last_pair[None]], 0)
+    grad_pair = jnp.concatenate([pair_done, last_pair[None]], 0)
     got_comp = got_back[: window * pad_rows].reshape(window, pad_rows, 2 * head_cols)
     comp_pair_grad = jnp.pad(rest, ((0, seg_count - rest.shape[0]), (0, 0), (0, 0))) + jnp.pad(
         got_comp, ((seg_count - window, 0), (0, 0), (0, 0))
@@ -865,7 +852,6 @@
     grad_packed = sum_over_heads(
         (columns_of(0), columns_of(2)), jnp.stack([columns_of(1), columns_of(3)])
     ).astype(bf16)
-    f_far = head_swap(f_far, 2)
     grad_packed, f_far = lax.optimization_barrier((grad_packed, f_far))
     out_tokens = (
         hidden + f_keep[0].astype(jnp.float32) + f_got[0].astype(jnp.float32) + f_far.astype(jnp.float32)
@@ -909,48 +895,47 @@
     )
     second_grads = jnp.concatenate(
         [
+            wq_rows,
             by_owner(grad_wkv[:, :head_cols]),
             by_owner(grad_wkv[:, head_cols:]),
             by_owner(grad_comp[0]),
             by_owner(grad_comp[1]),
             by_owner(grad_comp[2]),
             jnp.pad(gain_rows, ((0, 0), (0, 0), (0, 14), (0, head_cols - part))),
+            wo_rows,
         ],
         2,
     )
-    second_grads, query_part = lax.optimization_barrier((second_grads, query_part))
+    second_grads, first_sum = lax.optimization_barrier((second_grads, first_sum))
     first_sum = first_sum.astype(jnp.float32)
-    own_rows = 5 * part + 16
+    own_rows = 6 * part + 16
     second_part = lax.psum_scatter(
         second_grads.reshape(-1, head_cols), "blk", scatter_dimension=0, tiled=True
-    ).reshape(head_groups, own_rows, head_cols)
+    ).reshape(head_groups, own_rows + part, head_cols)
     second_sum = lax.all_to_all(
-        second_part, "head", split_axis=0, concat_axis=0, tiled=True
+        second_part[:, :own_rows], "head", split_axis=0, concat_axis=0, tiled=True
     ).astype(jnp.float32)
-    query_sum = lax.all_to_all(
-        query_part[:, :part], "head", split_axis=0, concat_axis=0, tiled=True
-    ).astype(jnp.float32)
-    gain_sum = jnp.sum(second_sum[:, 5 * part : 5 * part + 2, :part], axis=0)
+    gain_sum = jnp.sum(second_sum[:, 6 * part : 6 * part + 2, :part], axis=0)
     weight_sum = (
-        second_sum[:, : 5 * part]
-        .reshape(head_groups, 5, part, head_cols)
+        second_sum[:, : 6 * part]
+        .reshape(head_groups, 6, part, head_cols)
         .transpose(1, 2, 0, 3)
-        .reshape(5, part, width)
-    )
-    wo_sum = query_part[:, part:].astype(jnp.float32).transpose(1, 0, 2).reshape(part, width)
+        .reshape(6, part, width)
+    )
+    wo_sum = second_part[:, own_rows:].astype(jnp.float32).transpose(1, 0, 2).reshape(part, width)
     return (
         out_tokens,
         compressed,
         grad_tokens,
-        query_sum.transpose(1, 0, 2).reshape(part, width),
         weight_sum[0],
         weight_sum[1],
+        weight_sum[2],
         wo_sum,
         first_sum[:ff_part].T,
         first_sum[ff_part:],
         gain_sum[0],
         gain_sum[1],
-        weight_sum[2:],
+        weight_sum[3:],
     )
 
 

time: 612 us -> 628 us (1.026)
  waiting for transfers between devices: 253 us -> 285 us
    ppermute x33, waiting for transfers between devices: 124 us -> 175 us  [head_swap(): lax.ppermute(value, 'head', [(source, source ^ bit) for source in range(c...]
    reduce_scatter x1 -> x0, waiting for transfers between devices: 24.7 us -> none  [per_device(): lax.psum_scatter(query_grads.reshape(-1, head_cols), 'blk', scatter_dimen...]
    reduce_scatter x1, waiting for transfers between devices: 0.01 us -> 24.4 us  [per_device(): first_sum = lax.psum_scatter(first_grads, 'blk', scatter_dimension=0)]
    all_to_all x2 -> x1, waiting for transfers between devices: 22.1 us -> 1.51 us  [per_device(): lax.all_to_all(second_part[:, :own_rows], 'head', split_axis=0, concat_ax...]
    ppermute x2, waiting for transfers between devices: 37.1 us -> 43.6 us  [passed_along(): lax.ppermute(value, axis, [(source, source + steps) for source in range(l...]
    pallas_call x2 -> x1, Pallas kernels: 43.2 us -> 39.6 us  [attend_bwd(): pl.pallas_call(functools.partial(bwd_kernel, first), grid=(count,), in_sp...]
    unnamed x120 -> x127, local copies, waits for them, and re-layouts: 25.5 us -> 22.8 us
  transfers between devices with their start and end apart: 42 -> 40, of which waited for: 21 -> 24; matrix products, arithmetic and copies ran while one was open for 17% -> 16% of each run, Pallas kernels for 18% -> 11%
where the time goes in v10:
time: 628 us; the launch traced here: 619 us
  waiting for transfers between devices  285 us (45%)
  Pallas kernels  165 us (26%)
  local copies, waits for them, and re-layouts  51.4 us (8%)
  other arithmetic  40.5 us (6%)
  matrix products  25.8 us (4%)
  starting transfers between devices  24.1 us (4%)
  between operations  15.3 us (2%)
  blocking collectives  10.9 us (2%)
    ppermute x33, waiting for transfers between devices, head_swap(): lax.ppermute(value, 'head', [(source, source ^ bit) for source in range(c...  175 us
    pallas_call x1, Pallas kernels, feed_forward(): pl.pallas_call(ffn_kernel, grid=(count,), in_specs=[pl.BlockSpec(memory_s...  59.5 us
    ppermute x2, waiting for transfers between devices, passed_along(): lax.ppermute(value, axis, [(source, source + steps) for source in range(l...  43.6 us
    pallas_call x1, Pallas kernels, attend_bwd(): pl.pallas_call(functools.partial(bwd_kernel, first), grid=(count,), in_sp...  39.6 us
    pallas_call x3, Pallas kernels, attend_fwd(): pl.pallas_call(functools.partial(fwd_kernel, first, shift), grid=(count,)...  26.7 us
    reduce_scatter x1, waiting for transfers between devices, per_device(): first_sum = lax.psum_scatter(first_grads, 'blk', scatter_dimension=0)  24.4 us
    reduce_scatter x1, waiting for transfers between devices, per_device(): lax.psum_scatter(second_grads.reshape(-1, head_cols), 'blk', scatter_dime...  23.8 us
    unnamed x127, local copies, waits for them, and re-layouts  22.8 us
  transfers between devices with their start and end apart: 40, of which 24 were waited for; matrix products, arithmetic and copies ran while one was open for 16% of the time, Pallas kernels for 11%

profile of v10, /device:TPU:24, one launch (start us, length us, event | category | flops | bytes accessed | tf_op | source)
XLA Modules:
  0.0 618.9 jit_solution(3220697521026918054)
XLA Ops:
  12.4 10.9 %all_to_all.10 = bf16[4,208,256]{2,1,0:T(8,128)(2,1)} all-to-all(bf16[4,208,256]{2,1,0:T(8,128)(2,1)S(1)} %copy.246), channel_id=1, replica_groups=mesh['head'=4,'blk'=8] {'head'}, dimensions={0} | all-to-all | bytes 851968 | tf_op jit(solution)/shard_map/all_to_all | solution.py:694
  30.4 36.4 %collective-permute-done.1.t2 = bf16[6,128,1024]{2,1,0:T(8,128)(2,1)} collective-permute-done((bf16[6,128,1024]{2,1,0:T(8,128)(2,1)}, bf16[6,128,1024]{2,1,0:T(8,128)(2,1)}, u32[]{:S(2)}, u32[]{:S(2)}) %collective-permute-start.1) | collective-permute-done | bytes 1572896 | tf_op jit(solution)/shard_map/ppermute | solution.py:649
  68.5 17.0 %all-gather.5.cloned.1.call-done = bf16[32,208,256]{2,1,0:T(8,128)(2,1)} async-done(((bf16[4,208,256]{2,1,0:T(8,128)(2,1)}), bf16[32,208,256]{2,1,0:T(8,128)(2,1)}) %all-gather.5.cloned.1.call-update) | async-done | bytes 3407888 | tf_op jit(solution)/shard_map/all_gather | solution.py:696
  91.5 16.8 %prepare.1 = (bf16[6,512,768]{2,1,0:T(8,128)(2,1)}, bf16[6,512,1024]{2,1,0:T(8,128)(2,1)}, bf16[6,176,3072]{2,1,0:T(8,128)(2,1)}, bf16[6,176,256]{2,1,0:T(8,128)(2,1)}) custom-call(s32[1]{0:T(128)} %bitcast.head_ref, bf16[6,128,1024]{2,1,0:T(8,128)(2,1)} %t0.1, bf16[6,128,1024]{2,1,0:T(8,128)(2,1)} %collective-permute-done.t1, ...), custom_call_target="tpu_custom_call" | custom-call | flops 7000000000 | bytes 30000000 | tf_op jit(solution)/shard_map/prepare/pallas_call | solution.py:397
  116.4 6.9 %collective-permute-done.6 = bf16[1056,256]{1,0:T(8,128)(2,1)S(1)} collective-permute-done((bf16[1056,256]{1,0:T(8,128)(2,1)}, bf16[1056,256]{1,0:T(8,128)(2,1)S(1)}, u32[]{:S(2)}, u32[]{:S(2)}) %collective-permute-start.6) | collective-permute-done | bytes 540704 | tf_op jit(solution)/shard_map/ppermute | solution.py:649
  130.0 8.9 %attend_fwd.3 = (bf16[2,512,256]{2,1,0:T(8,128)(2,1)}, f32[2,2,512]{2,1,0:T(2,128)}) custom-call(s32[6]{0:T(128)} %fusion.51.place_ref, f32[2]{0:T(128)} %exponential_multiply_fusion.slope_ref, bf16[6,512,768]{2,1,0:T(8,128)(2,1)} %get-tuple-element.81.q_ref.own_ref.prev_ref, bf16[6,512,768]{2,1,0:T(8,128)(2,1)} %get-tuple-element.81.q_ref.own_ref.prev_ref, ...), custom_call_target="tpu_custom_call" | custom-call | flops 2000000000 | bytes 6000000 | tf_op jit(solution)/shard_map/attend_fwd/pallas_call | solution.py:230
  138.9 20.9 %collective-permute-done.3 = bf16[864,512]{1,0:T(8,128)(2,1)S(1)} collective-permute-done((bf16[864,512]{1,0:T(8,128)(2,1)S(1)}, bf16[864,512]{1,0:T(8,128)(2,1)S(1)}, u32[]{:S(2)}, u32[]{:S(2)}) %collective-permute-start.3) | collective-permute-done | bytes 884768 | tf_op jit(solution)/shard_map/ppermute | solution.py:24
  162.2 8.1 %collective-permute-done.12 = bf16[704,256]{1,0:T(8,128)(2,1)S(1)} collective-permute-done((bf16[704,256]{1,0:T(8,128)(2,1)S(1)}, bf16[704,256]{1,0:T(8,128)(2,1)S(1)}, u32[]{:S(2)}, u32[]{:S(2)}) %collective-permute-start.12) | collective-permute-done | bytes 360480 | tf_op jit(solution)/shard_map/ppermute | solution.py:649
  174.8 8.9 %attend_fwd.4 = (bf16[2,512,256]{2,1,0:T(8,128)(2,1)}, f32[2,2,512]{2,1,0:T(2,128)}) custom-call(s32[6]{0:T(128)} %fusion.51.place_ref, f32[2]{0:T(128)} %exponential_multiply_fusion.slope_ref, bf16[6,512,768]{2,1,0:T(8,128)(2,1)} %get-tuple-element.81.q_ref.own_ref.prev_ref, bf16[6,512,768]{2,1,0:T(8,128)(2,1)} %get-tuple-element.81.q_ref.own_ref.prev_ref, ...), custom_call_target="tpu_custom_call" | custom-call | flops 2000000000 | bytes 6000000 | tf_op jit(solution)/shard_map/attend_fwd/pallas_call | solution.py:230
  186.3 8.9 %attend_fwd.5 = (bf16[2,512,256]{2,1,0:T(8,128)(2,1)}, f32[2,2,512]{2,1,0:T(2,128)}) custom-call(s32[6]{0:T(128)} %fusion.51.place_ref, f32[2]{0:T(128)} %exponential_multiply_fusion.slope_ref, bf16[6,512,768]{2,1,0:T(8,128)(2,1)} %get-tuple-element.81.q_ref.own_ref.prev_ref, bf16[6,512,768]{2,1,0:T(8,128)(2,1)} %get-tuple-element.81.q_ref.own_ref.prev_ref, ...), custom_call_target="tpu_custom_call" | custom-call | flops 2000000000 | bytes 6000000 | tf_op jit(solution)/shard_map/attend_fwd/pallas_call | solution.py:230
  201.3 9.3 %collective-permute-done.16 = bf16[2,512,256]{2,1,0:T(8,128)(2,1)S(1)} collective-permute-done((bf16[2,512,256]{2,1,0:T(8,128)(2,1)}, bf16[2,512,256]{2,1,0:T(8,128)(2,1)S(1)}, u32[]{:S(2)}, u32[]{:S(2)}) %collective-permute-start.16) | collective-permute-done | bytes 524320 | tf_op jit(solution)/shard_map/ppermute | solution.py:649
  216.0 59.5 %feed_forward.1 = (bf16[2,6,128,1024]{3,2,1,0:T(8,128)(2,1)}, bf16[2,6,128,1024]{3,2,1,0:T(8,128)(2,1)}, bf16[2,6,128,1024]{3,2,1,0:T(8,128)(2,1)}, bf16[2,6,128...) custom-call(s32[1]{0:T(128)} %bitcast.head_ref, ...), custom_call_target="tpu_custom_call" | custom-call | flops 44999999488 | bytes 50000000 | tf_op jit(solution)/shard_map/feed_forward/pallas_call | solution.py:516
  276.0 8.5 %collective-permute-done.22.got_ref = bf16[2,6,128,1024]{3,2,1,0:T(8,128)(2,1)S(1)} collective-permute-done((bf16[2,6,128,1024]{3,2,1,0:T(8,128)(2,1)}, bf16[2,6,128,1024]{3,2,1,0:T(8,128)(2,1)S(1)}, u32[]{:S(2)}, u32[]{:S(2)}) %collective-permute-start.22) | collective-permute-done | bytes 3145760 | tf_op jit(solution)/shard_map/ppermute | solution.py:649
  289.8 35.9 %collective-permute-done.23.far_ref = bf16[6,128,1024]{2,1,0:T(8,128)(2,1)} collective-permute-done((bf16[6,128,1024]{2,1,0:T(8,128)(2,1)}, bf16[6,128,1024]{2,1,0:T(8,128)(2,1)}, u32[]{:S(2)}, u32[]{:S(2)}) %collective-permute-start.23) | collective-permute-done | bytes 1572896 | tf_op jit(solution)/shard_map/ppermute | solution.py:649
  325.7 9.0 %middle.1 = (f32[6,128,1024]{2,1,0:T(8,128)}, bf16[6,128,1024]{2,1,0:T(8,128)(2,1)}, f32[1,1024]{1,0:T(1,128)}, bf16[6,128,256]{2,1,0:T(8,128)(2,1)}, bf16[6,128...) custom-call(bf16[2,6,128,1024]{3,2,1,0:T(8,128)(2,1)} %get-tuple-element.105.keep_ref, ...), custom_call_target="tpu_custom_call" | custom-call | flops 1620000000 | bytes 24000000 | tf_op jit(solution)/shard_map/middle/pallas_call | solution.py:584
  352.1 6.7 %collective-permute-done.27.g3 = bf16[6,128,256]{2,1,0:T(8,128)(2,1)S(1)} collective-permute-done((bf16[6,128,256]{2,1,0:T(8,128)(2,1)S(1)}, bf16[6,128,256]{2,1,0:T(8,128)(2,1)S(1)}, u32[]{:S(2)}, u32[]{:S(2)}) %collective-permute-start.27) | collective-permute-done | bytes 393248 | tf_op jit(solution)/shard_map/ppermute | solution.py:649
  359.5 39.6 %attend_bwd.1 = (bf16[6,512,256]{2,1,0:T(8,128)(2,1)}, bf16[5,512,512]{2,1,0:T(8,128)(2,1)}, f32[512,512]{1,0:T(8,128)}, f32[4,176,512]{2,1,0:T(8,128)}, bf16[1216,512]{1,0:T(8,128)(2,1)}) custom-call(s32[6]{0:T(128)} %fusion.51.place_ref, f32[2]{0:T(128)} %exponential_multiply_fusion.slope_ref, ...), custom_call_target="tpu_custom_call" | custom-call | flops 12000000000 | bytes 24000000 | tf_op jit(solution)/shard_map/attend_bwd/pallas_call | solution.py:266
  412.9 6.6 %collective-permute-done.28 = bf16[256,1024]{1,0:T(8,128)(2,1)S(1)} collective-permute-done((bf16[256,1024]{1,0:T(8,128)(2,1)S(1)}, bf16[256,1024]{1,0:T(8,128)(2,1)S(1)}, u32[]{:S(2)}, u32[]{:S(2)}) %collective-permute-start.28) | collective-permute-done | bytes 524320 | tf_op jit(solution)/shard_map/ppermute | solution.py:649
  422.4 22.7 %collective-permute-done.29 = bf16[1216,512]{1,0:T(8,128)(2,1)} collective-permute-done((bf16[1216,512]{1,0:T(8,128)(2,1)}, bf16[1216,512]{1,0:T(8,128)(2,1)}, u32[]{:S(2)}, u32[]{:S(2)}) %collective-permute-start.29) | collective-permute-done | bytes 1245216 | tf_op jit(solution)/shard_map/ppermute | solution.py:24
  463.8 11.1 %collective-permute-done.31 = bf16[1056,256]{1,0:T(8,128)(2,1)S(1)} collective-permute-done((bf16[1056,256]{1,0:T(8,128)(2,1)S(1)}, bf16[1056,256]{1,0:T(8,128)(2,1)S(1)}, u32[]{:S(2)}, u32[]{:S(2)}) %collective-permute-start.31) | collective-permute-done | bytes 540704 | tf_op jit(solution)/shard_map/ppermute | solution.py:649
  482.6 24.4 %reduce-scatter.3.cloned.1.call-done = bf16[1,256,1024]{2,1,0:T(8,128)(2,1)} async-done(((bf16[8,256,1024]{2,1,0:T(8,128)(2,1)}), bf16[1,256,1024]{2,1,0:T(8,128)(2,1)}) %reduce-scatter.3.cloned.1.call-update) | async-done | bytes 524304 | tf_op jit(solution)/shard_map/reduce_scatter | solution.py:784
  507.0 13.8 %g_normed.1 = (bf16[2,6,128,1024]{3,2,1,0:T(8,128)(2,1)}, bf16[2,6,128,1024]{3,2,1,0:T(8,128)(2,1)}) custom-call(s32[1]{0:T(128)} %bitcast.head_ref, bf16[6,512,256]{2,1,0:T(8,128)(2,1)} %get-tuple-element.121.gq_ref, bf16[6,512,512]{2,1,0:T(8,128)(2,1)} %copy-done.9, bf16[6,176,256]{2,1,0:T(8,128)(2,1)} %bitcast.250, bf16[6,1024,256]{2,1,0:T(8,128)(2,1)} %bitcast.227), custom_call_target="tpu_custom_call" | custom-call | flops 7000000000 | bytes 20000000 | tf_op jit(solution)/shard_map/g_normed/pallas_call | solution.py:625
  543.8 23.6 %collective-permute-done.34 = bf16[6,128,1024]{2,1,0:T(8,128)(2,1)} collective-permute-done((bf16[6,128,1024]{2,1,0:T(8,128)(2,1)}, bf16[6,128,1024]{2,1,0:T(8,128)(2,1)}, u32[]{:S(2)}, u32[]{:S(2)}) %collective-permute-start.34) | collective-permute-done | bytes 1572896 | tf_op jit(solution)/shard_map/ppermute | solution.py:649
  571.2 23.8 %reduce-scatter.5.cloned.1.call-done = bf16[960,256]{1,0:T(8,128)(2,1)} async-done(((bf16[7680,256]{1,0:T(8,128)(2,1)}), bf16[960,256]{1,0:T(8,128)(2,1)}) %reduce-scatter.5.cloned.1.call-update) | async-done | bytes 491536 | tf_op jit(solution)/shard_map/reduce_scatter | solution.py:912
  (314 shorter events, 165.4 us)
Async XLA Ops:
  7.2 78.4 %all-gather.5.cloned.1.call-start = ((), (), s32[]{:S(2)}) async-start(), calls=%async_computation.6 | async-start | bytes 3833856 | tf_op jit(solution)/shard_map/all_gather | solution.py:696
  23.3 192.7 %all-gather.7.cloned.1.call-start = ((), (), s32[]{:S(2)}) async-start(), calls=%async_computation.7 | async-start | bytes 7077888 | tf_op jit(solution)/shard_map/all_gather | solution.py:697
  29.9 477.1 %reduce-scatter.3.cloned.1.call-start = ((), (), s32[]{:S(2)}) async-start(), calls=%async_computation.4 | async-start | bytes 4718592 | tf_op jit(solution)/shard_map/reduce_scatter | solution.py:784
  30.0 36.8 %collective-permute-start.1 = (bf16[6,128,1024]{2,1,0:T(8,128)(2,1)}, bf16[6,128,1024]{2,1,0:T(8,128)(2,1)}, u32[]{:S(2)}, u32[]{:S(2)}) collective-permute-start(bf16[6,128,1024]{2,1,0:T(8,128)(2,1)} %t0.1), channel_id=1, source_target_pairs={{0,16},{8,24},{16,0},{24,8},{1,17},{9,25},{17,1},{25,9},{2,18},{10... | collective-permute-start | bytes 4718600 | tf_op jit(solution)/shard_map/ppermute | solution.py:649
  30.4 61.1 %collective-permute-start = (bf16[6,128,1024]{2,1,0:T(8,128)(2,1)}, bf16[6,128,1024]{2,1,0:T(8,128)(2,1)}, u32[]{:S(2)}, u32[]{:S(2)}) collective-permute-start(bf16[6,128,1024]{2,1,0:T(8,128)(2,1)} %t0.1), channel_id=1, source_target_pairs={{0,8},{8,0},{16,24},{24,16},{1,9},{9,1},{17,25},{25,17},{2,10},{10... | collective-permute-start | bytes 4718600 | tf_op jit(solution)/shard_map/ppermute | solution.py:649
  66.8 24.7 %collective-permute-start.2 = (bf16[6,128,1024]{2,1,0:T(8,128)(2,1)}, bf16[6,128,1024]{2,1,0:T(8,128)(2,1)}, u32[]{:S(2)}, u32[]{:S(2)}) collective-permute-start(bf16[6,128,1024]{2,1,0:T(8,128)(2,1)} %collective-permute-done.1.t2), channel_id=1, source_target_pairs={{0,8},{8,0},{16,24},{24,16},{1,9},{9,1},{17,25},{25,17},{2,10},{10... | collective-permute-start | bytes 4718600 | tf_op jit(solution)/shard_map/ppermute | solution.py:649
  66.8 41.5 %collective-permute-start.4 = (bf16[6,128,1024]{2,1,0:T(8,128)(2,1)}, bf16[6,128,1024]{2,1,0:T(8,128)(2,1)}, u32[]{:S(2)}, u32[]{:S(2)}) collective-permute-start(bf16[6,128,1024]{2,1,0:T(8,128)(2,1)} %grad_ref.1), channel_id=1, source_target_pairs={{0,16},{8,24},{16,0},{24,8},{1,17},{9,25},{17,1},{25,9},{2,18},{10... | collective-permute-start | bytes 4718600 | tf_op jit(solution)/shard_map/ppermute | solution.py:649
  108.3 15.3 %collective-permute-start.5 = (bf16[1056,256]{1,0:T(8,128)(2,1)}, bf16[1056,256]{1,0:T(8,128)(2,1)S(1)}, u32[]{:S(2)}, u32[]{:S(2)}) collective-permute-start(bf16[1056,256]{1,0:T(8,128)(2,1)} %bitcast.241), channel_id=1, source_target_pairs={{0,8},{8,0},{16,24},{24,16},{1,9},{9,1},{17,25},{25,17},{2,10},{10... | collective-permute-start | bytes 1622024 | tf_op jit(solution)/shard_map/ppermute | solution.py:649
  108.4 14.9 %collective-permute-start.6 = (bf16[1056,256]{1,0:T(8,128)(2,1)}, bf16[1056,256]{1,0:T(8,128)(2,1)S(1)}, u32[]{:S(2)}, u32[]{:S(2)}) collective-permute-start(bf16[1056,256]{1,0:T(8,128)(2,1)} %bitcast.242), channel_id=1, source_target_pairs={{0,16},{8,24},{16,0},{24,8},{1,17},{9,25},{17,1},{25,9},{2,18},{10... | collective-permute-start | bytes 1622024 | tf_op jit(solution)/shard_map/ppermute | solution.py:649
  110.0 17.6 %collective-permute-start.8 = (bf16[6,128,1024]{2,1,0:T(8,128)(2,1)}, bf16[6,128,1024]{2,1,0:T(8,128)(2,1)S(1)}, u32[]{:S(2)}, u32[]{:S(2)}) collective-permute-start(bf16[6,128,1024]{2,1,0:T(8,128)(2,1)} %grad_ref.1), channel_id=1, source_target_pairs={{0,8},{8,0},{16,24},{24,16},{1,9},{9,1},{17,25},{25,17},{2,10},{10... | collective-permute-start | bytes 4718600 | tf_op jit(solution)/shard_map/ppermute | solution.py:649
  110.1 18.6 %collective-permute-start.9 = (bf16[6,128,1024]{2,1,0:T(8,128)(2,1)}, bf16[6,128,1024]{2,1,0:T(8,128)(2,1)S(1)}, u32[]{:S(2)}, u32[]{:S(2)}) collective-permute-start(bf16[6,128,1024]{2,1,0:T(8,128)(2,1)} %collective-permute-done.4.g2), channel_id=1, source_target_pairs={{0,8},{8,0},{16,24},{24,16},{1,9},{9,1},{17,25},{25,17},{2,10},{10... | collective-permute-start | bytes 4718600 | tf_op jit(solution)/shard_map/ppermute | solution.py:649
  113.9 45.8 %collective-permute-start.3 = (bf16[864,512]{1,0:T(8,128)(2,1)S(1)}, bf16[864,512]{1,0:T(8,128)(2,1)S(1)}, u32[]{:S(2)}, u32[]{:S(2)}) collective-permute-start(bf16[864,512]{1,0:T(8,128)(2,1)S(1)} %maximum_maximum_fusion), channel_id=1, source_target_pairs={{0,1},{1,2},{2,3},{3,4},{4,5},{5,6},{6,7},{8,9},{9,10},{10,11},{11... | collective-permute-start | bytes 2654216 | tf_op jit(solution)/shard_map/ppermute | solution.py:24
  171.1 14.3 %collective-permute-start.10 = (bf16[2,512,256]{2,1,0:T(8,128)(2,1)S(1)}, bf16[2,512,256]{2,1,0:T(8,128)(2,1)S(1)}, u32[]{:S(2)}, u32[]{:S(2)}) collective-permute-start(bf16[2,512,256]{2,1,0:T(8,128)(2,1)S(1)} %copy-done.28), channel_id=1, source_target_pairs={{0,16},{8,24},{16,0},{24,8},{1,17},{9,25},{17,1},{25,9},{2,18},{10... | collective-permute-start | bytes 1572872 | tf_op jit(solution)/shard_map/ppermute | solution.py:649
  185.5 15.0 %collective-permute-start.15 = (bf16[2,512,256]{2,1,0:T(8,128)(2,1)}, bf16[2,512,256]{2,1,0:T(8,128)(2,1)S(1)}, u32[]{:S(2)}, u32[]{:S(2)}) collective-permute-start(bf16[2,512,256]{2,1,0:T(8,128)(2,1)} %get-tuple-element.94), channel_id=1, source_target_pairs={{0,16},{8,24},{16,0},{24,8},{1,17},{9,25},{17,1},{25,9},{2,18},{10... | collective-permute-start | bytes 1572872 | tf_op jit(solution)/shard_map/ppermute | solution.py:649
  195.3 15.3 %collective-permute-start.16 = (bf16[2,512,256]{2,1,0:T(8,128)(2,1)}, bf16[2,512,256]{2,1,0:T(8,128)(2,1)S(1)}, u32[]{:S(2)}, u32[]{:S(2)}) collective-permute-start(bf16[2,512,256]{2,1,0:T(8,128)(2,1)} %get-tuple-element.96), channel_id=1, source_target_pairs={{0,16},{8,24},{16,0},{24,8},{1,17},{9,25},{17,1},{25,9},{2,18},{10... | collective-permute-start | bytes 1572872 | tf_op jit(solution)/shard_map/ppermute | solution.py:649
  275.7 65.9 %collective-permute-start.21 = (bf16[2,6,128,1024]{3,2,1,0:T(8,128)(2,1)}, bf16[2,6,128,1024]{3,2,1,0:T(8,128)(2,1)}, u32[]{:S(2)}, u32[]{:S(2)}) collective-permute-start(bf16[2,6,128,1024]{3,2,1,0:T(8,128)(2,1)} %get-tuple-element.104), channel_id=1, source_target_pairs={{0,8},{8,0},{16,24},{24,16},{1,9},{9,1},{17,25},{25,17},{2,10},{10... | collective-permute-start | bytes 9437192 | tf_op jit(solution)/shard_map/ppermute | solution.py:649
  288.9 36.8 %collective-permute-start.23 = (bf16[6,128,1024]{2,1,0:T(8,128)(2,1)}, bf16[6,128,1024]{2,1,0:T(8,128)(2,1)}, u32[]{:S(2)}, u32[]{:S(2)}) collective-permute-start(bf16[6,128,1024]{2,1,0:T(8,128)(2,1)} %fusion.20), channel_id=1, source_target_pairs={{0,16},{8,24},{16,0},{24,8},{1,17},{9,25},{17,1},{25,9},{2,18},{10... | collective-permute-start | bytes 4718600 | tf_op jit(solution)/shard_map/ppermute | solution.py:649
  341.0 17.8 %collective-permute-start.27 = (bf16[6,128,256]{2,1,0:T(8,128)(2,1)S(1)}, bf16[6,128,256]{2,1,0:T(8,128)(2,1)S(1)}, u32[]{:S(2)}, u32[]{:S(2)}) collective-permute-start(bf16[6,128,256]{2,1,0:T(8,128)(2,1)S(1)} %copy-done.40), channel_id=1, source_target_pairs={{0,24},{8,16},{16,8},{24,0},{1,25},{9,17},{17,9},{25,1},{2,26},{10... | collective-permute-start | bytes 1179656 | tf_op jit(solution)/shard_map/ppermute | solution.py:649
  399.1 46.0 %collective-permute-start.29 = (bf16[1216,512]{1,0:T(8,128)(2,1)}, bf16[1216,512]{1,0:T(8,128)(2,1)}, u32[]{:S(2)}, u32[]{:S(2)}) collective-permute-start(bf16[1216,512]{1,0:T(8,128)(2,1)} %get-tuple-element.125), channel_id=1, source_target_pairs={{1,0},{2,1},{3,2},{4,3},{5,4},{6,5},{7,6},{9,8},{10,9},{11,10},{12... | collective-permute-start | bytes 3735560 | tf_op jit(solution)/shard_map/ppermute | solution.py:24
  403.7 191.3 %reduce-scatter.5.cloned.1.call-start = ((), (), s32[]{:S(2)}) async-start(), calls=%async_computation.5 | async-start | bytes 4423680 | tf_op jit(solution)/shard_map/reduce_scatter | solution.py:912
  404.7 14.8 %collective-permute-start.28 = (bf16[256,1024]{1,0:T(8,128)(2,1)S(1)}, bf16[256,1024]{1,0:T(8,128)(2,1)S(1)}, u32[]{:S(2)}, u32[]{:S(2)}) collective-permute-start(bf16[256,1024]{1,0:T(8,128)(2,1)S(1)} %copy-done.30), channel_id=1, source_target_pairs={{0,16},{8,24},{16,0},{24,8},{1,17},{9,25},{17,1},{25,9},{2,18},{10... | collective-permute-start | bytes 1572872 | tf_op jit(solution)/shard_map/ppermute | solution.py:649
  411.7 63.5 %collective-permute-start.32 = (bf16[6,128,1024]{2,1,0:T(8,128)(2,1)}, bf16[6,128,1024]{2,1,0:T(8,128)(2,1)}, u32[]{:S(2)}, u32[]{:S(2)}) collective-permute-start(bf16[6,128,1024]{2,1,0:T(8,128)(2,1)} %fusion.19), channel_id=1, source_target_pairs={{0,16},{8,24},{16,0},{24,8},{1,17},{9,25},{17,1},{25,9},{2,18},{10... | collective-permute-start | bytes 4718600 | tf_op jit(solution)/shard_map/ppermute | solution.py:649
  460.5 14.4 %collective-permute-start.31 = (bf16[1056,256]{1,0:T(8,128)(2,1)S(1)}, bf16[1056,256]{1,0:T(8,128)(2,1)S(1)}, u32[]{:S(2)}, u32[]{:S(2)}) collective-permute-start(bf16[1056,256]{1,0:T(8,128)(2,1)S(1)} %fusion.36), channel_id=1, source_target_pairs={{0,16},{8,24},{16,0},{24,8},{1,17},{9,25},{17,1},{25,9},{2,18},{10... | collective-permute-start | bytes 1622024 | tf_op jit(solution)/shard_map/ppermute | solution.py:649
  530.6 36.8 %collective-permute-start.34 = (bf16[6,128,1024]{2,1,0:T(8,128)(2,1)}, bf16[6,128,1024]{2,1,0:T(8,128)(2,1)}, u32[]{:S(2)}, u32[]{:S(2)}) collective-permute-start(bf16[6,128,1024]{2,1,0:T(8,128)(2,1)} %fusion.21), channel_id=1, source_target_pairs={{0,16},{8,24},{16,0},{24,8},{1,17},{9,25},{17,1},{25,9},{2,18},{10... | collective-permute-start | bytes 4718600 | tf_op jit(solution)/shard_map/ppermute | solution.py:649
  (69 other events, 643.8 us)
Sparse Core Ops, SparseCore 0:
  23.4 62.0 all-gather.4
  87.7 108.4 all-gather.6
  403.8 103.1 reduce-scatter.2
  511.0 83.9 reduce-scatter.4

commit v11 on v10

--- a/solution.py
+++ b/solution.py
@@ -830,7 +830,9 @@
 
     wq_rows = by_owner(grad_wq)
     wo_rows = grad_wo.reshape(blk_count, part, head_groups, head_cols).transpose(0, 2, 1, 3)
-    wq_rows, wo_rows, got_back = lax.optimization_barrier((wq_rows, wo_rows, got_back))
+    wq_rows, wo_rows, got_back, first_sum = lax.optimization_barrier(
+        (wq_rows, wo_rows, got_back, first_sum)
+    )
     got_back = got_back.astype(jnp.float32)
     last_pair = (held + got_back[window * pad_rows :]).astype(bf16)
     grad_pair = jnp.concatenate([pair_done, last_pair[None]], 0)
@@ -906,7 +908,6 @@
         ],
         2,
     )
-    second_grads, first_sum = lax.optimization_barrier((second_grads, first_sum))
     first_sum = first_sum.astype(jnp.float32)
     own_rows = 6 * part + 16
     second_part = lax.psum_scatter(

time: 628 us -> 587 us (0.935)
  waiting for transfers between devices: 285 us -> 246 us
    reduce_scatter x1, waiting for transfers between devices: 24.4 us -> 0.01 us  [per_device(): first_sum = lax.psum_scatter(first_grads, 'blk', scatter_dimension=0)]
    ppermute x2, waiting for transfers between devices: 43.6 us -> 31 us  [passed_along(): lax.ppermute(value, axis, [(source, source + steps) for source in range(l...]
    unnamed x127 -> x125, local copies, waits for them, and re-layouts: 22.8 us -> 21.4 us
  transfers between devices with their start and end apart: 40 -> 40, of which waited for: 24 -> 23; matrix products, arithmetic and copies ran while one was open for 16% -> 16% of each run, Pallas kernels for 11% -> 18%
where the time goes in v11:
time: 587 us; the launch traced here: 578 us
  waiting for transfers between devices  246 us (42%)
  Pallas kernels  166 us (28%)
  local copies, waits for them, and re-layouts  50 us (9%)
  other arithmetic  40.4 us (7%)
  matrix products  25.8 us (4%)
  starting transfers between devices  23.6 us (4%)
  between operations  15.3 us (3%)
  blocking collectives  10.9 us (2%)
    ppermute x33, waiting for transfers between devices, head_swap(): lax.ppermute(value, 'head', [(source, source ^ bit) for source in range(c...  176 us
    pallas_call x1, Pallas kernels, feed_forward(): pl.pallas_call(ffn_kernel, grid=(count,), in_specs=[pl.BlockSpec(memory_s...  59.5 us
    pallas_call x1, Pallas kernels, attend_bwd(): pl.pallas_call(functools.partial(bwd_kernel, first), grid=(count,), in_sp...  39.7 us
    ppermute x2, waiting for transfers between devices, passed_along(): lax.ppermute(value, axis, [(source, source + steps) for source in range(l...  31 us
    pallas_call x3, Pallas kernels, attend_fwd(): pl.pallas_call(functools.partial(fwd_kernel, first, shift), grid=(count,)...  26.8 us
    unnamed x125, local copies, waits for them, and re-layouts  21.4 us
    reduce_scatter x1, waiting for transfers between devices, per_device(): lax.psum_scatter(second_grads.reshape(-1, head_cols), 'blk', scatter_dime...  20.7 us
    all_gather x1, waiting for transfers between devices, per_device(): first_all = lax.all_gather(columns, 'blk', axis=0)  16.9 us
  transfers between devices with their start and end apart: 40, of which 23 were waited for; matrix products, arithmetic and copies ran while one was open for 16% of the time, Pallas kernels for 18%

profile of v11, /device:TPU:24, one launch (start us, length us, event | category | flops | bytes accessed | tf_op | source)
XLA Modules:
  0.0 577.8 jit_solution(8800408625415608897)
XLA Ops:
  12.4 10.9 %all_to_all.10 = bf16[4,208,256]{2,1,0:T(8,128)(2,1)} all-to-all(bf16[4,208,256]{2,1,0:T(8,128)(2,1)S(1)} %copy.246), channel_id=1, replica_groups=mesh['head'=4,'blk'=8] {'head'}, dimensions={0} | all-to-all | bytes 851968 | tf_op jit(solution)/shard_map/all_to_all | solution.py:694
  30.4 36.4 %collective-permute-done.1.t2 = bf16[6,128,1024]{2,1,0:T(8,128)(2,1)} collective-permute-done((bf16[6,128,1024]{2,1,0:T(8,128)(2,1)}, bf16[6,128,1024]{2,1,0:T(8,128)(2,1)}, u32[]{:S(2)}, u32[]{:S(2)}) %collective-permute-start.1) | collective-permute-done | bytes 1572896 | tf_op jit(solution)/shard_map/ppermute | solution.py:649
  68.6 16.9 %all-gather.5.cloned.1.call-done = bf16[32,208,256]{2,1,0:T(8,128)(2,1)} async-done(((bf16[4,208,256]{2,1,0:T(8,128)(2,1)}), bf16[32,208,256]{2,1,0:T(8,128)(2,1)}) %all-gather.5.cloned.1.call-update) | async-done | bytes 3407888 | tf_op jit(solution)/shard_map/all_gather | solution.py:696
  91.5 16.9 %prepare.1 = (bf16[6,512,768]{2,1,0:T(8,128)(2,1)}, bf16[6,512,1024]{2,1,0:T(8,128)(2,1)}, bf16[6,176,3072]{2,1,0:T(8,128)(2,1)}, bf16[6,176,256]{2,1,0:T(8,128)(2,1)}) custom-call(s32[1]{0:T(128)} %bitcast.head_ref, bf16[6,128,1024]{2,1,0:T(8,128)(2,1)} %t0.1, bf16[6,128,1024]{2,1,0:T(8,128)(2,1)} %collective-permute-done.t1, ...), custom_call_target="tpu_custom_call" | custom-call | flops 7000000000 | bytes 30000000 | tf_op jit(solution)/shard_map/prepare/pallas_call | solution.py:397
  116.4 6.9 %collective-permute-done.6 = bf16[1056,256]{1,0:T(8,128)(2,1)S(1)} collective-permute-done((bf16[1056,256]{1,0:T(8,128)(2,1)}, bf16[1056,256]{1,0:T(8,128)(2,1)S(1)}, u32[]{:S(2)}, u32[]{:S(2)}) %collective-permute-start.6) | collective-permute-done | bytes 540704 | tf_op jit(solution)/shard_map/ppermute | solution.py:649
  130.0 8.9 %attend_fwd.3 = (bf16[2,512,256]{2,1,0:T(8,128)(2,1)}, f32[2,2,512]{2,1,0:T(2,128)}) custom-call(s32[6]{0:T(128)} %fusion.51.place_ref, f32[2]{0:T(128)} %exponential_multiply_fusion.slope_ref, bf16[6,512,768]{2,1,0:T(8,128)(2,1)} %get-tuple-element.80.q_ref.own_ref.prev_ref, bf16[6,512,768]{2,1,0:T(8,128)(2,1)} %get-tuple-element.80.q_ref.own_ref.prev_ref, ...), custom_call_target="tpu_custom_call" | custom-call | flops 2000000000 | bytes 6000000 | tf_op jit(solution)/shard_map/attend_fwd/pallas_call | solution.py:230
  138.9 21.0 %collective-permute-done.3 = bf16[864,512]{1,0:T(8,128)(2,1)S(1)} collective-permute-done((bf16[864,512]{1,0:T(8,128)(2,1)S(1)}, bf16[864,512]{1,0:T(8,128)(2,1)S(1)}, u32[]{:S(2)}, u32[]{:S(2)}) %collective-permute-start.3) | collective-permute-done | bytes 884768 | tf_op jit(solution)/shard_map/ppermute | solution.py:24
  162.2 8.2 %collective-permute-done.12 = bf16[704,256]{1,0:T(8,128)(2,1)S(1)} collective-permute-done((bf16[704,256]{1,0:T(8,128)(2,1)S(1)}, bf16[704,256]{1,0:T(8,128)(2,1)S(1)}, u32[]{:S(2)}, u32[]{:S(2)}) %collective-permute-start.12) | collective-permute-done | bytes 360480 | tf_op jit(solution)/shard_map/ppermute | solution.py:649
  174.9 8.9 %attend_fwd.4 = (bf16[2,512,256]{2,1,0:T(8,128)(2,1)}, f32[2,2,512]{2,1,0:T(2,128)}) custom-call(s32[6]{0:T(128)} %fusion.51.place_ref, f32[2]{0:T(128)} %exponential_multiply_fusion.slope_ref, bf16[6,512,768]{2,1,0:T(8,128)(2,1)} %get-tuple-element.80.q_ref.own_ref.prev_ref, bf16[6,512,768]{2,1,0:T(8,128)(2,1)} %get-tuple-element.80.q_ref.own_ref.prev_ref, ...), custom_call_target="tpu_custom_call" | custom-call | flops 2000000000 | bytes 6000000 | tf_op jit(solution)/shard_map/attend_fwd/pallas_call | solution.py:230
  186.5 8.9 %attend_fwd.5 = (bf16[2,512,256]{2,1,0:T(8,128)(2,1)}, f32[2,2,512]{2,1,0:T(2,128)}) custom-call(s32[6]{0:T(128)} %fusion.51.place_ref, f32[2]{0:T(128)} %exponential_multiply_fusion.slope_ref, bf16[6,512,768]{2,1,0:T(8,128)(2,1)} %get-tuple-element.80.q_ref.own_ref.prev_ref, bf16[6,512,768]{2,1,0:T(8,128)(2,1)} %get-tuple-element.80.q_ref.own_ref.prev_ref, ...), custom_call_target="tpu_custom_call" | custom-call | flops 2000000000 | bytes 6000000 | tf_op jit(solution)/shard_map/attend_fwd/pallas_call | solution.py:230
  201.4 9.3 %collective-permute-done.16 = bf16[2,512,256]{2,1,0:T(8,128)(2,1)S(1)} collective-permute-done((bf16[2,512,256]{2,1,0:T(8,128)(2,1)}, bf16[2,512,256]{2,1,0:T(8,128)(2,1)S(1)}, u32[]{:S(2)}, u32[]{:S(2)}) %collective-permute-start.16) | collective-permute-done | bytes 524320 | tf_op jit(solution)/shard_map/ppermute | solution.py:649
  216.1 59.5 %feed_forward.1 = (bf16[2,6,128,1024]{3,2,1,0:T(8,128)(2,1)}, bf16[2,6,128,1024]{3,2,1,0:T(8,128)(2,1)}, bf16[2,6,128,1024]{3,2,1,0:T(8,128)(2,1)}, bf16[2,6,128...) custom-call(s32[1]{0:T(128)} %bitcast.head_ref, ...), custom_call_target="tpu_custom_call" | custom-call | flops 44999999488 | bytes 50000000 | tf_op jit(solution)/shard_map/feed_forward/pallas_call | solution.py:516
  286.4 36.2 %collective-permute-done.23.far_ref = bf16[6,128,1024]{2,1,0:T(8,128)(2,1)} collective-permute-done((bf16[6,128,1024]{2,1,0:T(8,128)(2,1)}, bf16[6,128,1024]{2,1,0:T(8,128)(2,1)}, u32[]{:S(2)}, u32[]{:S(2)}) %collective-permute-start.23) | collective-permute-done | bytes 1572896 | tf_op jit(solution)/shard_map/ppermute | solution.py:649
  322.5 9.3 %middle.1 = (f32[6,128,1024]{2,1,0:T(8,128)}, bf16[6,128,1024]{2,1,0:T(8,128)(2,1)}, f32[1,1024]{1,0:T(1,128)}, bf16[6,128,256]{2,1,0:T(8,128)(2,1)}, bf16[6,128...) custom-call(bf16[2,6,128,1024]{3,2,1,0:T(8,128)(2,1)} %get-tuple-element.104.keep_ref, ...), custom_call_target="tpu_custom_call" | custom-call | flops 1620000000 | bytes 24000000 | tf_op jit(solution)/shard_map/middle/pallas_call | solution.py:584
  349.3 6.7 %collective-permute-done.27.g3 = bf16[6,128,256]{2,1,0:T(8,128)(2,1)S(1)} collective-permute-done((bf16[6,128,256]{2,1,0:T(8,128)(2,1)S(1)}, bf16[6,128,256]{2,1,0:T(8,128)(2,1)S(1)}, u32[]{:S(2)}, u32[]{:S(2)}) %collective-permute-start.27) | collective-permute-done | bytes 393248 | tf_op jit(solution)/shard_map/ppermute | solution.py:649
  356.7 39.7 %attend_bwd.1 = (bf16[6,512,256]{2,1,0:T(8,128)(2,1)}, bf16[5,512,512]{2,1,0:T(8,128)(2,1)}, f32[512,512]{1,0:T(8,128)}, f32[4,176,512]{2,1,0:T(8,128)}, bf16[1216,512]{1,0:T(8,128)(2,1)}) custom-call(s32[6]{0:T(128)} %fusion.51.place_ref, f32[2]{0:T(128)} %exponential_multiply_fusion.slope_ref, ...), custom_call_target="tpu_custom_call" | custom-call | flops 12000000000 | bytes 24000000 | tf_op jit(solution)/shard_map/attend_bwd/pallas_call | solution.py:266
  409.5 6.5 %collective-permute-done.28 = bf16[256,1024]{1,0:T(8,128)(2,1)S(1)} collective-permute-done((bf16[256,1024]{1,0:T(8,128)(2,1)S(1)}, bf16[256,1024]{1,0:T(8,128)(2,1)S(1)}, u32[]{:S(2)}, u32[]{:S(2)}) %collective-permute-start.28) | collective-permute-done | bytes 524320 | tf_op jit(solution)/shard_map/ppermute | solution.py:649
  418.9 10.0 %collective-permute-done.29 = bf16[1216,512]{1,0:T(8,128)(2,1)} collective-permute-done((bf16[1216,512]{1,0:T(8,128)(2,1)}, bf16[1216,512]{1,0:T(8,128)(2,1)}, u32[]{:S(2)}, u32[]{:S(2)}) %collective-permute-start.29) | collective-permute-done | bytes 1245216 | tf_op jit(solution)/shard_map/ppermute | solution.py:24
  447.3 14.1 %collective-permute-done.31 = bf16[1056,256]{1,0:T(8,128)(2,1)S(1)} collective-permute-done((bf16[1056,256]{1,0:T(8,128)(2,1)S(1)}, bf16[1056,256]{1,0:T(8,128)(2,1)S(1)}, u32[]{:S(2)}, u32[]{:S(2)}) %collective-permute-start.31) | collective-permute-done | bytes 540704 | tf_op jit(solution)/shard_map/ppermute | solution.py:649
  469.0 13.8 %g_normed.1 = (bf16[2,6,128,1024]{3,2,1,0:T(8,128)(2,1)}, bf16[2,6,128,1024]{3,2,1,0:T(8,128)(2,1)}) custom-call(s32[1]{0:T(128)} %bitcast.head_ref, bf16[6,512,256]{2,1,0:T(8,128)(2,1)} %get-tuple-element.120.gq_ref, bf16[6,512,512]{2,1,0:T(8,128)(2,1)} %copy-done.8, bf16[6,176,256]{2,1,0:T(8,128)(2,1)} %bitcast.250, bf16[6,1024,256]{2,1,0:T(8,128)(2,1)} %bitcast.227), custom_call_target="tpu_custom_call" | custom-call | flops 7000000000 | bytes 20000000 | tf_op jit(solution)/shard_map/g_normed/pallas_call | solution.py:625
  483.0 5.7 collective-permute-done.33
  499.1 5.9 %fusion.15 = bf16[6,128,1024]{2,1,0:T(8,128)(2,1)} fusion(f32[6,128,1024]{2,1,0:T(8,128)} %get-tuple-element.101.hidden_ref, bf16[6,128,1024]{2,1,0:T(8,128)(2,1)} %collective-permute-done.32, bf16[2,6,128,1024]{3,2,1,0:T(8,128)(2,1)} %collective-permute-done.21, bf16[2,6,128,1024]{3,2,1,0:T(8,128)(2,1)} %get-tuple-element.102), kind=kLoop, calls=%fused_computation.22 | loop fusion | flops 5505024 | bytes 9437184 | tf_op jit(solution)/shard_map/convert_element_type | solution.py:860
  505.0 24.4 %collective-permute-done.34 = bf16[6,128,1024]{2,1,0:T(8,128)(2,1)} collective-permute-done((bf16[6,128,1024]{2,1,0:T(8,128)(2,1)}, bf16[6,128,1024]{2,1,0:T(8,128)(2,1)}, u32[]{:S(2)}, u32[]{:S(2)}) %collective-permute-start.34) | collective-permute-done | bytes 1572896 | tf_op jit(solution)/shard_map/ppermute | solution.py:649
  533.3 20.7 %reduce-scatter.5.cloned.1.call-done = bf16[960,256]{1,0:T(8,128)(2,1)} async-done(((bf16[7680,256]{1,0:T(8,128)(2,1)}), bf16[960,256]{1,0:T(8,128)(2,1)}) %reduce-scatter.5.cloned.1.call-update) | async-done | bytes 491536 | tf_op jit(solution)/shard_map/reduce_scatter | solution.py:913
  (312 shorter events, 156.9 us)
Async XLA Ops:
  7.2 78.4 %all-gather.5.cloned.1.call-start = ((), (), s32[]{:S(2)}) async-start(), calls=%async_computation.6 | async-start | bytes 3833856 | tf_op jit(solution)/shard_map/all_gather | solution.py:696
  23.3 192.8 %all-gather.7.cloned.1.call-start = ((), (), s32[]{:S(2)}) async-start(), calls=%async_computation.7 | async-start | bytes 7077888 | tf_op jit(solution)/shard_map/all_gather | solution.py:697
  29.9 399.0 %reduce-scatter.3.cloned.1.call-start = ((), (), s32[]{:S(2)}) async-start(), calls=%async_computation.4 | async-start | bytes 4718592 | tf_op jit(solution)/shard_map/reduce_scatter | solution.py:784
  30.0 36.8 %collective-permute-start.1 = (bf16[6,128,1024]{2,1,0:T(8,128)(2,1)}, bf16[6,128,1024]{2,1,0:T(8,128)(2,1)}, u32[]{:S(2)}, u32[]{:S(2)}) collective-permute-start(bf16[6,128,1024]{2,1,0:T(8,128)(2,1)} %t0.1), channel_id=1, source_target_pairs={{0,16},{8,24},{16,0},{24,8},{1,17},{9,25},{17,1},{25,9},{2,18},{10... | collective-permute-start | bytes 4718600 | tf_op jit(solution)/shard_map/ppermute | solution.py:649
  30.4 61.1 %collective-permute-start = (bf16[6,128,1024]{2,1,0:T(8,128)(2,1)}, bf16[6,128,1024]{2,1,0:T(8,128)(2,1)}, u32[]{:S(2)}, u32[]{:S(2)}) collective-permute-start(bf16[6,128,1024]{2,1,0:T(8,128)(2,1)} %t0.1), channel_id=1, source_target_pairs={{0,8},{8,0},{16,24},{24,16},{1,9},{9,1},{17,25},{25,17},{2,10},{10... | collective-permute-start | bytes 4718600 | tf_op jit(solution)/shard_map/ppermute | solution.py:649
  66.8 24.7 %collective-permute-start.2 = (bf16[6,128,1024]{2,1,0:T(8,128)(2,1)}, bf16[6,128,1024]{2,1,0:T(8,128)(2,1)}, u32[]{:S(2)}, u32[]{:S(2)}) collective-permute-start(bf16[6,128,1024]{2,1,0:T(8,128)(2,1)} %collective-permute-done.1.t2), channel_id=1, source_target_pairs={{0,8},{8,0},{16,24},{24,16},{1,9},{9,1},{17,25},{25,17},{2,10},{10... | collective-permute-start | bytes 4718600 | tf_op jit(solution)/shard_map/ppermute | solution.py:649
  66.8 41.5 %collective-permute-start.4 = (bf16[6,128,1024]{2,1,0:T(8,128)(2,1)}, bf16[6,128,1024]{2,1,0:T(8,128)(2,1)}, u32[]{:S(2)}, u32[]{:S(2)}) collective-permute-start(bf16[6,128,1024]{2,1,0:T(8,128)(2,1)} %grad_ref.1), channel_id=1, source_target_pairs={{0,16},{8,24},{16,0},{24,8},{1,17},{9,25},{17,1},{25,9},{2,18},{10... | collective-permute-start | bytes 4718600 | tf_op jit(solution)/shard_map/ppermute | solution.py:649
  108.4 15.3 %collective-permute-start.5 = (bf16[1056,256]{1,0:T(8,128)(2,1)}, bf16[1056,256]{1,0:T(8,128)(2,1)S(1)}, u32[]{:S(2)}, u32[]{:S(2)}) collective-permute-start(bf16[1056,256]{1,0:T(8,128)(2,1)} %bitcast.241), channel_id=1, source_target_pairs={{0,8},{8,0},{16,24},{24,16},{1,9},{9,1},{17,25},{25,17},{2,10},{10... | collective-permute-start | bytes 1622024 | tf_op jit(solution)/shard_map/ppermute | solution.py:649
  108.4 14.9 %collective-permute-start.6 = (bf16[1056,256]{1,0:T(8,128)(2,1)}, bf16[1056,256]{1,0:T(8,128)(2,1)S(1)}, u32[]{:S(2)}, u32[]{:S(2)}) collective-permute-start(bf16[1056,256]{1,0:T(8,128)(2,1)} %bitcast.242), channel_id=1, source_target_pairs={{0,16},{8,24},{16,0},{24,8},{1,17},{9,25},{17,1},{25,9},{2,18},{10... | collective-permute-start | bytes 1622024 | tf_op jit(solution)/shard_map/ppermute | solution.py:649
  110.0 17.7 %collective-permute-start.8 = (bf16[6,128,1024]{2,1,0:T(8,128)(2,1)}, bf16[6,128,1024]{2,1,0:T(8,128)(2,1)S(1)}, u32[]{:S(2)}, u32[]{:S(2)}) collective-permute-start(bf16[6,128,1024]{2,1,0:T(8,128)(2,1)} %grad_ref.1), channel_id=1, source_target_pairs={{0,8},{8,0},{16,24},{24,16},{1,9},{9,1},{17,25},{25,17},{2,10},{10... | collective-permute-start | bytes 4718600 | tf_op jit(solution)/shard_map/ppermute | solution.py:649
  110.1 18.7 %collective-permute-start.9 = (bf16[6,128,1024]{2,1,0:T(8,128)(2,1)}, bf16[6,128,1024]{2,1,0:T(8,128)(2,1)S(1)}, u32[]{:S(2)}, u32[]{:S(2)}) collective-permute-start(bf16[6,128,1024]{2,1,0:T(8,128)(2,1)} %collective-permute-done.4.g2), channel_id=1, source_target_pairs={{0,8},{8,0},{16,24},{24,16},{1,9},{9,1},{17,25},{25,17},{2,10},{10... | collective-permute-start | bytes 4718600 | tf_op jit(solution)/shard_map/ppermute | solution.py:649
  114.0 45.9 %collective-permute-start.3 = (bf16[864,512]{1,0:T(8,128)(2,1)S(1)}, bf16[864,512]{1,0:T(8,128)(2,1)S(1)}, u32[]{:S(2)}, u32[]{:S(2)}) collective-permute-start(bf16[864,512]{1,0:T(8,128)(2,1)S(1)} %maximum_maximum_fusion), channel_id=1, source_target_pairs={{0,1},{1,2},{2,3},{3,4},{4,5},{5,6},{6,7},{8,9},{9,10},{10,11},{11... | collective-permute-start | bytes 2654216 | tf_op jit(solution)/shard_map/ppermute | solution.py:24
  171.3 14.3 %collective-permute-start.10 = (bf16[2,512,256]{2,1,0:T(8,128)(2,1)S(1)}, bf16[2,512,256]{2,1,0:T(8,128)(2,1)S(1)}, u32[]{:S(2)}, u32[]{:S(2)}) collective-permute-start(bf16[2,512,256]{2,1,0:T(8,128)(2,1)S(1)} %copy-done.27), channel_id=1, source_target_pairs={{0,16},{8,24},{16,0},{24,8},{1,17},{9,25},{17,1},{25,9},{2,18},{10... | collective-permute-start | bytes 1572872 | tf_op jit(solution)/shard_map/ppermute | solution.py:649
  185.6 15.0 %collective-permute-start.15 = (bf16[2,512,256]{2,1,0:T(8,128)(2,1)}, bf16[2,512,256]{2,1,0:T(8,128)(2,1)S(1)}, u32[]{:S(2)}, u32[]{:S(2)}) collective-permute-start(bf16[2,512,256]{2,1,0:T(8,128)(2,1)} %get-tuple-element.93), channel_id=1, source_target_pairs={{0,16},{8,24},{16,0},{24,8},{1,17},{9,25},{17,1},{25,9},{2,18},{10... | collective-permute-start | bytes 1572872 | tf_op jit(solution)/shard_map/ppermute | solution.py:649
  195.4 15.3 %collective-permute-start.16 = (bf16[2,512,256]{2,1,0:T(8,128)(2,1)}, bf16[2,512,256]{2,1,0:T(8,128)(2,1)S(1)}, u32[]{:S(2)}, u32[]{:S(2)}) collective-permute-start(bf16[2,512,256]{2,1,0:T(8,128)(2,1)} %get-tuple-element.95), channel_id=1, source_target_pairs={{0,16},{8,24},{16,0},{24,8},{1,17},{9,25},{17,1},{25,9},{2,18},{10... | collective-permute-start | bytes 1572872 | tf_op jit(solution)/shard_map/ppermute | solution.py:649
  275.8 278.1 %reduce-scatter.5.cloned.1.call-start = ((), (), s32[]{:S(2)}) async-start(), calls=%async_computation.5 | async-start | bytes 4423680 | tf_op jit(solution)/shard_map/reduce_scatter | solution.py:913
  275.9 62.9 %collective-permute-start.21 = (bf16[2,6,128,1024]{3,2,1,0:T(8,128)(2,1)}, bf16[2,6,128,1024]{3,2,1,0:T(8,128)(2,1)}, u32[]{:S(2)}, u32[]{:S(2)}) collective-permute-start(bf16[2,6,128,1024]{3,2,1,0:T(8,128)(2,1)} %get-tuple-element.103), channel_id=1, source_target_pairs={{0,8},{8,0},{16,24},{24,16},{1,9},{9,1},{17,25},{25,17},{2,10},{10... | collective-permute-start | bytes 9437192 | tf_op jit(solution)/shard_map/ppermute | solution.py:649
  285.8 36.7 %collective-permute-start.23 = (bf16[6,128,1024]{2,1,0:T(8,128)(2,1)}, bf16[6,128,1024]{2,1,0:T(8,128)(2,1)}, u32[]{:S(2)}, u32[]{:S(2)}) collective-permute-start(bf16[6,128,1024]{2,1,0:T(8,128)(2,1)} %fusion.20), channel_id=1, source_target_pairs={{0,16},{8,24},{16,0},{24,8},{1,17},{9,25},{17,1},{25,9},{2,18},{10... | collective-permute-start | bytes 4718600 | tf_op jit(solution)/shard_map/ppermute | solution.py:649
  337.9 18.0 %collective-permute-start.27 = (bf16[6,128,256]{2,1,0:T(8,128)(2,1)S(1)}, bf16[6,128,256]{2,1,0:T(8,128)(2,1)S(1)}, u32[]{:S(2)}, u32[]{:S(2)}) collective-permute-start(bf16[6,128,256]{2,1,0:T(8,128)(2,1)S(1)} %copy-done.39), channel_id=1, source_target_pairs={{0,24},{8,16},{16,8},{24,0},{1,25},{9,17},{17,9},{25,1},{2,26},{10... | collective-permute-start | bytes 1179656 | tf_op jit(solution)/shard_map/ppermute | solution.py:649
  396.4 32.5 %collective-permute-start.29 = (bf16[1216,512]{1,0:T(8,128)(2,1)}, bf16[1216,512]{1,0:T(8,128)(2,1)}, u32[]{:S(2)}, u32[]{:S(2)}) collective-permute-start(bf16[1216,512]{1,0:T(8,128)(2,1)} %get-tuple-element.124), channel_id=1, source_target_pairs={{1,0},{2,1},{3,2},{4,3},{5,4},{6,5},{7,6},{9,8},{10,9},{11,10},{12... | collective-permute-start | bytes 3735560 | tf_op jit(solution)/shard_map/ppermute | solution.py:24
  401.3 14.7 %collective-permute-start.28 = (bf16[256,1024]{1,0:T(8,128)(2,1)S(1)}, bf16[256,1024]{1,0:T(8,128)(2,1)S(1)}, u32[]{:S(2)}, u32[]{:S(2)}) collective-permute-start(bf16[256,1024]{1,0:T(8,128)(2,1)S(1)} %copy-done.29), channel_id=1, source_target_pairs={{0,16},{8,24},{16,0},{24,8},{1,17},{9,25},{17,1},{25,9},{2,18},{10... | collective-permute-start | bytes 1572872 | tf_op jit(solution)/shard_map/ppermute | solution.py:649
  408.1 53.5 %collective-permute-start.32 = (bf16[6,128,1024]{2,1,0:T(8,128)(2,1)}, bf16[6,128,1024]{2,1,0:T(8,128)(2,1)}, u32[]{:S(2)}, u32[]{:S(2)}) collective-permute-start(bf16[6,128,1024]{2,1,0:T(8,128)(2,1)} %fusion.19), channel_id=1, source_target_pairs={{0,16},{8,24},{16,0},{24,8},{1,17},{9,25},{17,1},{25,9},{2,18},{10... | collective-permute-start | bytes 4718600 | tf_op jit(solution)/shard_map/ppermute | solution.py:649
  444.0 17.3 %collective-permute-start.31 = (bf16[1056,256]{1,0:T(8,128)(2,1)S(1)}, bf16[1056,256]{1,0:T(8,128)(2,1)S(1)}, u32[]{:S(2)}, u32[]{:S(2)}) collective-permute-start(bf16[1056,256]{1,0:T(8,128)(2,1)S(1)} %fusion.36), channel_id=1, source_target_pairs={{0,16},{8,24},{16,0},{24,8},{1,17},{9,25},{17,1},{25,9},{2,18},{10... | collective-permute-start | bytes 1622024 | tf_op jit(solution)/shard_map/ppermute | solution.py:649
  492.6 36.8 %collective-permute-start.34 = (bf16[6,128,1024]{2,1,0:T(8,128)(2,1)}, bf16[6,128,1024]{2,1,0:T(8,128)(2,1)}, u32[]{:S(2)}, u32[]{:S(2)}) collective-permute-start(bf16[6,128,1024]{2,1,0:T(8,128)(2,1)} %fusion.21), channel_id=1, source_target_pairs={{0,16},{8,24},{16,0},{24,8},{1,17},{9,25},{17,1},{25,9},{2,18},{10... | collective-permute-start | bytes 4718600 | tf_op jit(solution)/shard_map/ppermute | solution.py:649
  (68 other events, 651.4 us)
Sparse Core Ops, SparseCore 0:
  23.4 62.0 all-gather.4
  87.7 108.4 all-gather.6
  275.9 86.3 reduce-scatter.2
  469.2 84.7 reduce-scatter.4

commit v12 on v11

--- a/solution.py
+++ b/solution.py
@@ -814,7 +814,9 @@
         none, head_cols,
     )
     back, f_far = lax.optimization_barrier((back, f_far))
-    got_back = passed_along(back, "blk", -1)
+    got_back = passed_along(back[: window * pad_rows], "blk", -1)
+    mem_back, got_back = lax.optimization_barrier((back[window * pad_rows :], got_back))
+    got_mem = passed_along(mem_back, "blk", -1)
     f_far = head_swap(f_far, 2)
     grad_hidden = grad_hidden.reshape(token_count, width)
     normed = normed.reshape(full_count, width)
@@ -834,9 +836,7 @@
         (wq_rows, wo_rows, got_back, first_sum)
     )
     got_back = got_back.astype(jnp.float32)
-    last_pair = (held + got_back[window * pad_rows :]).astype(bf16)
-    grad_pair = jnp.concatenate([pair_done, last_pair[None]], 0)
-    got_comp = got_back[: window * pad_rows].reshape(window, pad_rows, 2 * head_cols)
+    got_comp = got_back.reshape(window, pad_rows, 2 * head_cols)
     comp_pair_grad = jnp.pad(rest, ((0, seg_count - rest.shape[0]), (0, 0), (0, 0))) + jnp.pad(
         got_comp, ((seg_count - window, 0), (0, 0), (0, 0))
     )
@@ -845,14 +845,19 @@
         comp_grad_rows, wkv, COLS_IN, preferred_element_type=jnp.float32
     ).astype(bf16)
 
-    grad_packed_part, grad_pair = lax.optimization_barrier((grad_packed_part, grad_pair))
-
     def columns_of(bits):
         start = jnp.bitwise_xor(head_index, bits) * head_cols
         return lax.dynamic_slice_in_dim(grad_packed_part, start, head_cols, 1)
 
-    grad_packed = sum_over_heads(
-        (columns_of(0), columns_of(2)), jnp.stack([columns_of(1), columns_of(3)])
+    packed_got = head_swap(jnp.stack([columns_of(1), columns_of(3)]), 1).astype(jnp.float32)
+    packed_far = (columns_of(2).astype(jnp.float32) + packed_got[1]).astype(bf16)
+    got_mem, _ = lax.optimization_barrier((got_mem, packed_far))
+    last_pair = (held + got_mem.astype(jnp.float32)).astype(bf16)
+    grad_pair = jnp.concatenate([pair_done, last_pair[None]], 0)
+    grad_packed = (
+        columns_of(0).astype(jnp.float32)
+        + packed_got[0]
+        + head_swap(packed_far, 2).astype(jnp.float32)
     ).astype(bf16)
     grad_packed, f_far = lax.optimization_barrier((grad_packed, f_far))
     out_tokens = (

time: 587 us -> 606 us (1.032)
    ppermute x33, waiting for transfers between devices: 176 us -> 187 us  [head_swap(): lax.ppermute(value, 'head', [(source, source ^ bit) for source in range(c...]
    unnamed x125 -> x131, local copies, waits for them, and re-layouts: 21.4 us -> 19.4 us
    ppermute x2 -> x3, waiting for transfers between devices: 31 us -> 29.2 us  [passed_along(): lax.ppermute(value, axis, [(source, source + steps) for source in range(l...]
  transfers between devices with their start and end apart: 40 -> 41, of which waited for: 23 -> 23; matrix products, arithmetic and copies ran while one was open for 16% -> 16% of each run, Pallas kernels for 18% -> 18%
where the time goes in v12:
time: 606 us; the launch traced here: 596 us
  waiting for transfers between devices  252 us (42%)
  Pallas kernels  166 us (27%)
  local copies, waits for them, and re-layouts  52.9 us (9%)
  other arithmetic  44 us (7%)
  matrix products  28.3 us (5%)
  starting transfers between devices  27 us (4%)
  between operations  15.3 us (3%)
  blocking collectives  10.9 us (2%)
    ppermute x33, waiting for transfers between devices, head_swap(): lax.ppermute(value, 'head', [(source, source ^ bit) for source in range(c...  187 us
    pallas_call x1, Pallas kernels, feed_forward(): pl.pallas_call(ffn_kernel, grid=(count,), in_specs=[pl.BlockSpec(memory_s...  59.5 us
    pallas_call x1, Pallas kernels, attend_bwd(): pl.pallas_call(functools.partial(bwd_kernel, first), grid=(count,), in_sp...  39.6 us
    ppermute x3, waiting for transfers between devices, passed_along(): lax.ppermute(value, axis, [(source, source + steps) for source in range(l...  29.2 us
    pallas_call x3, Pallas kernels, attend_fwd(): pl.pallas_call(functools.partial(fwd_kernel, first, shift), grid=(count,)...  26.8 us
    unnamed x131, local copies, waits for them, and re-layouts  19.4 us
    all_gather x1, waiting for transfers between devices, per_device(): first_all = lax.all_gather(columns, 'blk', axis=0)  17 us
    pallas_call x1, Pallas kernels, prepare(): pl.pallas_call(prep_kernel, grid=(seg_count,), in_specs=[pl.BlockSpec(mem...  16.8 us
  transfers between devices with their start and end apart: 41, of which 23 were waited for; matrix products, arithmetic and copies ran while one was open for 16% of the time, Pallas kernels for 18%

profile of v12, /device:TPU:24, one launch (start us, length us, event | category | flops | bytes accessed | tf_op | source)
XLA Modules:
  0.0 596.0 jit_solution(13743109457489092890)
XLA Ops:
  12.4 10.9 %all_to_all.10 = bf16[4,208,256]{2,1,0:T(8,128)(2,1)} all-to-all(bf16[4,208,256]{2,1,0:T(8,128)(2,1)S(1)} %copy.246), channel_id=1, replica_groups=mesh['head'=4,'blk'=8] {'head'}, dimensions={0} | all-to-all | bytes 851968 | tf_op jit(solution)/shard_map/all_to_all | solution.py:694
  30.4 36.4 %collective-permute-done.1.t2 = bf16[6,128,1024]{2,1,0:T(8,128)(2,1)} collective-permute-done((bf16[6,128,1024]{2,1,0:T(8,128)(2,1)}, bf16[6,128,1024]{2,1,0:T(8,128)(2,1)}, u32[]{:S(2)}, u32[]{:S(2)}) %collective-permute-start.1) | collective-permute-done | bytes 1572896 | tf_op jit(solution)/shard_map/ppermute | solution.py:649
  68.6 17.0 %all-gather.5.cloned.1.call-done = bf16[32,208,256]{2,1,0:T(8,128)(2,1)} async-done(((bf16[4,208,256]{2,1,0:T(8,128)(2,1)}), bf16[32,208,256]{2,1,0:T(8,128)(2,1)}) %all-gather.5.cloned.1.call-update) | async-done | bytes 3407888 | tf_op jit(solution)/shard_map/all_gather | solution.py:696
  91.5 16.8 %prepare.1 = (bf16[6,512,768]{2,1,0:T(8,128)(2,1)}, bf16[6,512,1024]{2,1,0:T(8,128)(2,1)}, bf16[6,176,3072]{2,1,0:T(8,128)(2,1)}, bf16[6,176,256]{2,1,0:T(8,128)(2,1)}) custom-call(s32[1]{0:T(128)} %bitcast.head_ref, bf16[6,128,1024]{2,1,0:T(8,128)(2,1)} %t0.1, bf16[6,128,1024]{2,1,0:T(8,128)(2,1)} %collective-permute-done.t1, ...), custom_call_target="tpu_custom_call" | custom-call | flops 7000000000 | bytes 30000000 | tf_op jit(solution)/shard_map/prepare/pallas_call | solution.py:397
  116.4 6.9 %collective-permute-done.6 = bf16[1056,256]{1,0:T(8,128)(2,1)S(1)} collective-permute-done((bf16[1056,256]{1,0:T(8,128)(2,1)}, bf16[1056,256]{1,0:T(8,128)(2,1)S(1)}, u32[]{:S(2)}, u32[]{:S(2)}) %collective-permute-start.6) | collective-permute-done | bytes 540704 | tf_op jit(solution)/shard_map/ppermute | solution.py:649
  130.0 8.9 %attend_fwd.3 = (bf16[2,512,256]{2,1,0:T(8,128)(2,1)}, f32[2,2,512]{2,1,0:T(2,128)}) custom-call(s32[6]{0:T(128)} %fusion.50.place_ref, f32[2]{0:T(128)} %exponential_multiply_fusion.slope_ref, bf16[6,512,768]{2,1,0:T(8,128)(2,1)} %get-tuple-element.81.q_ref.own_ref.prev_ref, bf16[6,512,768]{2,1,0:T(8,128)(2,1)} %get-tuple-element.81.q_ref.own_ref.prev_ref, ...), custom_call_target="tpu_custom_call" | custom-call | flops 2000000000 | bytes 6000000 | tf_op jit(solution)/shard_map/attend_fwd/pallas_call | solution.py:230
  138.9 20.9 %collective-permute-done.3 = bf16[864,512]{1,0:T(8,128)(2,1)S(1)} collective-permute-done((bf16[864,512]{1,0:T(8,128)(2,1)S(1)}, bf16[864,512]{1,0:T(8,128)(2,1)S(1)}, u32[]{:S(2)}, u32[]{:S(2)}) %collective-permute-start.3) | collective-permute-done | bytes 884768 | tf_op jit(solution)/shard_map/ppermute | solution.py:24
  162.2 8.2 %collective-permute-done.12 = bf16[704,256]{1,0:T(8,128)(2,1)S(1)} collective-permute-done((bf16[704,256]{1,0:T(8,128)(2,1)S(1)}, bf16[704,256]{1,0:T(8,128)(2,1)S(1)}, u32[]{:S(2)}, u32[]{:S(2)}) %collective-permute-start.12) | collective-permute-done | bytes 360480 | tf_op jit(solution)/shard_map/ppermute | solution.py:649
  174.8 8.9 %attend_fwd.4 = (bf16[2,512,256]{2,1,0:T(8,128)(2,1)}, f32[2,2,512]{2,1,0:T(2,128)}) custom-call(s32[6]{0:T(128)} %fusion.50.place_ref, f32[2]{0:T(128)} %exponential_multiply_fusion.slope_ref, bf16[6,512,768]{2,1,0:T(8,128)(2,1)} %get-tuple-element.81.q_ref.own_ref.prev_ref, bf16[6,512,768]{2,1,0:T(8,128)(2,1)} %get-tuple-element.81.q_ref.own_ref.prev_ref, ...), custom_call_target="tpu_custom_call" | custom-call | flops 2000000000 | bytes 6000000 | tf_op jit(solution)/shard_map/attend_fwd/pallas_call | solution.py:230
  186.3 8.9 %attend_fwd.5 = (bf16[2,512,256]{2,1,0:T(8,128)(2,1)}, f32[2,2,512]{2,1,0:T(2,128)}) custom-call(s32[6]{0:T(128)} %fusion.50.place_ref, f32[2]{0:T(128)} %exponential_multiply_fusion.slope_ref, bf16[6,512,768]{2,1,0:T(8,128)(2,1)} %get-tuple-element.81.q_ref.own_ref.prev_ref, bf16[6,512,768]{2,1,0:T(8,128)(2,1)} %get-tuple-element.81.q_ref.own_ref.prev_ref, ...), custom_call_target="tpu_custom_call" | custom-call | flops 2000000000 | bytes 6000000 | tf_op jit(solution)/shard_map/attend_fwd/pallas_call | solution.py:230
  201.4 9.3 %collective-permute-done.16 = bf16[2,512,256]{2,1,0:T(8,128)(2,1)S(1)} collective-permute-done((bf16[2,512,256]{2,1,0:T(8,128)(2,1)}, bf16[2,512,256]{2,1,0:T(8,128)(2,1)S(1)}, u32[]{:S(2)}, u32[]{:S(2)}) %collective-permute-start.16) | collective-permute-done | bytes 524320 | tf_op jit(solution)/shard_map/ppermute | solution.py:649
  216.0 59.5 %feed_forward.1 = (bf16[2,6,128,1024]{3,2,1,0:T(8,128)(2,1)}, bf16[2,6,128,1024]{3,2,1,0:T(8,128)(2,1)}, bf16[2,6,128,1024]{3,2,1,0:T(8,128)(2,1)}, bf16[2,6,128...) custom-call(s32[1]{0:T(128)} %bitcast.head_ref, ...), custom_call_target="tpu_custom_call" | custom-call | flops 44999999488 | bytes 50000000 | tf_op jit(solution)/shard_map/feed_forward/pallas_call | solution.py:516
  286.2 36.2 %collective-permute-done.23.far_ref = bf16[6,128,1024]{2,1,0:T(8,128)(2,1)} collective-permute-done((bf16[6,128,1024]{2,1,0:T(8,128)(2,1)}, bf16[6,128,1024]{2,1,0:T(8,128)(2,1)}, u32[]{:S(2)}, u32[]{:S(2)}) %collective-permute-start.23) | collective-permute-done | bytes 1572896 | tf_op jit(solution)/shard_map/ppermute | solution.py:649
  322.5 9.4 %middle.1 = (f32[6,128,1024]{2,1,0:T(8,128)}, bf16[6,128,1024]{2,1,0:T(8,128)(2,1)}, f32[1,1024]{1,0:T(1,128)}, bf16[6,128,256]{2,1,0:T(8,128)(2,1)}, bf16[6,128...) custom-call(bf16[2,6,128,1024]{3,2,1,0:T(8,128)(2,1)} %get-tuple-element.105.keep_ref, ...), custom_call_target="tpu_custom_call" | custom-call | flops 1620000000 | bytes 24000000 | tf_op jit(solution)/shard_map/middle/pallas_call | solution.py:584
  350.3 6.7 %collective-permute-done.27.g3 = bf16[6,128,256]{2,1,0:T(8,128)(2,1)S(1)} collective-permute-done((bf16[6,128,256]{2,1,0:T(8,128)(2,1)S(1)}, bf16[6,128,256]{2,1,0:T(8,128)(2,1)S(1)}, u32[]{:S(2)}, u32[]{:S(2)}) %collective-permute-start.27) | collective-permute-done | bytes 393248 | tf_op jit(solution)/shard_map/ppermute | solution.py:649
  358.4 39.6 %attend_bwd.1 = (bf16[6,512,256]{2,1,0:T(8,128)(2,1)}, bf16[5,512,512]{2,1,0:T(8,128)(2,1)}, f32[512,512]{1,0:T(8,128)}, f32[4,176,512]{2,1,0:T(8,128)}, bf16[1216,512]{1,0:T(8,128)(2,1)}) custom-call(s32[6]{0:T(128)} %fusion.50.place_ref, f32[2]{0:T(128)} %exponential_multiply_fusion.slope_ref, ...), custom_call_target="tpu_custom_call" | custom-call | flops 12000000000 | bytes 24000000 | tf_op jit(solution)/shard_map/attend_bwd/pallas_call | solution.py:266
  410.8 8.1 %collective-permute-done.28 = bf16[256,1024]{1,0:T(8,128)(2,1)S(1)} collective-permute-done((bf16[256,1024]{1,0:T(8,128)(2,1)S(1)}, bf16[256,1024]{1,0:T(8,128)(2,1)S(1)}, u32[]{:S(2)}, u32[]{:S(2)}) %collective-permute-start.28) | collective-permute-done | bytes 524320 | tf_op jit(solution)/shard_map/ppermute | solution.py:649
  440.6 8.3 %collective-permute-done.33 = bf16[512,512]{1,0:T(8,128)(2,1)S(1)} collective-permute-done((bf16[512,512]{1,0:T(8,128)(2,1)}, bf16[512,512]{1,0:T(8,128)(2,1)S(1)}, u32[]{:S(2)}, u32[]{:S(2)}) %collective-permute-start.33) | collective-permute-done | bytes 524320 | tf_op jit(solution)/shard_map/ppermute | solution.py:24
  449.1 5.9 fusion.18
  456.9 23.4 %collective-permute-done.31 = bf16[1056,256]{1,0:T(8,128)(2,1)S(1)} collective-permute-done((bf16[1056,256]{1,0:T(8,128)(2,1)S(1)}, bf16[1056,256]{1,0:T(8,128)(2,1)S(1)}, u32[]{:S(2)}, u32[]{:S(2)}) %collective-permute-start.31) | collective-permute-done | bytes 540704 | tf_op jit(solution)/shard_map/ppermute | solution.py:649
  491.3 13.8 %g_normed.1 = (bf16[2,6,128,1024]{3,2,1,0:T(8,128)(2,1)}, bf16[2,6,128,1024]{3,2,1,0:T(8,128)(2,1)}) custom-call(s32[1]{0:T(128)} %bitcast.head_ref, bf16[6,512,256]{2,1,0:T(8,128)(2,1)} %get-tuple-element.121.gq_ref, bf16[6,512,512]{2,1,0:T(8,128)(2,1)} %pad_maximum_fusion.gkv_ref, bf16[6,176,256]{2,1,0:T(8,128)(2,1)} %bitcast.249, ...), custom_call_target="tpu_custom_call" | custom-call | flops 7000000000 | bytes 20000000 | tf_op jit(solution)/shard_map/g_normed/pallas_call | solution.py:625
  521.2 5.9 fusion.15
  527.1 24.5 %collective-permute-done.35 = bf16[6,128,1024]{2,1,0:T(8,128)(2,1)} collective-permute-done((bf16[6,128,1024]{2,1,0:T(8,128)(2,1)}, bf16[6,128,1024]{2,1,0:T(8,128)(2,1)}, u32[]{:S(2)}, u32[]{:S(2)}) %collective-permute-start.35) | collective-permute-done | bytes 1572896 | tf_op jit(solution)/shard_map/ppermute | solution.py:649
  555.4 16.8 %reduce-scatter.5.cloned.1.call-done = bf16[960,256]{1,0:T(8,128)(2,1)} async-done(((bf16[7680,256]{1,0:T(8,128)(2,1)}), bf16[960,256]{1,0:T(8,128)(2,1)}) %reduce-scatter.5.cloned.1.call-update) | async-done | bytes 491536 | tf_op jit(solution)/shard_map/reduce_scatter | solution.py:918
  (319 shorter events, 169.5 us)
Async XLA Ops:
  7.2 78.4 %all-gather.5.cloned.1.call-start = ((), (), s32[]{:S(2)}) async-start(), calls=%async_computation.6 | async-start | bytes 3833856 | tf_op jit(solution)/shard_map/all_gather | solution.py:696
  23.3 192.7 %all-gather.7.cloned.1.call-start = ((), (), s32[]{:S(2)}) async-start(), calls=%async_computation.7 | async-start | bytes 7077888 | tf_op jit(solution)/shard_map/all_gather | solution.py:697
  29.9 395.6 %reduce-scatter.3.cloned.1.call-start = ((), (), s32[]{:S(2)}) async-start(), calls=%async_computation.4 | async-start | bytes 4718592 | tf_op jit(solution)/shard_map/reduce_scatter | solution.py:784
  30.0 36.8 %collective-permute-start.1 = (bf16[6,128,1024]{2,1,0:T(8,128)(2,1)}, bf16[6,128,1024]{2,1,0:T(8,128)(2,1)}, u32[]{:S(2)}, u32[]{:S(2)}) collective-permute-start(bf16[6,128,1024]{2,1,0:T(8,128)(2,1)} %t0.1), channel_id=1, source_target_pairs={{0,16},{8,24},{16,0},{24,8},{1,17},{9,25},{17,1},{25,9},{2,18},{10... | collective-permute-start | bytes 4718600 | tf_op jit(solution)/shard_map/ppermute | solution.py:649
  30.4 61.1 %collective-permute-start = (bf16[6,128,1024]{2,1,0:T(8,128)(2,1)}, bf16[6,128,1024]{2,1,0:T(8,128)(2,1)}, u32[]{:S(2)}, u32[]{:S(2)}) collective-permute-start(bf16[6,128,1024]{2,1,0:T(8,128)(2,1)} %t0.1), channel_id=1, source_target_pairs={{0,8},{8,0},{16,24},{24,16},{1,9},{9,1},{17,25},{25,17},{2,10},{10... | collective-permute-start | bytes 4718600 | tf_op jit(solution)/shard_map/ppermute | solution.py:649
  66.8 24.7 %collective-permute-start.2 = (bf16[6,128,1024]{2,1,0:T(8,128)(2,1)}, bf16[6,128,1024]{2,1,0:T(8,128)(2,1)}, u32[]{:S(2)}, u32[]{:S(2)}) collective-permute-start(bf16[6,128,1024]{2,1,0:T(8,128)(2,1)} %collective-permute-done.1.t2), channel_id=1, source_target_pairs={{0,8},{8,0},{16,24},{24,16},{1,9},{9,1},{17,25},{25,17},{2,10},{10... | collective-permute-start | bytes 4718600 | tf_op jit(solution)/shard_map/ppermute | solution.py:649
  66.8 41.5 %collective-permute-start.4 = (bf16[6,128,1024]{2,1,0:T(8,128)(2,1)}, bf16[6,128,1024]{2,1,0:T(8,128)(2,1)}, u32[]{:S(2)}, u32[]{:S(2)}) collective-permute-start(bf16[6,128,1024]{2,1,0:T(8,128)(2,1)} %grad_ref.1), channel_id=1, source_target_pairs={{0,16},{8,24},{16,0},{24,8},{1,17},{9,25},{17,1},{25,9},{2,18},{10... | collective-permute-start | bytes 4718600 | tf_op jit(solution)/shard_map/ppermute | solution.py:649
  108.4 15.3 %collective-permute-start.5 = (bf16[1056,256]{1,0:T(8,128)(2,1)}, bf16[1056,256]{1,0:T(8,128)(2,1)S(1)}, u32[]{:S(2)}, u32[]{:S(2)}) collective-permute-start(bf16[1056,256]{1,0:T(8,128)(2,1)} %bitcast.240), channel_id=1, source_target_pairs={{0,8},{8,0},{16,24},{24,16},{1,9},{9,1},{17,25},{25,17},{2,10},{10... | collective-permute-start | bytes 1622024 | tf_op jit(solution)/shard_map/ppermute | solution.py:649
  108.4 14.9 %collective-permute-start.6 = (bf16[1056,256]{1,0:T(8,128)(2,1)}, bf16[1056,256]{1,0:T(8,128)(2,1)S(1)}, u32[]{:S(2)}, u32[]{:S(2)}) collective-permute-start(bf16[1056,256]{1,0:T(8,128)(2,1)} %bitcast.241), channel_id=1, source_target_pairs={{0,16},{8,24},{16,0},{24,8},{1,17},{9,25},{17,1},{25,9},{2,18},{10... | collective-permute-start | bytes 1622024 | tf_op jit(solution)/shard_map/ppermute | solution.py:649
  110.0 17.7 %collective-permute-start.8 = (bf16[6,128,1024]{2,1,0:T(8,128)(2,1)}, bf16[6,128,1024]{2,1,0:T(8,128)(2,1)S(1)}, u32[]{:S(2)}, u32[]{:S(2)}) collective-permute-start(bf16[6,128,1024]{2,1,0:T(8,128)(2,1)} %grad_ref.1), channel_id=1, source_target_pairs={{0,8},{8,0},{16,24},{24,16},{1,9},{9,1},{17,25},{25,17},{2,10},{10... | collective-permute-start | bytes 4718600 | tf_op jit(solution)/shard_map/ppermute | solution.py:649
  110.1 18.6 %collective-permute-start.9 = (bf16[6,128,1024]{2,1,0:T(8,128)(2,1)}, bf16[6,128,1024]{2,1,0:T(8,128)(2,1)S(1)}, u32[]{:S(2)}, u32[]{:S(2)}) collective-permute-start(bf16[6,128,1024]{2,1,0:T(8,128)(2,1)} %collective-permute-done.4.g2), channel_id=1, source_target_pairs={{0,8},{8,0},{16,24},{24,16},{1,9},{9,1},{17,25},{25,17},{2,10},{10... | collective-permute-start | bytes 4718600 | tf_op jit(solution)/shard_map/ppermute | solution.py:649
  113.9 45.8 %collective-permute-start.3 = (bf16[864,512]{1,0:T(8,128)(2,1)S(1)}, bf16[864,512]{1,0:T(8,128)(2,1)S(1)}, u32[]{:S(2)}, u32[]{:S(2)}) collective-permute-start(bf16[864,512]{1,0:T(8,128)(2,1)S(1)} %maximum_maximum_fusion), channel_id=1, source_target_pairs={{0,1},{1,2},{2,3},{3,4},{4,5},{5,6},{6,7},{8,9},{9,10},{10,11},{11... | collective-permute-start | bytes 2654216 | tf_op jit(solution)/shard_map/ppermute | solution.py:24
  185.5 15.0 %collective-permute-start.15 = (bf16[2,512,256]{2,1,0:T(8,128)(2,1)}, bf16[2,512,256]{2,1,0:T(8,128)(2,1)S(1)}, u32[]{:S(2)}, u32[]{:S(2)}) collective-permute-start(bf16[2,512,256]{2,1,0:T(8,128)(2,1)} %get-tuple-element.94), channel_id=1, source_target_pairs={{0,16},{8,24},{16,0},{24,8},{1,17},{9,25},{17,1},{25,9},{2,18},{10... | collective-permute-start | bytes 1572872 | tf_op jit(solution)/shard_map/ppermute | solution.py:649
  195.3 15.3 %collective-permute-start.16 = (bf16[2,512,256]{2,1,0:T(8,128)(2,1)}, bf16[2,512,256]{2,1,0:T(8,128)(2,1)S(1)}, u32[]{:S(2)}, u32[]{:S(2)}) collective-permute-start(bf16[2,512,256]{2,1,0:T(8,128)(2,1)} %get-tuple-element.96), channel_id=1, source_target_pairs={{0,16},{8,24},{16,0},{24,8},{1,17},{9,25},{17,1},{25,9},{2,18},{10... | collective-permute-start | bytes 1572872 | tf_op jit(solution)/shard_map/ppermute | solution.py:649
  275.7 296.5 %reduce-scatter.5.cloned.1.call-start = ((), (), s32[]{:S(2)}) async-start(), calls=%async_computation.5 | async-start | bytes 4423680 | tf_op jit(solution)/shard_map/reduce_scatter | solution.py:918
  275.8 64.0 %collective-permute-start.21 = (bf16[2,6,128,1024]{3,2,1,0:T(8,128)(2,1)}, bf16[2,6,128,1024]{3,2,1,0:T(8,128)(2,1)}, u32[]{:S(2)}, u32[]{:S(2)}) collective-permute-start(bf16[2,6,128,1024]{3,2,1,0:T(8,128)(2,1)} %get-tuple-element.104), channel_id=1, source_target_pairs={{0,8},{8,0},{16,24},{24,16},{1,9},{9,1},{17,25},{25,17},{2,10},{10... | collective-permute-start | bytes 9437192 | tf_op jit(solution)/shard_map/ppermute | solution.py:649
  285.7 36.7 %collective-permute-start.23 = (bf16[6,128,1024]{2,1,0:T(8,128)(2,1)}, bf16[6,128,1024]{2,1,0:T(8,128)(2,1)}, u32[]{:S(2)}, u32[]{:S(2)}) collective-permute-start(bf16[6,128,1024]{2,1,0:T(8,128)(2,1)} %fusion.20), channel_id=1, source_target_pairs={{0,16},{8,24},{16,0},{24,8},{1,17},{9,25},{17,1},{25,9},{2,18},{10... | collective-permute-start | bytes 4718600 | tf_op jit(solution)/shard_map/ppermute | solution.py:649
  338.9 18.1 %collective-permute-start.27 = (bf16[6,128,256]{2,1,0:T(8,128)(2,1)S(1)}, bf16[6,128,256]{2,1,0:T(8,128)(2,1)S(1)}, u32[]{:S(2)}, u32[]{:S(2)}) collective-permute-start(bf16[6,128,256]{2,1,0:T(8,128)(2,1)S(1)} %copy-done.44), channel_id=1, source_target_pairs={{0,24},{8,16},{16,8},{24,0},{1,25},{9,17},{17,9},{25,1},{2,26},{10... | collective-permute-start | bytes 1179656 | tf_op jit(solution)/shard_map/ppermute | solution.py:649
  402.0 23.4 %collective-permute-start.29 = (bf16[704,512]{1,0:T(8,128)(2,1)}, bf16[704,512]{1,0:T(8,128)(2,1)}, u32[]{:S(2)}, u32[]{:S(2)}) collective-permute-start(bf16[704,512]{1,0:T(8,128)(2,1)} %slice.200), channel_id=1, source_target_pairs={{1,0},{2,1},{3,2},{4,3},{5,4},{6,5},{7,6},{9,8},{10,9},{11,10},{12... | collective-permute-start | bytes 2162696 | tf_op jit(solution)/shard_map/ppermute | solution.py:24
  404.2 14.7 %collective-permute-start.28 = (bf16[256,1024]{1,0:T(8,128)(2,1)S(1)}, bf16[256,1024]{1,0:T(8,128)(2,1)S(1)}, u32[]{:S(2)}, u32[]{:S(2)}) collective-permute-start(bf16[256,1024]{1,0:T(8,128)(2,1)S(1)} %copy-done.34), channel_id=1, source_target_pairs={{0,16},{8,24},{16,0},{24,8},{1,17},{9,25},{17,1},{25,9},{2,18},{10... | collective-permute-start | bytes 1572872 | tf_op jit(solution)/shard_map/ppermute | solution.py:649
  432.0 48.5 %collective-permute-start.32 = (bf16[6,128,1024]{2,1,0:T(8,128)(2,1)}, bf16[6,128,1024]{2,1,0:T(8,128)(2,1)S(1)}, u32[]{:S(2)}, u32[]{:S(2)}) collective-permute-start(bf16[6,128,1024]{2,1,0:T(8,128)(2,1)} %fusion.19), channel_id=1, source_target_pairs={{0,16},{8,24},{16,0},{24,8},{1,17},{9,25},{17,1},{25,9},{2,18},{10... | collective-permute-start | bytes 4718600 | tf_op jit(solution)/shard_map/ppermute | solution.py:649
  432.5 16.4 %collective-permute-start.33 = (bf16[512,512]{1,0:T(8,128)(2,1)}, bf16[512,512]{1,0:T(8,128)(2,1)S(1)}, u32[]{:S(2)}, u32[]{:S(2)}) collective-permute-start(bf16[512,512]{1,0:T(8,128)(2,1)} %slice.199), channel_id=1, source_target_pairs={{1,0},{2,1},{3,2},{4,3},{5,4},{6,5},{7,6},{9,8},{10,9},{11,10},{12... | collective-permute-start | bytes 1572872 | tf_op jit(solution)/shard_map/ppermute | solution.py:24
  439.8 40.4 %collective-permute-start.31 = (bf16[1056,256]{1,0:T(8,128)(2,1)S(1)}, bf16[1056,256]{1,0:T(8,128)(2,1)S(1)}, u32[]{:S(2)}, u32[]{:S(2)}) collective-permute-start(bf16[1056,256]{1,0:T(8,128)(2,1)S(1)} %fusion.36), channel_id=1, source_target_pairs={{0,16},{8,24},{16,0},{24,8},{1,17},{9,25},{17,1},{25,9},{2,18},{10... | collective-permute-start | bytes 1622024 | tf_op jit(solution)/shard_map/ppermute | solution.py:649
  514.8 36.8 %collective-permute-start.35 = (bf16[6,128,1024]{2,1,0:T(8,128)(2,1)}, bf16[6,128,1024]{2,1,0:T(8,128)(2,1)}, u32[]{:S(2)}, u32[]{:S(2)}) collective-permute-start(bf16[6,128,1024]{2,1,0:T(8,128)(2,1)} %fusion.21), channel_id=1, source_target_pairs={{0,16},{8,24},{16,0},{24,8},{1,17},{9,25},{17,1},{25,9},{2,18},{10... | collective-permute-start | bytes 4718600 | tf_op jit(solution)/shard_map/ppermute | solution.py:649
  (72 other events, 712.9 us)
Sparse Core Ops, SparseCore 0:
  23.4 62.0 all-gather.4
  87.7 108.4 all-gather.6
  275.9 86.1 reduce-scatter.2
  487.7 84.4 reduce-scatter.4

commit v13 on v12

--- a/solution.py
+++ b/solution.py
@@ -813,11 +813,9 @@
         0, seg_count, head, seg_place, slopes, heads, recv_mem, comp_ext, mixed, attn_out, lse, none,
         none, head_cols,
     )
-    back, f_far = lax.optimization_barrier((back, f_far))
     got_back = passed_along(back[: window * pad_rows], "blk", -1)
     mem_back, got_back = lax.optimization_barrier((back[window * pad_rows :], got_back))
     got_mem = passed_along(mem_back, "blk", -1)
-    f_far = head_swap(f_far, 2)
     grad_hidden = grad_hidden.reshape(token_count, width)
     normed = normed.reshape(full_count, width)
     grad_wq = lax.dot_general(
@@ -859,7 +857,8 @@
         + packed_got[0]
         + head_swap(packed_far, 2).astype(jnp.float32)
     ).astype(bf16)
-    grad_packed, f_far = lax.optimization_barrier((grad_packed, f_far))
+    f_far, grad_packed = lax.optimization_barrier((f_far, grad_packed))
+    f_far = head_swap(f_far, 2)
     out_tokens = (
         hidden + f_keep[0].astype(jnp.float32) + f_got[0].astype(jnp.float32) + f_far.astype(jnp.float32)
     ).astype(bf16)

time: 606 us -> 589 us (0.972)
  waiting for transfers between devices: 252 us -> 236 us
    reduce_scatter x1, waiting for transfers between devices: 16.8 us -> 0.01 us  [per_device(): lax.psum_scatter(second_grads.reshape(-1, head_cols), 'blk', scatter_dime...]
    unnamed x131 -> x129, local copies, waits for them, and re-layouts: 19.4 us -> 20.6 us
  transfers between devices with their start and end apart: 41 -> 41, of which waited for: 23 -> 22; matrix products, arithmetic and copies ran while one was open for 16% -> 16% of each run, Pallas kernels for 18% -> 18%
where the time goes in v13:
time: 589 us; the launch traced here: 581 us
  waiting for transfers between devices  236 us (40%)
  Pallas kernels  166 us (28%)
  local copies, waits for them, and re-layouts  54 us (9%)
  other arithmetic  44 us (7%)
  matrix products  28.6 us (5%)
  starting transfers between devices  27 us (5%)
  between operations  15.3 us (3%)
  blocking collectives  10.9 us (2%)
    ppermute x33, waiting for transfers between devices, head_swap(): lax.ppermute(value, 'head', [(source, source ^ bit) for source in range(c...  188 us
    pallas_call x1, Pallas kernels, feed_forward(): pl.pallas_call(ffn_kernel, grid=(count,), in_specs=[pl.BlockSpec(memory_s...  59.5 us
    pallas_call x1, Pallas kernels, attend_bwd(): pl.pallas_call(functools.partial(bwd_kernel, first), grid=(count,), in_sp...  39.6 us
    ppermute x3, waiting for transfers between devices, passed_along(): lax.ppermute(value, axis, [(source, source + steps) for source in range(l...  29.5 us
    pallas_call x3, Pallas kernels, attend_fwd(): pl.pallas_call(functools.partial(fwd_kernel, first, shift), grid=(count,)...  26.7 us
    unnamed x129, local copies, waits for them, and re-layouts  20.6 us
    all_gather x1, waiting for transfers between devices, per_device(): first_all = lax.all_gather(columns, 'blk', axis=0)  17 us
    pallas_call x1, Pallas kernels, prepare(): pl.pallas_call(prep_kernel, grid=(seg_count,), in_specs=[pl.BlockSpec(mem...  16.8 us
  transfers between devices with their start and end apart: 41, of which 22 were waited for; matrix products, arithmetic and copies ran while one was open for 16% of the time, Pallas kernels for 18%

profile of v13, /device:TPU:24, one launch (start us, length us, event | category | flops | bytes accessed | tf_op | source)
XLA Modules:
  0.0 581.2 jit_solution(1760669002309639205)
XLA Ops:
  12.4 10.9 %all_to_all.10 = bf16[4,208,256]{2,1,0:T(8,128)(2,1)} all-to-all(bf16[4,208,256]{2,1,0:T(8,128)(2,1)S(1)} %copy.246), channel_id=1, replica_groups=mesh['head'=4,'blk'=8] {'head'}, dimensions={0} | all-to-all | bytes 851968 | tf_op jit(solution)/shard_map/all_to_all | solution.py:694
  30.4 36.4 %collective-permute-done.1.t2 = bf16[6,128,1024]{2,1,0:T(8,128)(2,1)} collective-permute-done((bf16[6,128,1024]{2,1,0:T(8,128)(2,1)}, bf16[6,128,1024]{2,1,0:T(8,128)(2,1)}, u32[]{:S(2)}, u32[]{:S(2)}) %collective-permute-start.1) | collective-permute-done | bytes 1572896 | tf_op jit(solution)/shard_map/ppermute | solution.py:649
  68.5 17.0 %all-gather.5.cloned.1.call-done = bf16[32,208,256]{2,1,0:T(8,128)(2,1)} async-done(((bf16[4,208,256]{2,1,0:T(8,128)(2,1)}), bf16[32,208,256]{2,1,0:T(8,128)(2,1)}) %all-gather.5.cloned.1.call-update) | async-done | bytes 3407888 | tf_op jit(solution)/shard_map/all_gather | solution.py:696
  91.5 16.8 %prepare.1 = (bf16[6,512,768]{2,1,0:T(8,128)(2,1)}, bf16[6,512,1024]{2,1,0:T(8,128)(2,1)}, bf16[6,176,3072]{2,1,0:T(8,128)(2,1)}, bf16[6,176,256]{2,1,0:T(8,128)(2,1)}) custom-call(s32[1]{0:T(128)} %bitcast.head_ref, bf16[6,128,1024]{2,1,0:T(8,128)(2,1)} %t0.1, bf16[6,128,1024]{2,1,0:T(8,128)(2,1)} %collective-permute-done.t1, ...), custom_call_target="tpu_custom_call" | custom-call | flops 7000000000 | bytes 30000000 | tf_op jit(solution)/shard_map/prepare/pallas_call | solution.py:397
  116.4 6.9 %collective-permute-done.6 = bf16[1056,256]{1,0:T(8,128)(2,1)S(1)} collective-permute-done((bf16[1056,256]{1,0:T(8,128)(2,1)}, bf16[1056,256]{1,0:T(8,128)(2,1)S(1)}, u32[]{:S(2)}, u32[]{:S(2)}) %collective-permute-start.6) | collective-permute-done | bytes 540704 | tf_op jit(solution)/shard_map/ppermute | solution.py:649
  129.9 8.9 %attend_fwd.3 = (bf16[2,512,256]{2,1,0:T(8,128)(2,1)}, f32[2,2,512]{2,1,0:T(2,128)}) custom-call(s32[6]{0:T(128)} %fusion.50.place_ref, f32[2]{0:T(128)} %exponential_multiply_fusion.slope_ref, bf16[6,512,768]{2,1,0:T(8,128)(2,1)} %get-tuple-element.79.q_ref.own_ref.prev_ref, bf16[6,512,768]{2,1,0:T(8,128)(2,1)} %get-tuple-element.79.q_ref.own_ref.prev_ref, ...), custom_call_target="tpu_custom_call" | custom-call | flops 2000000000 | bytes 6000000 | tf_op jit(solution)/shard_map/attend_fwd/pallas_call | solution.py:230
  138.9 20.9 %collective-permute-done.3 = bf16[864,512]{1,0:T(8,128)(2,1)S(1)} collective-permute-done((bf16[864,512]{1,0:T(8,128)(2,1)S(1)}, bf16[864,512]{1,0:T(8,128)(2,1)S(1)}, u32[]{:S(2)}, u32[]{:S(2)}) %collective-permute-start.3) | collective-permute-done | bytes 884768 | tf_op jit(solution)/shard_map/ppermute | solution.py:24
  162.2 8.1 %collective-permute-done.12 = bf16[704,256]{1,0:T(8,128)(2,1)S(1)} collective-permute-done((bf16[704,256]{1,0:T(8,128)(2,1)S(1)}, bf16[704,256]{1,0:T(8,128)(2,1)S(1)}, u32[]{:S(2)}, u32[]{:S(2)}) %collective-permute-start.12) | collective-permute-done | bytes 360480 | tf_op jit(solution)/shard_map/ppermute | solution.py:649
  174.8 8.9 %attend_fwd.4 = (bf16[2,512,256]{2,1,0:T(8,128)(2,1)}, f32[2,2,512]{2,1,0:T(2,128)}) custom-call(s32[6]{0:T(128)} %fusion.50.place_ref, f32[2]{0:T(128)} %exponential_multiply_fusion.slope_ref, bf16[6,512,768]{2,1,0:T(8,128)(2,1)} %get-tuple-element.79.q_ref.own_ref.prev_ref, bf16[6,512,768]{2,1,0:T(8,128)(2,1)} %get-tuple-element.79.q_ref.own_ref.prev_ref, ...), custom_call_target="tpu_custom_call" | custom-call | flops 2000000000 | bytes 6000000 | tf_op jit(solution)/shard_map/attend_fwd/pallas_call | solution.py:230
  186.3 8.9 %attend_fwd.5 = (bf16[2,512,256]{2,1,0:T(8,128)(2,1)}, f32[2,2,512]{2,1,0:T(2,128)}) custom-call(s32[6]{0:T(128)} %fusion.50.place_ref, f32[2]{0:T(128)} %exponential_multiply_fusion.slope_ref, bf16[6,512,768]{2,1,0:T(8,128)(2,1)} %get-tuple-element.79.q_ref.own_ref.prev_ref, bf16[6,512,768]{2,1,0:T(8,128)(2,1)} %get-tuple-element.79.q_ref.own_ref.prev_ref, ...), custom_call_target="tpu_custom_call" | custom-call | flops 2000000000 | bytes 6000000 | tf_op jit(solution)/shard_map/attend_fwd/pallas_call | solution.py:230
  201.3 9.3 %collective-permute-done.16 = bf16[2,512,256]{2,1,0:T(8,128)(2,1)S(1)} collective-permute-done((bf16[2,512,256]{2,1,0:T(8,128)(2,1)}, bf16[2,512,256]{2,1,0:T(8,128)(2,1)S(1)}, u32[]{:S(2)}, u32[]{:S(2)}) %collective-permute-start.16) | collective-permute-done | bytes 524320 | tf_op jit(solution)/shard_map/ppermute | solution.py:649
  216.0 59.5 %feed_forward.1 = (bf16[2,6,128,1024]{3,2,1,0:T(8,128)(2,1)}, bf16[2,6,128,1024]{3,2,1,0:T(8,128)(2,1)}, bf16[2,6,128,1024]{3,2,1,0:T(8,128)(2,1)}, bf16[2,6,128...) custom-call(s32[1]{0:T(128)} %bitcast.head_ref, ...), custom_call_target="tpu_custom_call" | custom-call | flops 44999999488 | bytes 50000000 | tf_op jit(solution)/shard_map/feed_forward/pallas_call | solution.py:516
  276.2 5.4 collective-permute-done.22.got_ref
  286.2 36.2 %collective-permute-done.23.far_ref = bf16[6,128,1024]{2,1,0:T(8,128)(2,1)} collective-permute-done((bf16[6,128,1024]{2,1,0:T(8,128)(2,1)}, bf16[6,128,1024]{2,1,0:T(8,128)(2,1)}, u32[]{:S(2)}, u32[]{:S(2)}) %collective-permute-start.23) | collective-permute-done | bytes 1572896 | tf_op jit(solution)/shard_map/ppermute | solution.py:649
  322.4 9.4 %middle.1 = (f32[6,128,1024]{2,1,0:T(8,128)}, bf16[6,128,1024]{2,1,0:T(8,128)(2,1)}, f32[1,1024]{1,0:T(1,128)}, bf16[6,128,256]{2,1,0:T(8,128)(2,1)}, bf16[6,128...) custom-call(bf16[2,6,128,1024]{3,2,1,0:T(8,128)(2,1)} %get-tuple-element.103.keep_ref, ...), custom_call_target="tpu_custom_call" | custom-call | flops 1620000000 | bytes 24000000 | tf_op jit(solution)/shard_map/middle/pallas_call | solution.py:584
  350.3 6.7 %collective-permute-done.27.g3 = bf16[6,128,256]{2,1,0:T(8,128)(2,1)S(1)} collective-permute-done((bf16[6,128,256]{2,1,0:T(8,128)(2,1)S(1)}, bf16[6,128,256]{2,1,0:T(8,128)(2,1)S(1)}, u32[]{:S(2)}, u32[]{:S(2)}) %collective-permute-start.27) | collective-permute-done | bytes 393248 | tf_op jit(solution)/shard_map/ppermute | solution.py:649
  358.3 39.6 %attend_bwd.1 = (bf16[6,512,256]{2,1,0:T(8,128)(2,1)}, bf16[5,512,512]{2,1,0:T(8,128)(2,1)}, f32[512,512]{1,0:T(8,128)}, f32[4,176,512]{2,1,0:T(8,128)}, bf16[1216,512]{1,0:T(8,128)(2,1)}) custom-call(s32[6]{0:T(128)} %fusion.50.place_ref, f32[2]{0:T(128)} %exponential_multiply_fusion.slope_ref, ...), custom_call_target="tpu_custom_call" | custom-call | flops 12000000000 | bytes 24000000 | tf_op jit(solution)/shard_map/attend_bwd/pallas_call | solution.py:266
  410.5 8.1 %collective-permute-done.28 = bf16[256,1024]{1,0:T(8,128)(2,1)S(1)} collective-permute-done((bf16[256,1024]{1,0:T(8,128)(2,1)S(1)}, bf16[256,1024]{1,0:T(8,128)(2,1)S(1)}, u32[]{:S(2)}, u32[]{:S(2)}) %collective-permute-start.28) | collective-permute-done | bytes 524320 | tf_op jit(solution)/shard_map/ppermute | solution.py:649
  439.7 8.6 %collective-permute-done.33 = bf16[512,512]{1,0:T(8,128)(2,1)S(1)} collective-permute-done((bf16[512,512]{1,0:T(8,128)(2,1)}, bf16[512,512]{1,0:T(8,128)(2,1)S(1)}, u32[]{:S(2)}, u32[]{:S(2)}) %collective-permute-start.33) | collective-permute-done | bytes 524320 | tf_op jit(solution)/shard_map/ppermute | solution.py:24
  448.5 6.2 %fusion.18 = (f32[1024]{0:T(1024)S(1)}, f32[1024,512,1]{1,0,2:T(8,128)S(1)}) fusion(bf16[1024,256]{1,0:T(8,128)(2,1)S(1)} %bitcast.257, bf16[1024,256]{1,0:T(8,128)(2,1)S(1)} %bitcast.253, bf16[6,512,1024]{2,1,0:T(8,128)(2,1)} %get-tuple-element.119, bf16[1,512,512]{2,1,0:T(8,128)(2,1)S(1)} %fusion.41, bf16[5,512,512]{2,1,0:T(8,128)(2,1)S(1)} %copy-done.8), kind=kOutput, calls=%fused_computation.33 | convolution fusion | flops 3225943040 | bytes 12587008 | tf_op jit(solution)/shard_map/dot_general | solution.py:881
  468.9 13.8 %g_normed.1 = (bf16[2,6,128,1024]{3,2,1,0:T(8,128)(2,1)}, bf16[2,6,128,1024]{3,2,1,0:T(8,128)(2,1)}) custom-call(s32[1]{0:T(128)} %bitcast.head_ref, bf16[6,512,256]{2,1,0:T(8,128)(2,1)} %get-tuple-element.120.gq_ref, bf16[6,512,512]{2,1,0:T(8,128)(2,1)} %pad_maximum_fusion.gkv_ref, bf16[6,176,256]{2,1,0:T(8,128)(2,1)} %bitcast.249, ...), custom_call_target="tpu_custom_call" | custom-call | flops 7000000000 | bytes 20000000 | tf_op jit(solution)/shard_map/g_normed/pallas_call | solution.py:625
  498.9 21.5 %collective-permute-done.32 = bf16[6,128,1024]{2,1,0:T(8,128)(2,1)} collective-permute-done((bf16[6,128,1024]{2,1,0:T(8,128)(2,1)}, bf16[6,128,1024]{2,1,0:T(8,128)(2,1)}, u32[]{:S(2)}, u32[]{:S(2)}) %collective-permute-start.32) | collective-permute-done | bytes 1572896 | tf_op jit(solution)/shard_map/ppermute | solution.py:649
  520.3 5.7 fusion.15
  526.0 27.5 %collective-permute-done.35 = bf16[6,128,1024]{2,1,0:T(8,128)(2,1)} collective-permute-done((bf16[6,128,1024]{2,1,0:T(8,128)(2,1)}, bf16[6,128,1024]{2,1,0:T(8,128)(2,1)}, u32[]{:S(2)}, u32[]{:S(2)}) %collective-permute-start.35) | collective-permute-done | bytes 1572896 | tf_op jit(solution)/shard_map/ppermute | solution.py:649
  (317 shorter events, 164.8 us)
Async XLA Ops:
  7.2 78.4 %all-gather.5.cloned.1.call-start = ((), (), s32[]{:S(2)}) async-start(), calls=%async_computation.6 | async-start | bytes 3833856 | tf_op jit(solution)/shard_map/all_gather | solution.py:696
  23.3 192.7 %all-gather.7.cloned.1.call-start = ((), (), s32[]{:S(2)}) async-start(), calls=%async_computation.7 | async-start | bytes 7077888 | tf_op jit(solution)/shard_map/all_gather | solution.py:697
  29.9 395.2 %reduce-scatter.3.cloned.1.call-start = ((), (), s32[]{:S(2)}) async-start(), calls=%async_computation.4 | async-start | bytes 4718592 | tf_op jit(solution)/shard_map/reduce_scatter | solution.py:784
  30.0 36.8 %collective-permute-start.1 = (bf16[6,128,1024]{2,1,0:T(8,128)(2,1)}, bf16[6,128,1024]{2,1,0:T(8,128)(2,1)}, u32[]{:S(2)}, u32[]{:S(2)}) collective-permute-start(bf16[6,128,1024]{2,1,0:T(8,128)(2,1)} %t0.1), channel_id=1, source_target_pairs={{0,16},{8,24},{16,0},{24,8},{1,17},{9,25},{17,1},{25,9},{2,18},{10... | collective-permute-start | bytes 4718600 | tf_op jit(solution)/shard_map/ppermute | solution.py:649
  30.4 61.1 %collective-permute-start = (bf16[6,128,1024]{2,1,0:T(8,128)(2,1)}, bf16[6,128,1024]{2,1,0:T(8,128)(2,1)}, u32[]{:S(2)}, u32[]{:S(2)}) collective-permute-start(bf16[6,128,1024]{2,1,0:T(8,128)(2,1)} %t0.1), channel_id=1, source_target_pairs={{0,8},{8,0},{16,24},{24,16},{1,9},{9,1},{17,25},{25,17},{2,10},{10... | collective-permute-start | bytes 4718600 | tf_op jit(solution)/shard_map/ppermute | solution.py:649
  66.8 24.7 %collective-permute-start.2 = (bf16[6,128,1024]{2,1,0:T(8,128)(2,1)}, bf16[6,128,1024]{2,1,0:T(8,128)(2,1)}, u32[]{:S(2)}, u32[]{:S(2)}) collective-permute-start(bf16[6,128,1024]{2,1,0:T(8,128)(2,1)} %collective-permute-done.1.t2), channel_id=1, source_target_pairs={{0,8},{8,0},{16,24},{24,16},{1,9},{9,1},{17,25},{25,17},{2,10},{10... | collective-permute-start | bytes 4718600 | tf_op jit(solution)/shard_map/ppermute | solution.py:649
  66.8 41.5 %collective-permute-start.4 = (bf16[6,128,1024]{2,1,0:T(8,128)(2,1)}, bf16[6,128,1024]{2,1,0:T(8,128)(2,1)}, u32[]{:S(2)}, u32[]{:S(2)}) collective-permute-start(bf16[6,128,1024]{2,1,0:T(8,128)(2,1)} %grad_ref.1), channel_id=1, source_target_pairs={{0,16},{8,24},{16,0},{24,8},{1,17},{9,25},{17,1},{25,9},{2,18},{10... | collective-permute-start | bytes 4718600 | tf_op jit(solution)/shard_map/ppermute | solution.py:649
  108.3 15.3 %collective-permute-start.5 = (bf16[1056,256]{1,0:T(8,128)(2,1)}, bf16[1056,256]{1,0:T(8,128)(2,1)S(1)}, u32[]{:S(2)}, u32[]{:S(2)}) collective-permute-start(bf16[1056,256]{1,0:T(8,128)(2,1)} %bitcast.240), channel_id=1, source_target_pairs={{0,8},{8,0},{16,24},{24,16},{1,9},{9,1},{17,25},{25,17},{2,10},{10... | collective-permute-start | bytes 1622024 | tf_op jit(solution)/shard_map/ppermute | solution.py:649
  108.4 14.9 %collective-permute-start.6 = (bf16[1056,256]{1,0:T(8,128)(2,1)}, bf16[1056,256]{1,0:T(8,128)(2,1)S(1)}, u32[]{:S(2)}, u32[]{:S(2)}) collective-permute-start(bf16[1056,256]{1,0:T(8,128)(2,1)} %bitcast.241), channel_id=1, source_target_pairs={{0,16},{8,24},{16,0},{24,8},{1,17},{9,25},{17,1},{25,9},{2,18},{10... | collective-permute-start | bytes 1622024 | tf_op jit(solution)/shard_map/ppermute | solution.py:649
  110.0 17.6 %collective-permute-start.8 = (bf16[6,128,1024]{2,1,0:T(8,128)(2,1)}, bf16[6,128,1024]{2,1,0:T(8,128)(2,1)S(1)}, u32[]{:S(2)}, u32[]{:S(2)}) collective-permute-start(bf16[6,128,1024]{2,1,0:T(8,128)(2,1)} %grad_ref.1), channel_id=1, source_target_pairs={{0,8},{8,0},{16,24},{24,16},{1,9},{9,1},{17,25},{25,17},{2,10},{10... | collective-permute-start | bytes 4718600 | tf_op jit(solution)/shard_map/ppermute | solution.py:649
  110.1 18.6 %collective-permute-start.9 = (bf16[6,128,1024]{2,1,0:T(8,128)(2,1)}, bf16[6,128,1024]{2,1,0:T(8,128)(2,1)S(1)}, u32[]{:S(2)}, u32[]{:S(2)}) collective-permute-start(bf16[6,128,1024]{2,1,0:T(8,128)(2,1)} %collective-permute-done.4.g2), channel_id=1, source_target_pairs={{0,8},{8,0},{16,24},{24,16},{1,9},{9,1},{17,25},{25,17},{2,10},{10... | collective-permute-start | bytes 4718600 | tf_op jit(solution)/shard_map/ppermute | solution.py:649
  113.9 45.8 %collective-permute-start.3 = (bf16[864,512]{1,0:T(8,128)(2,1)S(1)}, bf16[864,512]{1,0:T(8,128)(2,1)S(1)}, u32[]{:S(2)}, u32[]{:S(2)}) collective-permute-start(bf16[864,512]{1,0:T(8,128)(2,1)S(1)} %maximum_maximum_fusion), channel_id=1, source_target_pairs={{0,1},{1,2},{2,3},{3,4},{4,5},{5,6},{6,7},{8,9},{9,10},{10,11},{11... | collective-permute-start | bytes 2654216 | tf_op jit(solution)/shard_map/ppermute | solution.py:24
  185.5 15.0 %collective-permute-start.15 = (bf16[2,512,256]{2,1,0:T(8,128)(2,1)}, bf16[2,512,256]{2,1,0:T(8,128)(2,1)S(1)}, u32[]{:S(2)}, u32[]{:S(2)}) collective-permute-start(bf16[2,512,256]{2,1,0:T(8,128)(2,1)} %get-tuple-element.92), channel_id=1, source_target_pairs={{0,16},{8,24},{16,0},{24,8},{1,17},{9,25},{17,1},{25,9},{2,18},{10... | collective-permute-start | bytes 1572872 | tf_op jit(solution)/shard_map/ppermute | solution.py:649
  195.3 15.3 %collective-permute-start.16 = (bf16[2,512,256]{2,1,0:T(8,128)(2,1)}, bf16[2,512,256]{2,1,0:T(8,128)(2,1)S(1)}, u32[]{:S(2)}, u32[]{:S(2)}) collective-permute-start(bf16[2,512,256]{2,1,0:T(8,128)(2,1)} %get-tuple-element.94), channel_id=1, source_target_pairs={{0,16},{8,24},{16,0},{24,8},{1,17},{9,25},{17,1},{25,9},{2,18},{10... | collective-permute-start | bytes 1572872 | tf_op jit(solution)/shard_map/ppermute | solution.py:649
  275.7 281.7 %reduce-scatter.5.cloned.1.call-start = ((), (), s32[]{:S(2)}) async-start(), calls=%async_computation.5 | async-start | bytes 4423680 | tf_op jit(solution)/shard_map/reduce_scatter | solution.py:917
  275.7 64.0 %collective-permute-start.21 = (bf16[2,6,128,1024]{3,2,1,0:T(8,128)(2,1)}, bf16[2,6,128,1024]{3,2,1,0:T(8,128)(2,1)}, u32[]{:S(2)}, u32[]{:S(2)}) collective-permute-start(bf16[2,6,128,1024]{3,2,1,0:T(8,128)(2,1)} %get-tuple-element.102), channel_id=1, source_target_pairs={{0,8},{8,0},{16,24},{24,16},{1,9},{9,1},{17,25},{25,17},{2,10},{10... | collective-permute-start | bytes 9437192 | tf_op jit(solution)/shard_map/ppermute | solution.py:649
  285.7 36.7 %collective-permute-start.23 = (bf16[6,128,1024]{2,1,0:T(8,128)(2,1)}, bf16[6,128,1024]{2,1,0:T(8,128)(2,1)}, u32[]{:S(2)}, u32[]{:S(2)}) collective-permute-start(bf16[6,128,1024]{2,1,0:T(8,128)(2,1)} %fusion.20), channel_id=1, source_target_pairs={{0,16},{8,24},{16,0},{24,8},{1,17},{9,25},{17,1},{25,9},{2,18},{10... | collective-permute-start | bytes 4718600 | tf_op jit(solution)/shard_map/ppermute | solution.py:649
  338.8 18.1 %collective-permute-start.27 = (bf16[6,128,256]{2,1,0:T(8,128)(2,1)S(1)}, bf16[6,128,256]{2,1,0:T(8,128)(2,1)S(1)}, u32[]{:S(2)}, u32[]{:S(2)}) collective-permute-start(bf16[6,128,256]{2,1,0:T(8,128)(2,1)S(1)} %copy-done.43), channel_id=1, source_target_pairs={{0,24},{8,16},{16,8},{24,0},{1,25},{9,17},{17,9},{25,1},{2,26},{10... | collective-permute-start | bytes 1179656 | tf_op jit(solution)/shard_map/ppermute | solution.py:649
  402.0 23.2 %collective-permute-start.29 = (bf16[704,512]{1,0:T(8,128)(2,1)}, bf16[704,512]{1,0:T(8,128)(2,1)}, u32[]{:S(2)}, u32[]{:S(2)}) collective-permute-start(bf16[704,512]{1,0:T(8,128)(2,1)} %slice.200), channel_id=1, source_target_pairs={{1,0},{2,1},{3,2},{4,3},{5,4},{6,5},{7,6},{9,8},{10,9},{11,10},{12... | collective-permute-start | bytes 2162696 | tf_op jit(solution)/shard_map/ppermute | solution.py:24
  403.9 14.7 %collective-permute-start.28 = (bf16[256,1024]{1,0:T(8,128)(2,1)S(1)}, bf16[256,1024]{1,0:T(8,128)(2,1)S(1)}, u32[]{:S(2)}, u32[]{:S(2)}) collective-permute-start(bf16[256,1024]{1,0:T(8,128)(2,1)S(1)} %copy-done.33), channel_id=1, source_target_pairs={{0,16},{8,24},{16,0},{24,8},{1,17},{9,25},{17,1},{25,9},{2,18},{10... | collective-permute-start | bytes 1572872 | tf_op jit(solution)/shard_map/ppermute | solution.py:649
  431.6 16.6 %collective-permute-start.33 = (bf16[512,512]{1,0:T(8,128)(2,1)}, bf16[512,512]{1,0:T(8,128)(2,1)S(1)}, u32[]{:S(2)}, u32[]{:S(2)}) collective-permute-start(bf16[512,512]{1,0:T(8,128)(2,1)} %slice.199), channel_id=1, source_target_pairs={{1,0},{2,1},{3,2},{4,3},{5,4},{6,5},{7,6},{9,8},{10,9},{11,10},{12... | collective-permute-start | bytes 1572872 | tf_op jit(solution)/shard_map/ppermute | solution.py:24
  438.2 18.3 %collective-permute-start.31 = (bf16[1056,256]{1,0:T(8,128)(2,1)S(1)}, bf16[1056,256]{1,0:T(8,128)(2,1)S(1)}, u32[]{:S(2)}, u32[]{:S(2)}) collective-permute-start(bf16[1056,256]{1,0:T(8,128)(2,1)S(1)} %fusion.36), channel_id=1, source_target_pairs={{0,16},{8,24},{16,0},{24,8},{1,17},{9,25},{17,1},{25,9},{2,18},{10... | collective-permute-start | bytes 1622024 | tf_op jit(solution)/shard_map/ppermute | solution.py:649
  482.7 37.6 %collective-permute-start.32 = (bf16[6,128,1024]{2,1,0:T(8,128)(2,1)}, bf16[6,128,1024]{2,1,0:T(8,128)(2,1)}, u32[]{:S(2)}, u32[]{:S(2)}) collective-permute-start(bf16[6,128,1024]{2,1,0:T(8,128)(2,1)} %fusion.19), channel_id=1, source_target_pairs={{0,16},{8,24},{16,0},{24,8},{1,17},{9,25},{17,1},{25,9},{2,18},{10... | collective-permute-start | bytes 4718600 | tf_op jit(solution)/shard_map/ppermute | solution.py:649
  492.5 61.1 %collective-permute-start.35 = (bf16[6,128,1024]{2,1,0:T(8,128)(2,1)}, bf16[6,128,1024]{2,1,0:T(8,128)(2,1)}, u32[]{:S(2)}, u32[]{:S(2)}) collective-permute-start(bf16[6,128,1024]{2,1,0:T(8,128)(2,1)} %fusion.21), channel_id=1, source_target_pairs={{0,16},{8,24},{16,0},{24,8},{1,17},{9,25},{17,1},{25,9},{2,18},{10... | collective-permute-start | bytes 4718600 | tf_op jit(solution)/shard_map/ppermute | solution.py:649
  (71 other events, 718.9 us)
Sparse Core Ops, SparseCore 0:
  23.4 62.0 all-gather.4
  87.7 108.4 all-gather.6
  275.8 86.1 reduce-scatter.2
  465.3 84.0 reduce-scatter.4
